TPU v7x, 256 devices: a whole 4x4x8 slice. The times are simulated.
256 devices in a mesh: fsdp: 32 (over y, x, core), tp: 8 (over z).
Axes of the slice: x: 4, y: 4, z: 8, core: 2. Of those that a mesh axis runs over, the one named last changes fastest.
Arguments:
- momentum: bfloat16 [8192, 26624], P('fsdp', 'tp'), may hold values from -6 to 6
- gradient: bfloat16 [8192, 26624], P('fsdp', 'tp'), may hold values from -60 to 60
- weights: bfloat16 [8192, 26624], P('fsdp', 'tp'), may hold values from -6 to 6
- subspace: float32 [26624, 128], P('tp'), may hold values from -0.0390625 to 0.0390625
Outputs:
- new_momentum: bfloat16 [8192, 26624], P('fsdp', 'tp')
- new_weights: bfloat16 [8192, 26624], P('fsdp', 'tp')
- new_subspace: float32 [26624, 128], P('tp')
All inputs are finite; a program needn't handle non-finite values.
Results may differ from a plain program's by a relative error of at most 0.012.
Values may be sent and summed in bfloat16 or wider, within the bound.
No kernel may reach another device: no remote copies, remote signals or barrier semaphores. Data moves between devices by JAX's collectives and lax.ppermute only.
A program may use at most 64 MiB of HBM per device.

v0:
```python
import math

import jax
import jax.numpy as jnp
from jax import lax
from jax.sharding import PartitionSpec as P

ROWS = 8192
COLS = 26624
RANK = 128


inertia = 0.95
step_size = 0.5
shrinkage = 0.1
epsilon_sq = 1e-06


def orthonormalize(projected, gram_matrix):
    factor = jnp.linalg.cholesky(gram_matrix)
    return lax.linalg.triangular_solve(
        factor, projected, left_side=False, lower=True, transpose_a=True
    )


def on_device(momentum, gradient, weights, subspace):
    blended = (momentum.astype(jnp.float32) + gradient.astype(jnp.float32)).astype(jnp.bfloat16)
    lowered = subspace.astype(jnp.bfloat16)
    partial_proj = jnp.dot(blended, lowered, preferred_element_type=jnp.float32)
    projected = lax.psum(partial_proj, "tp")
    local_gram = jnp.dot(
        projected.T, projected, precision=lax.Precision.HIGHEST, preferred_element_type=jnp.float32
    )
    gram_matrix = lax.psum(local_gram, "fsdp")
    ortho_rounded = orthonormalize(projected, gram_matrix).astype(jnp.bfloat16)
    partial_coef = lax.dot_general(
        blended, ortho_rounded, (((0,), (0,)), ((), ())), preferred_element_type=jnp.float32
    )
    coefficients = lax.psum(partial_coef, "fsdp")
    col_squares = lax.psum(jnp.sum(coefficients * coefficients, axis=0), "tp")
    coeff_rounded = coefficients.astype(jnp.bfloat16)
    feedback = jnp.dot(ortho_rounded, coeff_rounded.T, preferred_element_type=jnp.float32)
    new_momentum = (blended.astype(jnp.float32) - (1.0 - inertia) * feedback).astype(jnp.bfloat16)
    new_subspace = coefficients / jnp.sqrt(col_squares + epsilon_sq)
    update = jnp.dot(
        ortho_rounded, new_subspace.astype(jnp.bfloat16).T, preferred_element_type=jnp.float32
    )
    scaling = math.sqrt(ROWS * COLS / RANK)
    new_weights = (
        weights.astype(jnp.float32) * (1.0 - step_size * shrinkage) - step_size * scaling * update
    ).astype(jnp.bfloat16)
    return (new_momentum, new_weights, new_subspace)


def solution(mesh):
    placed = (P("fsdp", "tp"), P("fsdp", "tp"), P("fsdp", "tp"), P("tp", None))
    return jax.shard_map(
        on_device,
        mesh=mesh,
        in_specs=placed,
        out_specs=(P("fsdp", "tp"), P("fsdp", "tp"), P("tp", None)),
        check_vma=False,
    )
```

profile of v0, /device:TPU:1, one launch (start us, length us, event | category | flops | bytes accessed | tf_op | source)
XLA Modules:
  0.0 367.6 jit_solution(17855046913591598423)
XLA Ops:
  7.2 0.0 all-reduce.4.cloned.1.call-start
  7.2 0.0 copy-start
  7.2 0.0 copy-start.1
  7.2 3.9 %fusion.6 = f32[256,128]{1,0:T(8,128)} fusion(f32[3328,128]{1,0:T(8,128)} %param.7, bf16[256,3328]{1,0:T(8,128)(2,1)} %param.5, bf16[256,3328]{1,0:T(8,128)(2,1)} %param.4), kind=kOutput, calls=%fused_computation.12 | convolution fusion | flops 221937664 | bytes 5242880 | tf_op jit(solution)/shard_map/dot_general | solution.py:29
  11.2 0.0 all-reduce.4.cloned.1.call-update
  11.2 0.0 all-reduce.6.cloned.1.call-start
  11.2 70.8 %all-reduce.4.cloned.1.call-done = f32[256,128]{1,0:T(8,128)} async-done(((f32[256,128]{1,0:T(8,128)}), f32[256,128]{1,0:T(8,128)}) %all-reduce.4.cloned.1.call-update) | async-done | bytes 131088 | tf_op jit(solution)/shard_map/psum | solution.py:30
  82.0 2.0 fusion.12
  84.0 0.0 all-reduce.6.cloned.1.call-update
  84.0 0.0 all-reduce.8.cloned.1.call-start
  84.1 111.6 %all-reduce.6.cloned.1.call-done = f32[128,128]{0,1:T(8,128)} async-done(((f32[128,128]{0,1:T(8,128)}), f32[128,128]{0,1:T(8,128)}) %all-reduce.6.cloned.1.call-update) | async-done | bytes 65552 | tf_op jit(solution)/shard_map/psum | solution.py:34
  195.7 0.9 copy.8
  196.6 0.9 fusion.10
  197.5 11.7 %cholesky.16 = f32[128,128]{1,0:T(8,128)S(1)} custom-call(f32[128,128]{1,0:T(8,128)S(1)} %fusion.10), custom_call_target="Cholesky" | custom-call | tf_op jit(solution)/shard_map/jit(cholesky)/cholesky | solution.py:20
  209.2 0.6 compare_reduce_fusion
  209.9 0.7 fusion.8
  210.5 10.4 %custom-call.6 = f32[1,128,128]{1,2,0:T(8,128)} custom-call(f32[1,128,128]{2,1,0:T(8,128)S(1)} %fusion.8), custom_call_target="InvertDiagBlocksLowerTriangular" | custom-call | tf_op jit(solution)/shard_map/triangular_solve | solution.py:21
  221.0 1.2 convolution_convert_fusion
  222.1 0.0 copy-done
  222.2 0.0 copy-done.1
  222.2 1.8 fusion.11
  224.0 0.0 all-reduce.8.cloned.1.call-update
  224.0 114.7 %all-reduce.8.cloned.1.call-done = f32[3328,128]{1,0:T(8,128)} async-done(((f32[3328,128]{1,0:T(8,128)}), f32[3328,128]{1,0:T(8,128)}) %all-reduce.8.cloned.1.call-update) | async-done | bytes 1703952 | tf_op jit(solution)/shard_map/psum | solution.py:39
  338.8 1.9 multiply_reduce_fusion
  340.7 13.7 %psum.31 = f32[128]{0:T(128)S(1)} all-reduce(f32[128]{0:T(128)S(1)} %multiply_reduce_fusion), channel_id=1, replica_groups=mesh['fsdp'=32,'tp'=8] {'tp'}, use_global_device_ids=true, to_apply=%region_6.7 | all-reduce | flops 128 | bytes 1024 | tf_op jit(solution)/shard_map/psum | solution.py:40
  354.4 0.0 copy-start.4
  354.4 1.7 broadcast_divide_fusion
  356.1 0.3 copy-done.4
  356.4 1.9 fusion.3
  358.3 0.0 copy-done.3
  358.3 0.8 copy-done.2
  359.0 2.0 fusion.2
  (4 shorter events, 0.0 us)
Async XLA Ops:
  7.2 74.9 %all-reduce.4.cloned.1.call-start = ((), (), s32[]{:S(2)}) async-start(), calls=%async_computation | async-start | bytes 262144 | tf_op jit(solution)/shard_map/psum | solution.py:30
  7.2 214.9 %copy-start = (bf16[256,3328]{1,0:T(8,128)(2,1)S(1)}, bf16[256,3328]{1,0:T(8,128)(2,1)}, u32[]{:S(2)}) copy-start(bf16[256,3328]{1,0:T(8,128)(2,1)} %param.5) | copy-start | bytes 5111812
  7.2 214.9 %copy-start.1 = (bf16[256,3328]{1,0:T(8,128)(2,1)S(1)}, bf16[256,3328]{1,0:T(8,128)(2,1)}, u32[]{:S(2)}) copy-start(bf16[256,3328]{1,0:T(8,128)(2,1)} %param.4) | copy-start | bytes 5111812
  11.2 184.5 %all-reduce.6.cloned.1.call-start = ((), (), s32[]{:S(2)}) async-start(), calls=%async_computation.1 | async-start | bytes 131072 | tf_op jit(solution)/shard_map/psum | solution.py:34
  84.0 254.7 %all-reduce.8.cloned.1.call-start = ((), (), s32[]{:S(2)}) async-start(), calls=%async_computation.2 | async-start | bytes 3407872 | tf_op jit(solution)/shard_map/psum | solution.py:39
  354.4 2.0 copy-start.4
  356.4 1.9 copy-start.3
  356.4 2.7 copy-start.2
Sparse Core Ops, SparseCore 0:
  11.3 70.6 all-reduce.3
  86.2 109.4 all-reduce.5
  224.2 114.5 all-reduce.7
where the time goes:
time: 372 us; the launch traced here: 368 us
  waiting for transfers between devices  297 us (80%)
  other arithmetic  28 us (8%)
  between operations  13.8 us (4%)
  blocking collectives  13.7 us (4%)
  matrix products  12.8 us (3%)
    psum x1, waiting for transfers between devices, on_device(): coefficients = lax.psum(partial_coef, 'fsdp')  115 us
    psum x1, waiting for transfers between devices, on_device(): gram_matrix = lax.psum(local_gram, 'fsdp')  112 us
    psum x1, waiting for transfers between devices, on_device(): projected = lax.psum(partial_proj, 'tp')  70.8 us
    psum x1, blocking collectives, on_device(): col_squares = lax.psum(jnp.sum(coefficients * coefficients, axis=0), 'tp')  13.7 us
    another operation x3, other arithmetic, orthonormalize(): factor = jnp.linalg.cholesky(gram_matrix)  12.4 us
    another operation x2, other arithmetic, orthonormalize(): lax.linalg.triangular_solve(factor, projected, left_side=False, lower=Tru...  11.1 us
  transfers between devices with their start and end apart: 3, of which 3 were waited for; matrix products, arithmetic and copies ran while one was open for 0% of the time, Pallas kernels for 0%

commit v1 on v0

v1 whole, which is shorter than its diff:
```python
import functools
import math

import jax
import jax.numpy as jnp
from jax import lax
from jax.experimental import pallas as pl
from jax.experimental.pallas import tpu as pltpu
from jax.sharding import PartitionSpec as P

ROWS = 8192
COLS = 26624
RANK = 128

inertia = 0.95
step_size = 0.5
shrinkage = 0.1
epsilon_sq = 1e-06

LOCAL_ROWS = 256
LOCAL_COLS = 3328
TP = 8
FSDP = 32
HALF = LOCAL_COLS // 2
CHUNK = HALF // 4
PIECE = HALF // 8
CUT = 40
WIDE = 256
TILES = LOCAL_COLS // WIDE
STRIPS = ((0, 512), (512, 768), (1280, 768), (2048, 768), (2816, 512))

X_ONE, Y_ONE, X_THREE, Y_THREE, CORE = 3, 9, 7, 25, 1
MASKS = ((X_ONE, X_THREE, Y_ONE, Y_THREE), (Y_ONE, Y_THREE, X_ONE, X_THREE))


def team(f):
    return (f % 2 + f // 2 + f // 8) % 2


Z_PAIRS = (
    ((0, 1), (2, 3), (4, 5), (6, 7)),
    ((1, 2), (3, 4), (5, 6), (7, 0)),
    ((2, 5), (1, 6), (4, 7), (3, 0)),
)

VMEM = pltpu.VMEM
VMEM_SPEC = pl.BlockSpec(memory_space=pltpu.VMEM)
HBM_SPEC = pl.BlockSpec(memory_space=pltpu.HBM)
PARAMS = pltpu.CompilerParams(vmem_limit_bytes=24 * 1024 * 1024)
NT = (((1,), (1,)), ((), ()))
TN = (((0,), (0,)), ((), ()))


def f32(*shape):
    return jax.ShapeDtypeStruct(shape, jnp.float32)


def bf16(*shape):
    return jax.ShapeDtypeStruct(shape, jnp.bfloat16)


def cost(flops, nbytes):
    return pl.CostEstimate(flops=flops, bytes_accessed=nbytes, transcendentals=0)


def swap_z(x, step):
    perm = []
    for f in range(FSDP):
        for a, b in Z_PAIRS[step]:
            one, two = f * TP + (a + f % 2) % TP, f * TP + (b + f % 2) % TP
            perm += [(one, two), (two, one)]
    return lax.ppermute(x, ("fsdp", "tp"), perm)


def cross_z(x, mask):
    perm = [(f * TP + z, (f ^ 1) * TP + (z ^ mask)) for f in range(FSDP) for z in range(TP)]
    return lax.ppermute(x, ("fsdp", "tp"), perm)


def xor_fsdp(x, mask):
    return lax.ppermute(x, "fsdp", [(i, i ^ mask) for i in range(FSDP)])


def xor_step(x, k):
    return lax.ppermute(x, "fsdp", [(i, i ^ MASKS[team(i)][k]) for i in range(FSDP)])


def step_bit(k):
    f = lax.axis_index("fsdp")
    place = jnp.where(team(f) == 0, (f // 2) % 4, f // 8)
    return place // 2 if k else place % 2 ^ place // 2


def project_kernel(m_hbm, g_hbm, s_hbm, b_ref, part_ref, m_buf, g_buf, s_buf, sems):
    copies = []
    for i, (start, size) in enumerate(STRIPS):
        cols = pl.ds(start, size)
        copies.append((
            pltpu.make_async_copy(m_hbm.at[:, cols], m_buf.at[:, cols], sems.at[0, i]),
            pltpu.make_async_copy(g_hbm.at[:, cols], g_buf.at[:, cols], sems.at[1, i]),
            pltpu.make_async_copy(s_hbm.at[cols, :], s_buf.at[cols, :], sems.at[2, i]),
        ))
    for trio in copies:
        for copy in trio:
            copy.start()
    for i, trio in enumerate(copies):
        for copy in trio:
            copy.wait()
        start, size = STRIPS[i]
        cols = slice(start, start + size)
        b = (m_buf[:, cols].astype(jnp.float32) + g_buf[:, cols].astype(jnp.float32)).astype(jnp.bfloat16)
        b_ref[:, cols] = b
        part = jnp.dot(b, s_buf[cols, :].astype(jnp.bfloat16), preferred_element_type=jnp.float32)
        if i == 0:
            part_ref[...] = part
        else:
            part_ref[...] += part


def project(momentum, gradient, subspace):
    momentum, gradient, subspace = [
        pltpu.with_memory_space_constraint(x, pltpu.HBM) for x in (momentum, gradient, subspace)
    ]
    return pl.pallas_call(
        project_kernel,
        in_specs=[HBM_SPEC] * 3,
        out_specs=[VMEM_SPEC] * 2,
        out_shape=[bf16(LOCAL_ROWS, LOCAL_COLS), f32(LOCAL_ROWS, RANK)],
        scratch_shapes=[
            VMEM((LOCAL_ROWS, LOCAL_COLS), jnp.bfloat16),
            VMEM((LOCAL_ROWS, LOCAL_COLS), jnp.bfloat16),
            VMEM((LOCAL_COLS, RANK), jnp.float32),
            pltpu.SemaphoreType.DMA((3, len(STRIPS))),
        ],
        compiler_params=PARAMS,
        cost_estimate=cost(2 * 256 * 3328 * 128, 7000000),
        name="project",
    )(momentum, gradient, subspace)


def local(kernel, out_shape, args, after=(), flops=0, nbytes=0, name=None, scratch=()):
    used = len(args)

    def body(*refs):
        kernel(*refs[:used], *refs[used + len(after):])

    single = not isinstance(out_shape, (list, tuple))
    return pl.pallas_call(
        body,
        in_specs=[VMEM_SPEC] * (used + len(after)),
        out_specs=VMEM_SPEC if single else [VMEM_SPEC] * len(out_shape),
        out_shape=out_shape,
        scratch_shapes=list(scratch),
        compiler_params=PARAMS,
        cost_estimate=cost(flops, nbytes),
        name=name,
    )(*args, *after)


def lift_half(p, b_ref, half, target):
    high = p.astype(jnp.bfloat16)
    low = (p - high.astype(jnp.float32)).astype(jnp.bfloat16)
    split = jnp.concatenate([high, low], axis=1)
    for k in range(HALF // 128):
        cols = pl.ds(pl.multiple_of(half * HALF + k * 128, 128), 128)
        d = lax.dot_general(b_ref[:, cols], split, TN, preferred_element_type=jnp.float32)
        target[k * 128:(k + 1) * 128, :] = d[:, :RANK] + d[:, RANK:]


def gram_kernel(p_ref, gram_ref):
    p = p_ref[...]
    gram_ref[...] = lax.dot_general(
        p, p, TN, precision=lax.Precision.HIGHEST, preferred_element_type=jnp.float32
    )


def lift_send_kernel(p_ref, b_ref, send_ref):
    c = team(lax.axis_index("fsdp"))
    lift_half(p_ref[...], b_ref, 1 - c, send_ref)


def lift_keep_kernel(p_ref, b_ref, keep_ref):
    lift_half(p_ref[...], b_ref, team(lax.axis_index("fsdp")), keep_ref)


def split_kernel(k, n, keep_ref, recv_ref, send_ref, next_ref):
    bit = step_bit(k)
    away = pl.ds(pl.multiple_of((1 - bit) * n, 8), n)
    stay = pl.ds(pl.multiple_of(bit * n, 8), n)
    send_ref[...] = keep_ref[away, :] + recv_ref[away, :]
    next_ref[...] = keep_ref[stay, :] + recv_ref[stay, :]


def split_step(k, n, keep, recv, after=()):
    return local(
        functools.partial(split_kernel, k, n), [f32(n, RANK), f32(n, RANK)], [keep, recv], after,
        flops=n * 256, nbytes=n * 2048, name=f"split{k}",
    )


def add_kernel(a_ref, b_ref, out_ref):
    out_ref[...] = a_ref[...] + b_ref[...]


def hold_kernel(a_ref, out_ref):
    out_ref[...] = a_ref[...]


def add(a, b, after, name):
    return local(add_kernel, f32(*a.shape), [a, b], after, nbytes=3 * 4 * a.size, name=name)


def reciprocal(x):
    r = pl.reciprocal(x, approx=True)
    r = r * (2.0 - x * r)
    return r * (2.0 - x * r)


def unit_scale(rows, lane, sub):
    diagonal = jnp.zeros((8, RANK), jnp.float32)
    for k, row in enumerate(rows):
        diagonal = diagonal + jnp.where(lane == sub + 8 * k, row, 0.0)
    return lax.rsqrt(jnp.sum(diagonal, axis=0, keepdims=True))


def eliminate_kernel(start, stop, in_ref, gram_ref, out_ref):
    groups = RANK // 8
    lane = lax.broadcasted_iota(jnp.int32, (8, RANK), 1)
    sub = lax.broadcasted_iota(jnp.int32, (8, RANK), 0)

    def across(x):
        return jnp.broadcast_to(x, (8, RANK))

    t = [in_ref[8 * r:8 * r + 8, :] for r in range(groups)]
    if start == 0 or stop == RANK:
        gram = [gram_ref[8 * r:8 * r + 8, :] for r in range(groups)]
        scale = unit_scale(gram, lane, sub)
    if start == 0:
        for r in range(groups):
            own = jnp.sum(jnp.where(lane == sub + 8 * r, t[r], 0.0), axis=1, keepdims=True)
            t[r] = t[r] * lax.rsqrt(own) * scale
    for r in range(start // 8, stop // 8):
        cols = {
            k: [across(t[k][:, 8 * r + i:8 * r + i + 1]) for i in range(8)]
            for k in range(r, groups)
        }
        for i in range(0, 8, 2):
            j = 8 * r + i
            p, q = across(cols[r][i][i:i + 1, :]), across(cols[r][i][i + 1:i + 2, :])
            d = across(cols[r][i + 1][i + 1:i + 2, :])
            inv_p = reciprocal(p)
            inv_d = p * reciprocal(p * d - q * q)
            ratio = q * inv_p
            above = {n: across(cols[r][n][i:i + 1, :]) for n in range(i + 2, 8)}
            below = {n: across(cols[r][n][i + 1:i + 2, :]) - ratio * above[n] for n in above}
            at_j, at_next = lane == j, lane == j + 1
            unit_a = jnp.where(at_j, 1.0, across(t[r][i:i + 1, :]))
            new_b = jnp.where(at_j, 0.0, across(t[r][i + 1:i + 2, :])) - ratio * unit_a
            row_a = jnp.where(at_next, 0.0, unit_a)
            row_b = jnp.where(at_next, 1.0, new_b)
            either = at_j | at_next
            for k in range(r, groups):
                first = cols[k][i] * inv_p
                second = (cols[k][i + 1] - first * q) * inv_d
                if k == r:
                    first = jnp.where(sub > i, first, 0.0)
                    second = jnp.where(sub > i + 1, second, 0.0)
                for n in above:
                    cols[k][n] = cols[k][n] - first * above[n] - second * below[n]
                new = jnp.where(either, 0.0, t[k]) - first * row_a - second * row_b
                if k == r:
                    new = jnp.where(sub > i + 1, new, jnp.where(sub == i + 1, new_b, t[k]))
                t[k] = new
    for k in range(groups):
        if stop == RANK:
            row_of = sub + 8 * k
            pivot = jnp.sum(jnp.where(lane == row_of, t[k], 0.0), axis=1, keepdims=True)
            unit = jnp.where(lane < row_of, t[k], jnp.where(lane == row_of, 1.0, 0.0))
            out_ref[8 * k:8 * k + 8, :] = unit * lax.rsqrt(pivot) * scale
        else:
            out_ref[8 * k:8 * k + 8, :] = t[k]


def eliminate(start, stop, state, gram, after=()):
    return local(
        functools.partial(eliminate_kernel, start, stop), f32(RANK, RANK), [state, gram], after,
        flops=4000000, nbytes=(stop - start) * 150000, name=f"eliminate{start}",
    )


def block_kernel(keep_ref, recv_ref, w_ref, out_ref):
    w = w_ref[...].T
    w_high = w.astype(jnp.bfloat16)
    w_low = (w - w_high.astype(jnp.float32)).astype(jnp.bfloat16)
    both = jnp.concatenate([
        jnp.concatenate([w_high, w_low], axis=1),
        jnp.concatenate([w_high, jnp.zeros_like(w_low)], axis=1),
    ], axis=0)
    d = keep_ref[...] + recv_ref[...]
    high = d.astype(jnp.bfloat16)
    low = (d - high.astype(jnp.float32)).astype(jnp.bfloat16)
    out = jnp.dot(jnp.concatenate([high, low], axis=1), both, preferred_element_type=jnp.float32)
    out_ref[...] = (out[:, :RANK] + out[:, RANK:]).astype(jnp.bfloat16)


def ortho_kernel(p_ref, w_ref, out_ref):
    out_ref[...] = lax.dot_general(
        p_ref[...], w_ref[...], NT, precision=lax.Precision.HIGHEST, preferred_element_type=jnp.float32
    ).astype(jnp.bfloat16)


def join_kernel(k, n, mine_ref, recv_ref, out_ref):
    bit = step_bit(k)
    out_ref[pl.ds(pl.multiple_of(bit * n, 16), n), :] = mine_ref[...]
    out_ref[pl.ds(pl.multiple_of((1 - bit) * n, 16), n), :] = recv_ref[...]


def unpack_kernel(own_ref, other_ref, coef_ref, sq_ref):
    c = team(lax.axis_index("fsdp"))
    squares = jnp.zeros((8, RANK), jnp.float32)
    for source, half in ((own_ref, c), (other_ref, 1 - c)):
        for i in range(0, HALF, PIECE):
            rows = source[i:i + PIECE, :].astype(jnp.float32)
            squares = squares + jnp.sum((rows * rows).reshape(PIECE // 8, 8, RANK), axis=0)
            coef_ref[pl.ds(pl.multiple_of(half * HALF + i, 8), PIECE), :] = rows
    sq_ref[...] = jnp.broadcast_to(jnp.sum(squares, axis=0, keepdims=True), (8, RANK))


def momentum_kernel(coef_ref, ortho_ref, b_ref, mom_hbm, buf, sems):
    ortho = ortho_ref[...]
    copies = []
    for i in range(TILES):
        cols = slice(i * WIDE, (i + 1) * WIDE)
        feedback = lax.dot_general(
            ortho, coef_ref[cols, :].astype(jnp.bfloat16), NT, preferred_element_type=jnp.float32
        )
        buf[:, cols] = (
            b_ref[:, cols].astype(jnp.float32) - (1.0 - inertia) * feedback
        ).astype(jnp.bfloat16)
        at = pl.ds(i * WIDE, WIDE)
        copies.append(pltpu.make_async_copy(buf.at[:, at], mom_hbm.at[:, at], sems.at[i]))
        copies[-1].start()
    for copy in copies:
        copy.wait()


def finish_momentum(coef, ortho, blended):
    return pl.pallas_call(
        momentum_kernel,
        in_specs=[VMEM_SPEC] * 3,
        out_specs=HBM_SPEC,
        out_shape=bf16(LOCAL_ROWS, LOCAL_COLS),
        scratch_shapes=[
            VMEM((LOCAL_ROWS, LOCAL_COLS), jnp.bfloat16),
            pltpu.SemaphoreType.DMA((TILES,)),
        ],
        compiler_params=PARAMS,
        cost_estimate=cost(2 * 256 * 3328 * 128, 5000000),
        name="finish_momentum",
    )(coef, ortho, blended)


def weights_kernel(sq_ref, coef_ref, ortho_ref, weights_ref, new_hbm, sub_hbm, buf, sub_buf, sems):
    scaling = math.sqrt(ROWS * COLS / RANK)
    norm = 1.0 / jnp.sqrt(sq_ref[0:1, :] + epsilon_sq)
    ortho = ortho_ref[...]
    copies = []
    for i in range(TILES):
        cols = slice(i * WIDE, (i + 1) * WIDE)
        at = pl.ds(i * WIDE, WIDE)
        subspace = coef_ref[cols, :] * norm
        sub_buf[cols, :] = subspace
        copies.append(pltpu.make_async_copy(sub_buf.at[at, :], sub_hbm.at[at, :], sems.at[0, i]))
        copies[-1].start()
        update = lax.dot_general(
            ortho, subspace.astype(jnp.bfloat16), NT, preferred_element_type=jnp.float32
        )
        buf[:, cols] = (
            weights_ref[:, cols].astype(jnp.float32) * (1.0 - step_size * shrinkage)
            - step_size * scaling * update
        ).astype(jnp.bfloat16)
        copies.append(pltpu.make_async_copy(buf.at[:, at], new_hbm.at[:, at], sems.at[1, i]))
        copies[-1].start()
    for copy in copies:
        copy.wait()


def finish_weights(squares, coef, ortho, weights):
    return pl.pallas_call(
        weights_kernel,
        in_specs=[VMEM_SPEC] * 4,
        out_specs=[HBM_SPEC] * 2,
        out_shape=[bf16(LOCAL_ROWS, LOCAL_COLS), f32(LOCAL_COLS, RANK)],
        scratch_shapes=[
            VMEM((LOCAL_ROWS, LOCAL_COLS), jnp.bfloat16),
            VMEM((LOCAL_COLS, RANK), jnp.float32),
            pltpu.SemaphoreType.DMA((2, TILES)),
        ],
        compiler_params=PARAMS,
        cost_estimate=cost(2 * 256 * 3328 * 128, 7000000),
        name="finish_weights",
    )(squares, coef, ortho, weights)


def on_device(momentum, gradient, weights, subspace):
    blended, projected = project(momentum, gradient, subspace)
    for step in range(3):
        projected = projected + swap_z(projected, step)

    gram = local(gram_kernel, f32(RANK, RANK), [projected], flops=6 * 256 * 128 * 256, nbytes=200000, name="gram")
    more = xor_fsdp(gram, X_ONE)
    send = local(
        lift_send_kernel, f32(HALF, RANK), [projected, blended], [gram],
        flops=2 * 256 * 3328 * 128, nbytes=2000000, name="lift_send",
    )
    recv = xor_fsdp(send, CORE)
    keep = local(
        lift_keep_kernel, f32(HALF, RANK), [projected, blended], [send],
        flops=2 * 256 * 3328 * 128, nbytes=2000000, name="lift_keep",
    )
    gram = add(gram, more, [keep], "add_x1")
    more = xor_fsdp(gram, X_THREE)
    n = HALF // 2
    moving, keep = split_step(0, n, keep, recv, [gram])
    recv = xor_step(moving, 0)
    gram = add(gram, more, [moving], "add_x3")
    gram = add(gram, xor_fsdp(gram, Y_ONE), [], "add_y1")
    n //= 2
    moving, keep = split_step(1, n, keep, recv, [gram])
    recv = xor_step(moving, 1)
    gram = local(hold_kernel, f32(RANK, RANK), [gram], [moving], nbytes=130000, name="hold")
    more = xor_fsdp(gram, Y_THREE)
    d = add(keep, recv, [more], "first_sum")
    recv = xor_step(d, 2)
    gram = add(gram, more, [d], "add_y3")
    gram = add(gram, xor_fsdp(gram, CORE), [], "add_core")
    state = eliminate(0, CUT, gram, gram)
    d = add(d, recv, [state], "second_sum")
    recv = xor_step(d, 3)
    inverse = eliminate(CUT, RANK, state, gram, [d])

    coef = local(
        block_kernel, bf16(CHUNK, RANK), [d, recv, inverse],
        flops=2 * CHUNK * 256 * 256, nbytes=700000, name="block",
    )
    ortho = local(
        ortho_kernel, bf16(LOCAL_ROWS, RANK), [projected, inverse], [coef],
        flops=6 * 256 * 256 * 128, nbytes=300000, name="ortho",
    )
    for k, n in ((1, CHUNK), (0, 2 * CHUNK)):
        coef = local(
            functools.partial(join_kernel, k, n), bf16(2 * n, RANK), [coef, xor_step(coef, k)],
            [ortho] if k else [], nbytes=n * 1024, name=f"join{k}",
        )
    coef, squares = local(
        unpack_kernel, [f32(LOCAL_COLS, RANK), f32(8, RANK)], [coef, xor_fsdp(coef, CORE)],
        flops=3328 * 256, nbytes=2600000, name="unpack",
    )
    squares = (squares + cross_z(squares, 1)) + (cross_z(squares, 2) + cross_z(squares, 3))
    squares = squares + cross_z(squares, 7)
    new_momentum = finish_momentum(coef, ortho, blended)
    new_weights, new_subspace = finish_weights(squares, coef, ortho, weights)
    return (new_momentum, new_weights, new_subspace)


def solution(mesh):
    placed = (P("fsdp", "tp"), P("fsdp", "tp"), P("fsdp", "tp"), P("tp", None))
    return jax.shard_map(
        on_device,
        mesh=mesh,
        in_specs=placed,
        out_specs=(P("fsdp", "tp"), P("fsdp", "tp"), P("tp", None)),
        check_vma=False,
    )
```

time: 372 us -> 90.3 us (0.24); the launches traced: 368 us -> 90.2 us
  waiting for transfers between devices: 297 us -> 39.8 us
  starting transfers between devices: 0.12 us -> 35.2 us
  other arithmetic: 28 us -> 0.06 us
  Pallas kernels: 0 us -> 13.7 us
  blocking collectives: 13.7 us -> 0 us
  between operations: 13.8 us -> 0.99 us
  matrix products: 12.8 us -> 0 us
    psum x3 -> x0, waiting for transfers between devices: 297 us -> none  [the longest x1 115 us: on_device(): coefficients = lax.psum(partial_coef, 'fsdp')]
    ppermute x0 -> x20, waiting for transfers between devices: none -> 39.8 us  [the longest x7 16.2 us: xor_fsdp(): return lax.ppermute(x, 'fsdp', [(i, i ^ mask) for i in range(FSDP)])]
    ppermute x0 -> x20, starting transfers between devices: none -> 35.2 us  [the longest x7 10.1 us: xor_fsdp(): return lax.ppermute(x, 'fsdp', [(i, i ^ mask) for i in range(FSDP)])]
    another operation x5 -> x0, other arithmetic: 23.5 us -> none  [the longest x3 12.4 us: orthonormalize(): factor = jnp.linalg.cholesky(gram_matrix)]
    psum x1 -> x0, blocking collectives: 13.7 us -> none  [on_device(): col_squares = lax.psum(jnp.sum(coefficients * coefficients, axis=0), 'tp')]
    pallas_call x0 -> x23, Pallas kernels: none -> 13.7 us  [the longest x20 7.13 us: local(): pl.pallas_call(body, in_specs=[VMEM_SPEC] * (used + len(after)), out_spec...]
    dot_general x5 -> x0, matrix products: 11.7 us -> none  [the longest x1 3.94 us: on_device(): partial_proj = jnp.dot(blended, lowered, preferred_element_type=jnp.float32)]
  transfers between devices with their start and end apart: 3 -> 20, of which waited for: 3 -> 15; matrix products, arithmetic and copies ran while one was open for 0% -> 0% of each run, Pallas kernels for 0% -> 8%
where the time goes in v1:
time: 90.3 us; the launch traced here: 90.2 us
  waiting for transfers between devices  39.8 us (44%)
  starting transfers between devices  35.2 us (39%)
  Pallas kernels  13.7 us (15%)
  between operations  0.99 us (1%)
    ppermute x7, waiting for transfers between devices, xor_fsdp(): return lax.ppermute(x, 'fsdp', [(i, i ^ mask) for i in range(FSDP)])  16.2 us
    ppermute x6, waiting for transfers between devices, xor_step(): lax.ppermute(x, 'fsdp', [(i, i ^ MASKS[team(i)][k]) for i in range(FSDP)])  11.5 us
    ppermute x3, waiting for transfers between devices, swap_z(): return lax.ppermute(x, ('fsdp', 'tp'), perm)  10.3 us
    ppermute x7, starting transfers between devices, xor_fsdp(): return lax.ppermute(x, 'fsdp', [(i, i ^ mask) for i in range(FSDP)])  10.1 us
    ppermute x3, starting transfers between devices, swap_z(): return lax.ppermute(x, ('fsdp', 'tp'), perm)  9.5 us
    ppermute x6, starting transfers between devices, xor_step(): lax.ppermute(x, 'fsdp', [(i, i ^ MASKS[team(i)][k]) for i in range(FSDP)])  8.41 us
    ppermute x4, starting transfers between devices, cross_z(): return lax.ppermute(x, ('fsdp', 'tp'), perm)  7.16 us
    pallas_call x20, Pallas kernels, local(): pl.pallas_call(body, in_specs=[VMEM_SPEC] * (used + len(after)), out_spec...  7.13 us
  transfers between devices with their start and end apart: 20, of which 15 were waited for; matrix products, arithmetic and copies ran while one was open for 0% of the time, Pallas kernels for 8%

profile of v1, /device:TPU:1, one launch (start us, length us, event | category | flops | bytes accessed | tf_op | source)
XLA Modules:
  0.0 90.2 jit_solution(13326142722160899657)
XLA Ops:
  0.6 2.9 %project.1 = (bf16[256,3328]{1,0:T(8,128)(2,1)S(1)}, f32[256,128]{1,0:T(8,128)S(1)}) custom-call(bf16[256,3328]{1,0:T(8,128)(2,1)} %m_hbm.1, bf16[256,3328]{1,0:T(8,128)(2,1)} %g_hbm.1, f32[3328,128]{1,0:T(8,128)} %s_hbm.1), custom_call_target="tpu_custom_call" | custom-call | flops 218103808 | bytes 7000000 | tf_op jit(solution)/shard_map/project/pallas_call | solution.py:124
  3.5 6.5 %collective-permute-start = (f32[256,128]{1,0:T(8,128)S(1)}, f32[256,128]{1,0:T(8,128)S(1)}, u32[]{:S(2)}, u32[]{:S(2)}) collective-permute-start(f32[256,128]{1,0:T(8,128)S(1)} %get-tuple-element.13), channel_id=1, source_target_pairs={{0,1},{1,0},{2,3},{3,2},{4,5},{5,4},{6,7},{7,6},{9,10},{10,9},{11,... | collective-permute-start | bytes 393224 | tf_op jit(solution)/shard_map/ppermute | solution.py:72
  10.0 2.4 %collective-permute-done = f32[256,128]{1,0:T(8,128)S(1)} collective-permute-done((f32[256,128]{1,0:T(8,128)S(1)}, f32[256,128]{1,0:T(8,128)S(1)}, u32[]{:S(2)}, u32[]{:S(2)}) %collective-permute-start) | collective-permute-done | bytes 131104 | tf_op jit(solution)/shard_map/ppermute | solution.py:72
  12.5 3.8 %collective-permute-done.1 = f32[256,128]{1,0:T(8,128)S(1)} collective-permute-done((f32[256,128]{1,0:T(8,128)S(1)}, f32[256,128]{1,0:T(8,128)S(1)}, u32[]{:S(2)}, u32[]{:S(2)}) %collective-permute-start.1) | collective-permute-done | bytes 131104 | tf_op jit(solution)/shard_map/ppermute | solution.py:72
  16.3 2.9 %collective-permute-start.2 = (f32[256,128]{1,0:T(8,128)S(1)}, f32[256,128]{1,0:T(8,128)S(1)}, u32[]{:S(2)}, u32[]{:S(2)}) collective-permute-start(f32[256,128]{1,0:T(8,128)S(1)} %add.22), channel_id=1, source_target_pairs={{2,5},{5,2},{1,6},{6,1},{4,7},{7,4},{3,0},{0,3},{11,14},{14,11},{1... | collective-permute-start | bytes 393224 | tf_op jit(solution)/shard_map/ppermute | solution.py:72
  19.2 4.1 %collective-permute-done.2 = f32[256,128]{1,0:T(8,128)S(1)} collective-permute-done((f32[256,128]{1,0:T(8,128)S(1)}, f32[256,128]{1,0:T(8,128)S(1)}, u32[]{:S(2)}, u32[]{:S(2)}) %collective-permute-start.2) | collective-permute-done | bytes 131104 | tf_op jit(solution)/shard_map/ppermute | solution.py:72
  24.2 4.1 %collective-permute-start.3 = (f32[1664,128]{1,0:T(8,128)S(1)}, f32[1664,128]{1,0:T(8,128)S(1)}, u32[]{:S(2)}, u32[]{:S(2)}) collective-permute-start(f32[1664,128]{1,0:T(8,128)S(1)} %lift_send.1.refs_2_), channel_id=1, source_target_pairs={{0,8},{8,0},{16,24},{24,16},{32,40},{40,32},{48,56},{56,48},{64,72... | collective-permute-start | bytes 2555912 | tf_op jit(solution)/shard_map/ppermute | solution.py:81
  28.3 1.2 %collective-permute-start.4 = (f32[128,128]{1,0:T(8,128)S(1)}, f32[128,128]{1,0:T(8,128)S(1)}, u32[]{:S(2)}, u32[]{:S(2)}) collective-permute-start(f32[128,128]{1,0:T(8,128)S(1)} %gram.1.refs_2_.refs_0_), channel_id=1, source_target_pairs={{0,24},{8,16},{16,8},{24,0},{32,56},{40,48},{48,40},{56,32},{64,88... | collective-permute-start | bytes 196616 | tf_op jit(solution)/shard_map/ppermute | solution.py:81
  29.9 2.1 %collective-permute-done.4.refs_1_ = f32[128,128]{1,0:T(8,128)S(1)} collective-permute-done((f32[128,128]{1,0:T(8,128)S(1)}, f32[128,128]{1,0:T(8,128)S(1)}, u32[]{:S(2)}, u32[]{:S(2)}) %collective-permute-start.4) | collective-permute-done | bytes 65568 | tf_op jit(solution)/shard_map/ppermute | solution.py:81
  32.2 1.4 %collective-permute-start.5 = (f32[832,128]{1,0:T(8,128)S(1)}, f32[832,128]{1,0:T(8,128)S(1)}, u32[]{:S(2)}, u32[]{:S(2)}) collective-permute-start(f32[832,128]{1,0:T(8,128)S(1)} %get-tuple-element.16.refs_2_), channel_id=1, source_target_pairs={{0,24},{8,64},{16,88},{24,0},{32,56},{40,96},{48,120},{56,32},{64,... | collective-permute-start | bytes 1277960 | tf_op jit(solution)/shard_map/ppermute | solution.py:85
  33.6 2.7 %collective-permute-start.6 = (f32[128,128]{1,0:T(8,128)S(1)}, f32[128,128]{1,0:T(8,128)S(1)}, u32[]{:S(2)}, u32[]{:S(2)}) collective-permute-start(f32[128,128]{1,0:T(8,128)S(1)} %add_x1.1.refs_2_.refs_0_), channel_id=1, source_target_pairs={{0,56},{8,48},{16,40},{24,32},{32,24},{40,16},{48,8},{56,0},{64,12... | collective-permute-start | bytes 196616 | tf_op jit(solution)/shard_map/ppermute | solution.py:81
  36.4 2.5 %collective-permute-done.6.refs_1_ = f32[128,128]{1,0:T(8,128)S(1)} collective-permute-done((f32[128,128]{1,0:T(8,128)S(1)}, f32[128,128]{1,0:T(8,128)S(1)}, u32[]{:S(2)}, u32[]{:S(2)}) %collective-permute-start.6) | collective-permute-done | bytes 65568 | tf_op jit(solution)/shard_map/ppermute | solution.py:81
  39.1 3.9 %collective-permute-done.7.refs_1_ = f32[128,128]{1,0:T(8,128)S(1)} collective-permute-done((f32[128,128]{1,0:T(8,128)S(1)}, f32[128,128]{1,0:T(8,128)S(1)}, u32[]{:S(2)}, u32[]{:S(2)}) %collective-permute-start.7) | collective-permute-done | bytes 65568 | tf_op jit(solution)/shard_map/ppermute | solution.py:81
  43.1 1.9 %collective-permute-start.8 = (f32[416,128]{1,0:T(8,128)S(1)}, f32[416,128]{1,0:T(8,128)S(1)}, u32[]{:S(2)}, u32[]{:S(2)}) collective-permute-start(f32[416,128]{1,0:T(8,128)S(1)} %get-tuple-element.18.refs_1_), channel_id=1, source_target_pairs={{0,56},{8,192},{16,216},{24,32},{32,24},{40,224},{48,248},{56,0},{... | collective-permute-start | bytes 638984 | tf_op jit(solution)/shard_map/ppermute | solution.py:85
  45.0 1.2 %collective-permute-start.9 = (f32[128,128]{1,0:T(8,128)S(1)}, f32[128,128]{1,0:T(8,128)S(1)}, u32[]{:S(2)}, u32[]{:S(2)}) collective-permute-start(f32[128,128]{1,0:T(8,128)S(1)} %hold.1.refs_0_), channel_id=1, source_target_pairs={{0,200},{8,192},{16,216},{24,208},{32,232},{40,224},{48,248},{56,2... | collective-permute-start | bytes 196616 | tf_op jit(solution)/shard_map/ppermute | solution.py:81
  46.2 5.1 %collective-permute-done.9.refs_2_.refs_1_ = f32[128,128]{1,0:T(8,128)S(1)} collective-permute-done((f32[128,128]{1,0:T(8,128)S(1)}, f32[128,128]{1,0:T(8,128)S(1)}, u32[]{:S(2)}, u32[]{:S(2)}) %collective-permute-start.9) | collective-permute-done | bytes 65568 | tf_op jit(solution)/shard_map/ppermute | solution.py:81
  52.0 1.2 %collective-permute-done.11.refs_1_ = f32[128,128]{1,0:T(8,128)S(1)} collective-permute-done((f32[128,128]{1,0:T(8,128)S(1)}, f32[128,128]{1,0:T(8,128)S(1)}, u32[]{:S(2)}, u32[]{:S(2)}) %collective-permute-start.11) | collective-permute-done | bytes 65568 | tf_op jit(solution)/shard_map/ppermute | solution.py:81
  53.2 2.1 %eliminate0.1.refs_2_.refs_0_ = f32[128,128]{1,0:T(8,128)S(1)} custom-call(f32[128,128]{1,0:T(8,128)S(1)} %add_core.1.refs_0_.refs_1_, f32[128,128]{1,0:T(8,128)S(1)} %add_core.1.refs_0_.refs_1_), custom_call_target="tpu_custom_call" | custom-call | flops 4000000 | bytes 6000000 | tf_op jit(solution)/shard_map/eliminate0/pallas_call | solution.py:148
  55.3 1.4 %collective-permute-done.10.refs_1_ = f32[416,128]{1,0:T(8,128)S(1)} collective-permute-done((f32[416,128]{1,0:T(8,128)S(1)}, f32[416,128]{1,0:T(8,128)S(1)}, u32[]{:S(2)}, u32[]{:S(2)}) %collective-permute-start.10) | collective-permute-done | bytes 213024 | tf_op jit(solution)/shard_map/ppermute | solution.py:85
  56.8 2.9 %collective-permute-start.12 = (f32[416,128]{1,0:T(8,128)S(1)}, f32[416,128]{1,0:T(8,128)S(1)}, u32[]{:S(2)}, u32[]{:S(2)}) collective-permute-start(f32[416,128]{1,0:T(8,128)S(1)} %second_sum.1.refs_2_.refs_0_), channel_id=1, source_target_pairs={{0,200},{8,48},{16,40},{24,208},{32,232},{40,16},{48,8},{56,240},{... | collective-permute-start | bytes 638984 | tf_op jit(solution)/shard_map/ppermute | solution.py:85
  59.7 2.6 %eliminate40.1.refs_2_.refs_1_ = f32[128,128]{1,0:T(8,128)S(1)} custom-call(f32[128,128]{1,0:T(8,128)S(1)} %eliminate0.1.refs_2_.refs_0_, f32[128,128]{1,0:T(8,128)S(1)} %add_core.1.refs_0_.refs_1_, f32[416,128]{1,0:T(8,128)S(1)} %second_sum.1.refs_2_.refs_0_), custom_call_target="tpu_custom_call" | custom-call | flops 4000000 | bytes 13200000 | tf_op jit(solution)/shard_map/eliminate40/pallas_call | solution.py:148
  62.3 1.2 %collective-permute-done.12.refs_1_ = f32[416,128]{1,0:T(8,128)S(1)} collective-permute-done((f32[416,128]{1,0:T(8,128)S(1)}, f32[416,128]{1,0:T(8,128)S(1)}, u32[]{:S(2)}, u32[]{:S(2)}) %collective-permute-start.12) | collective-permute-done | bytes 213024 | tf_op jit(solution)/shard_map/ppermute | solution.py:85
  63.9 1.6 %collective-permute-start.13 = (bf16[416,128]{1,0:T(8,128)(2,1)S(1)}, bf16[416,128]{1,0:T(8,128)(2,1)S(1)}, u32[]{:S(2)}, u32[]{:S(2)}) collective-permute-start(bf16[416,128]{1,0:T(8,128)(2,1)S(1)} %block.1.refs_2_.refs_0_), channel_id=1, source_target_pairs={{0,56},{8,192},{16,216},{24,32},{32,24},{40,224},{48,248},{56,0},{... | collective-permute-start | bytes 319496 | tf_op jit(solution)/shard_map/ppermute | solution.py:85
  65.7 3.6 %collective-permute-done.13.refs_1_ = bf16[416,128]{1,0:T(8,128)(2,1)S(1)} collective-permute-done((bf16[416,128]{1,0:T(8,128)(2,1)S(1)}, bf16[416,128]{1,0:T(8,128)(2,1)S(1)}, u32[]{:S(2)}, u32[]{:S(2)}) %collective-permute-start.13) | collective-permute-done | bytes 106528 | tf_op jit(solution)/shard_map/ppermute | solution.py:85
  69.4 5.3 %collective-permute-done.14.refs_1_ = bf16[832,128]{1,0:T(8,128)(2,1)S(1)} collective-permute-done((bf16[832,128]{1,0:T(8,128)(2,1)S(1)}, bf16[832,128]{1,0:T(8,128)(2,1)S(1)}, u32[]{:S(2)}, u32[]{:S(2)}) %collective-permute-start.14) | collective-permute-done | bytes 213024 | tf_op jit(solution)/shard_map/ppermute | solution.py:85
  75.2 1.4 %collective-permute-done.15.refs_1_ = bf16[1664,128]{1,0:T(8,128)(2,1)S(1)} collective-permute-done((bf16[1664,128]{1,0:T(8,128)(2,1)S(1)}, bf16[1664,128]{1,0:T(8,128)(2,1)S(1)}, u32[]{:S(2)}, u32[]{:S(2)}) %collective-permute-start.15) | collective-permute-done | bytes 426016 | tf_op jit(solution)/shard_map/ppermute | solution.py:81
  76.8 2.1 %collective-permute-start.18 = (f32[8,128]{1,0:T(8,128)S(1)}, f32[8,128]{1,0:T(8,128)S(1)}, u32[]{:S(2)}, u32[]{:S(2)}) collective-permute-start(f32[8,128]{1,0:T(8,128)S(1)} %get-tuple-element.20), channel_id=1, source_target_pairs={{0,11},{1,10},{2,9},{3,8},{4,15},{5,14},{6,13},{7,12},{8,3},{9,2},... | collective-permute-start | bytes 12296 | tf_op jit(solution)/shard_map/ppermute | solution.py:77
  78.9 2.1 %collective-permute-start.16 = (f32[8,128]{1,0:T(8,128)S(1)}, f32[8,128]{1,0:T(8,128)S(1)}, u32[]{:S(2)}, u32[]{:S(2)}) collective-permute-start(f32[8,128]{1,0:T(8,128)S(1)} %get-tuple-element.20), channel_id=1, source_target_pairs={{0,9},{1,8},{2,11},{3,10},{4,13},{5,12},{6,15},{7,14},{8,1},{9,0},... | collective-permute-start | bytes 12296 | tf_op jit(solution)/shard_map/ppermute | solution.py:77
  81.8 1.1 %collective-permute-done.17 = f32[8,128]{1,0:T(8,128)S(1)} collective-permute-done((f32[8,128]{1,0:T(8,128)S(1)}, f32[8,128]{1,0:T(8,128)S(1)}, u32[]{:S(2)}, u32[]{:S(2)}) %collective-permute-start.17) | collective-permute-done | bytes 4128 | tf_op jit(solution)/shard_map/ppermute | solution.py:77
  82.8 3.0 %collective-permute-start.19 = (f32[8,128]{1,0:T(8,128)S(1)}, f32[8,128]{1,0:T(8,128)S(1)}, u32[]{:S(2)}, u32[]{:S(2)}) collective-permute-start(f32[8,128]{1,0:T(8,128)S(1)} %add_add_fusion), channel_id=1, source_target_pairs={{0,15},{1,14},{2,13},{3,12},{4,11},{5,10},{6,9},{7,8},{8,7},{9,6},... | collective-permute-start | bytes 12296 | tf_op jit(solution)/shard_map/ppermute | solution.py:77
  85.8 1.5 %finish_momentum.1 = bf16[256,3328]{1,0:T(8,128)(2,1)} custom-call(f32[3328,128]{1,0:T(8,128)S(1)} %get-tuple-element.19.coef_ref, bf16[256,128]{1,0:T(8,128)(2,1)S(1)} %ortho.1.refs_2_.ortho_ref, bf16[256,3328]{1,0:T(8,128)(2,1)S(1)} %get-tuple-element.14.refs_1_.b_ref), custom_call_target="tpu_custom_call" | custom-call | flops 218103808 | bytes 5000000 | tf_op jit(solution)/shard_map/finish_momentum/pallas_call | solution.py:348
  87.9 2.2 %finish_weights.1 = (bf16[256,3328]{1,0:T(8,128)(2,1)}, f32[3328,128]{1,0:T(8,128)}) custom-call(f32[8,128]{1,0:T(8,128)S(1)} %add.27.sq_ref, f32[3328,128]{1,0:T(8,128)S(1)} %get-tuple-element.19.coef_ref, bf16[256,128]{1,0:T(8,128)(2,1)S(1)} %ortho.1.refs_2_.ortho_ref, bf16[256,3328]{1,0:T(8,128)(2,1)S(1)} %copy-done), custom_call_target="tpu_custom_call" | custom-call | flops 218103808 | bytes 7000000 | tf_op jit(solution)/shard_map/finish_weights/pallas_call | solution.py:389
  (38 shorter events, 5.3 us)
Async XLA Ops:
  3.5 8.8 %collective-permute-start = (f32[256,128]{1,0:T(8,128)S(1)}, f32[256,128]{1,0:T(8,128)S(1)}, u32[]{:S(2)}, u32[]{:S(2)}) collective-permute-start(f32[256,128]{1,0:T(8,128)S(1)} %get-tuple-element.13), channel_id=1, source_target_pairs={{0,1},{1,0},{2,3},{3,2},{4,5},{5,4},{6,7},{7,6},{9,10},{10,9},{11,... | collective-permute-start | bytes 393224 | tf_op jit(solution)/shard_map/ppermute | solution.py:72
  12.4 3.9 %collective-permute-start.1 = (f32[256,128]{1,0:T(8,128)S(1)}, f32[256,128]{1,0:T(8,128)S(1)}, u32[]{:S(2)}, u32[]{:S(2)}) collective-permute-start(f32[256,128]{1,0:T(8,128)S(1)} %add.21), channel_id=1, source_target_pairs={{1,2},{2,1},{3,4},{4,3},{5,6},{6,5},{7,0},{0,7},{10,11},{11,10},{1... | collective-permute-start | bytes 393224 | tf_op jit(solution)/shard_map/ppermute | solution.py:72
  16.3 7.1 %collective-permute-start.2 = (f32[256,128]{1,0:T(8,128)S(1)}, f32[256,128]{1,0:T(8,128)S(1)}, u32[]{:S(2)}, u32[]{:S(2)}) collective-permute-start(f32[256,128]{1,0:T(8,128)S(1)} %add.22), channel_id=1, source_target_pairs={{2,5},{5,2},{1,6},{6,1},{4,7},{7,4},{3,0},{0,3},{11,14},{14,11},{1... | collective-permute-start | bytes 393224 | tf_op jit(solution)/shard_map/ppermute | solution.py:72
  24.2 7.9 %collective-permute-start.3 = (f32[1664,128]{1,0:T(8,128)S(1)}, f32[1664,128]{1,0:T(8,128)S(1)}, u32[]{:S(2)}, u32[]{:S(2)}) collective-permute-start(f32[1664,128]{1,0:T(8,128)S(1)} %lift_send.1.refs_2_), channel_id=1, source_target_pairs={{0,8},{8,0},{16,24},{24,16},{32,40},{40,32},{48,56},{56,48},{64,72... | collective-permute-start | bytes 2555912 | tf_op jit(solution)/shard_map/ppermute | solution.py:81
  28.3 3.8 %collective-permute-start.4 = (f32[128,128]{1,0:T(8,128)S(1)}, f32[128,128]{1,0:T(8,128)S(1)}, u32[]{:S(2)}, u32[]{:S(2)}) collective-permute-start(f32[128,128]{1,0:T(8,128)S(1)} %gram.1.refs_2_.refs_0_), channel_id=1, source_target_pairs={{0,24},{8,16},{16,8},{24,0},{32,56},{40,48},{48,40},{56,32},{64,88... | collective-permute-start | bytes 196616 | tf_op jit(solution)/shard_map/ppermute | solution.py:81
  32.2 10.8 %collective-permute-start.5 = (f32[832,128]{1,0:T(8,128)S(1)}, f32[832,128]{1,0:T(8,128)S(1)}, u32[]{:S(2)}, u32[]{:S(2)}) collective-permute-start(f32[832,128]{1,0:T(8,128)S(1)} %get-tuple-element.16.refs_2_), channel_id=1, source_target_pairs={{0,24},{8,64},{16,88},{24,0},{32,56},{40,96},{48,120},{56,32},{64,... | collective-permute-start | bytes 1277960 | tf_op jit(solution)/shard_map/ppermute | solution.py:85
  33.6 5.2 %collective-permute-start.6 = (f32[128,128]{1,0:T(8,128)S(1)}, f32[128,128]{1,0:T(8,128)S(1)}, u32[]{:S(2)}, u32[]{:S(2)}) collective-permute-start(f32[128,128]{1,0:T(8,128)S(1)} %add_x1.1.refs_2_.refs_0_), channel_id=1, source_target_pairs={{0,56},{8,48},{16,40},{24,32},{32,24},{40,16},{48,8},{56,0},{64,12... | collective-permute-start | bytes 196616 | tf_op jit(solution)/shard_map/ppermute | solution.py:81
  38.8 4.2 %collective-permute-start.7 = (f32[128,128]{1,0:T(8,128)S(1)}, f32[128,128]{1,0:T(8,128)S(1)}, u32[]{:S(2)}, u32[]{:S(2)}) collective-permute-start(f32[128,128]{1,0:T(8,128)S(1)} %add_x3.1.refs_0_), channel_id=1, source_target_pairs={{0,72},{8,64},{16,88},{24,80},{32,104},{40,96},{48,120},{56,112},{... | collective-permute-start | bytes 196616 | tf_op jit(solution)/shard_map/ppermute | solution.py:81
  43.1 8.2 %collective-permute-start.8 = (f32[416,128]{1,0:T(8,128)S(1)}, f32[416,128]{1,0:T(8,128)S(1)}, u32[]{:S(2)}, u32[]{:S(2)}) collective-permute-start(f32[416,128]{1,0:T(8,128)S(1)} %get-tuple-element.18.refs_1_), channel_id=1, source_target_pairs={{0,56},{8,192},{16,216},{24,32},{32,24},{40,224},{48,248},{56,0},{... | collective-permute-start | bytes 638984 | tf_op jit(solution)/shard_map/ppermute | solution.py:85
  45.0 6.3 %collective-permute-start.9 = (f32[128,128]{1,0:T(8,128)S(1)}, f32[128,128]{1,0:T(8,128)S(1)}, u32[]{:S(2)}, u32[]{:S(2)}) collective-permute-start(f32[128,128]{1,0:T(8,128)S(1)} %hold.1.refs_0_), channel_id=1, source_target_pairs={{0,200},{8,192},{16,216},{24,208},{32,232},{40,224},{48,248},{56,2... | collective-permute-start | bytes 196616 | tf_op jit(solution)/shard_map/ppermute | solution.py:81
  51.3 5.5 %collective-permute-start.10 = (f32[416,128]{1,0:T(8,128)S(1)}, f32[416,128]{1,0:T(8,128)S(1)}, u32[]{:S(2)}, u32[]{:S(2)}) collective-permute-start(f32[416,128]{1,0:T(8,128)S(1)} %first_sum.1.refs_2_.refs_0_), channel_id=1, source_target_pairs={{0,72},{8,16},{16,8},{24,80},{32,104},{40,48},{48,40},{56,112},{64... | collective-permute-start | bytes 638984 | tf_op jit(solution)/shard_map/ppermute | solution.py:85
  51.8 1.3 %collective-permute-start.11 = (f32[128,128]{1,0:T(8,128)S(1)}, f32[128,128]{1,0:T(8,128)S(1)}, u32[]{:S(2)}, u32[]{:S(2)}) collective-permute-start(f32[128,128]{1,0:T(8,128)S(1)} %add_y3.1.refs_0_), channel_id=1, source_target_pairs={{0,8},{8,0},{16,24},{24,16},{32,40},{40,32},{48,56},{56,48},{64,72... | collective-permute-start | bytes 196616 | tf_op jit(solution)/shard_map/ppermute | solution.py:81
  56.8 6.7 %collective-permute-start.12 = (f32[416,128]{1,0:T(8,128)S(1)}, f32[416,128]{1,0:T(8,128)S(1)}, u32[]{:S(2)}, u32[]{:S(2)}) collective-permute-start(f32[416,128]{1,0:T(8,128)S(1)} %second_sum.1.refs_2_.refs_0_), channel_id=1, source_target_pairs={{0,200},{8,48},{16,40},{24,208},{32,232},{40,16},{48,8},{56,240},{... | collective-permute-start | bytes 638984 | tf_op jit(solution)/shard_map/ppermute | solution.py:85
  63.9 5.4 %collective-permute-start.13 = (bf16[416,128]{1,0:T(8,128)(2,1)S(1)}, bf16[416,128]{1,0:T(8,128)(2,1)S(1)}, u32[]{:S(2)}, u32[]{:S(2)}) collective-permute-start(bf16[416,128]{1,0:T(8,128)(2,1)S(1)} %block.1.refs_2_.refs_0_), channel_id=1, source_target_pairs={{0,56},{8,192},{16,216},{24,32},{32,24},{40,224},{48,248},{56,0},{... | collective-permute-start | bytes 319496 | tf_op jit(solution)/shard_map/ppermute | solution.py:85
  69.3 5.4 %collective-permute-start.14 = (bf16[832,128]{1,0:T(8,128)(2,1)S(1)}, bf16[832,128]{1,0:T(8,128)(2,1)S(1)}, u32[]{:S(2)}, u32[]{:S(2)}) collective-permute-start(bf16[832,128]{1,0:T(8,128)(2,1)S(1)} %join1.1.refs_0_), channel_id=1, source_target_pairs={{0,24},{8,64},{16,88},{24,0},{32,56},{40,96},{48,120},{56,32},{64,... | collective-permute-start | bytes 638984 | tf_op jit(solution)/shard_map/ppermute | solution.py:85
  74.8 1.9 %collective-permute-start.15 = (bf16[1664,128]{1,0:T(8,128)(2,1)S(1)}, bf16[1664,128]{1,0:T(8,128)(2,1)S(1)}, u32[]{:S(2)}, u32[]{:S(2)}) collective-permute-start(bf16[1664,128]{1,0:T(8,128)(2,1)S(1)} %join0.1.refs_0_), channel_id=1, source_target_pairs={{0,8},{8,0},{16,24},{24,16},{32,40},{40,32},{48,56},{56,48},{64,72... | collective-permute-start | bytes 1277960 | tf_op jit(solution)/shard_map/ppermute | solution.py:81
  76.8 4.9 %collective-permute-start.18 = (f32[8,128]{1,0:T(8,128)S(1)}, f32[8,128]{1,0:T(8,128)S(1)}, u32[]{:S(2)}, u32[]{:S(2)}) collective-permute-start(f32[8,128]{1,0:T(8,128)S(1)} %get-tuple-element.20), channel_id=1, source_target_pairs={{0,11},{1,10},{2,9},{3,8},{4,15},{5,14},{6,13},{7,12},{8,3},{9,2},... | collective-permute-start | bytes 12296 | tf_op jit(solution)/shard_map/ppermute | solution.py:77
  78.9 3.9 %collective-permute-start.17 = (f32[8,128]{1,0:T(8,128)S(1)}, f32[8,128]{1,0:T(8,128)S(1)}, u32[]{:S(2)}, u32[]{:S(2)}) collective-permute-start(f32[8,128]{1,0:T(8,128)S(1)} %get-tuple-element.20), channel_id=1, source_target_pairs={{0,10},{1,11},{2,8},{3,9},{4,14},{5,15},{6,12},{7,13},{8,2},{9,3},... | collective-permute-start | bytes 12296 | tf_op jit(solution)/shard_map/ppermute | solution.py:77
  78.9 3.9 %collective-permute-start.16 = (f32[8,128]{1,0:T(8,128)S(1)}, f32[8,128]{1,0:T(8,128)S(1)}, u32[]{:S(2)}, u32[]{:S(2)}) collective-permute-start(f32[8,128]{1,0:T(8,128)S(1)} %get-tuple-element.20), channel_id=1, source_target_pairs={{0,9},{1,8},{2,11},{3,10},{4,13},{5,12},{6,15},{7,14},{8,1},{9,0},... | collective-permute-start | bytes 12296 | tf_op jit(solution)/shard_map/ppermute | solution.py:77
  82.8 4.5 %collective-permute-start.19 = (f32[8,128]{1,0:T(8,128)S(1)}, f32[8,128]{1,0:T(8,128)S(1)}, u32[]{:S(2)}, u32[]{:S(2)}) collective-permute-start(f32[8,128]{1,0:T(8,128)S(1)} %add_add_fusion), channel_id=1, source_target_pairs={{0,15},{1,14},{2,13},{3,12},{4,11},{5,10},{6,9},{7,8},{8,7},{9,6},... | collective-permute-start | bytes 12296 | tf_op jit(solution)/shard_map/ppermute | solution.py:77
  85.8 2.1 %copy-start = (bf16[256,3328]{1,0:T(8,128)(2,1)S(1)}, bf16[256,3328]{1,0:T(8,128)(2,1)}, u32[]{:S(2)}) copy-start(bf16[256,3328]{1,0:T(8,128)(2,1)} %weights_ref.1) | copy-start | bytes 5111812

commit v2 on v1

--- a/solution.py
+++ b/solution.py
@@ -24,7 +24,6 @@
 HALF = LOCAL_COLS // 2
 CHUNK = HALF // 4
 PIECE = HALF // 8
-CUT = 40
 WIDE = 256
 TILES = LOCAL_COLS // WIDE
 STRIPS = ((0, 512), (512, 768), (1280, 768), (2048, 768), (2816, 512))
@@ -167,16 +166,13 @@
         target[k * 128:(k + 1) * 128, :] = d[:, :RANK] + d[:, RANK:]
 
 
-def gram_kernel(p_ref, gram_ref):
-    p = p_ref[...]
-    gram_ref[...] = lax.dot_general(
-        p, p, TN, precision=lax.Precision.HIGHEST, preferred_element_type=jnp.float32
-    )
-
-
 def lift_send_kernel(p_ref, b_ref, send_ref):
     c = team(lax.axis_index("fsdp"))
-    lift_half(p_ref[...], b_ref, 1 - c, send_ref)
+    p = p_ref[...]
+    lift_half(p, b_ref, 1 - c, send_ref)
+    send_ref[HALF:, :] = lax.dot_general(
+        p, p, TN, precision=lax.Precision.HIGHEST, preferred_element_type=jnp.float32
+    )
 
 
 def lift_keep_kernel(p_ref, b_ref, keep_ref):
@@ -200,6 +196,10 @@
 
 def add_kernel(a_ref, b_ref, out_ref):
     out_ref[...] = a_ref[...] + b_ref[...]
+
+
+def gram_pair_kernel(sent_ref, recv_ref, out_ref):
+    out_ref[...] = sent_ref[HALF:, :] + recv_ref[HALF:, :]
 
 
 def hold_kernel(a_ref, out_ref):
@@ -365,20 +365,22 @@
     norm = 1.0 / jnp.sqrt(sq_ref[0:1, :] + epsilon_sq)
     ortho = ortho_ref[...]
     copies = []
-    for i in range(TILES):
-        cols = slice(i * WIDE, (i + 1) * WIDE)
-        at = pl.ds(i * WIDE, WIDE)
-        subspace = coef_ref[cols, :] * norm
-        sub_buf[cols, :] = subspace
+    for i in range(4):
+        at = pl.ds(i * 2 * CHUNK, 2 * CHUNK)
+        sub_buf[at, :] = coef_ref[at, :] * norm
         copies.append(pltpu.make_async_copy(sub_buf.at[at, :], sub_hbm.at[at, :], sems.at[0, i]))
         copies[-1].start()
-        update = lax.dot_general(
-            ortho, subspace.astype(jnp.bfloat16), NT, preferred_element_type=jnp.float32
-        )
-        buf[:, cols] = (
-            weights_ref[:, cols].astype(jnp.float32) * (1.0 - step_size * shrinkage)
-            - step_size * scaling * update
-        ).astype(jnp.bfloat16)
+    for i, (start, size) in enumerate(STRIPS):
+        for first in range(start, start + size, WIDE):
+            cols = slice(first, first + WIDE)
+            update = lax.dot_general(
+                ortho, sub_buf[cols, :].astype(jnp.bfloat16), NT, preferred_element_type=jnp.float32
+            )
+            buf[:, cols] = (
+                weights_ref[:, cols].astype(jnp.float32) * (1.0 - step_size * shrinkage)
+                - step_size * scaling * update
+            ).astype(jnp.bfloat16)
+        at = pl.ds(start, size)
         copies.append(pltpu.make_async_copy(buf.at[:, at], new_hbm.at[:, at], sems.at[1, i]))
         copies[-1].start()
     for copy in copies:
@@ -394,7 +396,7 @@
         scratch_shapes=[
             VMEM((LOCAL_ROWS, LOCAL_COLS), jnp.bfloat16),
             VMEM((LOCAL_COLS, RANK), jnp.float32),
-            pltpu.SemaphoreType.DMA((2, TILES)),
+            pltpu.SemaphoreType.DMA((2, len(STRIPS))),
         ],
         compiler_params=PARAMS,
         cost_estimate=cost(2 * 256 * 3328 * 128, 7000000),
@@ -407,10 +409,8 @@
     for step in range(3):
         projected = projected + swap_z(projected, step)
 
-    gram = local(gram_kernel, f32(RANK, RANK), [projected], flops=6 * 256 * 128 * 256, nbytes=200000, name="gram")
-    more = xor_fsdp(gram, X_ONE)
     send = local(
-        lift_send_kernel, f32(HALF, RANK), [projected, blended], [gram],
+        lift_send_kernel, f32(HALF + RANK, RANK), [projected, blended],
         flops=2 * 256 * 3328 * 128, nbytes=2000000, name="lift_send",
     )
     recv = xor_fsdp(send, CORE)
@@ -418,26 +418,25 @@
         lift_keep_kernel, f32(HALF, RANK), [projected, blended], [send],
         flops=2 * 256 * 3328 * 128, nbytes=2000000, name="lift_keep",
     )
-    gram = add(gram, more, [keep], "add_x1")
-    more = xor_fsdp(gram, X_THREE)
     n = HALF // 2
-    moving, keep = split_step(0, n, keep, recv, [gram])
+    moving, keep = split_step(0, n, keep, recv)
+    gram = local(gram_pair_kernel, f32(RANK, RANK), [send, recv], [moving], nbytes=200000, name="gram_pair")
     recv = xor_step(moving, 0)
-    gram = add(gram, more, [moving], "add_x3")
-    gram = add(gram, xor_fsdp(gram, Y_ONE), [], "add_y1")
+    gram = add(gram, xor_fsdp(gram, X_THREE), [], "add_x3")
+    gram = add(gram, xor_fsdp(gram, Y_THREE), [], "add_y3")
     n //= 2
     moving, keep = split_step(1, n, keep, recv, [gram])
     recv = xor_step(moving, 1)
     gram = local(hold_kernel, f32(RANK, RANK), [gram], [moving], nbytes=130000, name="hold")
-    more = xor_fsdp(gram, Y_THREE)
+    more = xor_fsdp(gram, X_ONE)
     d = add(keep, recv, [more], "first_sum")
     recv = xor_step(d, 2)
-    gram = add(gram, more, [d], "add_y3")
-    gram = add(gram, xor_fsdp(gram, CORE), [], "add_core")
-    state = eliminate(0, CUT, gram, gram)
-    d = add(d, recv, [state], "second_sum")
+    gram = add(gram, more, [d], "add_x1")
+    more = xor_fsdp(gram, Y_ONE)
+    d = add(d, recv, [more], "second_sum")
     recv = xor_step(d, 3)
-    inverse = eliminate(CUT, RANK, state, gram, [d])
+    gram = add(gram, more, [d], "add_y1")
+    inverse = eliminate(0, RANK, gram, gram)
 
     coef = local(
         block_kernel, bf16(CHUNK, RANK), [d, recv, inverse],

time: 90.3 us -> 89.2 us (0.988)
  waiting for transfers between devices: 39.8 us -> 38.5 us
  starting transfers between devices: 35.2 us -> 36.4 us
  Pallas kernels: 13.7 us -> 12.7 us
    ppermute x6, waiting for transfers between devices: 11.5 us -> 10.1 us  [xor_step(): lax.ppermute(x, 'fsdp', [(i, i ^ MASKS[team(i)][k]) for i in range(FSDP)])]
    ppermute x6, starting transfers between devices: 8.41 us -> 9.5 us  [xor_step(): lax.ppermute(x, 'fsdp', [(i, i ^ MASKS[team(i)][k]) for i in range(FSDP)])]
    pallas_call x20 -> x18, Pallas kernels: 7.13 us -> 6.42 us  [local(): pl.pallas_call(body, in_specs=[VMEM_SPEC] * (used + len(after)), out_spec...]
    ppermute x7 -> x6, starting transfers between devices: 10.1 us -> 10.2 us  [xor_fsdp(): return lax.ppermute(x, 'fsdp', [(i, i ^ mask) for i in range(FSDP)])]
    ppermute x7 -> x6, waiting for transfers between devices: 16.2 us -> 16.3 us  [xor_fsdp(): return lax.ppermute(x, 'fsdp', [(i, i ^ mask) for i in range(FSDP)])]
  transfers between devices with their start and end apart: 20 -> 19, of which waited for: 15 -> 15; matrix products, arithmetic and copies ran while one was open for 0% -> 0% of each run, Pallas kernels for 8% -> 7%
where the time goes in v2:
time: 89.2 us; the launch traced here: 89.1 us
  waiting for transfers between devices  38.5 us (43%)
  starting transfers between devices  36.4 us (41%)
  Pallas kernels  12.7 us (14%)
  between operations  0.96 us (1%)
    ppermute x6, waiting for transfers between devices, xor_fsdp(): return lax.ppermute(x, 'fsdp', [(i, i ^ mask) for i in range(FSDP)])  16.3 us
    ppermute x3, waiting for transfers between devices, swap_z(): return lax.ppermute(x, ('fsdp', 'tp'), perm)  10.3 us
    ppermute x6, starting transfers between devices, xor_fsdp(): return lax.ppermute(x, 'fsdp', [(i, i ^ mask) for i in range(FSDP)])  10.2 us
    ppermute x6, waiting for transfers between devices, xor_step(): lax.ppermute(x, 'fsdp', [(i, i ^ MASKS[team(i)][k]) for i in range(FSDP)])  10.1 us
    ppermute x3, starting transfers between devices, swap_z(): return lax.ppermute(x, ('fsdp', 'tp'), perm)  9.5 us
    ppermute x6, starting transfers between devices, xor_step(): lax.ppermute(x, 'fsdp', [(i, i ^ MASKS[team(i)][k]) for i in range(FSDP)])  9.5 us
    ppermute x4, starting transfers between devices, cross_z(): return lax.ppermute(x, ('fsdp', 'tp'), perm)  7.17 us
    pallas_call x18, Pallas kernels, local(): pl.pallas_call(body, in_specs=[VMEM_SPEC] * (used + len(after)), out_spec...  6.42 us
  transfers between devices with their start and end apart: 19, of which 15 were waited for; matrix products, arithmetic and copies ran while one was open for 0% of the time, Pallas kernels for 7%

profile of v2, /device:TPU:1, one launch (start us, length us, event | category | flops | bytes accessed | tf_op | source)
XLA Modules:
  0.0 89.1 jit_solution(388898873760031748)
XLA Ops:
  0.6 2.9 %project.1 = (bf16[256,3328]{1,0:T(8,128)(2,1)S(1)}, f32[256,128]{1,0:T(8,128)S(1)}) custom-call(bf16[256,3328]{1,0:T(8,128)(2,1)} %m_hbm.1, bf16[256,3328]{1,0:T(8,128)(2,1)} %g_hbm.1, f32[3328,128]{1,0:T(8,128)} %s_hbm.1), custom_call_target="tpu_custom_call" | custom-call | flops 218103808 | bytes 7000000 | tf_op jit(solution)/shard_map/project/pallas_call | solution.py:123
  3.5 6.5 %collective-permute-start = (f32[256,128]{1,0:T(8,128)S(1)}, f32[256,128]{1,0:T(8,128)S(1)}, u32[]{:S(2)}, u32[]{:S(2)}) collective-permute-start(f32[256,128]{1,0:T(8,128)S(1)} %get-tuple-element.13), channel_id=1, source_target_pairs={{0,1},{1,0},{2,3},{3,2},{4,5},{5,4},{6,7},{7,6},{9,10},{10,9},{11,... | collective-permute-start | bytes 393224 | tf_op jit(solution)/shard_map/ppermute | solution.py:71
  10.0 2.4 %collective-permute-done = f32[256,128]{1,0:T(8,128)S(1)} collective-permute-done((f32[256,128]{1,0:T(8,128)S(1)}, f32[256,128]{1,0:T(8,128)S(1)}, u32[]{:S(2)}, u32[]{:S(2)}) %collective-permute-start) | collective-permute-done | bytes 131104 | tf_op jit(solution)/shard_map/ppermute | solution.py:71
  12.5 3.8 %collective-permute-done.1 = f32[256,128]{1,0:T(8,128)S(1)} collective-permute-done((f32[256,128]{1,0:T(8,128)S(1)}, f32[256,128]{1,0:T(8,128)S(1)}, u32[]{:S(2)}, u32[]{:S(2)}) %collective-permute-start.1) | collective-permute-done | bytes 131104 | tf_op jit(solution)/shard_map/ppermute | solution.py:71
  16.3 2.9 %collective-permute-start.2 = (f32[256,128]{1,0:T(8,128)S(1)}, f32[256,128]{1,0:T(8,128)S(1)}, u32[]{:S(2)}, u32[]{:S(2)}) collective-permute-start(f32[256,128]{1,0:T(8,128)S(1)} %add.22), channel_id=1, source_target_pairs={{2,5},{5,2},{1,6},{6,1},{4,7},{7,4},{3,0},{0,3},{11,14},{14,11},{1... | collective-permute-start | bytes 393224 | tf_op jit(solution)/shard_map/ppermute | solution.py:71
  19.2 4.1 %collective-permute-done.2 = f32[256,128]{1,0:T(8,128)S(1)} collective-permute-done((f32[256,128]{1,0:T(8,128)S(1)}, f32[256,128]{1,0:T(8,128)S(1)}, u32[]{:S(2)}, u32[]{:S(2)}) %collective-permute-start.2) | collective-permute-done | bytes 131104 | tf_op jit(solution)/shard_map/ppermute | solution.py:71
  24.0 4.1 %collective-permute-start.3 = (f32[1792,128]{1,0:T(8,128)S(1)}, f32[1792,128]{1,0:T(8,128)S(1)}, u32[]{:S(2)}, u32[]{:S(2)}) collective-permute-start(f32[1792,128]{1,0:T(8,128)S(1)} %lift_send.1.refs_2_.refs_0_), channel_id=1, source_target_pairs={{0,8},{8,0},{16,24},{24,16},{32,40},{40,32},{48,56},{56,48},{64,72... | collective-permute-start | bytes 2752520 | tf_op jit(solution)/shard_map/ppermute | solution.py:80
  28.5 1.6 %collective-permute-done.3.refs_1_ = f32[1792,128]{1,0:T(8,128)S(1)} collective-permute-done((f32[1792,128]{1,0:T(8,128)S(1)}, f32[1792,128]{1,0:T(8,128)S(1)}, u32[]{:S(2)}, u32[]{:S(2)}) %collective-permute-start.3) | collective-permute-done | bytes 917536 | tf_op jit(solution)/shard_map/ppermute | solution.py:80
  30.2 1.6 %collective-permute-start.4 = (f32[832,128]{1,0:T(8,128)S(1)}, f32[832,128]{1,0:T(8,128)S(1)}, u32[]{:S(2)}, u32[]{:S(2)}) collective-permute-start(f32[832,128]{1,0:T(8,128)S(1)} %get-tuple-element.16.refs_2_), channel_id=1, source_target_pairs={{0,24},{8,64},{16,88},{24,0},{32,56},{40,96},{48,120},{56,32},{64,... | collective-permute-start | bytes 1277960 | tf_op jit(solution)/shard_map/ppermute | solution.py:84
  31.9 2.6 %collective-permute-start.5 = (f32[128,128]{1,0:T(8,128)S(1)}, f32[128,128]{1,0:T(8,128)S(1)}, u32[]{:S(2)}, u32[]{:S(2)}) collective-permute-start(f32[128,128]{1,0:T(8,128)S(1)} %gram_pair.1.refs_0_), channel_id=1, source_target_pairs={{0,56},{8,48},{16,40},{24,32},{32,24},{40,16},{48,8},{56,0},{64,12... | collective-permute-start | bytes 196616 | tf_op jit(solution)/shard_map/ppermute | solution.py:80
  34.5 2.5 %collective-permute-done.5.refs_1_ = f32[128,128]{1,0:T(8,128)S(1)} collective-permute-done((f32[128,128]{1,0:T(8,128)S(1)}, f32[128,128]{1,0:T(8,128)S(1)}, u32[]{:S(2)}, u32[]{:S(2)}) %collective-permute-start.5) | collective-permute-done | bytes 65568 | tf_op jit(solution)/shard_map/ppermute | solution.py:80
  37.0 1.9 %collective-permute-start.6 = (f32[128,128]{1,0:T(8,128)S(1)}, f32[128,128]{1,0:T(8,128)S(1)}, u32[]{:S(2)}, u32[]{:S(2)}) collective-permute-start(f32[128,128]{1,0:T(8,128)S(1)} %add_x3.1.refs_0_), channel_id=1, source_target_pairs={{0,200},{8,192},{16,216},{24,208},{32,232},{40,224},{48,248},{56,2... | collective-permute-start | bytes 196616 | tf_op jit(solution)/shard_map/ppermute | solution.py:80
  38.9 3.2 %collective-permute-done.6.refs_1_ = f32[128,128]{1,0:T(8,128)S(1)} collective-permute-done((f32[128,128]{1,0:T(8,128)S(1)}, f32[128,128]{1,0:T(8,128)S(1)}, u32[]{:S(2)}, u32[]{:S(2)}) %collective-permute-start.6) | collective-permute-done | bytes 65568 | tf_op jit(solution)/shard_map/ppermute | solution.py:80
  42.2 1.8 %collective-permute-start.7 = (f32[416,128]{1,0:T(8,128)S(1)}, f32[416,128]{1,0:T(8,128)S(1)}, u32[]{:S(2)}, u32[]{:S(2)}) collective-permute-start(f32[416,128]{1,0:T(8,128)S(1)} %get-tuple-element.18.refs_1_), channel_id=1, source_target_pairs={{0,56},{8,192},{16,216},{24,32},{32,24},{40,224},{48,248},{56,0},{... | collective-permute-start | bytes 638984 | tf_op jit(solution)/shard_map/ppermute | solution.py:84
  44.0 1.0 %collective-permute-start.8 = (f32[128,128]{1,0:T(8,128)S(1)}, f32[128,128]{1,0:T(8,128)S(1)}, u32[]{:S(2)}, u32[]{:S(2)}) collective-permute-start(f32[128,128]{1,0:T(8,128)S(1)} %hold.1.refs_0_), channel_id=1, source_target_pairs={{0,24},{8,16},{16,8},{24,0},{32,56},{40,48},{48,40},{56,32},{64,88... | collective-permute-start | bytes 196616 | tf_op jit(solution)/shard_map/ppermute | solution.py:80
  45.0 3.0 %collective-permute-done.8.refs_2_.refs_1_ = f32[128,128]{1,0:T(8,128)S(1)} collective-permute-done((f32[128,128]{1,0:T(8,128)S(1)}, f32[128,128]{1,0:T(8,128)S(1)}, u32[]{:S(2)}, u32[]{:S(2)}) %collective-permute-start.8) | collective-permute-done | bytes 65568 | tf_op jit(solution)/shard_map/ppermute | solution.py:80
  48.0 0.9 %collective-permute-done.7.refs_1_ = f32[416,128]{1,0:T(8,128)S(1)} collective-permute-done((f32[416,128]{1,0:T(8,128)S(1)}, f32[416,128]{1,0:T(8,128)S(1)}, u32[]{:S(2)}, u32[]{:S(2)}) %collective-permute-start.7) | collective-permute-done | bytes 213024 | tf_op jit(solution)/shard_map/ppermute | solution.py:84
  49.0 0.8 collective-permute-start.9
  49.8 4.7 %collective-permute-done.10.refs_2_.refs_1_ = f32[128,128]{1,0:T(8,128)S(1)} collective-permute-done((f32[128,128]{1,0:T(8,128)S(1)}, f32[128,128]{1,0:T(8,128)S(1)}, u32[]{:S(2)}, u32[]{:S(2)}) %collective-permute-start.10) | collective-permute-done | bytes 65568 | tf_op jit(solution)/shard_map/ppermute | solution.py:80
  54.7 3.2 %collective-permute-start.11 = (f32[416,128]{1,0:T(8,128)S(1)}, f32[416,128]{1,0:T(8,128)S(1)}, u32[]{:S(2)}, u32[]{:S(2)}) collective-permute-start(f32[416,128]{1,0:T(8,128)S(1)} %second_sum.1.refs_2_.refs_0_), channel_id=1, source_target_pairs={{0,200},{8,48},{16,40},{24,208},{32,232},{40,16},{48,8},{56,240},{... | collective-permute-start | bytes 638984 | tf_op jit(solution)/shard_map/ppermute | solution.py:84
  57.9 4.2 %eliminate0.1.refs_2_.refs_1_ = f32[128,128]{1,0:T(8,128)S(1)} custom-call(f32[128,128]{1,0:T(8,128)S(1)} %add_y1.1.refs_0_.refs_1_, f32[128,128]{1,0:T(8,128)S(1)} %add_y1.1.refs_0_.refs_1_), custom_call_target="tpu_custom_call" | custom-call | flops 4000000 | bytes 19200000 | tf_op jit(solution)/shard_map/eliminate0/pallas_call | solution.py:147
  62.4 2.0 %collective-permute-start.12 = (bf16[416,128]{1,0:T(8,128)(2,1)S(1)}, bf16[416,128]{1,0:T(8,128)(2,1)S(1)}, u32[]{:S(2)}, u32[]{:S(2)}) collective-permute-start(bf16[416,128]{1,0:T(8,128)(2,1)S(1)} %block.1.refs_2_.refs_0_), channel_id=1, source_target_pairs={{0,56},{8,192},{16,216},{24,32},{32,24},{40,224},{48,248},{56,0},{... | collective-permute-start | bytes 319496 | tf_op jit(solution)/shard_map/ppermute | solution.py:84
  64.7 3.5 %collective-permute-done.12.refs_1_ = bf16[416,128]{1,0:T(8,128)(2,1)S(1)} collective-permute-done((bf16[416,128]{1,0:T(8,128)(2,1)S(1)}, bf16[416,128]{1,0:T(8,128)(2,1)S(1)}, u32[]{:S(2)}, u32[]{:S(2)}) %collective-permute-start.12) | collective-permute-done | bytes 106528 | tf_op jit(solution)/shard_map/ppermute | solution.py:84
  68.3 5.5 %collective-permute-done.13.refs_1_ = bf16[832,128]{1,0:T(8,128)(2,1)S(1)} collective-permute-done((bf16[832,128]{1,0:T(8,128)(2,1)S(1)}, bf16[832,128]{1,0:T(8,128)(2,1)S(1)}, u32[]{:S(2)}, u32[]{:S(2)}) %collective-permute-start.13) | collective-permute-done | bytes 213024 | tf_op jit(solution)/shard_map/ppermute | solution.py:84
  74.4 1.4 %collective-permute-done.14.refs_1_ = bf16[1664,128]{1,0:T(8,128)(2,1)S(1)} collective-permute-done((bf16[1664,128]{1,0:T(8,128)(2,1)S(1)}, bf16[1664,128]{1,0:T(8,128)(2,1)S(1)}, u32[]{:S(2)}, u32[]{:S(2)}) %collective-permute-start.14) | collective-permute-done | bytes 426016 | tf_op jit(solution)/shard_map/ppermute | solution.py:80
  76.0 2.0 %collective-permute-start.17 = (f32[8,128]{1,0:T(8,128)S(1)}, f32[8,128]{1,0:T(8,128)S(1)}, u32[]{:S(2)}, u32[]{:S(2)}) collective-permute-start(f32[8,128]{1,0:T(8,128)S(1)} %get-tuple-element.20), channel_id=1, source_target_pairs={{0,11},{1,10},{2,9},{3,8},{4,15},{5,14},{6,13},{7,12},{8,3},{9,2},... | collective-permute-start | bytes 12296 | tf_op jit(solution)/shard_map/ppermute | solution.py:76
  78.0 2.1 %collective-permute-start.15 = (f32[8,128]{1,0:T(8,128)S(1)}, f32[8,128]{1,0:T(8,128)S(1)}, u32[]{:S(2)}, u32[]{:S(2)}) collective-permute-start(f32[8,128]{1,0:T(8,128)S(1)} %get-tuple-element.20), channel_id=1, source_target_pairs={{0,9},{1,8},{2,11},{3,10},{4,13},{5,12},{6,15},{7,14},{8,1},{9,0},... | collective-permute-start | bytes 12296 | tf_op jit(solution)/shard_map/ppermute | solution.py:76
  80.2 0.7 collective-permute-done.17
  80.9 1.1 %collective-permute-done.16 = f32[8,128]{1,0:T(8,128)S(1)} collective-permute-done((f32[8,128]{1,0:T(8,128)S(1)}, f32[8,128]{1,0:T(8,128)S(1)}, u32[]{:S(2)}, u32[]{:S(2)}) %collective-permute-start.16) | collective-permute-done | bytes 4128 | tf_op jit(solution)/shard_map/ppermute | solution.py:76
  82.0 3.0 %collective-permute-start.18 = (f32[8,128]{1,0:T(8,128)S(1)}, f32[8,128]{1,0:T(8,128)S(1)}, u32[]{:S(2)}, u32[]{:S(2)}) collective-permute-start(f32[8,128]{1,0:T(8,128)S(1)} %add_add_fusion), channel_id=1, source_target_pairs={{0,15},{1,14},{2,13},{3,12},{4,11},{5,10},{6,9},{7,8},{8,7},{9,6},... | collective-permute-start | bytes 12296 | tf_op jit(solution)/shard_map/ppermute | solution.py:76
  85.0 1.5 %finish_momentum.1 = bf16[256,3328]{1,0:T(8,128)(2,1)} custom-call(f32[3328,128]{1,0:T(8,128)S(1)} %get-tuple-element.19.coef_ref, bf16[256,128]{1,0:T(8,128)(2,1)S(1)} %ortho.1.refs_2_.ortho_ref, bf16[256,3328]{1,0:T(8,128)(2,1)S(1)} %get-tuple-element.14.refs_1_.b_ref), custom_call_target="tpu_custom_call" | custom-call | flops 218103808 | bytes 5000000 | tf_op jit(solution)/shard_map/finish_momentum/pallas_call | solution.py:348
  87.0 1.9 %finish_weights.1 = (bf16[256,3328]{1,0:T(8,128)(2,1)}, f32[3328,128]{1,0:T(8,128)}) custom-call(f32[8,128]{1,0:T(8,128)S(1)} %add.27.sq_ref, f32[3328,128]{1,0:T(8,128)S(1)} %get-tuple-element.19.coef_ref, bf16[256,128]{1,0:T(8,128)(2,1)S(1)} %ortho.1.refs_2_.ortho_ref, bf16[256,3328]{1,0:T(8,128)(2,1)S(1)} %copy-done), custom_call_target="tpu_custom_call" | custom-call | flops 218103808 | bytes 7000000 | tf_op jit(solution)/shard_map/finish_weights/pallas_call | solution.py:391
  (34 shorter events, 3.7 us)
Async XLA Ops:
  3.5 8.8 %collective-permute-start = (f32[256,128]{1,0:T(8,128)S(1)}, f32[256,128]{1,0:T(8,128)S(1)}, u32[]{:S(2)}, u32[]{:S(2)}) collective-permute-start(f32[256,128]{1,0:T(8,128)S(1)} %get-tuple-element.13), channel_id=1, source_target_pairs={{0,1},{1,0},{2,3},{3,2},{4,5},{5,4},{6,7},{7,6},{9,10},{10,9},{11,... | collective-permute-start | bytes 393224 | tf_op jit(solution)/shard_map/ppermute | solution.py:71
  12.4 3.9 %collective-permute-start.1 = (f32[256,128]{1,0:T(8,128)S(1)}, f32[256,128]{1,0:T(8,128)S(1)}, u32[]{:S(2)}, u32[]{:S(2)}) collective-permute-start(f32[256,128]{1,0:T(8,128)S(1)} %add.21), channel_id=1, source_target_pairs={{1,2},{2,1},{3,4},{4,3},{5,6},{6,5},{7,0},{0,7},{10,11},{11,10},{1... | collective-permute-start | bytes 393224 | tf_op jit(solution)/shard_map/ppermute | solution.py:71
  16.3 7.1 %collective-permute-start.2 = (f32[256,128]{1,0:T(8,128)S(1)}, f32[256,128]{1,0:T(8,128)S(1)}, u32[]{:S(2)}, u32[]{:S(2)}) collective-permute-start(f32[256,128]{1,0:T(8,128)S(1)} %add.22), channel_id=1, source_target_pairs={{2,5},{5,2},{1,6},{6,1},{4,7},{7,4},{3,0},{0,3},{11,14},{14,11},{1... | collective-permute-start | bytes 393224 | tf_op jit(solution)/shard_map/ppermute | solution.py:71
  24.0 6.2 %collective-permute-start.3 = (f32[1792,128]{1,0:T(8,128)S(1)}, f32[1792,128]{1,0:T(8,128)S(1)}, u32[]{:S(2)}, u32[]{:S(2)}) collective-permute-start(f32[1792,128]{1,0:T(8,128)S(1)} %lift_send.1.refs_2_.refs_0_), channel_id=1, source_target_pairs={{0,8},{8,0},{16,24},{24,16},{32,40},{40,32},{48,56},{56,48},{64,72... | collective-permute-start | bytes 2752520 | tf_op jit(solution)/shard_map/ppermute | solution.py:80
  30.2 11.8 %collective-permute-start.4 = (f32[832,128]{1,0:T(8,128)S(1)}, f32[832,128]{1,0:T(8,128)S(1)}, u32[]{:S(2)}, u32[]{:S(2)}) collective-permute-start(f32[832,128]{1,0:T(8,128)S(1)} %get-tuple-element.16.refs_2_), channel_id=1, source_target_pairs={{0,24},{8,64},{16,88},{24,0},{32,56},{40,96},{48,120},{56,32},{64,... | collective-permute-start | bytes 1277960 | tf_op jit(solution)/shard_map/ppermute | solution.py:84
  31.9 5.1 %collective-permute-start.5 = (f32[128,128]{1,0:T(8,128)S(1)}, f32[128,128]{1,0:T(8,128)S(1)}, u32[]{:S(2)}, u32[]{:S(2)}) collective-permute-start(f32[128,128]{1,0:T(8,128)S(1)} %gram_pair.1.refs_0_), channel_id=1, source_target_pairs={{0,56},{8,48},{16,40},{24,32},{32,24},{40,16},{48,8},{56,0},{64,12... | collective-permute-start | bytes 196616 | tf_op jit(solution)/shard_map/ppermute | solution.py:80
  37.0 5.1 %collective-permute-start.6 = (f32[128,128]{1,0:T(8,128)S(1)}, f32[128,128]{1,0:T(8,128)S(1)}, u32[]{:S(2)}, u32[]{:S(2)}) collective-permute-start(f32[128,128]{1,0:T(8,128)S(1)} %add_x3.1.refs_0_), channel_id=1, source_target_pairs={{0,200},{8,192},{16,216},{24,208},{32,232},{40,224},{48,248},{56,2... | collective-permute-start | bytes 196616 | tf_op jit(solution)/shard_map/ppermute | solution.py:80
  42.2 6.8 %collective-permute-start.7 = (f32[416,128]{1,0:T(8,128)S(1)}, f32[416,128]{1,0:T(8,128)S(1)}, u32[]{:S(2)}, u32[]{:S(2)}) collective-permute-start(f32[416,128]{1,0:T(8,128)S(1)} %get-tuple-element.18.refs_1_), channel_id=1, source_target_pairs={{0,56},{8,192},{16,216},{24,32},{32,24},{40,224},{48,248},{56,0},{... | collective-permute-start | bytes 638984 | tf_op jit(solution)/shard_map/ppermute | solution.py:84
  44.0 4.0 %collective-permute-start.8 = (f32[128,128]{1,0:T(8,128)S(1)}, f32[128,128]{1,0:T(8,128)S(1)}, u32[]{:S(2)}, u32[]{:S(2)}) collective-permute-start(f32[128,128]{1,0:T(8,128)S(1)} %hold.1.refs_0_), channel_id=1, source_target_pairs={{0,24},{8,16},{16,8},{24,0},{32,56},{40,48},{48,40},{56,32},{64,88... | collective-permute-start | bytes 196616 | tf_op jit(solution)/shard_map/ppermute | solution.py:80
  49.0 5.7 %collective-permute-start.9 = (f32[416,128]{1,0:T(8,128)S(1)}, f32[416,128]{1,0:T(8,128)S(1)}, u32[]{:S(2)}, u32[]{:S(2)}) collective-permute-start(f32[416,128]{1,0:T(8,128)S(1)} %first_sum.1.refs_2_.refs_0_), channel_id=1, source_target_pairs={{0,72},{8,16},{16,8},{24,80},{32,104},{40,48},{48,40},{56,112},{64... | collective-permute-start | bytes 638984 | tf_op jit(solution)/shard_map/ppermute | solution.py:84
  49.7 4.8 %collective-permute-start.10 = (f32[128,128]{1,0:T(8,128)S(1)}, f32[128,128]{1,0:T(8,128)S(1)}, u32[]{:S(2)}, u32[]{:S(2)}) collective-permute-start(f32[128,128]{1,0:T(8,128)S(1)} %add_x1.1.refs_0_), channel_id=1, source_target_pairs={{0,72},{8,64},{16,88},{24,80},{32,104},{40,96},{48,120},{56,112},{... | collective-permute-start | bytes 196616 | tf_op jit(solution)/shard_map/ppermute | solution.py:80
  54.7 7.5 %collective-permute-start.11 = (f32[416,128]{1,0:T(8,128)S(1)}, f32[416,128]{1,0:T(8,128)S(1)}, u32[]{:S(2)}, u32[]{:S(2)}) collective-permute-start(f32[416,128]{1,0:T(8,128)S(1)} %second_sum.1.refs_2_.refs_0_), channel_id=1, source_target_pairs={{0,200},{8,48},{16,40},{24,208},{32,232},{40,16},{48,8},{56,240},{... | collective-permute-start | bytes 638984 | tf_op jit(solution)/shard_map/ppermute | solution.py:84
  62.4 5.7 %collective-permute-start.12 = (bf16[416,128]{1,0:T(8,128)(2,1)S(1)}, bf16[416,128]{1,0:T(8,128)(2,1)S(1)}, u32[]{:S(2)}, u32[]{:S(2)}) collective-permute-start(bf16[416,128]{1,0:T(8,128)(2,1)S(1)} %block.1.refs_2_.refs_0_), channel_id=1, source_target_pairs={{0,56},{8,192},{16,216},{24,32},{32,24},{40,224},{48,248},{56,0},{... | collective-permute-start | bytes 319496 | tf_op jit(solution)/shard_map/ppermute | solution.py:84
  68.2 5.6 %collective-permute-start.13 = (bf16[832,128]{1,0:T(8,128)(2,1)S(1)}, bf16[832,128]{1,0:T(8,128)(2,1)S(1)}, u32[]{:S(2)}, u32[]{:S(2)}) collective-permute-start(bf16[832,128]{1,0:T(8,128)(2,1)S(1)} %join1.1.refs_0_), channel_id=1, source_target_pairs={{0,24},{8,64},{16,88},{24,0},{32,56},{40,96},{48,120},{56,32},{64,... | collective-permute-start | bytes 638984 | tf_op jit(solution)/shard_map/ppermute | solution.py:84
  73.9 1.9 %collective-permute-start.14 = (bf16[1664,128]{1,0:T(8,128)(2,1)S(1)}, bf16[1664,128]{1,0:T(8,128)(2,1)S(1)}, u32[]{:S(2)}, u32[]{:S(2)}) collective-permute-start(bf16[1664,128]{1,0:T(8,128)(2,1)S(1)} %join0.1.refs_0_), channel_id=1, source_target_pairs={{0,8},{8,0},{16,24},{24,16},{32,40},{40,32},{48,56},{56,48},{64,72... | collective-permute-start | bytes 1277960 | tf_op jit(solution)/shard_map/ppermute | solution.py:80
  76.0 4.9 %collective-permute-start.17 = (f32[8,128]{1,0:T(8,128)S(1)}, f32[8,128]{1,0:T(8,128)S(1)}, u32[]{:S(2)}, u32[]{:S(2)}) collective-permute-start(f32[8,128]{1,0:T(8,128)S(1)} %get-tuple-element.20), channel_id=1, source_target_pairs={{0,11},{1,10},{2,9},{3,8},{4,15},{5,14},{6,13},{7,12},{8,3},{9,2},... | collective-permute-start | bytes 12296 | tf_op jit(solution)/shard_map/ppermute | solution.py:76
  78.0 3.9 %collective-permute-start.16 = (f32[8,128]{1,0:T(8,128)S(1)}, f32[8,128]{1,0:T(8,128)S(1)}, u32[]{:S(2)}, u32[]{:S(2)}) collective-permute-start(f32[8,128]{1,0:T(8,128)S(1)} %get-tuple-element.20), channel_id=1, source_target_pairs={{0,10},{1,11},{2,8},{3,9},{4,14},{5,15},{6,12},{7,13},{8,2},{9,3},... | collective-permute-start | bytes 12296 | tf_op jit(solution)/shard_map/ppermute | solution.py:76
  78.0 3.9 %collective-permute-start.15 = (f32[8,128]{1,0:T(8,128)S(1)}, f32[8,128]{1,0:T(8,128)S(1)}, u32[]{:S(2)}, u32[]{:S(2)}) collective-permute-start(f32[8,128]{1,0:T(8,128)S(1)} %get-tuple-element.20), channel_id=1, source_target_pairs={{0,9},{1,8},{2,11},{3,10},{4,13},{5,12},{6,15},{7,14},{8,1},{9,0},... | collective-permute-start | bytes 12296 | tf_op jit(solution)/shard_map/ppermute | solution.py:76
  82.0 4.5 %collective-permute-start.18 = (f32[8,128]{1,0:T(8,128)S(1)}, f32[8,128]{1,0:T(8,128)S(1)}, u32[]{:S(2)}, u32[]{:S(2)}) collective-permute-start(f32[8,128]{1,0:T(8,128)S(1)} %add_add_fusion), channel_id=1, source_target_pairs={{0,15},{1,14},{2,13},{3,12},{4,11},{5,10},{6,9},{7,8},{8,7},{9,6},... | collective-permute-start | bytes 12296 | tf_op jit(solution)/shard_map/ppermute | solution.py:76
  85.0 2.1 %copy-start = (bf16[256,3328]{1,0:T(8,128)(2,1)S(1)}, bf16[256,3328]{1,0:T(8,128)(2,1)}, u32[]{:S(2)}) copy-start(bf16[256,3328]{1,0:T(8,128)(2,1)} %weights_ref.1) | copy-start | bytes 5111812

commit v3 on v2

--- a/solution.py
+++ b/solution.py
@@ -61,6 +61,8 @@
 def cost(flops, nbytes):
     return pl.CostEstimate(flops=flops, bytes_accessed=nbytes, transcendentals=0)
 
+Z_TURNS = ((3, -3), (1, -1), (-2, 2))
+
 
 def swap_z(x, step):
     perm = []
@@ -71,8 +73,19 @@
     return lax.ppermute(x, ("fsdp", "tp"), perm)
 
 
-def cross_z(x, mask):
-    perm = [(f * TP + z, (f ^ 1) * TP + (z ^ mask)) for f in range(FSDP) for z in range(TP)]
+def pair_z(x, cross):
+    perm = [
+        (f * TP + z, (f ^ (MASKS[team(f)][0] if cross else 0)) * TP + (z ^ 1))
+        for f in range(FSDP) for z in range(TP)
+    ]
+    return lax.ppermute(x, ("fsdp", "tp"), perm)
+
+
+def turn_z(x, to_odd, to_even):
+    perm = [
+        ((f ^ 1) * TP + (z + (to_odd if z % 2 else to_even)) % TP, f * TP + z)
+        for f in range(FSDP) for z in range(TP)
+    ]
     return lax.ppermute(x, ("fsdp", "tp"), perm)
 
 
@@ -200,6 +213,10 @@
 
 def gram_pair_kernel(sent_ref, recv_ref, out_ref):
     out_ref[...] = sent_ref[HALF:, :] + recv_ref[HALF:, :]
+
+
+def gram_four_kernel(a_ref, b_ref, c_ref, d_ref, out_ref):
+    out_ref[...] = (a_ref[...] + b_ref[...]) + (c_ref[...] + d_ref[...])
 
 
 def hold_kernel(a_ref, out_ref):
@@ -315,15 +332,28 @@
     out_ref[pl.ds(pl.multiple_of((1 - bit) * n, 16), n), :] = recv_ref[...]
 
 
-def unpack_kernel(own_ref, other_ref, coef_ref, sq_ref):
+def chunk_squares(ref, start):
+    rows = ref[start:start + CHUNK, :].astype(jnp.float32)
+    return jnp.sum((rows * rows).reshape(CHUNK // 8, 8, RANK), axis=0)
+
+
+def squares_kernel(ref, out_ref):
+    out_ref[...] = chunk_squares(ref, 0) + chunk_squares(ref, CHUNK)
+
+
+def last_join_kernel(mine_ref, recv_ref, sq_ref, pair_ref, cross_ref, out_ref, sum_ref):
+    join_kernel(0, 2 * CHUNK, mine_ref, recv_ref, out_ref)
+    other = chunk_squares(recv_ref, 0) + chunk_squares(recv_ref, CHUNK)
+    sum_ref[...] = (sq_ref[...] + other) + (pair_ref[...] + cross_ref[...])
+
+
+def unpack_kernel(own_ref, other_ref, sq_ref, other_sq_ref, coef_ref, sum_ref):
     c = team(lax.axis_index("fsdp"))
-    squares = jnp.zeros((8, RANK), jnp.float32)
     for source, half in ((own_ref, c), (other_ref, 1 - c)):
         for i in range(0, HALF, PIECE):
             rows = source[i:i + PIECE, :].astype(jnp.float32)
-            squares = squares + jnp.sum((rows * rows).reshape(PIECE // 8, 8, RANK), axis=0)
             coef_ref[pl.ds(pl.multiple_of(half * HALF + i, 8), PIECE), :] = rows
-    sq_ref[...] = jnp.broadcast_to(jnp.sum(squares, axis=0, keepdims=True), (8, RANK))
+    sum_ref[...] = sq_ref[...] + other_sq_ref[...]
 
 
 def momentum_kernel(coef_ref, ortho_ref, b_ref, mom_hbm, buf, sems):
@@ -360,9 +390,10 @@
     )(coef, ortho, blended)
 
 
-def weights_kernel(sq_ref, coef_ref, ortho_ref, weights_ref, new_hbm, sub_hbm, buf, sub_buf, sems):
+def weights_kernel(sq_ref, opposite_ref, next_ref, previous_ref, coef_ref, ortho_ref, weights_ref, new_hbm, sub_hbm, buf, sub_buf, sems):
     scaling = math.sqrt(ROWS * COLS / RANK)
-    norm = 1.0 / jnp.sqrt(sq_ref[0:1, :] + epsilon_sq)
+    squares = (sq_ref[...] + opposite_ref[...]) + (next_ref[...] + previous_ref[...])
+    norm = 1.0 / jnp.sqrt(jnp.sum(squares, axis=0, keepdims=True) + epsilon_sq)
     ortho = ortho_ref[...]
     copies = []
     for i in range(4):
@@ -390,7 +421,7 @@
 def finish_weights(squares, coef, ortho, weights):
     return pl.pallas_call(
         weights_kernel,
-        in_specs=[VMEM_SPEC] * 4,
+        in_specs=[VMEM_SPEC] * 7,
         out_specs=[HBM_SPEC] * 2,
         out_shape=[bf16(LOCAL_ROWS, LOCAL_COLS), f32(LOCAL_COLS, RANK)],
         scratch_shapes=[
@@ -401,7 +432,7 @@
         compiler_params=PARAMS,
         cost_estimate=cost(2 * 256 * 3328 * 128, 7000000),
         name="finish_weights",
-    )(squares, coef, ortho, weights)
+    )(*squares, coef, ortho, weights)
 
 
 def on_device(momentum, gradient, weights, subspace):
@@ -422,8 +453,11 @@
     moving, keep = split_step(0, n, keep, recv)
     gram = local(gram_pair_kernel, f32(RANK, RANK), [send, recv], [moving], nbytes=200000, name="gram_pair")
     recv = xor_step(moving, 0)
-    gram = add(gram, xor_fsdp(gram, X_THREE), [], "add_x3")
-    gram = add(gram, xor_fsdp(gram, Y_THREE), [], "add_y3")
+    gram = local(
+        gram_four_kernel, f32(RANK, RANK),
+        [gram] + [xor_fsdp(gram, mask) for mask in (X_THREE, Y_THREE, X_THREE ^ Y_THREE)],
+        nbytes=400000, name="gram_four",
+    )
     n //= 2
     moving, keep = split_step(1, n, keep, recv, [gram])
     recv = xor_step(moving, 1)
@@ -446,17 +480,24 @@
         ortho_kernel, bf16(LOCAL_ROWS, RANK), [projected, inverse], [coef],
         flops=6 * 256 * 256 * 128, nbytes=300000, name="ortho",
     )
-    for k, n in ((1, CHUNK), (0, 2 * CHUNK)):
-        coef = local(
-            functools.partial(join_kernel, k, n), bf16(2 * n, RANK), [coef, xor_step(coef, k)],
-            [ortho] if k else [], nbytes=n * 1024, name=f"join{k}",
-        )
+    coef = local(
+        functools.partial(join_kernel, 1, CHUNK), bf16(2 * CHUNK, RANK), [coef, xor_step(coef, 1)],
+        [ortho], nbytes=CHUNK * 1024, name="join1",
+    )
+
+    recv = xor_step(coef, 0)
+    squares = local(squares_kernel, f32(8, RANK), [coef], flops=CHUNK * 512, nbytes=400000, name="squares")
     coef, squares = local(
-        unpack_kernel, [f32(LOCAL_COLS, RANK), f32(8, RANK)], [coef, xor_fsdp(coef, CORE)],
-        flops=3328 * 256, nbytes=2600000, name="unpack",
-    )
-    squares = (squares + cross_z(squares, 1)) + (cross_z(squares, 2) + cross_z(squares, 3))
-    squares = squares + cross_z(squares, 7)
+        last_join_kernel, [bf16(HALF, RANK), f32(8, RANK)],
+        [coef, recv, squares, pair_z(squares, False), pair_z(squares, True)],
+        nbytes=CHUNK * 4096, name="join0",
+    )
+    coef, squares = local(
+        unpack_kernel, [f32(LOCAL_COLS, RANK), f32(8, RANK)],
+        [coef, xor_fsdp(coef, CORE), squares, xor_fsdp(squares, CORE)],
+        flops=3328 * 128, nbytes=2600000, name="unpack",
+    )
+    squares = [squares] + [turn_z(squares, to_odd, to_even) for to_odd, to_even in Z_TURNS]
     new_momentum = finish_momentum(coef, ortho, blended)
     new_weights, new_subspace = finish_weights(squares, coef, ortho, weights)
     return (new_momentum, new_weights, new_subspace)

time: 89.2 us -> 87.9 us (0.985)
  waiting for transfers between devices: 38.5 us -> 37.4 us
    ppermute x4 -> x5, starting transfers between devices: 7.17 us -> 10.7 us  [the longest x3 7.68 us: turn_z(): return lax.ppermute(x, ('fsdp', 'tp'), perm)]
    ppermute x6, starting transfers between devices: 9.5 us -> 6.28 us  [xor_step(): lax.ppermute(x, 'fsdp', [(i, i ^ MASKS[team(i)][k]) for i in range(FSDP)])]
    ppermute x6, waiting for transfers between devices: 10.1 us -> 8.13 us  [xor_step(): lax.ppermute(x, 'fsdp', [(i, i ^ MASKS[team(i)][k]) for i in range(FSDP)])]
    ppermute x4 -> x5, waiting for transfers between devices: 1.82 us -> 2.65 us  [the longest x2 1.33 us: pair_z(): return lax.ppermute(x, ('fsdp', 'tp'), perm)]
    ppermute x6 -> x8, starting transfers between devices: 10.2 us -> 10.2 us  [xor_fsdp(): return lax.ppermute(x, 'fsdp', [(i, i ^ mask) for i in range(FSDP)])]
    ppermute x6 -> x8, waiting for transfers between devices: 16.3 us -> 16.3 us  [xor_fsdp(): return lax.ppermute(x, 'fsdp', [(i, i ^ mask) for i in range(FSDP)])]
  transfers between devices with their start and end apart: 19 -> 22, of which waited for: 15 -> 18; matrix products, arithmetic and copies ran while one was open for 0% -> 0% of each run, Pallas kernels for 7% -> 8%
where the time goes in v3:
time: 87.9 us; the launch traced here: 87.8 us
  waiting for transfers between devices  37.4 us (43%)
  starting transfers between devices  36.7 us (42%)
  Pallas kernels  12.7 us (14%)
  between operations  0.97 us (1%)
    ppermute x8, waiting for transfers between devices, xor_fsdp(): return lax.ppermute(x, 'fsdp', [(i, i ^ mask) for i in range(FSDP)])  16.3 us
    ppermute x3, waiting for transfers between devices, swap_z(): return lax.ppermute(x, ('fsdp', 'tp'), perm)  10.3 us
    ppermute x8, starting transfers between devices, xor_fsdp(): return lax.ppermute(x, 'fsdp', [(i, i ^ mask) for i in range(FSDP)])  10.2 us
    ppermute x3, starting transfers between devices, swap_z(): return lax.ppermute(x, ('fsdp', 'tp'), perm)  9.5 us
    ppermute x6, waiting for transfers between devices, xor_step(): lax.ppermute(x, 'fsdp', [(i, i ^ MASKS[team(i)][k]) for i in range(FSDP)])  8.13 us
    ppermute x3, starting transfers between devices, turn_z(): return lax.ppermute(x, ('fsdp', 'tp'), perm)  7.68 us
    pallas_call x18, Pallas kernels, local(): pl.pallas_call(body, in_specs=[VMEM_SPEC] * (used + len(after)), out_spec...  6.47 us
    ppermute x6, starting transfers between devices, xor_step(): lax.ppermute(x, 'fsdp', [(i, i ^ MASKS[team(i)][k]) for i in range(FSDP)])  6.28 us
  transfers between devices with their start and end apart: 22, of which 18 were waited for; matrix products, arithmetic and copies ran while one was open for 0% of the time, Pallas kernels for 8%

profile of v3, /device:TPU:1, one launch (start us, length us, event | category | flops | bytes accessed | tf_op | source)
XLA Modules:
  0.0 87.8 jit_solution(17009639541762439583)
XLA Ops:
  0.6 2.9 %project.1 = (bf16[256,3328]{1,0:T(8,128)(2,1)S(1)}, f32[256,128]{1,0:T(8,128)S(1)}) custom-call(bf16[256,3328]{1,0:T(8,128)(2,1)} %m_hbm.1, bf16[256,3328]{1,0:T(8,128)(2,1)} %g_hbm.1, f32[3328,128]{1,0:T(8,128)} %s_hbm.1), custom_call_target="tpu_custom_call" | custom-call | flops 218103808 | bytes 7000000 | tf_op jit(solution)/shard_map/project/pallas_call | solution.py:136
  3.5 6.5 %collective-permute-start = (f32[256,128]{1,0:T(8,128)S(1)}, f32[256,128]{1,0:T(8,128)S(1)}, u32[]{:S(2)}, u32[]{:S(2)}) collective-permute-start(f32[256,128]{1,0:T(8,128)S(1)} %get-tuple-element.15), channel_id=1, source_target_pairs={{0,1},{1,0},{2,3},{3,2},{4,5},{5,4},{6,7},{7,6},{9,10},{10,9},{11,... | collective-permute-start | bytes 393224 | tf_op jit(solution)/shard_map/ppermute | solution.py:73
  10.0 2.4 %collective-permute-done = f32[256,128]{1,0:T(8,128)S(1)} collective-permute-done((f32[256,128]{1,0:T(8,128)S(1)}, f32[256,128]{1,0:T(8,128)S(1)}, u32[]{:S(2)}, u32[]{:S(2)}) %collective-permute-start) | collective-permute-done | bytes 131104 | tf_op jit(solution)/shard_map/ppermute | solution.py:73
  12.5 3.8 %collective-permute-done.1 = f32[256,128]{1,0:T(8,128)S(1)} collective-permute-done((f32[256,128]{1,0:T(8,128)S(1)}, f32[256,128]{1,0:T(8,128)S(1)}, u32[]{:S(2)}, u32[]{:S(2)}) %collective-permute-start.1) | collective-permute-done | bytes 131104 | tf_op jit(solution)/shard_map/ppermute | solution.py:73
  16.3 2.9 %collective-permute-start.2 = (f32[256,128]{1,0:T(8,128)S(1)}, f32[256,128]{1,0:T(8,128)S(1)}, u32[]{:S(2)}, u32[]{:S(2)}) collective-permute-start(f32[256,128]{1,0:T(8,128)S(1)} %add.10), channel_id=1, source_target_pairs={{2,5},{5,2},{1,6},{6,1},{4,7},{7,4},{3,0},{0,3},{11,14},{14,11},{1... | collective-permute-start | bytes 393224 | tf_op jit(solution)/shard_map/ppermute | solution.py:73
  19.2 4.1 %collective-permute-done.2 = f32[256,128]{1,0:T(8,128)S(1)} collective-permute-done((f32[256,128]{1,0:T(8,128)S(1)}, f32[256,128]{1,0:T(8,128)S(1)}, u32[]{:S(2)}, u32[]{:S(2)}) %collective-permute-start.2) | collective-permute-done | bytes 131104 | tf_op jit(solution)/shard_map/ppermute | solution.py:73
  24.0 4.1 %collective-permute-start.3 = (f32[1792,128]{1,0:T(8,128)S(1)}, f32[1792,128]{1,0:T(8,128)S(1)}, u32[]{:S(2)}, u32[]{:S(2)}) collective-permute-start(f32[1792,128]{1,0:T(8,128)S(1)} %lift_send.1.refs_2_.refs_0_), channel_id=1, source_target_pairs={{0,8},{8,0},{16,24},{24,16},{32,40},{40,32},{48,56},{56,48},{64,72... | collective-permute-start | bytes 2752520 | tf_op jit(solution)/shard_map/ppermute | solution.py:93
  28.5 1.6 %collective-permute-done.3.refs_1_ = f32[1792,128]{1,0:T(8,128)S(1)} collective-permute-done((f32[1792,128]{1,0:T(8,128)S(1)}, f32[1792,128]{1,0:T(8,128)S(1)}, u32[]{:S(2)}, u32[]{:S(2)}) %collective-permute-start.3) | collective-permute-done | bytes 917536 | tf_op jit(solution)/shard_map/ppermute | solution.py:93
  30.2 1.6 %collective-permute-start.4 = (f32[832,128]{1,0:T(8,128)S(1)}, f32[832,128]{1,0:T(8,128)S(1)}, u32[]{:S(2)}, u32[]{:S(2)}) collective-permute-start(f32[832,128]{1,0:T(8,128)S(1)} %get-tuple-element.18.refs_2_), channel_id=1, source_target_pairs={{0,24},{8,64},{16,88},{24,0},{32,56},{40,96},{48,120},{56,32},{64,... | collective-permute-start | bytes 1277960 | tf_op jit(solution)/shard_map/ppermute | solution.py:97
  31.9 4.2 %collective-permute-start.7 = (f32[128,128]{1,0:T(8,128)S(1)}, f32[128,128]{1,0:T(8,128)S(1)}, u32[]{:S(2)}, u32[]{:S(2)}) collective-permute-start(f32[128,128]{1,0:T(8,128)S(1)} %gram_pair.1.refs_0_), channel_id=1, source_target_pairs={{0,240},{8,248},{16,224},{24,232},{32,208},{40,216},{48,192},{56,2... | collective-permute-start | bytes 196616 | tf_op jit(solution)/shard_map/ppermute | solution.py:93
  36.1 1.1 %collective-permute-start.6 = (f32[128,128]{1,0:T(8,128)S(1)}, f32[128,128]{1,0:T(8,128)S(1)}, u32[]{:S(2)}, u32[]{:S(2)}) collective-permute-start(f32[128,128]{1,0:T(8,128)S(1)} %gram_pair.1.refs_0_), channel_id=1, source_target_pairs={{0,200},{8,192},{16,216},{24,208},{32,232},{40,224},{48,248},{56,2... | collective-permute-start | bytes 196616 | tf_op jit(solution)/shard_map/ppermute | solution.py:93
  37.3 1.6 %collective-permute-done.7.refs_3_ = f32[128,128]{1,0:T(8,128)S(1)} collective-permute-done((f32[128,128]{1,0:T(8,128)S(1)}, f32[128,128]{1,0:T(8,128)S(1)}, u32[]{:S(2)}, u32[]{:S(2)}) %collective-permute-start.7) | collective-permute-done | bytes 65568 | tf_op jit(solution)/shard_map/ppermute | solution.py:93
  39.0 2.6 %collective-permute-done.6.refs_2_ = f32[128,128]{1,0:T(8,128)S(1)} collective-permute-done((f32[128,128]{1,0:T(8,128)S(1)}, f32[128,128]{1,0:T(8,128)S(1)}, u32[]{:S(2)}, u32[]{:S(2)}) %collective-permute-start.6) | collective-permute-done | bytes 65568 | tf_op jit(solution)/shard_map/ppermute | solution.py:93
  42.2 2.0 %collective-permute-start.8 = (f32[416,128]{1,0:T(8,128)S(1)}, f32[416,128]{1,0:T(8,128)S(1)}, u32[]{:S(2)}, u32[]{:S(2)}) collective-permute-start(f32[416,128]{1,0:T(8,128)S(1)} %get-tuple-element.20.refs_1_), channel_id=1, source_target_pairs={{0,56},{8,192},{16,216},{24,32},{32,24},{40,224},{48,248},{56,0},{... | collective-permute-start | bytes 638984 | tf_op jit(solution)/shard_map/ppermute | solution.py:97
  44.2 4.0 %collective-permute-done.9.refs_2_.refs_1_ = f32[128,128]{1,0:T(8,128)S(1)} collective-permute-done((f32[128,128]{1,0:T(8,128)S(1)}, f32[128,128]{1,0:T(8,128)S(1)}, u32[]{:S(2)}, u32[]{:S(2)}) %collective-permute-start.9) | collective-permute-done | bytes 65568 | tf_op jit(solution)/shard_map/ppermute | solution.py:93
  49.0 4.7 %collective-permute-done.11.refs_2_.refs_1_ = f32[128,128]{1,0:T(8,128)S(1)} collective-permute-done((f32[128,128]{1,0:T(8,128)S(1)}, f32[128,128]{1,0:T(8,128)S(1)}, u32[]{:S(2)}, u32[]{:S(2)}) %collective-permute-start.11) | collective-permute-done | bytes 65568 | tf_op jit(solution)/shard_map/ppermute | solution.py:93
  53.6 0.8 collective-permute-done.10.refs_1_
  54.4 1.0 %collective-permute-start.12 = (f32[416,128]{1,0:T(8,128)S(1)}, f32[416,128]{1,0:T(8,128)S(1)}, u32[]{:S(2)}, u32[]{:S(2)}) collective-permute-start(f32[416,128]{1,0:T(8,128)S(1)} %second_sum.1.refs_2_.refs_0_), channel_id=1, source_target_pairs={{0,200},{8,48},{16,40},{24,208},{32,232},{40,16},{48,8},{56,240},{... | collective-permute-start | bytes 638984 | tf_op jit(solution)/shard_map/ppermute | solution.py:97
  55.4 4.2 %eliminate0.1.refs_2_.refs_1_ = f32[128,128]{1,0:T(8,128)S(1)} custom-call(f32[128,128]{1,0:T(8,128)S(1)} %add_y1.1.refs_0_.refs_1_, f32[128,128]{1,0:T(8,128)S(1)} %add_y1.1.refs_0_.refs_1_), custom_call_target="tpu_custom_call" | custom-call | flops 4000000 | bytes 19200000 | tf_op jit(solution)/shard_map/eliminate0/pallas_call | solution.py:160
  59.7 1.8 %collective-permute-done.12.refs_1_ = f32[416,128]{1,0:T(8,128)S(1)} collective-permute-done((f32[416,128]{1,0:T(8,128)S(1)}, f32[416,128]{1,0:T(8,128)S(1)}, u32[]{:S(2)}, u32[]{:S(2)}) %collective-permute-start.12) | collective-permute-done | bytes 213024 | tf_op jit(solution)/shard_map/ppermute | solution.py:97
  61.8 1.4 %collective-permute-start.13 = (bf16[416,128]{1,0:T(8,128)(2,1)S(1)}, bf16[416,128]{1,0:T(8,128)(2,1)S(1)}, u32[]{:S(2)}, u32[]{:S(2)}) collective-permute-start(bf16[416,128]{1,0:T(8,128)(2,1)S(1)} %block.1.refs_2_.refs_0_), channel_id=1, source_target_pairs={{0,56},{8,192},{16,216},{24,32},{32,24},{40,224},{48,248},{56,0},{... | collective-permute-start | bytes 319496 | tf_op jit(solution)/shard_map/ppermute | solution.py:97
  63.5 4.0 %collective-permute-done.13.refs_1_ = bf16[416,128]{1,0:T(8,128)(2,1)S(1)} collective-permute-done((bf16[416,128]{1,0:T(8,128)(2,1)S(1)}, bf16[416,128]{1,0:T(8,128)(2,1)S(1)}, u32[]{:S(2)}, u32[]{:S(2)}) %collective-permute-start.13) | collective-permute-done | bytes 106528 | tf_op jit(solution)/shard_map/ppermute | solution.py:97
  67.7 1.4 %collective-permute-start.16 = (f32[8,128]{1,0:T(8,128)S(1)}, f32[8,128]{1,0:T(8,128)S(1)}, u32[]{:S(2)}, u32[]{:S(2)}) collective-permute-start(f32[8,128]{1,0:T(8,128)S(1)} %squares.1.refs_2_), channel_id=1, source_target_pairs={{0,25},{1,24},{2,27},{3,26},{4,29},{5,28},{6,31},{7,30},{8,65},{9,... | collective-permute-start | bytes 12296 | tf_op jit(solution)/shard_map/ppermute | solution.py:81
  69.2 1.6 %collective-permute-start.15 = (f32[8,128]{1,0:T(8,128)S(1)}, f32[8,128]{1,0:T(8,128)S(1)}, u32[]{:S(2)}, u32[]{:S(2)}) collective-permute-start(f32[8,128]{1,0:T(8,128)S(1)} %squares.1.refs_2_), channel_id=1, source_target_pairs={{0,1},{1,0},{2,3},{3,2},{4,5},{5,4},{6,7},{7,6},{8,9},{9,8},{10,11... | collective-permute-start | bytes 12296 | tf_op jit(solution)/shard_map/ppermute | solution.py:81
  70.7 1.1 %collective-permute-done.16.refs_4_ = f32[8,128]{1,0:T(8,128)S(1)} collective-permute-done((f32[8,128]{1,0:T(8,128)S(1)}, f32[8,128]{1,0:T(8,128)S(1)}, u32[]{:S(2)}, u32[]{:S(2)}) %collective-permute-start.16) | collective-permute-done | bytes 4128 | tf_op jit(solution)/shard_map/ppermute | solution.py:81
  72.1 1.0 %collective-permute-done.14.refs_1_ = bf16[832,128]{1,0:T(8,128)(2,1)S(1)} collective-permute-done((bf16[832,128]{1,0:T(8,128)(2,1)S(1)}, bf16[832,128]{1,0:T(8,128)(2,1)S(1)}, u32[]{:S(2)}, u32[]{:S(2)}) %collective-permute-start.14) | collective-permute-done | bytes 213024 | tf_op jit(solution)/shard_map/ppermute | solution.py:97
  73.8 1.3 %collective-permute-done.18.refs_3_ = f32[8,128]{1,0:T(8,128)S(1)} collective-permute-done((f32[8,128]{1,0:T(8,128)S(1)}, f32[8,128]{1,0:T(8,128)S(1)}, u32[]{:S(2)}, u32[]{:S(2)}) %collective-permute-start.18) | collective-permute-done | bytes 4128 | tf_op jit(solution)/shard_map/ppermute | solution.py:93
  75.2 4.2 %collective-permute-start.21 = (f32[8,128]{1,0:T(8,128)S(1)}, f32[8,128]{1,0:T(8,128)S(1)}, u32[]{:S(2)}, u32[]{:S(2)}) collective-permute-start(f32[8,128]{1,0:T(8,128)S(1)} %get-tuple-element.24.sq_ref), channel_id=1, source_target_pairs={{10,0},{15,1},{12,2},{9,3},{14,4},{11,5},{8,6},{13,7},{2,8},{7,9},... | collective-permute-start | bytes 12296 | tf_op jit(solution)/shard_map/ppermute | solution.py:89
  79.7 3.2 %collective-permute-start.19 = (f32[8,128]{1,0:T(8,128)S(1)}, f32[8,128]{1,0:T(8,128)S(1)}, u32[]{:S(2)}, u32[]{:S(2)}) collective-permute-start(f32[8,128]{1,0:T(8,128)S(1)} %get-tuple-element.24.sq_ref), channel_id=1, source_target_pairs={{13,0},{12,1},{15,2},{14,3},{9,4},{8,5},{11,6},{10,7},{5,8},{4,9},... | collective-permute-start | bytes 12296 | tf_op jit(solution)/shard_map/ppermute | solution.py:89
  82.9 1.5 %finish_momentum.1 = bf16[256,3328]{1,0:T(8,128)(2,1)} custom-call(f32[3328,128]{1,0:T(8,128)S(1)} %get-tuple-element.23.coef_ref, bf16[256,128]{1,0:T(8,128)(2,1)S(1)} %ortho.1.refs_2_.ortho_ref, bf16[256,3328]{1,0:T(8,128)(2,1)S(1)} %get-tuple-element.16.refs_1_.b_ref), custom_call_target="tpu_custom_call" | custom-call | flops 218103808 | bytes 5000000 | tf_op jit(solution)/shard_map/finish_momentum/pallas_call | solution.py:378
  84.4 1.3 %collective-permute-done.19.opposite_ref = f32[8,128]{1,0:T(8,128)S(1)} collective-permute-done((f32[8,128]{1,0:T(8,128)S(1)}, f32[8,128]{1,0:T(8,128)S(1)}, u32[]{:S(2)}, u32[]{:S(2)}) %collective-permute-start.19) | collective-permute-done | bytes 4128 | tf_op jit(solution)/shard_map/ppermute | solution.py:89
  85.7 1.9 %finish_weights.1 = (bf16[256,3328]{1,0:T(8,128)(2,1)}, f32[3328,128]{1,0:T(8,128)}) custom-call(f32[8,128]{1,0:T(8,128)S(1)} %get-tuple-element.24.sq_ref, f32[8,128]{1,0:T(8,128)S(1)} %collective-permute-done.19.opposite_ref, f32[8,128]{1,0:T(8,128)S(1)} %collective-permute-done.20.next_ref, f32[8,128]{1,0:T(8,128)S(1)} %collective-permute-done.21.previous_ref, ...), custom_call_target="tpu_custom_call" | custom-call | flops 218103808 | bytes 7000000 | tf_op jit(solution)/shard_map/finish_weights/pallas_call | solution.py:422
  (38 shorter events, 4.9 us)
Async XLA Ops:
  3.5 8.8 %collective-permute-start = (f32[256,128]{1,0:T(8,128)S(1)}, f32[256,128]{1,0:T(8,128)S(1)}, u32[]{:S(2)}, u32[]{:S(2)}) collective-permute-start(f32[256,128]{1,0:T(8,128)S(1)} %get-tuple-element.15), channel_id=1, source_target_pairs={{0,1},{1,0},{2,3},{3,2},{4,5},{5,4},{6,7},{7,6},{9,10},{10,9},{11,... | collective-permute-start | bytes 393224 | tf_op jit(solution)/shard_map/ppermute | solution.py:73
  12.4 3.9 %collective-permute-start.1 = (f32[256,128]{1,0:T(8,128)S(1)}, f32[256,128]{1,0:T(8,128)S(1)}, u32[]{:S(2)}, u32[]{:S(2)}) collective-permute-start(f32[256,128]{1,0:T(8,128)S(1)} %add.9), channel_id=1, source_target_pairs={{1,2},{2,1},{3,4},{4,3},{5,6},{6,5},{7,0},{0,7},{10,11},{11,10},{1... | collective-permute-start | bytes 393224 | tf_op jit(solution)/shard_map/ppermute | solution.py:73
  16.3 7.1 %collective-permute-start.2 = (f32[256,128]{1,0:T(8,128)S(1)}, f32[256,128]{1,0:T(8,128)S(1)}, u32[]{:S(2)}, u32[]{:S(2)}) collective-permute-start(f32[256,128]{1,0:T(8,128)S(1)} %add.10), channel_id=1, source_target_pairs={{2,5},{5,2},{1,6},{6,1},{4,7},{7,4},{3,0},{0,3},{11,14},{14,11},{1... | collective-permute-start | bytes 393224 | tf_op jit(solution)/shard_map/ppermute | solution.py:73
  24.0 6.2 %collective-permute-start.3 = (f32[1792,128]{1,0:T(8,128)S(1)}, f32[1792,128]{1,0:T(8,128)S(1)}, u32[]{:S(2)}, u32[]{:S(2)}) collective-permute-start(f32[1792,128]{1,0:T(8,128)S(1)} %lift_send.1.refs_2_.refs_0_), channel_id=1, source_target_pairs={{0,8},{8,0},{16,24},{24,16},{32,40},{40,32},{48,56},{56,48},{64,72... | collective-permute-start | bytes 2752520 | tf_op jit(solution)/shard_map/ppermute | solution.py:93
  30.2 11.8 %collective-permute-start.4 = (f32[832,128]{1,0:T(8,128)S(1)}, f32[832,128]{1,0:T(8,128)S(1)}, u32[]{:S(2)}, u32[]{:S(2)}) collective-permute-start(f32[832,128]{1,0:T(8,128)S(1)} %get-tuple-element.18.refs_2_), channel_id=1, source_target_pairs={{0,24},{8,64},{16,88},{24,0},{32,56},{40,96},{48,120},{56,32},{64,... | collective-permute-start | bytes 1277960 | tf_op jit(solution)/shard_map/ppermute | solution.py:97
  31.9 7.1 %collective-permute-start.7 = (f32[128,128]{1,0:T(8,128)S(1)}, f32[128,128]{1,0:T(8,128)S(1)}, u32[]{:S(2)}, u32[]{:S(2)}) collective-permute-start(f32[128,128]{1,0:T(8,128)S(1)} %gram_pair.1.refs_0_), channel_id=1, source_target_pairs={{0,240},{8,248},{16,224},{24,232},{32,208},{40,216},{48,192},{56,2... | collective-permute-start | bytes 196616 | tf_op jit(solution)/shard_map/ppermute | solution.py:93
  36.1 5.5 %collective-permute-start.6 = (f32[128,128]{1,0:T(8,128)S(1)}, f32[128,128]{1,0:T(8,128)S(1)}, u32[]{:S(2)}, u32[]{:S(2)}) collective-permute-start(f32[128,128]{1,0:T(8,128)S(1)} %gram_pair.1.refs_0_), channel_id=1, source_target_pairs={{0,200},{8,192},{16,216},{24,208},{32,232},{40,224},{48,248},{56,2... | collective-permute-start | bytes 196616 | tf_op jit(solution)/shard_map/ppermute | solution.py:93
  37.2 4.9 %collective-permute-start.5 = (f32[128,128]{1,0:T(8,128)S(1)}, f32[128,128]{1,0:T(8,128)S(1)}, u32[]{:S(2)}, u32[]{:S(2)}) collective-permute-start(f32[128,128]{1,0:T(8,128)S(1)} %gram_pair.1.refs_0_), channel_id=1, source_target_pairs={{0,56},{8,48},{16,40},{24,32},{32,24},{40,16},{48,8},{56,0},{64,12... | collective-permute-start | bytes 196616 | tf_op jit(solution)/shard_map/ppermute | solution.py:93
  42.2 6.6 %collective-permute-start.8 = (f32[416,128]{1,0:T(8,128)S(1)}, f32[416,128]{1,0:T(8,128)S(1)}, u32[]{:S(2)}, u32[]{:S(2)}) collective-permute-start(f32[416,128]{1,0:T(8,128)S(1)} %get-tuple-element.20.refs_1_), channel_id=1, source_target_pairs={{0,56},{8,192},{16,216},{24,32},{32,24},{40,224},{48,248},{56,0},{... | collective-permute-start | bytes 638984 | tf_op jit(solution)/shard_map/ppermute | solution.py:97
  44.2 4.0 %collective-permute-start.9 = (f32[128,128]{1,0:T(8,128)S(1)}, f32[128,128]{1,0:T(8,128)S(1)}, u32[]{:S(2)}, u32[]{:S(2)}) collective-permute-start(f32[128,128]{1,0:T(8,128)S(1)} %hold.1.refs_0_), channel_id=1, source_target_pairs={{0,24},{8,16},{16,8},{24,0},{32,56},{40,48},{48,40},{56,32},{64,88... | collective-permute-start | bytes 196616 | tf_op jit(solution)/shard_map/ppermute | solution.py:93
  48.8 5.7 %collective-permute-start.10 = (f32[416,128]{1,0:T(8,128)S(1)}, f32[416,128]{1,0:T(8,128)S(1)}, u32[]{:S(2)}, u32[]{:S(2)}) collective-permute-start(f32[416,128]{1,0:T(8,128)S(1)} %first_sum.1.refs_2_.refs_0_), channel_id=1, source_target_pairs={{0,72},{8,16},{16,8},{24,80},{32,104},{40,48},{48,40},{56,112},{64... | collective-permute-start | bytes 638984 | tf_op jit(solution)/shard_map/ppermute | solution.py:97
  48.9 4.8 %collective-permute-start.11 = (f32[128,128]{1,0:T(8,128)S(1)}, f32[128,128]{1,0:T(8,128)S(1)}, u32[]{:S(2)}, u32[]{:S(2)}) collective-permute-start(f32[128,128]{1,0:T(8,128)S(1)} %add_x1.1.refs_0_), channel_id=1, source_target_pairs={{0,72},{8,64},{16,88},{24,80},{32,104},{40,96},{48,120},{56,112},{... | collective-permute-start | bytes 196616 | tf_op jit(solution)/shard_map/ppermute | solution.py:93
  54.4 7.0 %collective-permute-start.12 = (f32[416,128]{1,0:T(8,128)S(1)}, f32[416,128]{1,0:T(8,128)S(1)}, u32[]{:S(2)}, u32[]{:S(2)}) collective-permute-start(f32[416,128]{1,0:T(8,128)S(1)} %second_sum.1.refs_2_.refs_0_), channel_id=1, source_target_pairs={{0,200},{8,48},{16,40},{24,208},{32,232},{40,16},{48,8},{56,240},{... | collective-permute-start | bytes 638984 | tf_op jit(solution)/shard_map/ppermute | solution.py:97
  61.8 5.7 %collective-permute-start.13 = (bf16[416,128]{1,0:T(8,128)(2,1)S(1)}, bf16[416,128]{1,0:T(8,128)(2,1)S(1)}, u32[]{:S(2)}, u32[]{:S(2)}) collective-permute-start(bf16[416,128]{1,0:T(8,128)(2,1)S(1)} %block.1.refs_2_.refs_0_), channel_id=1, source_target_pairs={{0,56},{8,192},{16,216},{24,32},{32,24},{40,224},{48,248},{56,0},{... | collective-permute-start | bytes 319496 | tf_op jit(solution)/shard_map/ppermute | solution.py:97
  67.6 5.5 %collective-permute-start.14 = (bf16[832,128]{1,0:T(8,128)(2,1)S(1)}, bf16[832,128]{1,0:T(8,128)(2,1)S(1)}, u32[]{:S(2)}, u32[]{:S(2)}) collective-permute-start(bf16[832,128]{1,0:T(8,128)(2,1)S(1)} %join1.1.refs_0_), channel_id=1, source_target_pairs={{0,24},{8,64},{16,88},{24,0},{32,56},{40,96},{48,120},{56,32},{64,... | collective-permute-start | bytes 638984 | tf_op jit(solution)/shard_map/ppermute | solution.py:97
  67.7 4.1 %collective-permute-start.16 = (f32[8,128]{1,0:T(8,128)S(1)}, f32[8,128]{1,0:T(8,128)S(1)}, u32[]{:S(2)}, u32[]{:S(2)}) collective-permute-start(f32[8,128]{1,0:T(8,128)S(1)} %squares.1.refs_2_), channel_id=1, source_target_pairs={{0,25},{1,24},{2,27},{3,26},{4,29},{5,28},{6,31},{7,30},{8,65},{9,... | collective-permute-start | bytes 12296 | tf_op jit(solution)/shard_map/ppermute | solution.py:81
  69.2 2.9 %collective-permute-start.15 = (f32[8,128]{1,0:T(8,128)S(1)}, f32[8,128]{1,0:T(8,128)S(1)}, u32[]{:S(2)}, u32[]{:S(2)}) collective-permute-start(f32[8,128]{1,0:T(8,128)S(1)} %squares.1.refs_2_), channel_id=1, source_target_pairs={{0,1},{1,0},{2,3},{3,2},{4,5},{5,4},{6,7},{7,6},{8,9},{9,8},{10,11... | collective-permute-start | bytes 12296 | tf_op jit(solution)/shard_map/ppermute | solution.py:81
  73.2 1.9 %collective-permute-start.17 = (bf16[1664,128]{1,0:T(8,128)(2,1)S(1)}, bf16[1664,128]{1,0:T(8,128)(2,1)S(1)}, u32[]{:S(2)}, u32[]{:S(2)}) collective-permute-start(bf16[1664,128]{1,0:T(8,128)(2,1)S(1)} %get-tuple-element.21.refs_0_), channel_id=1, source_target_pairs={{0,8},{8,0},{16,24},{24,16},{32,40},{40,32},{48,56},{56,48},{64,72... | collective-permute-start | bytes 1277960 | tf_op jit(solution)/shard_map/ppermute | solution.py:93
  73.6 1.4 %collective-permute-start.18 = (f32[8,128]{1,0:T(8,128)S(1)}, f32[8,128]{1,0:T(8,128)S(1)}, u32[]{:S(2)}, u32[]{:S(2)}) collective-permute-start(f32[8,128]{1,0:T(8,128)S(1)} %get-tuple-element.22.refs_2_), channel_id=1, source_target_pairs={{0,8},{8,0},{16,24},{24,16},{32,40},{40,32},{48,56},{56,48},{64,72... | collective-permute-start | bytes 12296 | tf_op jit(solution)/shard_map/ppermute | solution.py:93
  75.2 9.2 %collective-permute-start.21 = (f32[8,128]{1,0:T(8,128)S(1)}, f32[8,128]{1,0:T(8,128)S(1)}, u32[]{:S(2)}, u32[]{:S(2)}) collective-permute-start(f32[8,128]{1,0:T(8,128)S(1)} %get-tuple-element.24.sq_ref), channel_id=1, source_target_pairs={{10,0},{15,1},{12,2},{9,3},{14,4},{11,5},{8,6},{13,7},{2,8},{7,9},... | collective-permute-start | bytes 12296 | tf_op jit(solution)/shard_map/ppermute | solution.py:89
  79.4 5.0 %collective-permute-start.20 = (f32[8,128]{1,0:T(8,128)S(1)}, f32[8,128]{1,0:T(8,128)S(1)}, u32[]{:S(2)}, u32[]{:S(2)}) collective-permute-start(f32[8,128]{1,0:T(8,128)S(1)} %get-tuple-element.24.sq_ref), channel_id=1, source_target_pairs={{15,0},{10,1},{9,2},{12,3},{11,4},{14,5},{13,6},{8,7},{7,8},{2,9},... | collective-permute-start | bytes 12296 | tf_op jit(solution)/shard_map/ppermute | solution.py:89
  79.7 6.0 %collective-permute-start.19 = (f32[8,128]{1,0:T(8,128)S(1)}, f32[8,128]{1,0:T(8,128)S(1)}, u32[]{:S(2)}, u32[]{:S(2)}) collective-permute-start(f32[8,128]{1,0:T(8,128)S(1)} %get-tuple-element.24.sq_ref), channel_id=1, source_target_pairs={{13,0},{12,1},{15,2},{14,3},{9,4},{8,5},{11,6},{10,7},{5,8},{4,9},... | collective-permute-start | bytes 12296 | tf_op jit(solution)/shard_map/ppermute | solution.py:89
  82.9 2.9 %copy-start = (bf16[256,3328]{1,0:T(8,128)(2,1)S(1)}, bf16[256,3328]{1,0:T(8,128)(2,1)}, u32[]{:S(2)}) copy-start(bf16[256,3328]{1,0:T(8,128)(2,1)} %weights_ref.1) | copy-start | bytes 5111812

commit v4 on v3

--- a/solution.py
+++ b/solution.py
@@ -24,12 +24,13 @@
 HALF = LOCAL_COLS // 2
 CHUNK = HALF // 4
 PIECE = HALF // 8
+CUT = 40
 WIDE = 256
 TILES = LOCAL_COLS // WIDE
 STRIPS = ((0, 512), (512, 768), (1280, 768), (2048, 768), (2816, 512))
 
 X_ONE, Y_ONE, X_THREE, Y_THREE, CORE = 3, 9, 7, 25, 1
-MASKS = ((X_ONE, X_THREE, Y_ONE, Y_THREE), (Y_ONE, Y_THREE, X_ONE, X_THREE))
+MASKS = ((X_ONE, X_THREE, Y_THREE, Y_ONE), (Y_ONE, Y_THREE, X_THREE, X_ONE))
 
 
 def team(f):
@@ -60,9 +61,6 @@
 
 def cost(flops, nbytes):
     return pl.CostEstimate(flops=flops, bytes_accessed=nbytes, transcendentals=0)
-
-Z_TURNS = ((3, -3), (1, -1), (-2, 2))
-
 
 def swap_z(x, step):
     perm = []
@@ -81,9 +79,9 @@
     return lax.ppermute(x, ("fsdp", "tp"), perm)
 
 
-def turn_z(x, to_odd, to_even):
+def turn_z(x, turns):
     perm = [
-        ((f ^ 1) * TP + (z + (to_odd if z % 2 else to_even)) % TP, f * TP + z)
+        ((f ^ 1) * TP + (z + turns[f % 2] * (1 if z % 2 else -1)) % TP, f * TP + z)
         for f in range(FSDP) for z in range(TP)
     ]
     return lax.ppermute(x, ("fsdp", "tp"), perm)
@@ -91,6 +89,11 @@
 
 def xor_fsdp(x, mask):
     return lax.ppermute(x, "fsdp", [(i, i ^ mask) for i in range(FSDP)])
+
+
+def split_xy(x, x_mask, y_mask):
+    split = [(f ^ (y_mask if f % 2 else x_mask), f) for f in range(FSDP)]
+    return lax.ppermute(x, "fsdp", split), xor_fsdp(x, x_mask ^ y_mask)
 
 
 def xor_step(x, k):
@@ -217,6 +220,10 @@
 
 def gram_four_kernel(a_ref, b_ref, c_ref, d_ref, out_ref):
     out_ref[...] = (a_ref[...] + b_ref[...]) + (c_ref[...] + d_ref[...])
+
+
+def gram_four(a, b, c, d, after):
+    return local(gram_four_kernel, f32(RANK, RANK), [a, b, c, d], after, nbytes=400000, name="gram_four")
 
 
 def hold_kernel(a_ref, out_ref):
@@ -453,24 +460,21 @@
     moving, keep = split_step(0, n, keep, recv)
     gram = local(gram_pair_kernel, f32(RANK, RANK), [send, recv], [moving], nbytes=200000, name="gram_pair")
     recv = xor_step(moving, 0)
-    gram = local(
-        gram_four_kernel, f32(RANK, RANK),
-        [gram] + [xor_fsdp(gram, mask) for mask in (X_THREE, Y_THREE, X_THREE ^ Y_THREE)],
-        nbytes=400000, name="gram_four",
-    )
+    split, both = split_xy(gram, X_THREE, Y_THREE)
+    gram = gram_four(gram, both, split, xor_fsdp(split, CORE), [])
     n //= 2
     moving, keep = split_step(1, n, keep, recv, [gram])
     recv = xor_step(moving, 1)
     gram = local(hold_kernel, f32(RANK, RANK), [gram], [moving], nbytes=130000, name="hold")
-    more = xor_fsdp(gram, X_ONE)
-    d = add(keep, recv, [more], "first_sum")
+    split, both = split_xy(gram, X_ONE, Y_ONE)
+    d = add(keep, recv, [split, both], "first_sum")
     recv = xor_step(d, 2)
-    gram = add(gram, more, [d], "add_x1")
-    more = xor_fsdp(gram, Y_ONE)
-    d = add(d, recv, [more], "second_sum")
+    split = local(hold_kernel, f32(RANK, RANK), [split], [d], nbytes=130000, name="hold_split")
+    gram = gram_four(gram, both, split, xor_fsdp(split, CORE), [d])
+    state = eliminate(0, CUT, gram, gram)
+    d = add(d, recv, [state], "second_sum")
     recv = xor_step(d, 3)
-    gram = add(gram, more, [d], "add_y1")
-    inverse = eliminate(0, RANK, gram, gram)
+    inverse = eliminate(CUT, RANK, state, gram, [d])
 
     coef = local(
         block_kernel, bf16(CHUNK, RANK), [d, recv, inverse],
@@ -497,7 +501,8 @@
         [coef, xor_fsdp(coef, CORE), squares, xor_fsdp(squares, CORE)],
         flops=3328 * 128, nbytes=2600000, name="unpack",
     )
-    squares = [squares] + [turn_z(squares, to_odd, to_even) for to_odd, to_even in Z_TURNS]
+    split = turn_z(squares, (1, -2))
+    squares = [squares, turn_z(squares, (3, 3)), split, xor_fsdp(split, CORE)]
     new_momentum = finish_momentum(coef, ortho, blended)
     new_weights, new_subspace = finish_weights(squares, coef, ortho, weights)
     return (new_momentum, new_weights, new_subspace)

time: 87.9 us -> 87 us (0.990)
  waiting for transfers between devices: 37.4 us -> 35.2 us
    ppermute x8, waiting for transfers between devices: 16.3 us -> 11.3 us  [xor_fsdp(): return lax.ppermute(x, 'fsdp', [(i, i ^ mask) for i in range(FSDP)])]
    ppermute x0 -> x2, starting transfers between devices: none -> 3.79 us  [split_xy(): return (lax.ppermute(x, 'fsdp', split), xor_fsdp(x, x_mask ^ y_mask))]
    ppermute x8, starting transfers between devices: 10.2 us -> 6.55 us  [xor_fsdp(): return lax.ppermute(x, 'fsdp', [(i, i ^ mask) for i in range(FSDP)])]
    ppermute x6, starting transfers between devices: 6.28 us -> 8.07 us  [xor_step(): lax.ppermute(x, 'fsdp', [(i, i ^ MASKS[team(i)][k]) for i in range(FSDP)])]
    ppermute x0 -> x2, waiting for transfers between devices: none -> 1.51 us  [split_xy(): return (lax.ppermute(x, 'fsdp', split), xor_fsdp(x, x_mask ^ y_mask))]
    ppermute x3 -> x2, starting transfers between devices: 7.68 us -> 6.5 us  [turn_z(): return lax.ppermute(x, ('fsdp', 'tp'), perm)]
    ppermute x3 -> x2, waiting for transfers between devices: 1.33 us -> 2.41 us  [turn_z(): return lax.ppermute(x, ('fsdp', 'tp'), perm)]
    pallas_call x18 -> x19, Pallas kernels: 6.47 us -> 6.96 us  [local(): pl.pallas_call(body, in_specs=[VMEM_SPEC] * (used + len(after)), out_spec...]
  transfers between devices with their start and end apart: 22 -> 23, of which waited for: 18 -> 17; matrix products, arithmetic and copies ran while one was open for 0% -> 0% of each run, Pallas kernels for 8% -> 8%
where the time goes in v4:
time: 87 us; the launch traced here: 86.9 us
  starting transfers between devices  37.4 us (43%)
  waiting for transfers between devices  35.2 us (40%)
  Pallas kernels  13.2 us (15%)
  between operations  0.96 us (1%)
    ppermute x8, waiting for transfers between devices, xor_fsdp(): return lax.ppermute(x, 'fsdp', [(i, i ^ mask) for i in range(FSDP)])  11.3 us
    ppermute x3, waiting for transfers between devices, swap_z(): return lax.ppermute(x, ('fsdp', 'tp'), perm)  10.3 us
    ppermute x3, starting transfers between devices, swap_z(): return lax.ppermute(x, ('fsdp', 'tp'), perm)  9.5 us
    ppermute x6, waiting for transfers between devices, xor_step(): lax.ppermute(x, 'fsdp', [(i, i ^ MASKS[team(i)][k]) for i in range(FSDP)])  8.34 us
    ppermute x6, starting transfers between devices, xor_step(): lax.ppermute(x, 'fsdp', [(i, i ^ MASKS[team(i)][k]) for i in range(FSDP)])  8.07 us
    pallas_call x19, Pallas kernels, local(): pl.pallas_call(body, in_specs=[VMEM_SPEC] * (used + len(after)), out_spec...  6.96 us
    ppermute x8, starting transfers between devices, xor_fsdp(): return lax.ppermute(x, 'fsdp', [(i, i ^ mask) for i in range(FSDP)])  6.55 us
    ppermute x2, starting transfers between devices, turn_z(): return lax.ppermute(x, ('fsdp', 'tp'), perm)  6.5 us
  transfers between devices with their start and end apart: 23, of which 17 were waited for; matrix products, arithmetic and copies ran while one was open for 0% of the time, Pallas kernels for 8%

profile of v4, /device:TPU:1, one launch (start us, length us, event | category | flops | bytes accessed | tf_op | source)
XLA Modules:
  0.0 86.9 jit_solution(8359576098933174893)
XLA Ops:
  0.6 2.9 %project.1 = (bf16[256,3328]{1,0:T(8,128)(2,1)S(1)}, f32[256,128]{1,0:T(8,128)S(1)}) custom-call(bf16[256,3328]{1,0:T(8,128)(2,1)} %m_hbm.1, bf16[256,3328]{1,0:T(8,128)(2,1)} %g_hbm.1, f32[3328,128]{1,0:T(8,128)} %s_hbm.1), custom_call_target="tpu_custom_call" | custom-call | flops 218103808 | bytes 7000000 | tf_op jit(solution)/shard_map/project/pallas_call | solution.py:139
  3.5 6.5 %collective-permute-start = (f32[256,128]{1,0:T(8,128)S(1)}, f32[256,128]{1,0:T(8,128)S(1)}, u32[]{:S(2)}, u32[]{:S(2)}) collective-permute-start(f32[256,128]{1,0:T(8,128)S(1)} %get-tuple-element.15), channel_id=1, source_target_pairs={{0,1},{1,0},{2,3},{3,2},{4,5},{5,4},{6,7},{7,6},{9,10},{10,9},{11,... | collective-permute-start | bytes 393224 | tf_op jit(solution)/shard_map/ppermute | solution.py:71
  10.0 2.4 %collective-permute-done = f32[256,128]{1,0:T(8,128)S(1)} collective-permute-done((f32[256,128]{1,0:T(8,128)S(1)}, f32[256,128]{1,0:T(8,128)S(1)}, u32[]{:S(2)}, u32[]{:S(2)}) %collective-permute-start) | collective-permute-done | bytes 131104 | tf_op jit(solution)/shard_map/ppermute | solution.py:71
  12.5 3.8 %collective-permute-done.1 = f32[256,128]{1,0:T(8,128)S(1)} collective-permute-done((f32[256,128]{1,0:T(8,128)S(1)}, f32[256,128]{1,0:T(8,128)S(1)}, u32[]{:S(2)}, u32[]{:S(2)}) %collective-permute-start.1) | collective-permute-done | bytes 131104 | tf_op jit(solution)/shard_map/ppermute | solution.py:71
  16.3 2.9 %collective-permute-start.2 = (f32[256,128]{1,0:T(8,128)S(1)}, f32[256,128]{1,0:T(8,128)S(1)}, u32[]{:S(2)}, u32[]{:S(2)}) collective-permute-start(f32[256,128]{1,0:T(8,128)S(1)} %add.10), channel_id=1, source_target_pairs={{2,5},{5,2},{1,6},{6,1},{4,7},{7,4},{3,0},{0,3},{11,14},{14,11},{1... | collective-permute-start | bytes 393224 | tf_op jit(solution)/shard_map/ppermute | solution.py:71
  19.2 4.1 %collective-permute-done.2 = f32[256,128]{1,0:T(8,128)S(1)} collective-permute-done((f32[256,128]{1,0:T(8,128)S(1)}, f32[256,128]{1,0:T(8,128)S(1)}, u32[]{:S(2)}, u32[]{:S(2)}) %collective-permute-start.2) | collective-permute-done | bytes 131104 | tf_op jit(solution)/shard_map/ppermute | solution.py:71
  24.0 4.1 %collective-permute-start.3 = (f32[1792,128]{1,0:T(8,128)S(1)}, f32[1792,128]{1,0:T(8,128)S(1)}, u32[]{:S(2)}, u32[]{:S(2)}) collective-permute-start(f32[1792,128]{1,0:T(8,128)S(1)} %lift_send.1.refs_2_.refs_0_), channel_id=1, source_target_pairs={{0,8},{8,0},{16,24},{24,16},{32,40},{40,32},{48,56},{56,48},{64,72... | collective-permute-start | bytes 2752520 | tf_op jit(solution)/shard_map/ppermute | solution.py:91
  28.5 1.6 %collective-permute-done.3.refs_1_ = f32[1792,128]{1,0:T(8,128)S(1)} collective-permute-done((f32[1792,128]{1,0:T(8,128)S(1)}, f32[1792,128]{1,0:T(8,128)S(1)}, u32[]{:S(2)}, u32[]{:S(2)}) %collective-permute-start.3) | collective-permute-done | bytes 917536 | tf_op jit(solution)/shard_map/ppermute | solution.py:91
  30.2 1.6 %collective-permute-start.4 = (f32[832,128]{1,0:T(8,128)S(1)}, f32[832,128]{1,0:T(8,128)S(1)}, u32[]{:S(2)}, u32[]{:S(2)}) collective-permute-start(f32[832,128]{1,0:T(8,128)S(1)} %get-tuple-element.18.refs_2_), channel_id=1, source_target_pairs={{0,24},{8,64},{16,88},{24,0},{32,56},{40,96},{48,120},{56,32},{64,... | collective-permute-start | bytes 1277960 | tf_op jit(solution)/shard_map/ppermute | solution.py:100
  31.9 2.6 %collective-permute-start.6 = (f32[128,128]{1,0:T(8,128)S(1)}, f32[128,128]{1,0:T(8,128)S(1)}, u32[]{:S(2)}, u32[]{:S(2)}) collective-permute-start(f32[128,128]{1,0:T(8,128)S(1)} %gram_pair.1.refs_0_), channel_id=1, source_target_pairs={{56,0},{192,8},{40,16},{208,24},{24,32},{224,40},{8,48},{240,56},{... | collective-permute-start | bytes 196616 | tf_op jit(solution)/shard_map/ppermute | solution.py:96
  34.5 1.8 %collective-permute-start.5 = (f32[128,128]{1,0:T(8,128)S(1)}, f32[128,128]{1,0:T(8,128)S(1)}, u32[]{:S(2)}, u32[]{:S(2)}) collective-permute-start(f32[128,128]{1,0:T(8,128)S(1)} %gram_pair.1.refs_0_), channel_id=1, source_target_pairs={{0,240},{8,248},{16,224},{24,232},{32,208},{40,216},{48,192},{56,2... | collective-permute-start | bytes 196616 | tf_op jit(solution)/shard_map/ppermute | solution.py:91
  36.9 4.0 %collective-permute-done.5.refs_1_ = f32[128,128]{1,0:T(8,128)S(1)} collective-permute-done((f32[128,128]{1,0:T(8,128)S(1)}, f32[128,128]{1,0:T(8,128)S(1)}, u32[]{:S(2)}, u32[]{:S(2)}) %collective-permute-start.5) | collective-permute-done | bytes 65568 | tf_op jit(solution)/shard_map/ppermute | solution.py:91
  41.0 1.7 %collective-permute-start.8 = (f32[416,128]{1,0:T(8,128)S(1)}, f32[416,128]{1,0:T(8,128)S(1)}, u32[]{:S(2)}, u32[]{:S(2)}) collective-permute-start(f32[416,128]{1,0:T(8,128)S(1)} %get-tuple-element.20.refs_1_), channel_id=1, source_target_pairs={{0,56},{8,192},{16,216},{24,32},{32,24},{40,224},{48,248},{56,0},{... | collective-permute-start | bytes 638984 | tf_op jit(solution)/shard_map/ppermute | solution.py:100
  42.7 1.2 %collective-permute-start.9 = (f32[128,128]{1,0:T(8,128)S(1)}, f32[128,128]{1,0:T(8,128)S(1)}, u32[]{:S(2)}, u32[]{:S(2)}) collective-permute-start(f32[128,128]{1,0:T(8,128)S(1)} %hold.1.refs_0_), channel_id=1, source_target_pairs={{24,0},{64,8},{8,16},{80,24},{56,32},{96,40},{40,48},{112,56},{88,... | collective-permute-start | bytes 196616 | tf_op jit(solution)/shard_map/ppermute | solution.py:96
  44.0 3.2 %collective-permute-done.10.refs_3_.refs_1_ = f32[128,128]{1,0:T(8,128)S(1)} collective-permute-done((f32[128,128]{1,0:T(8,128)S(1)}, f32[128,128]{1,0:T(8,128)S(1)}, u32[]{:S(2)}, u32[]{:S(2)}) %collective-permute-start.10) | collective-permute-done | bytes 65568 | tf_op jit(solution)/shard_map/ppermute | solution.py:91
  47.1 0.9 %collective-permute-done.9.refs_2_.refs_0_ = f32[128,128]{1,0:T(8,128)S(1)} collective-permute-done((f32[128,128]{1,0:T(8,128)S(1)}, f32[128,128]{1,0:T(8,128)S(1)}, u32[]{:S(2)}, u32[]{:S(2)}) %collective-permute-start.9) | collective-permute-done | bytes 65568 | tf_op jit(solution)/shard_map/ppermute | solution.py:96
  48.1 2.9 %collective-permute-start.11 = (f32[416,128]{1,0:T(8,128)S(1)}, f32[416,128]{1,0:T(8,128)S(1)}, u32[]{:S(2)}, u32[]{:S(2)}) collective-permute-start(f32[416,128]{1,0:T(8,128)S(1)} %first_sum.1.refs_1_.refs_4_.refs_0_), channel_id=1, source_target_pairs={{0,200},{8,48},{16,40},{24,208},{32,232},{40,16},{48,8},{56,240},{... | collective-permute-start | bytes 638984 | tf_op jit(solution)/shard_map/ppermute | solution.py:100
  51.0 1.2 %collective-permute-done.12.refs_3_ = f32[128,128]{1,0:T(8,128)S(1)} collective-permute-done((f32[128,128]{1,0:T(8,128)S(1)}, f32[128,128]{1,0:T(8,128)S(1)}, u32[]{:S(2)}, u32[]{:S(2)}) %collective-permute-start.12) | collective-permute-done | bytes 65568 | tf_op jit(solution)/shard_map/ppermute | solution.py:91
  52.3 2.1 %eliminate0.1.refs_2_.refs_0_ = f32[128,128]{1,0:T(8,128)S(1)} custom-call(f32[128,128]{1,0:T(8,128)S(1)} %gram_four.3.refs_0_.refs_1_, f32[128,128]{1,0:T(8,128)S(1)} %gram_four.3.refs_0_.refs_1_), custom_call_target="tpu_custom_call" | custom-call | flops 4000000 | bytes 6000000 | tf_op jit(solution)/shard_map/eliminate0/pallas_call | solution.py:163
  55.3 2.6 %eliminate40.1.refs_2_.refs_1_ = f32[128,128]{1,0:T(8,128)S(1)} custom-call(f32[128,128]{1,0:T(8,128)S(1)} %eliminate0.1.refs_2_.refs_0_, f32[128,128]{1,0:T(8,128)S(1)} %gram_four.3.refs_0_.refs_1_, f32[416,128]{1,0:T(8,128)S(1)} %second_sum.1.refs_2_.refs_0_), custom_call_target="tpu_custom_call" | custom-call | flops 4000000 | bytes 13200000 | tf_op jit(solution)/shard_map/eliminate40/pallas_call | solution.py:163
  57.8 3.0 %collective-permute-done.13.refs_1_ = f32[416,128]{1,0:T(8,128)S(1)} collective-permute-done((f32[416,128]{1,0:T(8,128)S(1)}, f32[416,128]{1,0:T(8,128)S(1)}, u32[]{:S(2)}, u32[]{:S(2)}) %collective-permute-start.13) | collective-permute-done | bytes 213024 | tf_op jit(solution)/shard_map/ppermute | solution.py:100
  61.1 1.4 %collective-permute-start.14 = (bf16[416,128]{1,0:T(8,128)(2,1)S(1)}, bf16[416,128]{1,0:T(8,128)(2,1)S(1)}, u32[]{:S(2)}, u32[]{:S(2)}) collective-permute-start(bf16[416,128]{1,0:T(8,128)(2,1)S(1)} %block.1.refs_2_.refs_0_), channel_id=1, source_target_pairs={{0,56},{8,192},{16,216},{24,32},{32,24},{40,224},{48,248},{56,0},{... | collective-permute-start | bytes 319496 | tf_op jit(solution)/shard_map/ppermute | solution.py:100
  62.8 4.0 %collective-permute-done.14.refs_1_ = bf16[416,128]{1,0:T(8,128)(2,1)S(1)} collective-permute-done((bf16[416,128]{1,0:T(8,128)(2,1)S(1)}, bf16[416,128]{1,0:T(8,128)(2,1)S(1)}, u32[]{:S(2)}, u32[]{:S(2)}) %collective-permute-start.14) | collective-permute-done | bytes 106528 | tf_op jit(solution)/shard_map/ppermute | solution.py:100
  67.0 1.4 %collective-permute-start.17 = (f32[8,128]{1,0:T(8,128)S(1)}, f32[8,128]{1,0:T(8,128)S(1)}, u32[]{:S(2)}, u32[]{:S(2)}) collective-permute-start(f32[8,128]{1,0:T(8,128)S(1)} %squares.1.refs_2_), channel_id=1, source_target_pairs={{0,25},{1,24},{2,27},{3,26},{4,29},{5,28},{6,31},{7,30},{8,65},{9,... | collective-permute-start | bytes 12296 | tf_op jit(solution)/shard_map/ppermute | solution.py:79
  68.4 1.6 %collective-permute-start.16 = (f32[8,128]{1,0:T(8,128)S(1)}, f32[8,128]{1,0:T(8,128)S(1)}, u32[]{:S(2)}, u32[]{:S(2)}) collective-permute-start(f32[8,128]{1,0:T(8,128)S(1)} %squares.1.refs_2_), channel_id=1, source_target_pairs={{0,1},{1,0},{2,3},{3,2},{4,5},{5,4},{6,7},{7,6},{8,9},{9,8},{10,11... | collective-permute-start | bytes 12296 | tf_op jit(solution)/shard_map/ppermute | solution.py:79
  70.0 1.1 %collective-permute-done.17.refs_4_ = f32[8,128]{1,0:T(8,128)S(1)} collective-permute-done((f32[8,128]{1,0:T(8,128)S(1)}, f32[8,128]{1,0:T(8,128)S(1)}, u32[]{:S(2)}, u32[]{:S(2)}) %collective-permute-start.17) | collective-permute-done | bytes 4128 | tf_op jit(solution)/shard_map/ppermute | solution.py:79
  73.0 1.3 %collective-permute-done.19.refs_3_ = f32[8,128]{1,0:T(8,128)S(1)} collective-permute-done((f32[8,128]{1,0:T(8,128)S(1)}, f32[8,128]{1,0:T(8,128)S(1)}, u32[]{:S(2)}, u32[]{:S(2)}) %collective-permute-start.19) | collective-permute-done | bytes 4128 | tf_op jit(solution)/shard_map/ppermute | solution.py:91
  74.4 4.4 %collective-permute-start.21 = (f32[8,128]{1,0:T(8,128)S(1)}, f32[8,128]{1,0:T(8,128)S(1)}, u32[]{:S(2)}, u32[]{:S(2)}) collective-permute-start(f32[8,128]{1,0:T(8,128)S(1)} %get-tuple-element.24.sq_ref), channel_id=1, source_target_pairs={{15,0},{10,1},{9,2},{12,3},{11,4},{14,5},{13,6},{8,7},{2,8},{7,9},... | collective-permute-start | bytes 12296 | tf_op jit(solution)/shard_map/ppermute | solution.py:87
  78.8 2.1 %collective-permute-start.20 = (f32[8,128]{1,0:T(8,128)S(1)}, f32[8,128]{1,0:T(8,128)S(1)}, u32[]{:S(2)}, u32[]{:S(2)}) collective-permute-start(f32[8,128]{1,0:T(8,128)S(1)} %get-tuple-element.24.sq_ref), channel_id=1, source_target_pairs={{13,0},{12,1},{15,2},{14,3},{9,4},{8,5},{11,6},{10,7},{5,8},{4,9},... | collective-permute-start | bytes 12296 | tf_op jit(solution)/shard_map/ppermute | solution.py:87
  80.9 1.5 %finish_momentum.1 = bf16[256,3328]{1,0:T(8,128)(2,1)} custom-call(f32[3328,128]{1,0:T(8,128)S(1)} %get-tuple-element.23.coef_ref, bf16[256,128]{1,0:T(8,128)(2,1)S(1)} %ortho.1.refs_2_.ortho_ref, bf16[256,3328]{1,0:T(8,128)(2,1)S(1)} %get-tuple-element.16.refs_1_.b_ref), custom_call_target="tpu_custom_call" | custom-call | flops 218103808 | bytes 5000000 | tf_op jit(solution)/shard_map/finish_momentum/pallas_call | solution.py:385
  82.4 2.4 %collective-permute-done.20.opposite_ref = f32[8,128]{1,0:T(8,128)S(1)} collective-permute-done((f32[8,128]{1,0:T(8,128)S(1)}, f32[8,128]{1,0:T(8,128)S(1)}, u32[]{:S(2)}, u32[]{:S(2)}) %collective-permute-start.20) | collective-permute-done | bytes 4128 | tf_op jit(solution)/shard_map/ppermute | solution.py:87
  84.8 1.9 %finish_weights.1 = (bf16[256,3328]{1,0:T(8,128)(2,1)}, f32[3328,128]{1,0:T(8,128)}) custom-call(f32[8,128]{1,0:T(8,128)S(1)} %get-tuple-element.24.sq_ref, f32[8,128]{1,0:T(8,128)S(1)} %collective-permute-done.20.opposite_ref, f32[8,128]{1,0:T(8,128)S(1)} %collective-permute-done.21.next_ref, f32[8,128]{1,0:T(8,128)S(1)} %collective-permute-done.22.previous_ref, ...), custom_call_target="tpu_custom_call" | custom-call | flops 218103808 | bytes 7000000 | tf_op jit(solution)/shard_map/finish_weights/pallas_call | solution.py:429
  (41 shorter events, 5.6 us)
Async XLA Ops:
  3.5 8.8 %collective-permute-start = (f32[256,128]{1,0:T(8,128)S(1)}, f32[256,128]{1,0:T(8,128)S(1)}, u32[]{:S(2)}, u32[]{:S(2)}) collective-permute-start(f32[256,128]{1,0:T(8,128)S(1)} %get-tuple-element.15), channel_id=1, source_target_pairs={{0,1},{1,0},{2,3},{3,2},{4,5},{5,4},{6,7},{7,6},{9,10},{10,9},{11,... | collective-permute-start | bytes 393224 | tf_op jit(solution)/shard_map/ppermute | solution.py:71
  12.4 3.9 %collective-permute-start.1 = (f32[256,128]{1,0:T(8,128)S(1)}, f32[256,128]{1,0:T(8,128)S(1)}, u32[]{:S(2)}, u32[]{:S(2)}) collective-permute-start(f32[256,128]{1,0:T(8,128)S(1)} %add.9), channel_id=1, source_target_pairs={{1,2},{2,1},{3,4},{4,3},{5,6},{6,5},{7,0},{0,7},{10,11},{11,10},{1... | collective-permute-start | bytes 393224 | tf_op jit(solution)/shard_map/ppermute | solution.py:71
  16.3 7.1 %collective-permute-start.2 = (f32[256,128]{1,0:T(8,128)S(1)}, f32[256,128]{1,0:T(8,128)S(1)}, u32[]{:S(2)}, u32[]{:S(2)}) collective-permute-start(f32[256,128]{1,0:T(8,128)S(1)} %add.10), channel_id=1, source_target_pairs={{2,5},{5,2},{1,6},{6,1},{4,7},{7,4},{3,0},{0,3},{11,14},{14,11},{1... | collective-permute-start | bytes 393224 | tf_op jit(solution)/shard_map/ppermute | solution.py:71
  24.0 6.2 %collective-permute-start.3 = (f32[1792,128]{1,0:T(8,128)S(1)}, f32[1792,128]{1,0:T(8,128)S(1)}, u32[]{:S(2)}, u32[]{:S(2)}) collective-permute-start(f32[1792,128]{1,0:T(8,128)S(1)} %lift_send.1.refs_2_.refs_0_), channel_id=1, source_target_pairs={{0,8},{8,0},{16,24},{24,16},{32,40},{40,32},{48,56},{56,48},{64,72... | collective-permute-start | bytes 2752520 | tf_op jit(solution)/shard_map/ppermute | solution.py:91
  30.2 10.7 %collective-permute-start.4 = (f32[832,128]{1,0:T(8,128)S(1)}, f32[832,128]{1,0:T(8,128)S(1)}, u32[]{:S(2)}, u32[]{:S(2)}) collective-permute-start(f32[832,128]{1,0:T(8,128)S(1)} %get-tuple-element.18.refs_2_), channel_id=1, source_target_pairs={{0,24},{8,64},{16,88},{24,0},{32,56},{40,96},{48,120},{56,32},{64,... | collective-permute-start | bytes 1277960 | tf_op jit(solution)/shard_map/ppermute | solution.py:100
  31.9 5.0 %collective-permute-start.6 = (f32[128,128]{1,0:T(8,128)S(1)}, f32[128,128]{1,0:T(8,128)S(1)}, u32[]{:S(2)}, u32[]{:S(2)}) collective-permute-start(f32[128,128]{1,0:T(8,128)S(1)} %gram_pair.1.refs_0_), channel_id=1, source_target_pairs={{56,0},{192,8},{40,16},{208,24},{24,32},{224,40},{8,48},{240,56},{... | collective-permute-start | bytes 196616 | tf_op jit(solution)/shard_map/ppermute | solution.py:96
  34.5 6.4 %collective-permute-start.5 = (f32[128,128]{1,0:T(8,128)S(1)}, f32[128,128]{1,0:T(8,128)S(1)}, u32[]{:S(2)}, u32[]{:S(2)}) collective-permute-start(f32[128,128]{1,0:T(8,128)S(1)} %gram_pair.1.refs_0_), channel_id=1, source_target_pairs={{0,240},{8,248},{16,224},{24,232},{32,208},{40,216},{48,192},{56,2... | collective-permute-start | bytes 196616 | tf_op jit(solution)/shard_map/ppermute | solution.py:91
  36.9 4.0 %collective-permute-start.7 = (f32[128,128]{1,0:T(8,128)S(1)}, f32[128,128]{1,0:T(8,128)S(1)}, u32[]{:S(2)}, u32[]{:S(2)}) collective-permute-start(f32[128,128]{1,0:T(8,128)S(1)} %collective-permute-done.6.refs_2_), channel_id=1, source_target_pairs={{0,8},{8,0},{16,24},{24,16},{32,40},{40,32},{48,56},{56,48},{64,72... | collective-permute-start | bytes 196616 | tf_op jit(solution)/shard_map/ppermute | solution.py:91
  41.0 7.0 %collective-permute-start.8 = (f32[416,128]{1,0:T(8,128)S(1)}, f32[416,128]{1,0:T(8,128)S(1)}, u32[]{:S(2)}, u32[]{:S(2)}) collective-permute-start(f32[416,128]{1,0:T(8,128)S(1)} %get-tuple-element.20.refs_1_), channel_id=1, source_target_pairs={{0,56},{8,192},{16,216},{24,32},{32,24},{40,224},{48,248},{56,0},{... | collective-permute-start | bytes 638984 | tf_op jit(solution)/shard_map/ppermute | solution.py:100
  42.7 4.4 %collective-permute-start.10 = (f32[128,128]{1,0:T(8,128)S(1)}, f32[128,128]{1,0:T(8,128)S(1)}, u32[]{:S(2)}, u32[]{:S(2)}) collective-permute-start(f32[128,128]{1,0:T(8,128)S(1)} %hold.1.refs_0_), channel_id=1, source_target_pairs={{0,80},{8,88},{16,64},{24,72},{32,112},{40,120},{48,96},{56,104},{... | collective-permute-start | bytes 196616 | tf_op jit(solution)/shard_map/ppermute | solution.py:91
  42.7 5.3 %collective-permute-start.9 = (f32[128,128]{1,0:T(8,128)S(1)}, f32[128,128]{1,0:T(8,128)S(1)}, u32[]{:S(2)}, u32[]{:S(2)}) collective-permute-start(f32[128,128]{1,0:T(8,128)S(1)} %hold.1.refs_0_), channel_id=1, source_target_pairs={{24,0},{64,8},{8,16},{80,24},{56,32},{96,40},{40,48},{112,56},{88,... | collective-permute-start | bytes 196616 | tf_op jit(solution)/shard_map/ppermute | solution.py:96
  48.1 6.9 %collective-permute-start.11 = (f32[416,128]{1,0:T(8,128)S(1)}, f32[416,128]{1,0:T(8,128)S(1)}, u32[]{:S(2)}, u32[]{:S(2)}) collective-permute-start(f32[416,128]{1,0:T(8,128)S(1)} %first_sum.1.refs_1_.refs_4_.refs_0_), channel_id=1, source_target_pairs={{0,200},{8,48},{16,40},{24,208},{32,232},{40,16},{48,8},{56,240},{... | collective-permute-start | bytes 638984 | tf_op jit(solution)/shard_map/ppermute | solution.py:100
  51.0 1.3 %collective-permute-start.12 = (f32[128,128]{1,0:T(8,128)S(1)}, f32[128,128]{1,0:T(8,128)S(1)}, u32[]{:S(2)}, u32[]{:S(2)}) collective-permute-start(f32[128,128]{1,0:T(8,128)S(1)} %hold_split.1.refs_2_), channel_id=1, source_target_pairs={{0,8},{8,0},{16,24},{24,16},{32,40},{40,32},{48,56},{56,48},{64,72... | collective-permute-start | bytes 196616 | tf_op jit(solution)/shard_map/ppermute | solution.py:91
  55.0 5.8 %collective-permute-start.13 = (f32[416,128]{1,0:T(8,128)S(1)}, f32[416,128]{1,0:T(8,128)S(1)}, u32[]{:S(2)}, u32[]{:S(2)}) collective-permute-start(f32[416,128]{1,0:T(8,128)S(1)} %second_sum.1.refs_2_.refs_0_), channel_id=1, source_target_pairs={{0,72},{8,16},{16,8},{24,80},{32,104},{40,48},{48,40},{56,112},{64... | collective-permute-start | bytes 638984 | tf_op jit(solution)/shard_map/ppermute | solution.py:100
  61.1 5.7 %collective-permute-start.14 = (bf16[416,128]{1,0:T(8,128)(2,1)S(1)}, bf16[416,128]{1,0:T(8,128)(2,1)S(1)}, u32[]{:S(2)}, u32[]{:S(2)}) collective-permute-start(bf16[416,128]{1,0:T(8,128)(2,1)S(1)} %block.1.refs_2_.refs_0_), channel_id=1, source_target_pairs={{0,56},{8,192},{16,216},{24,32},{32,24},{40,224},{48,248},{56,0},{... | collective-permute-start | bytes 319496 | tf_op jit(solution)/shard_map/ppermute | solution.py:100
  66.9 5.4 %collective-permute-start.15 = (bf16[832,128]{1,0:T(8,128)(2,1)S(1)}, bf16[832,128]{1,0:T(8,128)(2,1)S(1)}, u32[]{:S(2)}, u32[]{:S(2)}) collective-permute-start(bf16[832,128]{1,0:T(8,128)(2,1)S(1)} %join1.1.refs_0_), channel_id=1, source_target_pairs={{0,24},{8,64},{16,88},{24,0},{32,56},{40,96},{48,120},{56,32},{64,... | collective-permute-start | bytes 638984 | tf_op jit(solution)/shard_map/ppermute | solution.py:100
  67.0 4.1 %collective-permute-start.17 = (f32[8,128]{1,0:T(8,128)S(1)}, f32[8,128]{1,0:T(8,128)S(1)}, u32[]{:S(2)}, u32[]{:S(2)}) collective-permute-start(f32[8,128]{1,0:T(8,128)S(1)} %squares.1.refs_2_), channel_id=1, source_target_pairs={{0,25},{1,24},{2,27},{3,26},{4,29},{5,28},{6,31},{7,30},{8,65},{9,... | collective-permute-start | bytes 12296 | tf_op jit(solution)/shard_map/ppermute | solution.py:79
  68.4 2.9 %collective-permute-start.16 = (f32[8,128]{1,0:T(8,128)S(1)}, f32[8,128]{1,0:T(8,128)S(1)}, u32[]{:S(2)}, u32[]{:S(2)}) collective-permute-start(f32[8,128]{1,0:T(8,128)S(1)} %squares.1.refs_2_), channel_id=1, source_target_pairs={{0,1},{1,0},{2,3},{3,2},{4,5},{5,4},{6,7},{7,6},{8,9},{9,8},{10,11... | collective-permute-start | bytes 12296 | tf_op jit(solution)/shard_map/ppermute | solution.py:79
  72.4 1.9 %collective-permute-start.18 = (bf16[1664,128]{1,0:T(8,128)(2,1)S(1)}, bf16[1664,128]{1,0:T(8,128)(2,1)S(1)}, u32[]{:S(2)}, u32[]{:S(2)}) collective-permute-start(bf16[1664,128]{1,0:T(8,128)(2,1)S(1)} %get-tuple-element.21.refs_0_), channel_id=1, source_target_pairs={{0,8},{8,0},{16,24},{24,16},{32,40},{40,32},{48,56},{56,48},{64,72... | collective-permute-start | bytes 1277960 | tf_op jit(solution)/shard_map/ppermute | solution.py:91
  72.8 1.4 %collective-permute-start.19 = (f32[8,128]{1,0:T(8,128)S(1)}, f32[8,128]{1,0:T(8,128)S(1)}, u32[]{:S(2)}, u32[]{:S(2)}) collective-permute-start(f32[8,128]{1,0:T(8,128)S(1)} %get-tuple-element.22.refs_2_), channel_id=1, source_target_pairs={{0,8},{8,0},{16,24},{24,16},{32,40},{40,32},{48,56},{56,48},{64,72... | collective-permute-start | bytes 12296 | tf_op jit(solution)/shard_map/ppermute | solution.py:91
  74.4 6.5 %collective-permute-start.21 = (f32[8,128]{1,0:T(8,128)S(1)}, f32[8,128]{1,0:T(8,128)S(1)}, u32[]{:S(2)}, u32[]{:S(2)}) collective-permute-start(f32[8,128]{1,0:T(8,128)S(1)} %get-tuple-element.24.sq_ref), channel_id=1, source_target_pairs={{15,0},{10,1},{9,2},{12,3},{11,4},{14,5},{13,6},{8,7},{2,8},{7,9},... | collective-permute-start | bytes 12296 | tf_op jit(solution)/shard_map/ppermute | solution.py:87
  78.8 6.0 %collective-permute-start.20 = (f32[8,128]{1,0:T(8,128)S(1)}, f32[8,128]{1,0:T(8,128)S(1)}, u32[]{:S(2)}, u32[]{:S(2)}) collective-permute-start(f32[8,128]{1,0:T(8,128)S(1)} %get-tuple-element.24.sq_ref), channel_id=1, source_target_pairs={{13,0},{12,1},{15,2},{14,3},{9,4},{8,5},{11,6},{10,7},{5,8},{4,9},... | collective-permute-start | bytes 12296 | tf_op jit(solution)/shard_map/ppermute | solution.py:87
  80.9 3.9 %collective-permute-start.22 = (f32[8,128]{1,0:T(8,128)S(1)}, f32[8,128]{1,0:T(8,128)S(1)}, u32[]{:S(2)}, u32[]{:S(2)}) collective-permute-start(f32[8,128]{1,0:T(8,128)S(1)} %collective-permute-done.21.next_ref), channel_id=1, source_target_pairs={{0,8},{8,0},{16,24},{24,16},{32,40},{40,32},{48,56},{56,48},{64,72... | collective-permute-start | bytes 12296 | tf_op jit(solution)/shard_map/ppermute | solution.py:91
  80.9 3.9 %copy-start = (bf16[256,3328]{1,0:T(8,128)(2,1)S(1)}, bf16[256,3328]{1,0:T(8,128)(2,1)}, u32[]{:S(2)}) copy-start(bf16[256,3328]{1,0:T(8,128)(2,1)} %weights_ref.1) | copy-start | bytes 5111812

commit v5 on v4

--- a/solution.py
+++ b/solution.py
@@ -363,7 +363,12 @@
     sum_ref[...] = sq_ref[...] + other_sq_ref[...]
 
 
-def momentum_kernel(coef_ref, ortho_ref, b_ref, mom_hbm, buf, sems):
+def stack_kernel(opposite_ref, next_ref, out_ref):
+    out_ref[:8, :] = opposite_ref[...]
+    out_ref[8:, :] = next_ref[...]
+
+
+def momentum_kernel(coef_ref, ortho_ref, b_ref, mom_hbm, done_ref, buf, sems):
     ortho = ortho_ref[...]
     copies = []
     for i in range(TILES):
@@ -379,14 +384,15 @@
         copies[-1].start()
     for copy in copies:
         copy.wait()
+    done_ref[...] = jnp.zeros_like(done_ref)
 
 
 def finish_momentum(coef, ortho, blended):
     return pl.pallas_call(
         momentum_kernel,
         in_specs=[VMEM_SPEC] * 3,
-        out_specs=HBM_SPEC,
-        out_shape=bf16(LOCAL_ROWS, LOCAL_COLS),
+        out_specs=[HBM_SPEC, VMEM_SPEC],
+        out_shape=[bf16(LOCAL_ROWS, LOCAL_COLS), f32(8, RANK)],
         scratch_shapes=[
             VMEM((LOCAL_ROWS, LOCAL_COLS), jnp.bfloat16),
             pltpu.SemaphoreType.DMA((TILES,)),
@@ -397,9 +403,10 @@
     )(coef, ortho, blended)
 
 
-def weights_kernel(sq_ref, opposite_ref, next_ref, previous_ref, coef_ref, ortho_ref, weights_ref, new_hbm, sub_hbm, buf, sub_buf, sems):
+def weights_kernel(sq_ref, moved_ref, other_ref, coef_ref, ortho_ref, weights_ref, new_hbm, sub_hbm, buf, sub_buf, sems):
     scaling = math.sqrt(ROWS * COLS / RANK)
-    squares = (sq_ref[...] + opposite_ref[...]) + (next_ref[...] + previous_ref[...])
+    moved = moved_ref[...] + other_ref[...]
+    squares = (sq_ref[...] + moved[:8, :]) + moved[8:, :]
     norm = 1.0 / jnp.sqrt(jnp.sum(squares, axis=0, keepdims=True) + epsilon_sq)
     ortho = ortho_ref[...]
     copies = []
@@ -428,7 +435,7 @@
 def finish_weights(squares, coef, ortho, weights):
     return pl.pallas_call(
         weights_kernel,
-        in_specs=[VMEM_SPEC] * 7,
+        in_specs=[VMEM_SPEC] * 6,
         out_specs=[HBM_SPEC] * 2,
         out_shape=[bf16(LOCAL_ROWS, LOCAL_COLS), f32(LOCAL_COLS, RANK)],
         scratch_shapes=[
@@ -496,14 +503,18 @@
         [coef, recv, squares, pair_z(squares, False), pair_z(squares, True)],
         nbytes=CHUNK * 4096, name="join0",
     )
+    opposite = turn_z(squares, (3, 3))
     coef, squares = local(
         unpack_kernel, [f32(LOCAL_COLS, RANK), f32(8, RANK)],
         [coef, xor_fsdp(coef, CORE), squares, xor_fsdp(squares, CORE)],
-        flops=3328 * 128, nbytes=2600000, name="unpack",
-    )
-    split = turn_z(squares, (1, -2))
-    squares = [squares, turn_z(squares, (3, 3)), split, xor_fsdp(split, CORE)]
-    new_momentum = finish_momentum(coef, ortho, blended)
+        flops=3328 * 128, nbytes=20000000, name="unpack",
+    )
+    new_momentum, done = finish_momentum(coef, ortho, blended)
+    moved = local(
+        stack_kernel, f32(16, RANK), [opposite, turn_z(squares, (1, -2))], [done],
+        nbytes=30000, name="stack",
+    )
+    squares = [squares, moved, xor_fsdp(moved, CORE)]
     new_weights, new_subspace = finish_weights(squares, coef, ortho, weights)
     return (new_momentum, new_weights, new_subspace)
 

time: 87 us -> 85.3 us (0.980)
  waiting for transfers between devices: 35.2 us -> 34 us
    pallas_call x19 -> x20, Pallas kernels: 6.96 us -> 6.97 us  [local(): pl.pallas_call(body, in_specs=[VMEM_SPEC] * (used + len(after)), out_spec...]
where the time goes in v5:
time: 85.3 us; the launch traced here: 85.2 us
  starting transfers between devices  37 us (43%)
  waiting for transfers between devices  34 us (40%)
  Pallas kernels  13.2 us (15%)
  between operations  0.96 us (1%)
    ppermute x8, waiting for transfers between devices, xor_fsdp(): return lax.ppermute(x, 'fsdp', [(i, i ^ mask) for i in range(FSDP)])  10.9 us
    ppermute x3, waiting for transfers between devices, swap_z(): return lax.ppermute(x, ('fsdp', 'tp'), perm)  10.3 us
    ppermute x3, starting transfers between devices, swap_z(): return lax.ppermute(x, ('fsdp', 'tp'), perm)  9.5 us
    ppermute x6, waiting for transfers between devices, xor_step(): lax.ppermute(x, 'fsdp', [(i, i ^ MASKS[team(i)][k]) for i in range(FSDP)])  8.34 us
    ppermute x6, starting transfers between devices, xor_step(): lax.ppermute(x, 'fsdp', [(i, i ^ MASKS[team(i)][k]) for i in range(FSDP)])  8.07 us
    pallas_call x20, Pallas kernels, local(): pl.pallas_call(body, in_specs=[VMEM_SPEC] * (used + len(after)), out_spec...  6.97 us
    ppermute x8, starting transfers between devices, xor_fsdp(): return lax.ppermute(x, 'fsdp', [(i, i ^ mask) for i in range(FSDP)])  6.94 us
    ppermute x2, starting transfers between devices, turn_z(): return lax.ppermute(x, ('fsdp', 'tp'), perm)  5.68 us
  transfers between devices with their start and end apart: 23, of which 17 were waited for; matrix products, arithmetic and copies ran while one was open for 0% of the time, Pallas kernels for 8%

profile of v5, /device:TPU:1, one launch (start us, length us, event | category | flops | bytes accessed | tf_op | source)
XLA Modules:
  0.0 85.2 jit_solution(4686242232529946962)
XLA Ops:
  0.6 2.9 %project.1 = (bf16[256,3328]{1,0:T(8,128)(2,1)S(1)}, f32[256,128]{1,0:T(8,128)S(1)}) custom-call(bf16[256,3328]{1,0:T(8,128)(2,1)} %m_hbm.1, bf16[256,3328]{1,0:T(8,128)(2,1)} %g_hbm.1, f32[3328,128]{1,0:T(8,128)} %s_hbm.1), custom_call_target="tpu_custom_call" | custom-call | flops 218103808 | bytes 7000000 | tf_op jit(solution)/shard_map/project/pallas_call | solution.py:139
  3.5 6.5 %collective-permute-start = (f32[256,128]{1,0:T(8,128)S(1)}, f32[256,128]{1,0:T(8,128)S(1)}, u32[]{:S(2)}, u32[]{:S(2)}) collective-permute-start(f32[256,128]{1,0:T(8,128)S(1)} %get-tuple-element.17), channel_id=1, source_target_pairs={{0,1},{1,0},{2,3},{3,2},{4,5},{5,4},{6,7},{7,6},{9,10},{10,9},{11,... | collective-permute-start | bytes 393224 | tf_op jit(solution)/shard_map/ppermute | solution.py:71
  10.0 2.4 %collective-permute-done = f32[256,128]{1,0:T(8,128)S(1)} collective-permute-done((f32[256,128]{1,0:T(8,128)S(1)}, f32[256,128]{1,0:T(8,128)S(1)}, u32[]{:S(2)}, u32[]{:S(2)}) %collective-permute-start) | collective-permute-done | bytes 131104 | tf_op jit(solution)/shard_map/ppermute | solution.py:71
  12.5 3.8 %collective-permute-done.1 = f32[256,128]{1,0:T(8,128)S(1)} collective-permute-done((f32[256,128]{1,0:T(8,128)S(1)}, f32[256,128]{1,0:T(8,128)S(1)}, u32[]{:S(2)}, u32[]{:S(2)}) %collective-permute-start.1) | collective-permute-done | bytes 131104 | tf_op jit(solution)/shard_map/ppermute | solution.py:71
  16.3 2.9 %collective-permute-start.2 = (f32[256,128]{1,0:T(8,128)S(1)}, f32[256,128]{1,0:T(8,128)S(1)}, u32[]{:S(2)}, u32[]{:S(2)}) collective-permute-start(f32[256,128]{1,0:T(8,128)S(1)} %add.10), channel_id=1, source_target_pairs={{2,5},{5,2},{1,6},{6,1},{4,7},{7,4},{3,0},{0,3},{11,14},{14,11},{1... | collective-permute-start | bytes 393224 | tf_op jit(solution)/shard_map/ppermute | solution.py:71
  19.2 4.1 %collective-permute-done.2 = f32[256,128]{1,0:T(8,128)S(1)} collective-permute-done((f32[256,128]{1,0:T(8,128)S(1)}, f32[256,128]{1,0:T(8,128)S(1)}, u32[]{:S(2)}, u32[]{:S(2)}) %collective-permute-start.2) | collective-permute-done | bytes 131104 | tf_op jit(solution)/shard_map/ppermute | solution.py:71
  24.0 4.1 %collective-permute-start.3 = (f32[1792,128]{1,0:T(8,128)S(1)}, f32[1792,128]{1,0:T(8,128)S(1)}, u32[]{:S(2)}, u32[]{:S(2)}) collective-permute-start(f32[1792,128]{1,0:T(8,128)S(1)} %lift_send.1.refs_2_.refs_0_), channel_id=1, source_target_pairs={{0,8},{8,0},{16,24},{24,16},{32,40},{40,32},{48,56},{56,48},{64,72... | collective-permute-start | bytes 2752520 | tf_op jit(solution)/shard_map/ppermute | solution.py:91
  28.5 1.6 %collective-permute-done.3.refs_1_ = f32[1792,128]{1,0:T(8,128)S(1)} collective-permute-done((f32[1792,128]{1,0:T(8,128)S(1)}, f32[1792,128]{1,0:T(8,128)S(1)}, u32[]{:S(2)}, u32[]{:S(2)}) %collective-permute-start.3) | collective-permute-done | bytes 917536 | tf_op jit(solution)/shard_map/ppermute | solution.py:91
  30.2 1.6 %collective-permute-start.4 = (f32[832,128]{1,0:T(8,128)S(1)}, f32[832,128]{1,0:T(8,128)S(1)}, u32[]{:S(2)}, u32[]{:S(2)}) collective-permute-start(f32[832,128]{1,0:T(8,128)S(1)} %get-tuple-element.20.refs_2_), channel_id=1, source_target_pairs={{0,24},{8,64},{16,88},{24,0},{32,56},{40,96},{48,120},{56,32},{64,... | collective-permute-start | bytes 1277960 | tf_op jit(solution)/shard_map/ppermute | solution.py:100
  31.9 2.6 %collective-permute-start.6 = (f32[128,128]{1,0:T(8,128)S(1)}, f32[128,128]{1,0:T(8,128)S(1)}, u32[]{:S(2)}, u32[]{:S(2)}) collective-permute-start(f32[128,128]{1,0:T(8,128)S(1)} %gram_pair.1.refs_0_), channel_id=1, source_target_pairs={{56,0},{192,8},{40,16},{208,24},{24,32},{224,40},{8,48},{240,56},{... | collective-permute-start | bytes 196616 | tf_op jit(solution)/shard_map/ppermute | solution.py:96
  34.5 1.8 %collective-permute-start.5 = (f32[128,128]{1,0:T(8,128)S(1)}, f32[128,128]{1,0:T(8,128)S(1)}, u32[]{:S(2)}, u32[]{:S(2)}) collective-permute-start(f32[128,128]{1,0:T(8,128)S(1)} %gram_pair.1.refs_0_), channel_id=1, source_target_pairs={{0,240},{8,248},{16,224},{24,232},{32,208},{40,216},{48,192},{56,2... | collective-permute-start | bytes 196616 | tf_op jit(solution)/shard_map/ppermute | solution.py:91
  36.9 4.0 %collective-permute-done.5.refs_1_ = f32[128,128]{1,0:T(8,128)S(1)} collective-permute-done((f32[128,128]{1,0:T(8,128)S(1)}, f32[128,128]{1,0:T(8,128)S(1)}, u32[]{:S(2)}, u32[]{:S(2)}) %collective-permute-start.5) | collective-permute-done | bytes 65568 | tf_op jit(solution)/shard_map/ppermute | solution.py:91
  41.0 1.7 %collective-permute-start.8 = (f32[416,128]{1,0:T(8,128)S(1)}, f32[416,128]{1,0:T(8,128)S(1)}, u32[]{:S(2)}, u32[]{:S(2)}) collective-permute-start(f32[416,128]{1,0:T(8,128)S(1)} %get-tuple-element.22.refs_1_), channel_id=1, source_target_pairs={{0,56},{8,192},{16,216},{24,32},{32,24},{40,224},{48,248},{56,0},{... | collective-permute-start | bytes 638984 | tf_op jit(solution)/shard_map/ppermute | solution.py:100
  42.7 1.2 %collective-permute-start.9 = (f32[128,128]{1,0:T(8,128)S(1)}, f32[128,128]{1,0:T(8,128)S(1)}, u32[]{:S(2)}, u32[]{:S(2)}) collective-permute-start(f32[128,128]{1,0:T(8,128)S(1)} %hold.1.refs_0_), channel_id=1, source_target_pairs={{24,0},{64,8},{8,16},{80,24},{56,32},{96,40},{40,48},{112,56},{88,... | collective-permute-start | bytes 196616 | tf_op jit(solution)/shard_map/ppermute | solution.py:96
  44.0 3.2 %collective-permute-done.10.refs_3_.refs_1_ = f32[128,128]{1,0:T(8,128)S(1)} collective-permute-done((f32[128,128]{1,0:T(8,128)S(1)}, f32[128,128]{1,0:T(8,128)S(1)}, u32[]{:S(2)}, u32[]{:S(2)}) %collective-permute-start.10) | collective-permute-done | bytes 65568 | tf_op jit(solution)/shard_map/ppermute | solution.py:91
  47.1 0.9 %collective-permute-done.9.refs_2_.refs_0_ = f32[128,128]{1,0:T(8,128)S(1)} collective-permute-done((f32[128,128]{1,0:T(8,128)S(1)}, f32[128,128]{1,0:T(8,128)S(1)}, u32[]{:S(2)}, u32[]{:S(2)}) %collective-permute-start.9) | collective-permute-done | bytes 65568 | tf_op jit(solution)/shard_map/ppermute | solution.py:96
  48.1 2.9 %collective-permute-start.11 = (f32[416,128]{1,0:T(8,128)S(1)}, f32[416,128]{1,0:T(8,128)S(1)}, u32[]{:S(2)}, u32[]{:S(2)}) collective-permute-start(f32[416,128]{1,0:T(8,128)S(1)} %first_sum.1.refs_1_.refs_4_.refs_0_), channel_id=1, source_target_pairs={{0,200},{8,48},{16,40},{24,208},{32,232},{40,16},{48,8},{56,240},{... | collective-permute-start | bytes 638984 | tf_op jit(solution)/shard_map/ppermute | solution.py:100
  51.0 1.2 %collective-permute-done.12.refs_3_ = f32[128,128]{1,0:T(8,128)S(1)} collective-permute-done((f32[128,128]{1,0:T(8,128)S(1)}, f32[128,128]{1,0:T(8,128)S(1)}, u32[]{:S(2)}, u32[]{:S(2)}) %collective-permute-start.12) | collective-permute-done | bytes 65568 | tf_op jit(solution)/shard_map/ppermute | solution.py:91
  52.3 2.1 %eliminate0.1.refs_2_.refs_0_ = f32[128,128]{1,0:T(8,128)S(1)} custom-call(f32[128,128]{1,0:T(8,128)S(1)} %gram_four.3.refs_0_.refs_1_, f32[128,128]{1,0:T(8,128)S(1)} %gram_four.3.refs_0_.refs_1_), custom_call_target="tpu_custom_call" | custom-call | flops 4000000 | bytes 6000000 | tf_op jit(solution)/shard_map/eliminate0/pallas_call | solution.py:163
  55.3 2.6 %eliminate40.1.refs_2_.refs_1_ = f32[128,128]{1,0:T(8,128)S(1)} custom-call(f32[128,128]{1,0:T(8,128)S(1)} %eliminate0.1.refs_2_.refs_0_, f32[128,128]{1,0:T(8,128)S(1)} %gram_four.3.refs_0_.refs_1_, f32[416,128]{1,0:T(8,128)S(1)} %second_sum.1.refs_2_.refs_0_), custom_call_target="tpu_custom_call" | custom-call | flops 4000000 | bytes 13200000 | tf_op jit(solution)/shard_map/eliminate40/pallas_call | solution.py:163
  57.8 3.0 %collective-permute-done.13.refs_1_ = f32[416,128]{1,0:T(8,128)S(1)} collective-permute-done((f32[416,128]{1,0:T(8,128)S(1)}, f32[416,128]{1,0:T(8,128)S(1)}, u32[]{:S(2)}, u32[]{:S(2)}) %collective-permute-start.13) | collective-permute-done | bytes 213024 | tf_op jit(solution)/shard_map/ppermute | solution.py:100
  61.1 1.4 %collective-permute-start.14 = (bf16[416,128]{1,0:T(8,128)(2,1)S(1)}, bf16[416,128]{1,0:T(8,128)(2,1)S(1)}, u32[]{:S(2)}, u32[]{:S(2)}) collective-permute-start(bf16[416,128]{1,0:T(8,128)(2,1)S(1)} %block.1.refs_2_.refs_0_), channel_id=1, source_target_pairs={{0,56},{8,192},{16,216},{24,32},{32,24},{40,224},{48,248},{56,0},{... | collective-permute-start | bytes 319496 | tf_op jit(solution)/shard_map/ppermute | solution.py:100
  62.8 4.0 %collective-permute-done.14.refs_1_ = bf16[416,128]{1,0:T(8,128)(2,1)S(1)} collective-permute-done((bf16[416,128]{1,0:T(8,128)(2,1)S(1)}, bf16[416,128]{1,0:T(8,128)(2,1)S(1)}, u32[]{:S(2)}, u32[]{:S(2)}) %collective-permute-start.14) | collective-permute-done | bytes 106528 | tf_op jit(solution)/shard_map/ppermute | solution.py:100
  67.0 1.4 %collective-permute-start.17 = (f32[8,128]{1,0:T(8,128)S(1)}, f32[8,128]{1,0:T(8,128)S(1)}, u32[]{:S(2)}, u32[]{:S(2)}) collective-permute-start(f32[8,128]{1,0:T(8,128)S(1)} %squares.1.refs_2_), channel_id=1, source_target_pairs={{0,25},{1,24},{2,27},{3,26},{4,29},{5,28},{6,31},{7,30},{8,65},{9,... | collective-permute-start | bytes 12296 | tf_op jit(solution)/shard_map/ppermute | solution.py:79
  68.4 1.6 %collective-permute-start.16 = (f32[8,128]{1,0:T(8,128)S(1)}, f32[8,128]{1,0:T(8,128)S(1)}, u32[]{:S(2)}, u32[]{:S(2)}) collective-permute-start(f32[8,128]{1,0:T(8,128)S(1)} %squares.1.refs_2_), channel_id=1, source_target_pairs={{0,1},{1,0},{2,3},{3,2},{4,5},{5,4},{6,7},{7,6},{8,9},{9,8},{10,11... | collective-permute-start | bytes 12296 | tf_op jit(solution)/shard_map/ppermute | solution.py:79
  70.0 1.1 %collective-permute-done.17.refs_4_ = f32[8,128]{1,0:T(8,128)S(1)} collective-permute-done((f32[8,128]{1,0:T(8,128)S(1)}, f32[8,128]{1,0:T(8,128)S(1)}, u32[]{:S(2)}, u32[]{:S(2)}) %collective-permute-start.17) | collective-permute-done | bytes 4128 | tf_op jit(solution)/shard_map/ppermute | solution.py:79
  71.3 0.9 %collective-permute-done.15.refs_1_ = bf16[832,128]{1,0:T(8,128)(2,1)S(1)} collective-permute-done((bf16[832,128]{1,0:T(8,128)(2,1)S(1)}, bf16[832,128]{1,0:T(8,128)(2,1)S(1)}, u32[]{:S(2)}, u32[]{:S(2)}) %collective-permute-start.15) | collective-permute-done | bytes 213024 | tf_op jit(solution)/shard_map/ppermute | solution.py:100
  73.0 4.8 %collective-permute-start.20 = (f32[8,128]{1,0:T(8,128)S(1)}, f32[8,128]{1,0:T(8,128)S(1)}, u32[]{:S(2)}, u32[]{:S(2)}) collective-permute-start(f32[8,128]{1,0:T(8,128)S(1)} %get-tuple-element.24.refs_2_), channel_id=1, source_target_pairs={{13,0},{12,1},{15,2},{14,3},{9,4},{8,5},{11,6},{10,7},{5,8},{4,9},... | collective-permute-start | bytes 12296 | tf_op jit(solution)/shard_map/ppermute | solution.py:87
  77.9 0.9 %collective-permute-start.21 = (f32[8,128]{1,0:T(8,128)S(1)}, f32[8,128]{1,0:T(8,128)S(1)}, u32[]{:S(2)}, u32[]{:S(2)}) collective-permute-start(f32[8,128]{1,0:T(8,128)S(1)} %get-tuple-element.27.sq_ref), channel_id=1, source_target_pairs={{15,0},{10,1},{9,2},{12,3},{11,4},{14,5},{13,6},{8,7},{2,8},{7,9},... | collective-permute-start | bytes 12296 | tf_op jit(solution)/shard_map/ppermute | solution.py:87
  78.8 1.5 %finish_momentum.1 = (bf16[256,3328]{1,0:T(8,128)(2,1)}, f32[8,128]{1,0:T(8,128)S(1)}) custom-call(f32[3328,128]{1,0:T(8,128)S(1)} %get-tuple-element.25.coef_ref, bf16[256,128]{1,0:T(8,128)(2,1)S(1)} %ortho.1.refs_2_.ortho_ref, bf16[256,3328]{1,0:T(8,128)(2,1)S(1)} %get-tuple-element.18.refs_1_.b_ref), custom_call_target="tpu_custom_call" | custom-call | flops 218103808 | bytes 5000000 | tf_op jit(solution)/shard_map/finish_momentum/pallas_call | solution.py:391
  80.3 1.6 %collective-permute-done.21.refs_1_ = f32[8,128]{1,0:T(8,128)S(1)} collective-permute-done((f32[8,128]{1,0:T(8,128)S(1)}, f32[8,128]{1,0:T(8,128)S(1)}, u32[]{:S(2)}, u32[]{:S(2)}) %collective-permute-start.21) | collective-permute-done | bytes 4128 | tf_op jit(solution)/shard_map/ppermute | solution.py:87
  83.2 1.9 %finish_weights.1 = (bf16[256,3328]{1,0:T(8,128)(2,1)}, f32[3328,128]{1,0:T(8,128)}) custom-call(f32[8,128]{1,0:T(8,128)S(1)} %get-tuple-element.27.sq_ref, f32[16,128]{1,0:T(8,128)S(1)} %stack.1.moved_ref, f32[16,128]{1,0:T(8,128)S(1)} %collective-permute-done.22.other_ref, f32[3328,128]{1,0:T(8,128)S(1)} %get-tuple-element.25.coef_ref, ...), custom_call_target="tpu_custom_call" | custom-call | flops 218103808 | bytes 7000000 | tf_op jit(solution)/shard_map/finish_weights/pallas_call | solution.py:436
  (42 shorter events, 5.9 us)
Async XLA Ops:
  3.5 8.8 %collective-permute-start = (f32[256,128]{1,0:T(8,128)S(1)}, f32[256,128]{1,0:T(8,128)S(1)}, u32[]{:S(2)}, u32[]{:S(2)}) collective-permute-start(f32[256,128]{1,0:T(8,128)S(1)} %get-tuple-element.17), channel_id=1, source_target_pairs={{0,1},{1,0},{2,3},{3,2},{4,5},{5,4},{6,7},{7,6},{9,10},{10,9},{11,... | collective-permute-start | bytes 393224 | tf_op jit(solution)/shard_map/ppermute | solution.py:71
  12.4 3.9 %collective-permute-start.1 = (f32[256,128]{1,0:T(8,128)S(1)}, f32[256,128]{1,0:T(8,128)S(1)}, u32[]{:S(2)}, u32[]{:S(2)}) collective-permute-start(f32[256,128]{1,0:T(8,128)S(1)} %add.9), channel_id=1, source_target_pairs={{1,2},{2,1},{3,4},{4,3},{5,6},{6,5},{7,0},{0,7},{10,11},{11,10},{1... | collective-permute-start | bytes 393224 | tf_op jit(solution)/shard_map/ppermute | solution.py:71
  16.3 7.1 %collective-permute-start.2 = (f32[256,128]{1,0:T(8,128)S(1)}, f32[256,128]{1,0:T(8,128)S(1)}, u32[]{:S(2)}, u32[]{:S(2)}) collective-permute-start(f32[256,128]{1,0:T(8,128)S(1)} %add.10), channel_id=1, source_target_pairs={{2,5},{5,2},{1,6},{6,1},{4,7},{7,4},{3,0},{0,3},{11,14},{14,11},{1... | collective-permute-start | bytes 393224 | tf_op jit(solution)/shard_map/ppermute | solution.py:71
  24.0 6.2 %collective-permute-start.3 = (f32[1792,128]{1,0:T(8,128)S(1)}, f32[1792,128]{1,0:T(8,128)S(1)}, u32[]{:S(2)}, u32[]{:S(2)}) collective-permute-start(f32[1792,128]{1,0:T(8,128)S(1)} %lift_send.1.refs_2_.refs_0_), channel_id=1, source_target_pairs={{0,8},{8,0},{16,24},{24,16},{32,40},{40,32},{48,56},{56,48},{64,72... | collective-permute-start | bytes 2752520 | tf_op jit(solution)/shard_map/ppermute | solution.py:91
  30.2 10.7 %collective-permute-start.4 = (f32[832,128]{1,0:T(8,128)S(1)}, f32[832,128]{1,0:T(8,128)S(1)}, u32[]{:S(2)}, u32[]{:S(2)}) collective-permute-start(f32[832,128]{1,0:T(8,128)S(1)} %get-tuple-element.20.refs_2_), channel_id=1, source_target_pairs={{0,24},{8,64},{16,88},{24,0},{32,56},{40,96},{48,120},{56,32},{64,... | collective-permute-start | bytes 1277960 | tf_op jit(solution)/shard_map/ppermute | solution.py:100
  31.9 5.0 %collective-permute-start.6 = (f32[128,128]{1,0:T(8,128)S(1)}, f32[128,128]{1,0:T(8,128)S(1)}, u32[]{:S(2)}, u32[]{:S(2)}) collective-permute-start(f32[128,128]{1,0:T(8,128)S(1)} %gram_pair.1.refs_0_), channel_id=1, source_target_pairs={{56,0},{192,8},{40,16},{208,24},{24,32},{224,40},{8,48},{240,56},{... | collective-permute-start | bytes 196616 | tf_op jit(solution)/shard_map/ppermute | solution.py:96
  34.5 6.4 %collective-permute-start.5 = (f32[128,128]{1,0:T(8,128)S(1)}, f32[128,128]{1,0:T(8,128)S(1)}, u32[]{:S(2)}, u32[]{:S(2)}) collective-permute-start(f32[128,128]{1,0:T(8,128)S(1)} %gram_pair.1.refs_0_), channel_id=1, source_target_pairs={{0,240},{8,248},{16,224},{24,232},{32,208},{40,216},{48,192},{56,2... | collective-permute-start | bytes 196616 | tf_op jit(solution)/shard_map/ppermute | solution.py:91
  36.9 4.0 %collective-permute-start.7 = (f32[128,128]{1,0:T(8,128)S(1)}, f32[128,128]{1,0:T(8,128)S(1)}, u32[]{:S(2)}, u32[]{:S(2)}) collective-permute-start(f32[128,128]{1,0:T(8,128)S(1)} %collective-permute-done.6.refs_2_), channel_id=1, source_target_pairs={{0,8},{8,0},{16,24},{24,16},{32,40},{40,32},{48,56},{56,48},{64,72... | collective-permute-start | bytes 196616 | tf_op jit(solution)/shard_map/ppermute | solution.py:91
  41.0 7.0 %collective-permute-start.8 = (f32[416,128]{1,0:T(8,128)S(1)}, f32[416,128]{1,0:T(8,128)S(1)}, u32[]{:S(2)}, u32[]{:S(2)}) collective-permute-start(f32[416,128]{1,0:T(8,128)S(1)} %get-tuple-element.22.refs_1_), channel_id=1, source_target_pairs={{0,56},{8,192},{16,216},{24,32},{32,24},{40,224},{48,248},{56,0},{... | collective-permute-start | bytes 638984 | tf_op jit(solution)/shard_map/ppermute | solution.py:100
  42.7 4.4 %collective-permute-start.10 = (f32[128,128]{1,0:T(8,128)S(1)}, f32[128,128]{1,0:T(8,128)S(1)}, u32[]{:S(2)}, u32[]{:S(2)}) collective-permute-start(f32[128,128]{1,0:T(8,128)S(1)} %hold.1.refs_0_), channel_id=1, source_target_pairs={{0,80},{8,88},{16,64},{24,72},{32,112},{40,120},{48,96},{56,104},{... | collective-permute-start | bytes 196616 | tf_op jit(solution)/shard_map/ppermute | solution.py:91
  42.7 5.3 %collective-permute-start.9 = (f32[128,128]{1,0:T(8,128)S(1)}, f32[128,128]{1,0:T(8,128)S(1)}, u32[]{:S(2)}, u32[]{:S(2)}) collective-permute-start(f32[128,128]{1,0:T(8,128)S(1)} %hold.1.refs_0_), channel_id=1, source_target_pairs={{24,0},{64,8},{8,16},{80,24},{56,32},{96,40},{40,48},{112,56},{88,... | collective-permute-start | bytes 196616 | tf_op jit(solution)/shard_map/ppermute | solution.py:96
  48.1 6.9 %collective-permute-start.11 = (f32[416,128]{1,0:T(8,128)S(1)}, f32[416,128]{1,0:T(8,128)S(1)}, u32[]{:S(2)}, u32[]{:S(2)}) collective-permute-start(f32[416,128]{1,0:T(8,128)S(1)} %first_sum.1.refs_1_.refs_4_.refs_0_), channel_id=1, source_target_pairs={{0,200},{8,48},{16,40},{24,208},{32,232},{40,16},{48,8},{56,240},{... | collective-permute-start | bytes 638984 | tf_op jit(solution)/shard_map/ppermute | solution.py:100
  51.0 1.3 %collective-permute-start.12 = (f32[128,128]{1,0:T(8,128)S(1)}, f32[128,128]{1,0:T(8,128)S(1)}, u32[]{:S(2)}, u32[]{:S(2)}) collective-permute-start(f32[128,128]{1,0:T(8,128)S(1)} %hold_split.1.refs_2_), channel_id=1, source_target_pairs={{0,8},{8,0},{16,24},{24,16},{32,40},{40,32},{48,56},{56,48},{64,72... | collective-permute-start | bytes 196616 | tf_op jit(solution)/shard_map/ppermute | solution.py:91
  55.0 5.8 %collective-permute-start.13 = (f32[416,128]{1,0:T(8,128)S(1)}, f32[416,128]{1,0:T(8,128)S(1)}, u32[]{:S(2)}, u32[]{:S(2)}) collective-permute-start(f32[416,128]{1,0:T(8,128)S(1)} %second_sum.1.refs_2_.refs_0_), channel_id=1, source_target_pairs={{0,72},{8,16},{16,8},{24,80},{32,104},{40,48},{48,40},{56,112},{64... | collective-permute-start | bytes 638984 | tf_op jit(solution)/shard_map/ppermute | solution.py:100
  61.1 5.7 %collective-permute-start.14 = (bf16[416,128]{1,0:T(8,128)(2,1)S(1)}, bf16[416,128]{1,0:T(8,128)(2,1)S(1)}, u32[]{:S(2)}, u32[]{:S(2)}) collective-permute-start(bf16[416,128]{1,0:T(8,128)(2,1)S(1)} %block.1.refs_2_.refs_0_), channel_id=1, source_target_pairs={{0,56},{8,192},{16,216},{24,32},{32,24},{40,224},{48,248},{56,0},{... | collective-permute-start | bytes 319496 | tf_op jit(solution)/shard_map/ppermute | solution.py:100
  66.9 5.4 %collective-permute-start.15 = (bf16[832,128]{1,0:T(8,128)(2,1)S(1)}, bf16[832,128]{1,0:T(8,128)(2,1)S(1)}, u32[]{:S(2)}, u32[]{:S(2)}) collective-permute-start(bf16[832,128]{1,0:T(8,128)(2,1)S(1)} %join1.1.refs_0_), channel_id=1, source_target_pairs={{0,24},{8,64},{16,88},{24,0},{32,56},{40,96},{48,120},{56,32},{64,... | collective-permute-start | bytes 638984 | tf_op jit(solution)/shard_map/ppermute | solution.py:100
  67.0 4.1 %collective-permute-start.17 = (f32[8,128]{1,0:T(8,128)S(1)}, f32[8,128]{1,0:T(8,128)S(1)}, u32[]{:S(2)}, u32[]{:S(2)}) collective-permute-start(f32[8,128]{1,0:T(8,128)S(1)} %squares.1.refs_2_), channel_id=1, source_target_pairs={{0,25},{1,24},{2,27},{3,26},{4,29},{5,28},{6,31},{7,30},{8,65},{9,... | collective-permute-start | bytes 12296 | tf_op jit(solution)/shard_map/ppermute | solution.py:79
  68.4 2.9 %collective-permute-start.16 = (f32[8,128]{1,0:T(8,128)S(1)}, f32[8,128]{1,0:T(8,128)S(1)}, u32[]{:S(2)}, u32[]{:S(2)}) collective-permute-start(f32[8,128]{1,0:T(8,128)S(1)} %squares.1.refs_2_), channel_id=1, source_target_pairs={{0,1},{1,0},{2,3},{3,2},{4,5},{5,4},{6,7},{7,6},{8,9},{9,8},{10,11... | collective-permute-start | bytes 12296 | tf_op jit(solution)/shard_map/ppermute | solution.py:79
  72.4 5.4 %collective-permute-start.18 = (bf16[1664,128]{1,0:T(8,128)(2,1)S(1)}, bf16[1664,128]{1,0:T(8,128)(2,1)S(1)}, u32[]{:S(2)}, u32[]{:S(2)}) collective-permute-start(bf16[1664,128]{1,0:T(8,128)(2,1)S(1)} %get-tuple-element.23.refs_0_), channel_id=1, source_target_pairs={{0,8},{8,0},{16,24},{24,16},{32,40},{40,32},{48,56},{56,48},{64,72... | collective-permute-start | bytes 1277960 | tf_op jit(solution)/shard_map/ppermute | solution.py:91
  72.8 4.9 %collective-permute-start.19 = (f32[8,128]{1,0:T(8,128)S(1)}, f32[8,128]{1,0:T(8,128)S(1)}, u32[]{:S(2)}, u32[]{:S(2)}) collective-permute-start(f32[8,128]{1,0:T(8,128)S(1)} %get-tuple-element.24.refs_2_), channel_id=1, source_target_pairs={{0,8},{8,0},{16,24},{24,16},{32,40},{40,32},{48,56},{56,48},{64,72... | collective-permute-start | bytes 12296 | tf_op jit(solution)/shard_map/ppermute | solution.py:91
  73.0 7.3 %collective-permute-start.20 = (f32[8,128]{1,0:T(8,128)S(1)}, f32[8,128]{1,0:T(8,128)S(1)}, u32[]{:S(2)}, u32[]{:S(2)}) collective-permute-start(f32[8,128]{1,0:T(8,128)S(1)} %get-tuple-element.24.refs_2_), channel_id=1, source_target_pairs={{13,0},{12,1},{15,2},{14,3},{9,4},{8,5},{11,6},{10,7},{5,8},{4,9},... | collective-permute-start | bytes 12296 | tf_op jit(solution)/shard_map/ppermute | solution.py:87
  77.9 4.0 %collective-permute-start.21 = (f32[8,128]{1,0:T(8,128)S(1)}, f32[8,128]{1,0:T(8,128)S(1)}, u32[]{:S(2)}, u32[]{:S(2)}) collective-permute-start(f32[8,128]{1,0:T(8,128)S(1)} %get-tuple-element.27.sq_ref), channel_id=1, source_target_pairs={{15,0},{10,1},{9,2},{12,3},{11,4},{14,5},{13,6},{8,7},{2,8},{7,9},... | collective-permute-start | bytes 12296 | tf_op jit(solution)/shard_map/ppermute | solution.py:87
  78.8 4.4 %copy-start = (bf16[256,3328]{1,0:T(8,128)(2,1)S(1)}, bf16[256,3328]{1,0:T(8,128)(2,1)}, u32[]{:S(2)}) copy-start(bf16[256,3328]{1,0:T(8,128)(2,1)} %weights_ref.1) | copy-start | bytes 5111812
  81.9 1.2 %collective-permute-start.22 = (f32[16,128]{1,0:T(8,128)S(1)}, f32[16,128]{1,0:T(8,128)S(1)}, u32[]{:S(2)}, u32[]{:S(2)}) collective-permute-start(f32[16,128]{1,0:T(8,128)S(1)} %stack.1.moved_ref), channel_id=1, source_target_pairs={{0,8},{8,0},{16,24},{24,16},{32,40},{40,32},{48,56},{56,48},{64,72... | collective-permute-start | bytes 24584 | tf_op jit(solution)/shard_map/ppermute | solution.py:91

commit v6 on v5

--- a/solution.py
+++ b/solution.py
@@ -22,6 +22,7 @@
 TP = 8
 FSDP = 32
 HALF = LOCAL_COLS // 2
+PART = LOCAL_ROWS // 2
 CHUNK = HALF // 4
 PIECE = HALF // 8
 CUT = 40
@@ -106,7 +107,7 @@
     return place // 2 if k else place % 2 ^ place // 2
 
 
-def project_kernel(m_hbm, g_hbm, s_hbm, b_ref, part_ref, m_buf, g_buf, s_buf, sems):
+def project_kernel(m_hbm, g_hbm, s_hbm, b_ref, top_ref, low_ref, m_buf, g_buf, s_buf, sems):
     copies = []
     for i, (start, size) in enumerate(STRIPS):
         cols = pl.ds(start, size)
@@ -126,10 +127,11 @@
         b = (m_buf[:, cols].astype(jnp.float32) + g_buf[:, cols].astype(jnp.float32)).astype(jnp.bfloat16)
         b_ref[:, cols] = b
         part = jnp.dot(b, s_buf[cols, :].astype(jnp.bfloat16), preferred_element_type=jnp.float32)
-        if i == 0:
-            part_ref[...] = part
-        else:
-            part_ref[...] += part
+        for ref, rows in ((top_ref, part[:PART, :]), (low_ref, part[PART:, :])):
+            if i == 0:
+                ref[...] = rows
+            else:
+                ref[...] += rows
 
 
 def project(momentum, gradient, subspace):
@@ -139,8 +141,8 @@
     return pl.pallas_call(
         project_kernel,
         in_specs=[HBM_SPEC] * 3,
-        out_specs=[VMEM_SPEC] * 2,
-        out_shape=[bf16(LOCAL_ROWS, LOCAL_COLS), f32(LOCAL_ROWS, RANK)],
+        out_specs=[VMEM_SPEC] * 3,
+        out_shape=[bf16(LOCAL_ROWS, LOCAL_COLS), f32(PART, RANK), f32(PART, RANK)],
         scratch_shapes=[
             VMEM((LOCAL_ROWS, LOCAL_COLS), jnp.bfloat16),
             VMEM((LOCAL_ROWS, LOCAL_COLS), jnp.bfloat16),
@@ -182,17 +184,18 @@
         target[k * 128:(k + 1) * 128, :] = d[:, :RANK] + d[:, RANK:]
 
 
-def lift_send_kernel(p_ref, b_ref, send_ref):
+def lift_send_kernel(top_ref, low_ref, b_ref, send_ref):
     c = team(lax.axis_index("fsdp"))
-    p = p_ref[...]
+    p = jnp.concatenate([top_ref[...], low_ref[...]], axis=0)
     lift_half(p, b_ref, 1 - c, send_ref)
     send_ref[HALF:, :] = lax.dot_general(
         p, p, TN, precision=lax.Precision.HIGHEST, preferred_element_type=jnp.float32
     )
 
 
-def lift_keep_kernel(p_ref, b_ref, keep_ref):
-    lift_half(p_ref[...], b_ref, team(lax.axis_index("fsdp")), keep_ref)
+def lift_keep_kernel(top_ref, low_ref, b_ref, keep_ref):
+    p = jnp.concatenate([top_ref[...], low_ref[...]], axis=0)
+    lift_half(p, b_ref, team(lax.axis_index("fsdp")), keep_ref)
 
 
 def split_kernel(k, n, keep_ref, recv_ref, send_ref, next_ref):
@@ -327,9 +330,10 @@
     out_ref[...] = (out[:, :RANK] + out[:, RANK:]).astype(jnp.bfloat16)
 
 
-def ortho_kernel(p_ref, w_ref, out_ref):
+def ortho_kernel(top_ref, low_ref, w_ref, out_ref):
+    p = jnp.concatenate([top_ref[...], low_ref[...]], axis=0)
     out_ref[...] = lax.dot_general(
-        p_ref[...], w_ref[...], NT, precision=lax.Precision.HIGHEST, preferred_element_type=jnp.float32
+        p, w_ref[...], NT, precision=lax.Precision.HIGHEST, preferred_element_type=jnp.float32
     ).astype(jnp.bfloat16)
 
 
@@ -450,17 +454,17 @@
 
 
 def on_device(momentum, gradient, weights, subspace):
-    blended, projected = project(momentum, gradient, subspace)
+    blended, *projected = project(momentum, gradient, subspace)
     for step in range(3):
-        projected = projected + swap_z(projected, step)
+        projected = [rows + swap_z(rows, step) for rows in projected]
 
     send = local(
-        lift_send_kernel, f32(HALF + RANK, RANK), [projected, blended],
+        lift_send_kernel, f32(HALF + RANK, RANK), [*projected, blended],
         flops=2 * 256 * 3328 * 128, nbytes=2000000, name="lift_send",
     )
     recv = xor_fsdp(send, CORE)
     keep = local(
-        lift_keep_kernel, f32(HALF, RANK), [projected, blended], [send],
+        lift_keep_kernel, f32(HALF, RANK), [*projected, blended], [send],
         flops=2 * 256 * 3328 * 128, nbytes=2000000, name="lift_keep",
     )
     n = HALF // 2
@@ -488,7 +492,7 @@
         flops=2 * CHUNK * 256 * 256, nbytes=700000, name="block",
     )
     ortho = local(
-        ortho_kernel, bf16(LOCAL_ROWS, RANK), [projected, inverse], [coef],
+        ortho_kernel, bf16(LOCAL_ROWS, RANK), [*projected, inverse], [coef],
         flops=6 * 256 * 256 * 128, nbytes=300000, name="ortho",
     )
     coef = local(

time: 85.3 us -> 84.6 us (level)
  waiting for transfers between devices: 34 us -> 31.2 us
  starting transfers between devices: 37 us -> 39.1 us
    ppermute x3 -> x6, starting transfers between devices: 9.5 us -> 11.5 us  [swap_z(): return lax.ppermute(x, ('fsdp', 'tp'), perm)]
    ppermute x2, waiting for transfers between devices: 1.62 us -> 0.01 us  [turn_z(): return lax.ppermute(x, ('fsdp', 'tp'), perm)]
    ppermute x8, starting transfers between devices: 6.94 us -> 8.35 us  [xor_fsdp(): return lax.ppermute(x, 'fsdp', [(i, i ^ mask) for i in range(FSDP)])]
    ppermute x3 -> x6, waiting for transfers between devices: 10.3 us -> 9 us  [swap_z(): return lax.ppermute(x, ('fsdp', 'tp'), perm)]
    ppermute x2, starting transfers between devices: 5.68 us -> 4.51 us  [turn_z(): return lax.ppermute(x, ('fsdp', 'tp'), perm)]
  transfers between devices with their start and end apart: 23 -> 26, of which waited for: 17 -> 18; matrix products, arithmetic and copies ran while one was open for 0% -> 0% of each run, Pallas kernels for 8% -> 9%
where the time goes in v6:
time: 84.6 us; the launch traced here: 84.5 us
  starting transfers between devices  39.1 us (46%)
  waiting for transfers between devices  31.2 us (37%)
  Pallas kernels  13.2 us (16%)
  between operations  1 us (1%)
    ppermute x6, starting transfers between devices, swap_z(): return lax.ppermute(x, ('fsdp', 'tp'), perm)  11.5 us
    ppermute x8, waiting for transfers between devices, xor_fsdp(): return lax.ppermute(x, 'fsdp', [(i, i ^ mask) for i in range(FSDP)])  11 us
    ppermute x6, waiting for transfers between devices, swap_z(): return lax.ppermute(x, ('fsdp', 'tp'), perm)  9 us
    ppermute x8, starting transfers between devices, xor_fsdp(): return lax.ppermute(x, 'fsdp', [(i, i ^ mask) for i in range(FSDP)])  8.35 us
    ppermute x6, waiting for transfers between devices, xor_step(): lax.ppermute(x, 'fsdp', [(i, i ^ MASKS[team(i)][k]) for i in range(FSDP)])  8.34 us
    ppermute x6, starting transfers between devices, xor_step(): lax.ppermute(x, 'fsdp', [(i, i ^ MASKS[team(i)][k]) for i in range(FSDP)])  7.91 us
    pallas_call x20, Pallas kernels, local(): pl.pallas_call(body, in_specs=[VMEM_SPEC] * (used + len(after)), out_spec...  6.97 us
    ppermute x2, starting transfers between devices, turn_z(): return lax.ppermute(x, ('fsdp', 'tp'), perm)  4.51 us
  transfers between devices with their start and end apart: 26, of which 18 were waited for; matrix products, arithmetic and copies ran while one was open for 0% of the time, Pallas kernels for 9%

profile of v6, /device:TPU:1, one launch (start us, length us, event | category | flops | bytes accessed | tf_op | source)
XLA Modules:
  0.0 84.5 jit_solution(15429746524721568276)
XLA Ops:
  0.6 2.9 %project.1 = (bf16[256,3328]{1,0:T(8,128)(2,1)S(1)}, f32[128,128]{1,0:T(8,128)S(1)}, f32[128,128]{1,0:T(8,128)S(1)}) custom-call(bf16[256,3328]{1,0:T(8,128)(2,1)} %m_hbm.1, bf16[256,3328]{1,0:T(8,128)(2,1)} %g_hbm.1, f32[3328,128]{1,0:T(8,128)} %s_hbm.1), custom_call_target="tpu_custom_call" | custom-call | flops 218103808 | bytes 7000000 | tf_op jit(solution)/shard_map/project/pallas_call | solution.py:141
  3.5 6.5 %collective-permute-start = (f32[128,128]{1,0:T(8,128)S(1)}, f32[128,128]{1,0:T(8,128)S(1)}, u32[]{:S(2)}, u32[]{:S(2)}) collective-permute-start(f32[128,128]{1,0:T(8,128)S(1)} %get-tuple-element.18), channel_id=1, source_target_pairs={{0,1},{1,0},{2,3},{3,2},{4,5},{5,4},{6,7},{7,6},{9,10},{10,9},{11,... | collective-permute-start | bytes 196616 | tf_op jit(solution)/shard_map/ppermute | solution.py:72
  10.1 1.6 %collective-permute-done = f32[128,128]{1,0:T(8,128)S(1)} collective-permute-done((f32[128,128]{1,0:T(8,128)S(1)}, f32[128,128]{1,0:T(8,128)S(1)}, u32[]{:S(2)}, u32[]{:S(2)}) %collective-permute-start) | collective-permute-done | bytes 65568 | tf_op jit(solution)/shard_map/ppermute | solution.py:72
  11.8 2.6 %collective-permute-done.3 = f32[128,128]{1,0:T(8,128)S(1)} collective-permute-done((f32[128,128]{1,0:T(8,128)S(1)}, f32[128,128]{1,0:T(8,128)S(1)}, u32[]{:S(2)}, u32[]{:S(2)}) %collective-permute-start.3) | collective-permute-done | bytes 65568 | tf_op jit(solution)/shard_map/ppermute | solution.py:72
  14.9 2.9 %collective-permute-start.2 = (f32[128,128]{1,0:T(8,128)S(1)}, f32[128,128]{1,0:T(8,128)S(1)}, u32[]{:S(2)}, u32[]{:S(2)}) collective-permute-start(f32[128,128]{1,0:T(8,128)S(1)} %add.19), channel_id=1, source_target_pairs={{2,5},{5,2},{1,6},{6,1},{4,7},{7,4},{3,0},{0,3},{11,14},{14,11},{1... | collective-permute-start | bytes 196616 | tf_op jit(solution)/shard_map/ppermute | solution.py:72
  17.8 1.8 %collective-permute-start.5 = (f32[128,128]{1,0:T(8,128)S(1)}, f32[128,128]{1,0:T(8,128)S(1)}, u32[]{:S(2)}, u32[]{:S(2)}) collective-permute-start(f32[128,128]{1,0:T(8,128)S(1)} %add.22), channel_id=1, source_target_pairs={{2,5},{5,2},{1,6},{6,1},{4,7},{7,4},{3,0},{0,3},{11,14},{14,11},{1... | collective-permute-start | bytes 196616 | tf_op jit(solution)/shard_map/ppermute | solution.py:72
  19.7 1.6 %collective-permute-done.2 = f32[128,128]{1,0:T(8,128)S(1)} collective-permute-done((f32[128,128]{1,0:T(8,128)S(1)}, f32[128,128]{1,0:T(8,128)S(1)}, u32[]{:S(2)}, u32[]{:S(2)}) %collective-permute-start.2) | collective-permute-done | bytes 65568 | tf_op jit(solution)/shard_map/ppermute | solution.py:72
  21.2 2.9 %collective-permute-done.5 = f32[128,128]{1,0:T(8,128)S(1)} collective-permute-done((f32[128,128]{1,0:T(8,128)S(1)}, f32[128,128]{1,0:T(8,128)S(1)}, u32[]{:S(2)}, u32[]{:S(2)}) %collective-permute-start.5) | collective-permute-done | bytes 65568 | tf_op jit(solution)/shard_map/ppermute | solution.py:72
  24.7 5.6 %collective-permute-start.6 = (f32[1792,128]{1,0:T(8,128)S(1)}, f32[1792,128]{1,0:T(8,128)S(1)}, u32[]{:S(2)}, u32[]{:S(2)}) collective-permute-start(f32[1792,128]{1,0:T(8,128)S(1)} %lift_send.1.refs_3_.refs_0_), channel_id=1, source_target_pairs={{0,8},{8,0},{16,24},{24,16},{32,40},{40,32},{48,56},{56,48},{64,72... | collective-permute-start | bytes 2752520 | tf_op jit(solution)/shard_map/ppermute | solution.py:92
  30.8 1.6 %collective-permute-done.6.refs_1_ = f32[1792,128]{1,0:T(8,128)S(1)} collective-permute-done((f32[1792,128]{1,0:T(8,128)S(1)}, f32[1792,128]{1,0:T(8,128)S(1)}, u32[]{:S(2)}, u32[]{:S(2)}) %collective-permute-start.6) | collective-permute-done | bytes 917536 | tf_op jit(solution)/shard_map/ppermute | solution.py:92
  32.5 1.6 %collective-permute-start.7 = (f32[832,128]{1,0:T(8,128)S(1)}, f32[832,128]{1,0:T(8,128)S(1)}, u32[]{:S(2)}, u32[]{:S(2)}) collective-permute-start(f32[832,128]{1,0:T(8,128)S(1)} %get-tuple-element.22.refs_2_), channel_id=1, source_target_pairs={{0,24},{8,64},{16,88},{24,0},{32,56},{40,96},{48,120},{56,32},{64,... | collective-permute-start | bytes 1277960 | tf_op jit(solution)/shard_map/ppermute | solution.py:101
  34.1 2.6 %collective-permute-start.9 = (f32[128,128]{1,0:T(8,128)S(1)}, f32[128,128]{1,0:T(8,128)S(1)}, u32[]{:S(2)}, u32[]{:S(2)}) collective-permute-start(f32[128,128]{1,0:T(8,128)S(1)} %gram_pair.1.refs_0_), channel_id=1, source_target_pairs={{56,0},{192,8},{40,16},{208,24},{24,32},{224,40},{8,48},{240,56},{... | collective-permute-start | bytes 196616 | tf_op jit(solution)/shard_map/ppermute | solution.py:97
  36.7 1.8 %collective-permute-start.8 = (f32[128,128]{1,0:T(8,128)S(1)}, f32[128,128]{1,0:T(8,128)S(1)}, u32[]{:S(2)}, u32[]{:S(2)}) collective-permute-start(f32[128,128]{1,0:T(8,128)S(1)} %gram_pair.1.refs_0_), channel_id=1, source_target_pairs={{0,240},{8,248},{16,224},{24,232},{32,208},{40,216},{48,192},{56,2... | collective-permute-start | bytes 196616 | tf_op jit(solution)/shard_map/ppermute | solution.py:92
  39.2 4.0 %collective-permute-done.8.refs_1_ = f32[128,128]{1,0:T(8,128)S(1)} collective-permute-done((f32[128,128]{1,0:T(8,128)S(1)}, f32[128,128]{1,0:T(8,128)S(1)}, u32[]{:S(2)}, u32[]{:S(2)}) %collective-permute-start.8) | collective-permute-done | bytes 65568 | tf_op jit(solution)/shard_map/ppermute | solution.py:92
  43.3 1.7 %collective-permute-start.11 = (f32[416,128]{1,0:T(8,128)S(1)}, f32[416,128]{1,0:T(8,128)S(1)}, u32[]{:S(2)}, u32[]{:S(2)}) collective-permute-start(f32[416,128]{1,0:T(8,128)S(1)} %get-tuple-element.24.refs_1_), channel_id=1, source_target_pairs={{0,56},{8,192},{16,216},{24,32},{32,24},{40,224},{48,248},{56,0},{... | collective-permute-start | bytes 638984 | tf_op jit(solution)/shard_map/ppermute | solution.py:101
  45.0 1.2 %collective-permute-start.12 = (f32[128,128]{1,0:T(8,128)S(1)}, f32[128,128]{1,0:T(8,128)S(1)}, u32[]{:S(2)}, u32[]{:S(2)}) collective-permute-start(f32[128,128]{1,0:T(8,128)S(1)} %hold.1.refs_0_), channel_id=1, source_target_pairs={{24,0},{64,8},{8,16},{80,24},{56,32},{96,40},{40,48},{112,56},{88,... | collective-permute-start | bytes 196616 | tf_op jit(solution)/shard_map/ppermute | solution.py:97
  46.2 3.2 %collective-permute-done.13.refs_3_.refs_1_ = f32[128,128]{1,0:T(8,128)S(1)} collective-permute-done((f32[128,128]{1,0:T(8,128)S(1)}, f32[128,128]{1,0:T(8,128)S(1)}, u32[]{:S(2)}, u32[]{:S(2)}) %collective-permute-start.13) | collective-permute-done | bytes 65568 | tf_op jit(solution)/shard_map/ppermute | solution.py:92
  49.4 0.9 %collective-permute-done.12.refs_2_.refs_0_ = f32[128,128]{1,0:T(8,128)S(1)} collective-permute-done((f32[128,128]{1,0:T(8,128)S(1)}, f32[128,128]{1,0:T(8,128)S(1)}, u32[]{:S(2)}, u32[]{:S(2)}) %collective-permute-start.12) | collective-permute-done | bytes 65568 | tf_op jit(solution)/shard_map/ppermute | solution.py:97
  50.3 2.9 %collective-permute-start.14 = (f32[416,128]{1,0:T(8,128)S(1)}, f32[416,128]{1,0:T(8,128)S(1)}, u32[]{:S(2)}, u32[]{:S(2)}) collective-permute-start(f32[416,128]{1,0:T(8,128)S(1)} %first_sum.1.refs_1_.refs_4_.refs_0_), channel_id=1, source_target_pairs={{0,200},{8,48},{16,40},{24,208},{32,232},{40,16},{48,8},{56,240},{... | collective-permute-start | bytes 638984 | tf_op jit(solution)/shard_map/ppermute | solution.py:101
  53.3 1.2 %collective-permute-done.15.refs_3_ = f32[128,128]{1,0:T(8,128)S(1)} collective-permute-done((f32[128,128]{1,0:T(8,128)S(1)}, f32[128,128]{1,0:T(8,128)S(1)}, u32[]{:S(2)}, u32[]{:S(2)}) %collective-permute-start.15) | collective-permute-done | bytes 65568 | tf_op jit(solution)/shard_map/ppermute | solution.py:92
  54.6 2.1 %eliminate0.1.refs_2_.refs_0_ = f32[128,128]{1,0:T(8,128)S(1)} custom-call(f32[128,128]{1,0:T(8,128)S(1)} %gram_four.3.refs_0_.refs_1_, f32[128,128]{1,0:T(8,128)S(1)} %gram_four.3.refs_0_.refs_1_), custom_call_target="tpu_custom_call" | custom-call | flops 4000000 | bytes 6000000 | tf_op jit(solution)/shard_map/eliminate0/pallas_call | solution.py:165
  57.3 2.6 %eliminate40.1.refs_2_ = f32[128,128]{1,0:T(8,128)S(1)} custom-call(f32[128,128]{1,0:T(8,128)S(1)} %eliminate0.1.refs_2_.refs_0_, f32[128,128]{1,0:T(8,128)S(1)} %gram_four.3.refs_0_.refs_1_, f32[416,128]{1,0:T(8,128)S(1)} %second_sum.1.refs_2_.refs_0_), custom_call_target="tpu_custom_call" | custom-call | flops 4000000 | bytes 13200000 | tf_op jit(solution)/shard_map/eliminate40/pallas_call | solution.py:165
  59.9 3.0 %collective-permute-done.16.refs_1_ = f32[416,128]{1,0:T(8,128)S(1)} collective-permute-done((f32[416,128]{1,0:T(8,128)S(1)}, f32[416,128]{1,0:T(8,128)S(1)}, u32[]{:S(2)}, u32[]{:S(2)}) %collective-permute-start.16) | collective-permute-done | bytes 213024 | tf_op jit(solution)/shard_map/ppermute | solution.py:101
  63.2 1.4 %collective-permute-start.17 = (bf16[416,128]{1,0:T(8,128)(2,1)S(1)}, bf16[416,128]{1,0:T(8,128)(2,1)S(1)}, u32[]{:S(2)}, u32[]{:S(2)}) collective-permute-start(bf16[416,128]{1,0:T(8,128)(2,1)S(1)} %block.1.refs_3_.refs_0_), channel_id=1, source_target_pairs={{0,56},{8,192},{16,216},{24,32},{32,24},{40,224},{48,248},{56,0},{... | collective-permute-start | bytes 319496 | tf_op jit(solution)/shard_map/ppermute | solution.py:101
  64.9 4.0 %collective-permute-done.17.refs_1_ = bf16[416,128]{1,0:T(8,128)(2,1)S(1)} collective-permute-done((bf16[416,128]{1,0:T(8,128)(2,1)S(1)}, bf16[416,128]{1,0:T(8,128)(2,1)S(1)}, u32[]{:S(2)}, u32[]{:S(2)}) %collective-permute-start.17) | collective-permute-done | bytes 106528 | tf_op jit(solution)/shard_map/ppermute | solution.py:101
  69.8 2.3 %collective-permute-start.19 = (f32[8,128]{1,0:T(8,128)S(1)}, f32[8,128]{1,0:T(8,128)S(1)}, u32[]{:S(2)}, u32[]{:S(2)}) collective-permute-start(f32[8,128]{1,0:T(8,128)S(1)} %squares.1.refs_2_), channel_id=1, source_target_pairs={{0,1},{1,0},{2,3},{3,2},{4,5},{5,4},{6,7},{7,6},{8,9},{9,8},{10,11... | collective-permute-start | bytes 12296 | tf_op jit(solution)/shard_map/ppermute | solution.py:80
  72.1 1.1 %collective-permute-done.20.refs_4_ = f32[8,128]{1,0:T(8,128)S(1)} collective-permute-done((f32[8,128]{1,0:T(8,128)S(1)}, f32[8,128]{1,0:T(8,128)S(1)}, u32[]{:S(2)}, u32[]{:S(2)}) %collective-permute-start.20) | collective-permute-done | bytes 4128 | tf_op jit(solution)/shard_map/ppermute | solution.py:80
  75.0 1.7 %collective-permute-start.23 = (f32[8,128]{1,0:T(8,128)S(1)}, f32[8,128]{1,0:T(8,128)S(1)}, u32[]{:S(2)}, u32[]{:S(2)}) collective-permute-start(f32[8,128]{1,0:T(8,128)S(1)} %get-tuple-element.26.refs_2_), channel_id=1, source_target_pairs={{13,0},{12,1},{15,2},{14,3},{9,4},{8,5},{11,6},{10,7},{5,8},{4,9},... | collective-permute-start | bytes 12296 | tf_op jit(solution)/shard_map/ppermute | solution.py:88
  76.9 2.8 %collective-permute-start.24 = (f32[8,128]{1,0:T(8,128)S(1)}, f32[8,128]{1,0:T(8,128)S(1)}, u32[]{:S(2)}, u32[]{:S(2)}) collective-permute-start(f32[8,128]{1,0:T(8,128)S(1)} %get-tuple-element.29.sq_ref), channel_id=1, source_target_pairs={{15,0},{10,1},{9,2},{12,3},{11,4},{14,5},{13,6},{8,7},{2,8},{7,9},... | collective-permute-start | bytes 12296 | tf_op jit(solution)/shard_map/ppermute | solution.py:88
  79.7 1.5 %finish_momentum.1 = (bf16[256,3328]{1,0:T(8,128)(2,1)}, f32[8,128]{1,0:T(8,128)S(1)}) custom-call(f32[3328,128]{1,0:T(8,128)S(1)} %get-tuple-element.27.coef_ref, bf16[256,128]{1,0:T(8,128)(2,1)S(1)} %ortho.1.refs_2_.ortho_ref, bf16[256,3328]{1,0:T(8,128)(2,1)S(1)} %get-tuple-element.20.refs_2_.b_ref), custom_call_target="tpu_custom_call" | custom-call | flops 218103808 | bytes 5000000 | tf_op jit(solution)/shard_map/finish_momentum/pallas_call | solution.py:395
  81.5 0.9 %collective-permute-done.25.other_ref = f32[16,128]{1,0:T(8,128)S(1)} collective-permute-done((f32[16,128]{1,0:T(8,128)S(1)}, f32[16,128]{1,0:T(8,128)S(1)}, u32[]{:S(2)}, u32[]{:S(2)}) %collective-permute-start.25) | collective-permute-done | bytes 8224 | tf_op jit(solution)/shard_map/ppermute | solution.py:92
  82.5 1.9 %finish_weights.1 = (bf16[256,3328]{1,0:T(8,128)(2,1)}, f32[3328,128]{1,0:T(8,128)}) custom-call(f32[8,128]{1,0:T(8,128)S(1)} %get-tuple-element.29.sq_ref, f32[16,128]{1,0:T(8,128)S(1)} %stack.1.moved_ref, f32[16,128]{1,0:T(8,128)S(1)} %collective-permute-done.25.other_ref, f32[3328,128]{1,0:T(8,128)S(1)} %get-tuple-element.27.coef_ref, ...), custom_call_target="tpu_custom_call" | custom-call | flops 218103808 | bytes 7000000 | tf_op jit(solution)/shard_map/finish_weights/pallas_call | solution.py:440
  (51 shorter events, 7.1 us)
Async XLA Ops:
  3.5 8.1 %collective-permute-start = (f32[128,128]{1,0:T(8,128)S(1)}, f32[128,128]{1,0:T(8,128)S(1)}, u32[]{:S(2)}, u32[]{:S(2)}) collective-permute-start(f32[128,128]{1,0:T(8,128)S(1)} %get-tuple-element.18), channel_id=1, source_target_pairs={{0,1},{1,0},{2,3},{3,2},{4,5},{5,4},{6,7},{7,6},{9,10},{10,9},{11,... | collective-permute-start | bytes 196616 | tf_op jit(solution)/shard_map/ppermute | solution.py:72
  10.0 4.3 %collective-permute-start.3 = (f32[128,128]{1,0:T(8,128)S(1)}, f32[128,128]{1,0:T(8,128)S(1)}, u32[]{:S(2)}, u32[]{:S(2)}) collective-permute-start(f32[128,128]{1,0:T(8,128)S(1)} %get-tuple-element.19), channel_id=1, source_target_pairs={{0,1},{1,0},{2,3},{3,2},{4,5},{5,4},{6,7},{7,6},{9,10},{10,9},{11,... | collective-permute-start | bytes 196616 | tf_op jit(solution)/shard_map/ppermute | solution.py:72
  11.7 3.2 %collective-permute-start.1 = (f32[128,128]{1,0:T(8,128)S(1)}, f32[128,128]{1,0:T(8,128)S(1)}, u32[]{:S(2)}, u32[]{:S(2)}) collective-permute-start(f32[128,128]{1,0:T(8,128)S(1)} %add.18), channel_id=1, source_target_pairs={{1,2},{2,1},{3,4},{4,3},{5,6},{6,5},{7,0},{0,7},{10,11},{11,10},{1... | collective-permute-start | bytes 196616 | tf_op jit(solution)/shard_map/ppermute | solution.py:72
  14.4 3.5 %collective-permute-start.4 = (f32[128,128]{1,0:T(8,128)S(1)}, f32[128,128]{1,0:T(8,128)S(1)}, u32[]{:S(2)}, u32[]{:S(2)}) collective-permute-start(f32[128,128]{1,0:T(8,128)S(1)} %add.21), channel_id=1, source_target_pairs={{1,2},{2,1},{3,4},{4,3},{5,6},{6,5},{7,0},{0,7},{10,11},{11,10},{1... | collective-permute-start | bytes 196616 | tf_op jit(solution)/shard_map/ppermute | solution.py:72
  14.9 6.3 %collective-permute-start.2 = (f32[128,128]{1,0:T(8,128)S(1)}, f32[128,128]{1,0:T(8,128)S(1)}, u32[]{:S(2)}, u32[]{:S(2)}) collective-permute-start(f32[128,128]{1,0:T(8,128)S(1)} %add.19), channel_id=1, source_target_pairs={{2,5},{5,2},{1,6},{6,1},{4,7},{7,4},{3,0},{0,3},{11,14},{14,11},{1... | collective-permute-start | bytes 196616 | tf_op jit(solution)/shard_map/ppermute | solution.py:72
  17.8 6.3 %collective-permute-start.5 = (f32[128,128]{1,0:T(8,128)S(1)}, f32[128,128]{1,0:T(8,128)S(1)}, u32[]{:S(2)}, u32[]{:S(2)}) collective-permute-start(f32[128,128]{1,0:T(8,128)S(1)} %add.22), channel_id=1, source_target_pairs={{2,5},{5,2},{1,6},{6,1},{4,7},{7,4},{3,0},{0,3},{11,14},{14,11},{1... | collective-permute-start | bytes 196616 | tf_op jit(solution)/shard_map/ppermute | solution.py:72
  24.7 7.7 %collective-permute-start.6 = (f32[1792,128]{1,0:T(8,128)S(1)}, f32[1792,128]{1,0:T(8,128)S(1)}, u32[]{:S(2)}, u32[]{:S(2)}) collective-permute-start(f32[1792,128]{1,0:T(8,128)S(1)} %lift_send.1.refs_3_.refs_0_), channel_id=1, source_target_pairs={{0,8},{8,0},{16,24},{24,16},{32,40},{40,32},{48,56},{56,48},{64,72... | collective-permute-start | bytes 2752520 | tf_op jit(solution)/shard_map/ppermute | solution.py:92
  32.5 10.7 %collective-permute-start.7 = (f32[832,128]{1,0:T(8,128)S(1)}, f32[832,128]{1,0:T(8,128)S(1)}, u32[]{:S(2)}, u32[]{:S(2)}) collective-permute-start(f32[832,128]{1,0:T(8,128)S(1)} %get-tuple-element.22.refs_2_), channel_id=1, source_target_pairs={{0,24},{8,64},{16,88},{24,0},{32,56},{40,96},{48,120},{56,32},{64,... | collective-permute-start | bytes 1277960 | tf_op jit(solution)/shard_map/ppermute | solution.py:101
  34.1 5.0 %collective-permute-start.9 = (f32[128,128]{1,0:T(8,128)S(1)}, f32[128,128]{1,0:T(8,128)S(1)}, u32[]{:S(2)}, u32[]{:S(2)}) collective-permute-start(f32[128,128]{1,0:T(8,128)S(1)} %gram_pair.1.refs_0_), channel_id=1, source_target_pairs={{56,0},{192,8},{40,16},{208,24},{24,32},{224,40},{8,48},{240,56},{... | collective-permute-start | bytes 196616 | tf_op jit(solution)/shard_map/ppermute | solution.py:97
  36.7 6.4 %collective-permute-start.8 = (f32[128,128]{1,0:T(8,128)S(1)}, f32[128,128]{1,0:T(8,128)S(1)}, u32[]{:S(2)}, u32[]{:S(2)}) collective-permute-start(f32[128,128]{1,0:T(8,128)S(1)} %gram_pair.1.refs_0_), channel_id=1, source_target_pairs={{0,240},{8,248},{16,224},{24,232},{32,208},{40,216},{48,192},{56,2... | collective-permute-start | bytes 196616 | tf_op jit(solution)/shard_map/ppermute | solution.py:92
  39.1 4.0 %collective-permute-start.10 = (f32[128,128]{1,0:T(8,128)S(1)}, f32[128,128]{1,0:T(8,128)S(1)}, u32[]{:S(2)}, u32[]{:S(2)}) collective-permute-start(f32[128,128]{1,0:T(8,128)S(1)} %collective-permute-done.9.refs_2_), channel_id=1, source_target_pairs={{0,8},{8,0},{16,24},{24,16},{32,40},{40,32},{48,56},{56,48},{64,72... | collective-permute-start | bytes 196616 | tf_op jit(solution)/shard_map/ppermute | solution.py:92
  43.3 7.0 %collective-permute-start.11 = (f32[416,128]{1,0:T(8,128)S(1)}, f32[416,128]{1,0:T(8,128)S(1)}, u32[]{:S(2)}, u32[]{:S(2)}) collective-permute-start(f32[416,128]{1,0:T(8,128)S(1)} %get-tuple-element.24.refs_1_), channel_id=1, source_target_pairs={{0,56},{8,192},{16,216},{24,32},{32,24},{40,224},{48,248},{56,0},{... | collective-permute-start | bytes 638984 | tf_op jit(solution)/shard_map/ppermute | solution.py:101
  45.0 4.4 %collective-permute-start.13 = (f32[128,128]{1,0:T(8,128)S(1)}, f32[128,128]{1,0:T(8,128)S(1)}, u32[]{:S(2)}, u32[]{:S(2)}) collective-permute-start(f32[128,128]{1,0:T(8,128)S(1)} %hold.1.refs_0_), channel_id=1, source_target_pairs={{0,80},{8,88},{16,64},{24,72},{32,112},{40,120},{48,96},{56,104},{... | collective-permute-start | bytes 196616 | tf_op jit(solution)/shard_map/ppermute | solution.py:92
  45.0 5.3 %collective-permute-start.12 = (f32[128,128]{1,0:T(8,128)S(1)}, f32[128,128]{1,0:T(8,128)S(1)}, u32[]{:S(2)}, u32[]{:S(2)}) collective-permute-start(f32[128,128]{1,0:T(8,128)S(1)} %hold.1.refs_0_), channel_id=1, source_target_pairs={{24,0},{64,8},{8,16},{80,24},{56,32},{96,40},{40,48},{112,56},{88,... | collective-permute-start | bytes 196616 | tf_op jit(solution)/shard_map/ppermute | solution.py:97
  50.3 6.9 %collective-permute-start.14 = (f32[416,128]{1,0:T(8,128)S(1)}, f32[416,128]{1,0:T(8,128)S(1)}, u32[]{:S(2)}, u32[]{:S(2)}) collective-permute-start(f32[416,128]{1,0:T(8,128)S(1)} %first_sum.1.refs_1_.refs_4_.refs_0_), channel_id=1, source_target_pairs={{0,200},{8,48},{16,40},{24,208},{32,232},{40,16},{48,8},{56,240},{... | collective-permute-start | bytes 638984 | tf_op jit(solution)/shard_map/ppermute | solution.py:101
  53.3 1.3 %collective-permute-start.15 = (f32[128,128]{1,0:T(8,128)S(1)}, f32[128,128]{1,0:T(8,128)S(1)}, u32[]{:S(2)}, u32[]{:S(2)}) collective-permute-start(f32[128,128]{1,0:T(8,128)S(1)} %hold_split.1.refs_2_), channel_id=1, source_target_pairs={{0,8},{8,0},{16,24},{24,16},{32,40},{40,32},{48,56},{56,48},{64,72... | collective-permute-start | bytes 196616 | tf_op jit(solution)/shard_map/ppermute | solution.py:92
  57.2 5.7 %collective-permute-start.16 = (f32[416,128]{1,0:T(8,128)S(1)}, f32[416,128]{1,0:T(8,128)S(1)}, u32[]{:S(2)}, u32[]{:S(2)}) collective-permute-start(f32[416,128]{1,0:T(8,128)S(1)} %second_sum.1.refs_2_.refs_0_), channel_id=1, source_target_pairs={{0,72},{8,16},{16,8},{24,80},{32,104},{40,48},{48,40},{56,112},{64... | collective-permute-start | bytes 638984 | tf_op jit(solution)/shard_map/ppermute | solution.py:101
  63.2 5.7 %collective-permute-start.17 = (bf16[416,128]{1,0:T(8,128)(2,1)S(1)}, bf16[416,128]{1,0:T(8,128)(2,1)S(1)}, u32[]{:S(2)}, u32[]{:S(2)}) collective-permute-start(bf16[416,128]{1,0:T(8,128)(2,1)S(1)} %block.1.refs_3_.refs_0_), channel_id=1, source_target_pairs={{0,56},{8,192},{16,216},{24,32},{32,24},{40,224},{48,248},{56,0},{... | collective-permute-start | bytes 319496 | tf_op jit(solution)/shard_map/ppermute | solution.py:101
  68.9 5.4 %collective-permute-start.18 = (bf16[832,128]{1,0:T(8,128)(2,1)S(1)}, bf16[832,128]{1,0:T(8,128)(2,1)S(1)}, u32[]{:S(2)}, u32[]{:S(2)}) collective-permute-start(bf16[832,128]{1,0:T(8,128)(2,1)S(1)} %join1.1.refs_0_), channel_id=1, source_target_pairs={{0,24},{8,64},{16,88},{24,0},{32,56},{40,96},{48,120},{56,32},{64,... | collective-permute-start | bytes 638984 | tf_op jit(solution)/shard_map/ppermute | solution.py:101
  69.1 4.1 %collective-permute-start.20 = (f32[8,128]{1,0:T(8,128)S(1)}, f32[8,128]{1,0:T(8,128)S(1)}, u32[]{:S(2)}, u32[]{:S(2)}) collective-permute-start(f32[8,128]{1,0:T(8,128)S(1)} %squares.1.refs_2_), channel_id=1, source_target_pairs={{0,25},{1,24},{2,27},{3,26},{4,29},{5,28},{6,31},{7,30},{8,65},{9,... | collective-permute-start | bytes 12296 | tf_op jit(solution)/shard_map/ppermute | solution.py:80
  69.8 3.6 %collective-permute-start.19 = (f32[8,128]{1,0:T(8,128)S(1)}, f32[8,128]{1,0:T(8,128)S(1)}, u32[]{:S(2)}, u32[]{:S(2)}) collective-permute-start(f32[8,128]{1,0:T(8,128)S(1)} %squares.1.refs_2_), channel_id=1, source_target_pairs={{0,1},{1,0},{2,3},{3,2},{4,5},{5,4},{6,7},{7,6},{8,9},{9,8},{10,11... | collective-permute-start | bytes 12296 | tf_op jit(solution)/shard_map/ppermute | solution.py:80
  74.4 2.3 %collective-permute-start.21 = (bf16[1664,128]{1,0:T(8,128)(2,1)S(1)}, bf16[1664,128]{1,0:T(8,128)(2,1)S(1)}, u32[]{:S(2)}, u32[]{:S(2)}) collective-permute-start(bf16[1664,128]{1,0:T(8,128)(2,1)S(1)} %get-tuple-element.25.refs_0_), channel_id=1, source_target_pairs={{0,8},{8,0},{16,24},{24,16},{32,40},{40,32},{48,56},{56,48},{64,72... | collective-permute-start | bytes 1277960 | tf_op jit(solution)/shard_map/ppermute | solution.py:92
  74.9 1.8 %collective-permute-start.22 = (f32[8,128]{1,0:T(8,128)S(1)}, f32[8,128]{1,0:T(8,128)S(1)}, u32[]{:S(2)}, u32[]{:S(2)}) collective-permute-start(f32[8,128]{1,0:T(8,128)S(1)} %get-tuple-element.26.refs_2_), channel_id=1, source_target_pairs={{0,8},{8,0},{16,24},{24,16},{32,40},{40,32},{48,56},{56,48},{64,72... | collective-permute-start | bytes 12296 | tf_op jit(solution)/shard_map/ppermute | solution.py:92
  75.0 6.2 %collective-permute-start.23 = (f32[8,128]{1,0:T(8,128)S(1)}, f32[8,128]{1,0:T(8,128)S(1)}, u32[]{:S(2)}, u32[]{:S(2)}) collective-permute-start(f32[8,128]{1,0:T(8,128)S(1)} %get-tuple-element.26.refs_2_), channel_id=1, source_target_pairs={{13,0},{12,1},{15,2},{14,3},{9,4},{8,5},{11,6},{10,7},{5,8},{4,9},... | collective-permute-start | bytes 12296 | tf_op jit(solution)/shard_map/ppermute | solution.py:88
  76.9 4.3 %collective-permute-start.24 = (f32[8,128]{1,0:T(8,128)S(1)}, f32[8,128]{1,0:T(8,128)S(1)}, u32[]{:S(2)}, u32[]{:S(2)}) collective-permute-start(f32[8,128]{1,0:T(8,128)S(1)} %get-tuple-element.29.sq_ref), channel_id=1, source_target_pairs={{15,0},{10,1},{9,2},{12,3},{11,4},{14,5},{13,6},{8,7},{2,8},{7,9},... | collective-permute-start | bytes 12296 | tf_op jit(solution)/shard_map/ppermute | solution.py:88
  79.7 2.8 %copy-start = (bf16[256,3328]{1,0:T(8,128)(2,1)S(1)}, bf16[256,3328]{1,0:T(8,128)(2,1)}, u32[]{:S(2)}) copy-start(bf16[256,3328]{1,0:T(8,128)(2,1)} %weights_ref.1) | copy-start | bytes 5111812
  81.2 1.3 %collective-permute-start.25 = (f32[16,128]{1,0:T(8,128)S(1)}, f32[16,128]{1,0:T(8,128)S(1)}, u32[]{:S(2)}, u32[]{:S(2)}) collective-permute-start(f32[16,128]{1,0:T(8,128)S(1)} %stack.1.moved_ref), channel_id=1, source_target_pairs={{0,8},{8,0},{16,24},{24,16},{32,40},{40,32},{48,56},{56,48},{64,72... | collective-permute-start | bytes 24584 | tf_op jit(solution)/shard_map/ppermute | solution.py:92

commit v7 on v6

--- a/solution.py
+++ b/solution.py
@@ -92,9 +92,8 @@
     return lax.ppermute(x, "fsdp", [(i, i ^ mask) for i in range(FSDP)])
 
 
-def split_xy(x, x_mask, y_mask):
-    split = [(f ^ (y_mask if f % 2 else x_mask), f) for f in range(FSDP)]
-    return lax.ppermute(x, "fsdp", split), xor_fsdp(x, x_mask ^ y_mask)
+def split_cores(x, first, second):
+    return lax.ppermute(x, "fsdp", [(f ^ (second if f % 2 else first), f) for f in range(FSDP)])
 
 
 def xor_step(x, k):
@@ -234,7 +233,7 @@
 
 
 def add(a, b, after, name):
-    return local(add_kernel, f32(*a.shape), [a, b], after, nbytes=3 * 4 * a.size, name=name)
+    return local(add_kernel, f32(*a.shape), [a, b], after, nbytes=12 * a.size, name=name)
 
 
 def reciprocal(x):
@@ -471,13 +470,13 @@
     moving, keep = split_step(0, n, keep, recv)
     gram = local(gram_pair_kernel, f32(RANK, RANK), [send, recv], [moving], nbytes=200000, name="gram_pair")
     recv = xor_step(moving, 0)
-    split, both = split_xy(gram, X_THREE, Y_THREE)
-    gram = gram_four(gram, both, split, xor_fsdp(split, CORE), [])
+    split = split_cores(gram, X_THREE, X_THREE ^ Y_THREE ^ CORE)
+    gram = gram_four(gram, xor_fsdp(gram, Y_THREE), split, xor_fsdp(split, CORE), [])
     n //= 2
     moving, keep = split_step(1, n, keep, recv, [gram])
     recv = xor_step(moving, 1)
     gram = local(hold_kernel, f32(RANK, RANK), [gram], [moving], nbytes=130000, name="hold")
-    split, both = split_xy(gram, X_ONE, Y_ONE)
+    split, both = split_cores(gram, X_ONE, Y_ONE), xor_fsdp(gram, X_ONE ^ Y_ONE)
     d = add(keep, recv, [split, both], "first_sum")
     recv = xor_step(d, 2)
     split = local(hold_kernel, f32(RANK, RANK), [split], [d], nbytes=130000, name="hold_split")

time: 84.6 us -> 84.3 us (level)
  starting transfers between devices: 39.1 us -> 37.7 us
  waiting for transfers between devices: 31.2 us -> 32.2 us
    ppermute x2, waiting for transfers between devices: 1.51 us -> 3.23 us  [split_cores(): lax.ppermute(x, 'fsdp', [(f ^ (second if f % 2 else first), f) for f in r...]
    ppermute x8, waiting for transfers between devices: 11 us -> 9.74 us  [xor_fsdp(): return lax.ppermute(x, 'fsdp', [(i, i ^ mask) for i in range(FSDP)])]
    ppermute x2, starting transfers between devices: 3.8 us -> 2.66 us  [split_cores(): lax.ppermute(x, 'fsdp', [(f ^ (second if f % 2 else first), f) for f in r...]
  transfers between devices with their start and end apart: 26 -> 26, of which waited for: 18 -> 19; matrix products, arithmetic and copies ran while one was open for 0% -> 0% of each run, Pallas kernels for 9% -> 9%
where the time goes in v7:
time: 84.3 us
  starting transfers between devices  37.7 us (45%)
  waiting for transfers between devices  32.2 us (38%)
  Pallas kernels  13.2 us (16%)
  between operations  1.01 us (1%)
    ppermute x6, starting transfers between devices, swap_z(): return lax.ppermute(x, ('fsdp', 'tp'), perm)  11.5 us
    ppermute x8, waiting for transfers between devices, xor_fsdp(): return lax.ppermute(x, 'fsdp', [(i, i ^ mask) for i in range(FSDP)])  9.74 us
    ppermute x6, waiting for transfers between devices, swap_z(): return lax.ppermute(x, ('fsdp', 'tp'), perm)  9 us
    ppermute x6, waiting for transfers between devices, xor_step(): lax.ppermute(x, 'fsdp', [(i, i ^ MASKS[team(i)][k]) for i in range(FSDP)])  8.91 us
    ppermute x8, starting transfers between devices, xor_fsdp(): return lax.ppermute(x, 'fsdp', [(i, i ^ mask) for i in range(FSDP)])  8.39 us
    ppermute x6, starting transfers between devices, xor_step(): lax.ppermute(x, 'fsdp', [(i, i ^ MASKS[team(i)][k]) for i in range(FSDP)])  7.65 us
    pallas_call x20, Pallas kernels, local(): pl.pallas_call(body, in_specs=[VMEM_SPEC] * (used + len(after)), out_spec...  6.97 us
    ppermute x2, starting transfers between devices, turn_z(): return lax.ppermute(x, ('fsdp', 'tp'), perm)  4.51 us
  transfers between devices with their start and end apart: 26, of which 19 were waited for; matrix products, arithmetic and copies ran while one was open for 0% of the time, Pallas kernels for 9%

profile of v7, /device:TPU:1, one launch (start us, length us, event | category | flops | bytes accessed | tf_op | source)
XLA Modules:
  0.0 84.3 jit_solution(9081855767940272683)
XLA Ops:
  0.6 2.9 %project.1 = (bf16[256,3328]{1,0:T(8,128)(2,1)S(1)}, f32[128,128]{1,0:T(8,128)S(1)}, f32[128,128]{1,0:T(8,128)S(1)}) custom-call(bf16[256,3328]{1,0:T(8,128)(2,1)} %m_hbm.1, bf16[256,3328]{1,0:T(8,128)(2,1)} %g_hbm.1, f32[3328,128]{1,0:T(8,128)} %s_hbm.1), custom_call_target="tpu_custom_call" | custom-call | flops 218103808 | bytes 7000000 | tf_op jit(solution)/shard_map/project/pallas_call | solution.py:140
  3.5 6.5 %collective-permute-start = (f32[128,128]{1,0:T(8,128)S(1)}, f32[128,128]{1,0:T(8,128)S(1)}, u32[]{:S(2)}, u32[]{:S(2)}) collective-permute-start(f32[128,128]{1,0:T(8,128)S(1)} %get-tuple-element.18), channel_id=1, source_target_pairs={{0,1},{1,0},{2,3},{3,2},{4,5},{5,4},{6,7},{7,6},{9,10},{10,9},{11,... | collective-permute-start | bytes 196616 | tf_op jit(solution)/shard_map/ppermute | solution.py:72
  10.1 1.6 %collective-permute-done = f32[128,128]{1,0:T(8,128)S(1)} collective-permute-done((f32[128,128]{1,0:T(8,128)S(1)}, f32[128,128]{1,0:T(8,128)S(1)}, u32[]{:S(2)}, u32[]{:S(2)}) %collective-permute-start) | collective-permute-done | bytes 65568 | tf_op jit(solution)/shard_map/ppermute | solution.py:72
  11.8 2.6 %collective-permute-done.3 = f32[128,128]{1,0:T(8,128)S(1)} collective-permute-done((f32[128,128]{1,0:T(8,128)S(1)}, f32[128,128]{1,0:T(8,128)S(1)}, u32[]{:S(2)}, u32[]{:S(2)}) %collective-permute-start.3) | collective-permute-done | bytes 65568 | tf_op jit(solution)/shard_map/ppermute | solution.py:72
  14.9 2.9 %collective-permute-start.2 = (f32[128,128]{1,0:T(8,128)S(1)}, f32[128,128]{1,0:T(8,128)S(1)}, u32[]{:S(2)}, u32[]{:S(2)}) collective-permute-start(f32[128,128]{1,0:T(8,128)S(1)} %add.19), channel_id=1, source_target_pairs={{2,5},{5,2},{1,6},{6,1},{4,7},{7,4},{3,0},{0,3},{11,14},{14,11},{1... | collective-permute-start | bytes 196616 | tf_op jit(solution)/shard_map/ppermute | solution.py:72
  17.8 1.8 %collective-permute-start.5 = (f32[128,128]{1,0:T(8,128)S(1)}, f32[128,128]{1,0:T(8,128)S(1)}, u32[]{:S(2)}, u32[]{:S(2)}) collective-permute-start(f32[128,128]{1,0:T(8,128)S(1)} %add.22), channel_id=1, source_target_pairs={{2,5},{5,2},{1,6},{6,1},{4,7},{7,4},{3,0},{0,3},{11,14},{14,11},{1... | collective-permute-start | bytes 196616 | tf_op jit(solution)/shard_map/ppermute | solution.py:72
  19.7 1.6 %collective-permute-done.2 = f32[128,128]{1,0:T(8,128)S(1)} collective-permute-done((f32[128,128]{1,0:T(8,128)S(1)}, f32[128,128]{1,0:T(8,128)S(1)}, u32[]{:S(2)}, u32[]{:S(2)}) %collective-permute-start.2) | collective-permute-done | bytes 65568 | tf_op jit(solution)/shard_map/ppermute | solution.py:72
  21.2 2.9 %collective-permute-done.5 = f32[128,128]{1,0:T(8,128)S(1)} collective-permute-done((f32[128,128]{1,0:T(8,128)S(1)}, f32[128,128]{1,0:T(8,128)S(1)}, u32[]{:S(2)}, u32[]{:S(2)}) %collective-permute-start.5) | collective-permute-done | bytes 65568 | tf_op jit(solution)/shard_map/ppermute | solution.py:72
  24.7 5.6 %collective-permute-start.6 = (f32[1792,128]{1,0:T(8,128)S(1)}, f32[1792,128]{1,0:T(8,128)S(1)}, u32[]{:S(2)}, u32[]{:S(2)}) collective-permute-start(f32[1792,128]{1,0:T(8,128)S(1)} %lift_send.1.refs_3_.refs_0_), channel_id=1, source_target_pairs={{0,8},{8,0},{16,24},{24,16},{32,40},{40,32},{48,56},{56,48},{64,72... | collective-permute-start | bytes 2752520 | tf_op jit(solution)/shard_map/ppermute | solution.py:92
  30.8 1.6 %collective-permute-done.6.refs_1_ = f32[1792,128]{1,0:T(8,128)S(1)} collective-permute-done((f32[1792,128]{1,0:T(8,128)S(1)}, f32[1792,128]{1,0:T(8,128)S(1)}, u32[]{:S(2)}, u32[]{:S(2)}) %collective-permute-start.6) | collective-permute-done | bytes 917536 | tf_op jit(solution)/shard_map/ppermute | solution.py:92
  32.5 1.6 %collective-permute-start.7 = (f32[832,128]{1,0:T(8,128)S(1)}, f32[832,128]{1,0:T(8,128)S(1)}, u32[]{:S(2)}, u32[]{:S(2)}) collective-permute-start(f32[832,128]{1,0:T(8,128)S(1)} %get-tuple-element.22.refs_2_), channel_id=1, source_target_pairs={{0,24},{8,64},{16,88},{24,0},{32,56},{40,96},{48,120},{56,32},{64,... | collective-permute-start | bytes 1277960 | tf_op jit(solution)/shard_map/ppermute | solution.py:100
  34.1 2.6 %collective-permute-start.9 = (f32[128,128]{1,0:T(8,128)S(1)}, f32[128,128]{1,0:T(8,128)S(1)}, u32[]{:S(2)}, u32[]{:S(2)}) collective-permute-start(f32[128,128]{1,0:T(8,128)S(1)} %gram_pair.1.refs_0_), channel_id=1, source_target_pairs={{56,0},{240,8},{40,16},{224,24},{24,32},{208,40},{8,48},{192,56},{... | collective-permute-start | bytes 196616 | tf_op jit(solution)/shard_map/ppermute | solution.py:96
  36.7 1.9 %collective-permute-start.8 = (f32[128,128]{1,0:T(8,128)S(1)}, f32[128,128]{1,0:T(8,128)S(1)}, u32[]{:S(2)}, u32[]{:S(2)}) collective-permute-start(f32[128,128]{1,0:T(8,128)S(1)} %gram_pair.1.refs_0_), channel_id=1, source_target_pairs={{0,200},{8,192},{16,216},{24,208},{32,232},{40,224},{48,248},{56,2... | collective-permute-start | bytes 196616 | tf_op jit(solution)/shard_map/ppermute | solution.py:92
  38.6 2.6 %collective-permute-done.9.refs_2_ = f32[128,128]{1,0:T(8,128)S(1)} collective-permute-done((f32[128,128]{1,0:T(8,128)S(1)}, f32[128,128]{1,0:T(8,128)S(1)}, u32[]{:S(2)}, u32[]{:S(2)}) %collective-permute-start.9) | collective-permute-done | bytes 65568 | tf_op jit(solution)/shard_map/ppermute | solution.py:96
  42.6 2.9 %collective-permute-start.11 = (f32[416,128]{1,0:T(8,128)S(1)}, f32[416,128]{1,0:T(8,128)S(1)}, u32[]{:S(2)}, u32[]{:S(2)}) collective-permute-start(f32[416,128]{1,0:T(8,128)S(1)} %get-tuple-element.24.refs_1_), channel_id=1, source_target_pairs={{0,56},{8,192},{16,216},{24,32},{32,24},{40,224},{48,248},{56,0},{... | collective-permute-start | bytes 638984 | tf_op jit(solution)/shard_map/ppermute | solution.py:100
  45.6 4.7 %collective-permute-done.13.refs_3_.refs_1_ = f32[128,128]{1,0:T(8,128)S(1)} collective-permute-done((f32[128,128]{1,0:T(8,128)S(1)}, f32[128,128]{1,0:T(8,128)S(1)}, u32[]{:S(2)}, u32[]{:S(2)}) %collective-permute-start.13) | collective-permute-done | bytes 65568 | tf_op jit(solution)/shard_map/ppermute | solution.py:92
  50.9 1.8 %collective-permute-start.14 = (f32[416,128]{1,0:T(8,128)S(1)}, f32[416,128]{1,0:T(8,128)S(1)}, u32[]{:S(2)}, u32[]{:S(2)}) collective-permute-start(f32[416,128]{1,0:T(8,128)S(1)} %first_sum.1.refs_1_.refs_4_.refs_0_), channel_id=1, source_target_pairs={{0,200},{8,48},{16,40},{24,208},{32,232},{40,16},{48,8},{56,240},{... | collective-permute-start | bytes 638984 | tf_op jit(solution)/shard_map/ppermute | solution.py:100
  52.7 1.2 %collective-permute-done.15.refs_3_ = f32[128,128]{1,0:T(8,128)S(1)} collective-permute-done((f32[128,128]{1,0:T(8,128)S(1)}, f32[128,128]{1,0:T(8,128)S(1)}, u32[]{:S(2)}, u32[]{:S(2)}) %collective-permute-start.15) | collective-permute-done | bytes 65568 | tf_op jit(solution)/shard_map/ppermute | solution.py:92
  53.9 2.1 %eliminate0.1.refs_2_.refs_0_ = f32[128,128]{1,0:T(8,128)S(1)} custom-call(f32[128,128]{1,0:T(8,128)S(1)} %gram_four.3.refs_0_.refs_1_, f32[128,128]{1,0:T(8,128)S(1)} %gram_four.3.refs_0_.refs_1_), custom_call_target="tpu_custom_call" | custom-call | flops 4000000 | bytes 6000000 | tf_op jit(solution)/shard_map/eliminate0/pallas_call | solution.py:164
  56.1 1.4 %collective-permute-done.14.refs_1_ = f32[416,128]{1,0:T(8,128)S(1)} collective-permute-done((f32[416,128]{1,0:T(8,128)S(1)}, f32[416,128]{1,0:T(8,128)S(1)}, u32[]{:S(2)}, u32[]{:S(2)}) %collective-permute-start.14) | collective-permute-done | bytes 213024 | tf_op jit(solution)/shard_map/ppermute | solution.py:100
  57.6 2.6 %eliminate40.1.refs_2_ = f32[128,128]{1,0:T(8,128)S(1)} custom-call(f32[128,128]{1,0:T(8,128)S(1)} %eliminate0.1.refs_2_.refs_0_, f32[128,128]{1,0:T(8,128)S(1)} %gram_four.3.refs_0_.refs_1_, f32[416,128]{1,0:T(8,128)S(1)} %second_sum.1.refs_2_.refs_0_), custom_call_target="tpu_custom_call" | custom-call | flops 4000000 | bytes 13200000 | tf_op jit(solution)/shard_map/eliminate40/pallas_call | solution.py:164
  60.2 2.7 %collective-permute-done.16.refs_1_ = f32[416,128]{1,0:T(8,128)S(1)} collective-permute-done((f32[416,128]{1,0:T(8,128)S(1)}, f32[416,128]{1,0:T(8,128)S(1)}, u32[]{:S(2)}, u32[]{:S(2)}) %collective-permute-start.16) | collective-permute-done | bytes 213024 | tf_op jit(solution)/shard_map/ppermute | solution.py:100
  63.1 1.2 %collective-permute-start.17 = (bf16[416,128]{1,0:T(8,128)(2,1)S(1)}, bf16[416,128]{1,0:T(8,128)(2,1)S(1)}, u32[]{:S(2)}, u32[]{:S(2)}) collective-permute-start(bf16[416,128]{1,0:T(8,128)(2,1)S(1)} %block.1.refs_3_.refs_0_), channel_id=1, source_target_pairs={{0,56},{8,192},{16,216},{24,32},{32,24},{40,224},{48,248},{56,0},{... | collective-permute-start | bytes 319496 | tf_op jit(solution)/shard_map/ppermute | solution.py:100
  64.6 3.9 %collective-permute-done.17.refs_1_ = bf16[416,128]{1,0:T(8,128)(2,1)S(1)} collective-permute-done((bf16[416,128]{1,0:T(8,128)(2,1)S(1)}, bf16[416,128]{1,0:T(8,128)(2,1)S(1)}, u32[]{:S(2)}, u32[]{:S(2)}) %collective-permute-start.17) | collective-permute-done | bytes 106528 | tf_op jit(solution)/shard_map/ppermute | solution.py:100
  69.5 2.3 %collective-permute-start.19 = (f32[8,128]{1,0:T(8,128)S(1)}, f32[8,128]{1,0:T(8,128)S(1)}, u32[]{:S(2)}, u32[]{:S(2)}) collective-permute-start(f32[8,128]{1,0:T(8,128)S(1)} %squares.1.refs_2_), channel_id=1, source_target_pairs={{0,1},{1,0},{2,3},{3,2},{4,5},{5,4},{6,7},{7,6},{8,9},{9,8},{10,11... | collective-permute-start | bytes 12296 | tf_op jit(solution)/shard_map/ppermute | solution.py:80
  71.8 1.1 %collective-permute-done.20.refs_4_ = f32[8,128]{1,0:T(8,128)S(1)} collective-permute-done((f32[8,128]{1,0:T(8,128)S(1)}, f32[8,128]{1,0:T(8,128)S(1)}, u32[]{:S(2)}, u32[]{:S(2)}) %collective-permute-start.20) | collective-permute-done | bytes 4128 | tf_op jit(solution)/shard_map/ppermute | solution.py:80
  73.1 0.9 %collective-permute-done.18.refs_1_ = bf16[832,128]{1,0:T(8,128)(2,1)S(1)} collective-permute-done((bf16[832,128]{1,0:T(8,128)(2,1)S(1)}, bf16[832,128]{1,0:T(8,128)(2,1)S(1)}, u32[]{:S(2)}, u32[]{:S(2)}) %collective-permute-start.18) | collective-permute-done | bytes 213024 | tf_op jit(solution)/shard_map/ppermute | solution.py:100
  74.7 1.7 %collective-permute-start.23 = (f32[8,128]{1,0:T(8,128)S(1)}, f32[8,128]{1,0:T(8,128)S(1)}, u32[]{:S(2)}, u32[]{:S(2)}) collective-permute-start(f32[8,128]{1,0:T(8,128)S(1)} %get-tuple-element.26.refs_2_), channel_id=1, source_target_pairs={{13,0},{12,1},{15,2},{14,3},{9,4},{8,5},{11,6},{10,7},{5,8},{4,9},... | collective-permute-start | bytes 12296 | tf_op jit(solution)/shard_map/ppermute | solution.py:88
  76.6 2.8 %collective-permute-start.24 = (f32[8,128]{1,0:T(8,128)S(1)}, f32[8,128]{1,0:T(8,128)S(1)}, u32[]{:S(2)}, u32[]{:S(2)}) collective-permute-start(f32[8,128]{1,0:T(8,128)S(1)} %get-tuple-element.29.sq_ref), channel_id=1, source_target_pairs={{15,0},{10,1},{9,2},{12,3},{11,4},{14,5},{13,6},{8,7},{2,8},{7,9},... | collective-permute-start | bytes 12296 | tf_op jit(solution)/shard_map/ppermute | solution.py:88
  79.4 1.5 %finish_momentum.1 = (bf16[256,3328]{1,0:T(8,128)(2,1)}, f32[8,128]{1,0:T(8,128)S(1)}) custom-call(f32[3328,128]{1,0:T(8,128)S(1)} %get-tuple-element.27.coef_ref, bf16[256,128]{1,0:T(8,128)(2,1)S(1)} %ortho.1.refs_2_.ortho_ref, bf16[256,3328]{1,0:T(8,128)(2,1)S(1)} %get-tuple-element.20.refs_2_.b_ref), custom_call_target="tpu_custom_call" | custom-call | flops 218103808 | bytes 5000000 | tf_op jit(solution)/shard_map/finish_momentum/pallas_call | solution.py:394
  81.3 0.9 %collective-permute-done.25.other_ref = f32[16,128]{1,0:T(8,128)S(1)} collective-permute-done((f32[16,128]{1,0:T(8,128)S(1)}, f32[16,128]{1,0:T(8,128)S(1)}, u32[]{:S(2)}, u32[]{:S(2)}) %collective-permute-start.25) | collective-permute-done | bytes 8224 | tf_op jit(solution)/shard_map/ppermute | solution.py:92
  82.2 1.9 %finish_weights.1 = (bf16[256,3328]{1,0:T(8,128)(2,1)}, f32[3328,128]{1,0:T(8,128)}) custom-call(f32[8,128]{1,0:T(8,128)S(1)} %get-tuple-element.29.sq_ref, f32[16,128]{1,0:T(8,128)S(1)} %stack.1.moved_ref, f32[16,128]{1,0:T(8,128)S(1)} %collective-permute-done.25.other_ref, f32[3328,128]{1,0:T(8,128)S(1)} %get-tuple-element.27.coef_ref, ...), custom_call_target="tpu_custom_call" | custom-call | flops 218103808 | bytes 7000000 | tf_op jit(solution)/shard_map/finish_weights/pallas_call | solution.py:439
  (51 shorter events, 7.1 us)
Async XLA Ops:
  3.5 8.1 %collective-permute-start = (f32[128,128]{1,0:T(8,128)S(1)}, f32[128,128]{1,0:T(8,128)S(1)}, u32[]{:S(2)}, u32[]{:S(2)}) collective-permute-start(f32[128,128]{1,0:T(8,128)S(1)} %get-tuple-element.18), channel_id=1, source_target_pairs={{0,1},{1,0},{2,3},{3,2},{4,5},{5,4},{6,7},{7,6},{9,10},{10,9},{11,... | collective-permute-start | bytes 196616 | tf_op jit(solution)/shard_map/ppermute | solution.py:72
  10.0 4.3 %collective-permute-start.3 = (f32[128,128]{1,0:T(8,128)S(1)}, f32[128,128]{1,0:T(8,128)S(1)}, u32[]{:S(2)}, u32[]{:S(2)}) collective-permute-start(f32[128,128]{1,0:T(8,128)S(1)} %get-tuple-element.19), channel_id=1, source_target_pairs={{0,1},{1,0},{2,3},{3,2},{4,5},{5,4},{6,7},{7,6},{9,10},{10,9},{11,... | collective-permute-start | bytes 196616 | tf_op jit(solution)/shard_map/ppermute | solution.py:72
  11.7 3.2 %collective-permute-start.1 = (f32[128,128]{1,0:T(8,128)S(1)}, f32[128,128]{1,0:T(8,128)S(1)}, u32[]{:S(2)}, u32[]{:S(2)}) collective-permute-start(f32[128,128]{1,0:T(8,128)S(1)} %add.18), channel_id=1, source_target_pairs={{1,2},{2,1},{3,4},{4,3},{5,6},{6,5},{7,0},{0,7},{10,11},{11,10},{1... | collective-permute-start | bytes 196616 | tf_op jit(solution)/shard_map/ppermute | solution.py:72
  14.4 3.5 %collective-permute-start.4 = (f32[128,128]{1,0:T(8,128)S(1)}, f32[128,128]{1,0:T(8,128)S(1)}, u32[]{:S(2)}, u32[]{:S(2)}) collective-permute-start(f32[128,128]{1,0:T(8,128)S(1)} %add.21), channel_id=1, source_target_pairs={{1,2},{2,1},{3,4},{4,3},{5,6},{6,5},{7,0},{0,7},{10,11},{11,10},{1... | collective-permute-start | bytes 196616 | tf_op jit(solution)/shard_map/ppermute | solution.py:72
  14.9 6.3 %collective-permute-start.2 = (f32[128,128]{1,0:T(8,128)S(1)}, f32[128,128]{1,0:T(8,128)S(1)}, u32[]{:S(2)}, u32[]{:S(2)}) collective-permute-start(f32[128,128]{1,0:T(8,128)S(1)} %add.19), channel_id=1, source_target_pairs={{2,5},{5,2},{1,6},{6,1},{4,7},{7,4},{3,0},{0,3},{11,14},{14,11},{1... | collective-permute-start | bytes 196616 | tf_op jit(solution)/shard_map/ppermute | solution.py:72
  17.8 6.3 %collective-permute-start.5 = (f32[128,128]{1,0:T(8,128)S(1)}, f32[128,128]{1,0:T(8,128)S(1)}, u32[]{:S(2)}, u32[]{:S(2)}) collective-permute-start(f32[128,128]{1,0:T(8,128)S(1)} %add.22), channel_id=1, source_target_pairs={{2,5},{5,2},{1,6},{6,1},{4,7},{7,4},{3,0},{0,3},{11,14},{14,11},{1... | collective-permute-start | bytes 196616 | tf_op jit(solution)/shard_map/ppermute | solution.py:72
  24.7 7.7 %collective-permute-start.6 = (f32[1792,128]{1,0:T(8,128)S(1)}, f32[1792,128]{1,0:T(8,128)S(1)}, u32[]{:S(2)}, u32[]{:S(2)}) collective-permute-start(f32[1792,128]{1,0:T(8,128)S(1)} %lift_send.1.refs_3_.refs_0_), channel_id=1, source_target_pairs={{0,8},{8,0},{16,24},{24,16},{32,40},{40,32},{48,56},{56,48},{64,72... | collective-permute-start | bytes 2752520 | tf_op jit(solution)/shard_map/ppermute | solution.py:92
  32.5 10.1 %collective-permute-start.7 = (f32[832,128]{1,0:T(8,128)S(1)}, f32[832,128]{1,0:T(8,128)S(1)}, u32[]{:S(2)}, u32[]{:S(2)}) collective-permute-start(f32[832,128]{1,0:T(8,128)S(1)} %get-tuple-element.22.refs_2_), channel_id=1, source_target_pairs={{0,24},{8,64},{16,88},{24,0},{32,56},{40,96},{48,120},{56,32},{64,... | collective-permute-start | bytes 1277960 | tf_op jit(solution)/shard_map/ppermute | solution.py:100
  34.1 7.1 %collective-permute-start.9 = (f32[128,128]{1,0:T(8,128)S(1)}, f32[128,128]{1,0:T(8,128)S(1)}, u32[]{:S(2)}, u32[]{:S(2)}) collective-permute-start(f32[128,128]{1,0:T(8,128)S(1)} %gram_pair.1.refs_0_), channel_id=1, source_target_pairs={{56,0},{240,8},{40,16},{224,24},{24,32},{208,40},{8,48},{192,56},{... | collective-permute-start | bytes 196616 | tf_op jit(solution)/shard_map/ppermute | solution.py:96
  36.7 5.2 %collective-permute-start.8 = (f32[128,128]{1,0:T(8,128)S(1)}, f32[128,128]{1,0:T(8,128)S(1)}, u32[]{:S(2)}, u32[]{:S(2)}) collective-permute-start(f32[128,128]{1,0:T(8,128)S(1)} %gram_pair.1.refs_0_), channel_id=1, source_target_pairs={{0,200},{8,192},{16,216},{24,208},{32,232},{40,224},{48,248},{56,2... | collective-permute-start | bytes 196616 | tf_op jit(solution)/shard_map/ppermute | solution.py:92
  41.3 1.3 %collective-permute-start.10 = (f32[128,128]{1,0:T(8,128)S(1)}, f32[128,128]{1,0:T(8,128)S(1)}, u32[]{:S(2)}, u32[]{:S(2)}) collective-permute-start(f32[128,128]{1,0:T(8,128)S(1)} %collective-permute-done.9.refs_2_), channel_id=1, source_target_pairs={{0,8},{8,0},{16,24},{24,16},{32,40},{40,32},{48,56},{56,48},{64,72... | collective-permute-start | bytes 196616 | tf_op jit(solution)/shard_map/ppermute | solution.py:92
  42.6 8.2 %collective-permute-start.11 = (f32[416,128]{1,0:T(8,128)S(1)}, f32[416,128]{1,0:T(8,128)S(1)}, u32[]{:S(2)}, u32[]{:S(2)}) collective-permute-start(f32[416,128]{1,0:T(8,128)S(1)} %get-tuple-element.24.refs_1_), channel_id=1, source_target_pairs={{0,56},{8,192},{16,216},{24,32},{32,24},{40,224},{48,248},{56,0},{... | collective-permute-start | bytes 638984 | tf_op jit(solution)/shard_map/ppermute | solution.py:100
  45.5 4.8 %collective-permute-start.13 = (f32[128,128]{1,0:T(8,128)S(1)}, f32[128,128]{1,0:T(8,128)S(1)}, u32[]{:S(2)}, u32[]{:S(2)}) collective-permute-start(f32[128,128]{1,0:T(8,128)S(1)} %hold.1.refs_0_), channel_id=1, source_target_pairs={{0,80},{8,88},{16,64},{24,72},{32,112},{40,120},{48,96},{56,104},{... | collective-permute-start | bytes 196616 | tf_op jit(solution)/shard_map/ppermute | solution.py:92
  45.5 5.3 %collective-permute-start.12 = (f32[128,128]{1,0:T(8,128)S(1)}, f32[128,128]{1,0:T(8,128)S(1)}, u32[]{:S(2)}, u32[]{:S(2)}) collective-permute-start(f32[128,128]{1,0:T(8,128)S(1)} %hold.1.refs_0_), channel_id=1, source_target_pairs={{24,0},{64,8},{8,16},{80,24},{56,32},{96,40},{40,48},{112,56},{88,... | collective-permute-start | bytes 196616 | tf_op jit(solution)/shard_map/ppermute | solution.py:96
  50.9 6.6 %collective-permute-start.14 = (f32[416,128]{1,0:T(8,128)S(1)}, f32[416,128]{1,0:T(8,128)S(1)}, u32[]{:S(2)}, u32[]{:S(2)}) collective-permute-start(f32[416,128]{1,0:T(8,128)S(1)} %first_sum.1.refs_1_.refs_4_.refs_0_), channel_id=1, source_target_pairs={{0,200},{8,48},{16,40},{24,208},{32,232},{40,16},{48,8},{56,240},{... | collective-permute-start | bytes 638984 | tf_op jit(solution)/shard_map/ppermute | solution.py:100
  52.6 1.3 %collective-permute-start.15 = (f32[128,128]{1,0:T(8,128)S(1)}, f32[128,128]{1,0:T(8,128)S(1)}, u32[]{:S(2)}, u32[]{:S(2)}) collective-permute-start(f32[128,128]{1,0:T(8,128)S(1)} %hold_split.1.refs_2_), channel_id=1, source_target_pairs={{0,8},{8,0},{16,24},{24,16},{32,40},{40,32},{48,56},{56,48},{64,72... | collective-permute-start | bytes 196616 | tf_op jit(solution)/shard_map/ppermute | solution.py:92
  57.5 5.4 %collective-permute-start.16 = (f32[416,128]{1,0:T(8,128)S(1)}, f32[416,128]{1,0:T(8,128)S(1)}, u32[]{:S(2)}, u32[]{:S(2)}) collective-permute-start(f32[416,128]{1,0:T(8,128)S(1)} %second_sum.1.refs_2_.refs_0_), channel_id=1, source_target_pairs={{0,72},{8,16},{16,8},{24,80},{32,104},{40,48},{48,40},{56,112},{64... | collective-permute-start | bytes 638984 | tf_op jit(solution)/shard_map/ppermute | solution.py:100
  63.1 5.4 %collective-permute-start.17 = (bf16[416,128]{1,0:T(8,128)(2,1)S(1)}, bf16[416,128]{1,0:T(8,128)(2,1)S(1)}, u32[]{:S(2)}, u32[]{:S(2)}) collective-permute-start(bf16[416,128]{1,0:T(8,128)(2,1)S(1)} %block.1.refs_3_.refs_0_), channel_id=1, source_target_pairs={{0,56},{8,192},{16,216},{24,32},{32,24},{40,224},{48,248},{56,0},{... | collective-permute-start | bytes 319496 | tf_op jit(solution)/shard_map/ppermute | solution.py:100
  68.6 5.4 %collective-permute-start.18 = (bf16[832,128]{1,0:T(8,128)(2,1)S(1)}, bf16[832,128]{1,0:T(8,128)(2,1)S(1)}, u32[]{:S(2)}, u32[]{:S(2)}) collective-permute-start(bf16[832,128]{1,0:T(8,128)(2,1)S(1)} %join1.1.refs_0_), channel_id=1, source_target_pairs={{0,24},{8,64},{16,88},{24,0},{32,56},{40,96},{48,120},{56,32},{64,... | collective-permute-start | bytes 638984 | tf_op jit(solution)/shard_map/ppermute | solution.py:100
  68.8 4.1 %collective-permute-start.20 = (f32[8,128]{1,0:T(8,128)S(1)}, f32[8,128]{1,0:T(8,128)S(1)}, u32[]{:S(2)}, u32[]{:S(2)}) collective-permute-start(f32[8,128]{1,0:T(8,128)S(1)} %squares.1.refs_2_), channel_id=1, source_target_pairs={{0,25},{1,24},{2,27},{3,26},{4,29},{5,28},{6,31},{7,30},{8,65},{9,... | collective-permute-start | bytes 12296 | tf_op jit(solution)/shard_map/ppermute | solution.py:80
  69.5 3.6 %collective-permute-start.19 = (f32[8,128]{1,0:T(8,128)S(1)}, f32[8,128]{1,0:T(8,128)S(1)}, u32[]{:S(2)}, u32[]{:S(2)}) collective-permute-start(f32[8,128]{1,0:T(8,128)S(1)} %squares.1.refs_2_), channel_id=1, source_target_pairs={{0,1},{1,0},{2,3},{3,2},{4,5},{5,4},{6,7},{7,6},{8,9},{9,8},{10,11... | collective-permute-start | bytes 12296 | tf_op jit(solution)/shard_map/ppermute | solution.py:80
  74.1 2.3 %collective-permute-start.21 = (bf16[1664,128]{1,0:T(8,128)(2,1)S(1)}, bf16[1664,128]{1,0:T(8,128)(2,1)S(1)}, u32[]{:S(2)}, u32[]{:S(2)}) collective-permute-start(bf16[1664,128]{1,0:T(8,128)(2,1)S(1)} %get-tuple-element.25.refs_0_), channel_id=1, source_target_pairs={{0,8},{8,0},{16,24},{24,16},{32,40},{40,32},{48,56},{56,48},{64,72... | collective-permute-start | bytes 1277960 | tf_op jit(solution)/shard_map/ppermute | solution.py:92
  74.6 1.8 %collective-permute-start.22 = (f32[8,128]{1,0:T(8,128)S(1)}, f32[8,128]{1,0:T(8,128)S(1)}, u32[]{:S(2)}, u32[]{:S(2)}) collective-permute-start(f32[8,128]{1,0:T(8,128)S(1)} %get-tuple-element.26.refs_2_), channel_id=1, source_target_pairs={{0,8},{8,0},{16,24},{24,16},{32,40},{40,32},{48,56},{56,48},{64,72... | collective-permute-start | bytes 12296 | tf_op jit(solution)/shard_map/ppermute | solution.py:92
  74.7 6.2 %collective-permute-start.23 = (f32[8,128]{1,0:T(8,128)S(1)}, f32[8,128]{1,0:T(8,128)S(1)}, u32[]{:S(2)}, u32[]{:S(2)}) collective-permute-start(f32[8,128]{1,0:T(8,128)S(1)} %get-tuple-element.26.refs_2_), channel_id=1, source_target_pairs={{13,0},{12,1},{15,2},{14,3},{9,4},{8,5},{11,6},{10,7},{5,8},{4,9},... | collective-permute-start | bytes 12296 | tf_op jit(solution)/shard_map/ppermute | solution.py:88
  76.6 4.3 %collective-permute-start.24 = (f32[8,128]{1,0:T(8,128)S(1)}, f32[8,128]{1,0:T(8,128)S(1)}, u32[]{:S(2)}, u32[]{:S(2)}) collective-permute-start(f32[8,128]{1,0:T(8,128)S(1)} %get-tuple-element.29.sq_ref), channel_id=1, source_target_pairs={{15,0},{10,1},{9,2},{12,3},{11,4},{14,5},{13,6},{8,7},{2,8},{7,9},... | collective-permute-start | bytes 12296 | tf_op jit(solution)/shard_map/ppermute | solution.py:88
  79.4 2.8 %copy-start = (bf16[256,3328]{1,0:T(8,128)(2,1)S(1)}, bf16[256,3328]{1,0:T(8,128)(2,1)}, u32[]{:S(2)}) copy-start(bf16[256,3328]{1,0:T(8,128)(2,1)} %weights_ref.1) | copy-start | bytes 5111812
  80.9 1.3 %collective-permute-start.25 = (f32[16,128]{1,0:T(8,128)S(1)}, f32[16,128]{1,0:T(8,128)S(1)}, u32[]{:S(2)}, u32[]{:S(2)}) collective-permute-start(f32[16,128]{1,0:T(8,128)S(1)} %stack.1.moved_ref), channel_id=1, source_target_pairs={{0,8},{8,0},{16,24},{24,16},{32,40},{40,32},{48,56},{56,48},{64,72... | collective-permute-start | bytes 24584 | tf_op jit(solution)/shard_map/ppermute | solution.py:92

commit v8 on v7

--- a/solution.py
+++ b/solution.py
@@ -361,8 +361,7 @@
     c = team(lax.axis_index("fsdp"))
     for source, half in ((own_ref, c), (other_ref, 1 - c)):
         for i in range(0, HALF, PIECE):
-            rows = source[i:i + PIECE, :].astype(jnp.float32)
-            coef_ref[pl.ds(pl.multiple_of(half * HALF + i, 8), PIECE), :] = rows
+            coef_ref[pl.ds(pl.multiple_of(half * HALF + i, 16), PIECE), :] = source[i:i + PIECE, :]
     sum_ref[...] = sq_ref[...] + other_sq_ref[...]
 
 
@@ -377,7 +376,7 @@
     for i in range(TILES):
         cols = slice(i * WIDE, (i + 1) * WIDE)
         feedback = lax.dot_general(
-            ortho, coef_ref[cols, :].astype(jnp.bfloat16), NT, preferred_element_type=jnp.float32
+            ortho, coef_ref[cols, :], NT, preferred_element_type=jnp.float32
         )
         buf[:, cols] = (
             b_ref[:, cols].astype(jnp.float32) - (1.0 - inertia) * feedback
@@ -411,18 +410,18 @@
     moved = moved_ref[...] + other_ref[...]
     squares = (sq_ref[...] + moved[:8, :]) + moved[8:, :]
     norm = 1.0 / jnp.sqrt(jnp.sum(squares, axis=0, keepdims=True) + epsilon_sq)
-    ortho = ortho_ref[...]
+    ortho = (ortho_ref[...].astype(jnp.float32) * norm).astype(jnp.bfloat16)
     copies = []
     for i in range(4):
         at = pl.ds(i * 2 * CHUNK, 2 * CHUNK)
-        sub_buf[at, :] = coef_ref[at, :] * norm
+        sub_buf[at, :] = coef_ref[at, :].astype(jnp.float32) * norm
         copies.append(pltpu.make_async_copy(sub_buf.at[at, :], sub_hbm.at[at, :], sems.at[0, i]))
         copies[-1].start()
     for i, (start, size) in enumerate(STRIPS):
         for first in range(start, start + size, WIDE):
             cols = slice(first, first + WIDE)
             update = lax.dot_general(
-                ortho, sub_buf[cols, :].astype(jnp.bfloat16), NT, preferred_element_type=jnp.float32
+                ortho, coef_ref[cols, :], NT, preferred_element_type=jnp.float32
             )
             buf[:, cols] = (
                 weights_ref[:, cols].astype(jnp.float32) * (1.0 - step_size * shrinkage)
@@ -508,7 +507,7 @@
     )
     opposite = turn_z(squares, (3, 3))
     coef, squares = local(
-        unpack_kernel, [f32(LOCAL_COLS, RANK), f32(8, RANK)],
+        unpack_kernel, [bf16(LOCAL_COLS, RANK), f32(8, RANK)],
         [coef, xor_fsdp(coef, CORE), squares, xor_fsdp(squares, CORE)],
         flops=3328 * 128, nbytes=20000000, name="unpack",
     )

time: 84.3 us -> 84.6 us (level)
  no operation moved by 1% of the time
where the time goes in v8:
time: 84.6 us; the launch traced here: 84.5 us
  starting transfers between devices  37.7 us (45%)
  waiting for transfers between devices  32.2 us (38%)
  Pallas kernels  13.5 us (16%)
  between operations  1.01 us (1%)
    ppermute x6, starting transfers between devices, swap_z(): return lax.ppermute(x, ('fsdp', 'tp'), perm)  11.5 us
    ppermute x8, waiting for transfers between devices, xor_fsdp(): return lax.ppermute(x, 'fsdp', [(i, i ^ mask) for i in range(FSDP)])  9.74 us
    ppermute x6, waiting for transfers between devices, swap_z(): return lax.ppermute(x, ('fsdp', 'tp'), perm)  9 us
    ppermute x6, waiting for transfers between devices, xor_step(): lax.ppermute(x, 'fsdp', [(i, i ^ MASKS[team(i)][k]) for i in range(FSDP)])  8.91 us
    ppermute x8, starting transfers between devices, xor_fsdp(): return lax.ppermute(x, 'fsdp', [(i, i ^ mask) for i in range(FSDP)])  8.38 us
    ppermute x6, starting transfers between devices, xor_step(): lax.ppermute(x, 'fsdp', [(i, i ^ MASKS[team(i)][k]) for i in range(FSDP)])  7.65 us
    pallas_call x20, Pallas kernels, local(): pl.pallas_call(body, in_specs=[VMEM_SPEC] * (used + len(after)), out_spec...  6.91 us
    ppermute x2, starting transfers between devices, turn_z(): return lax.ppermute(x, ('fsdp', 'tp'), perm)  4.52 us
  transfers between devices with their start and end apart: 26, of which 19 were waited for; matrix products, arithmetic and copies ran while one was open for 0% of the time, Pallas kernels for 9%

profile of v8, /device:TPU:1, one launch (start us, length us, event | category | flops | bytes accessed | tf_op | source)
XLA Modules:
  0.0 84.5 jit_solution(14676449655005007350)
XLA Ops:
  0.6 2.9 %project.1 = (bf16[256,3328]{1,0:T(8,128)(2,1)S(1)}, f32[128,128]{1,0:T(8,128)S(1)}, f32[128,128]{1,0:T(8,128)S(1)}) custom-call(bf16[256,3328]{1,0:T(8,128)(2,1)} %m_hbm.1, bf16[256,3328]{1,0:T(8,128)(2,1)} %g_hbm.1, f32[3328,128]{1,0:T(8,128)} %s_hbm.1), custom_call_target="tpu_custom_call" | custom-call | flops 218103808 | bytes 7000000 | tf_op jit(solution)/shard_map/project/pallas_call | solution.py:140
  3.5 6.5 %collective-permute-start = (f32[128,128]{1,0:T(8,128)S(1)}, f32[128,128]{1,0:T(8,128)S(1)}, u32[]{:S(2)}, u32[]{:S(2)}) collective-permute-start(f32[128,128]{1,0:T(8,128)S(1)} %get-tuple-element.18), channel_id=1, source_target_pairs={{0,1},{1,0},{2,3},{3,2},{4,5},{5,4},{6,7},{7,6},{9,10},{10,9},{11,... | collective-permute-start | bytes 196616 | tf_op jit(solution)/shard_map/ppermute | solution.py:72
  10.1 1.6 %collective-permute-done = f32[128,128]{1,0:T(8,128)S(1)} collective-permute-done((f32[128,128]{1,0:T(8,128)S(1)}, f32[128,128]{1,0:T(8,128)S(1)}, u32[]{:S(2)}, u32[]{:S(2)}) %collective-permute-start) | collective-permute-done | bytes 65568 | tf_op jit(solution)/shard_map/ppermute | solution.py:72
  11.8 2.6 %collective-permute-done.3 = f32[128,128]{1,0:T(8,128)S(1)} collective-permute-done((f32[128,128]{1,0:T(8,128)S(1)}, f32[128,128]{1,0:T(8,128)S(1)}, u32[]{:S(2)}, u32[]{:S(2)}) %collective-permute-start.3) | collective-permute-done | bytes 65568 | tf_op jit(solution)/shard_map/ppermute | solution.py:72
  14.9 2.9 %collective-permute-start.2 = (f32[128,128]{1,0:T(8,128)S(1)}, f32[128,128]{1,0:T(8,128)S(1)}, u32[]{:S(2)}, u32[]{:S(2)}) collective-permute-start(f32[128,128]{1,0:T(8,128)S(1)} %add.19), channel_id=1, source_target_pairs={{2,5},{5,2},{1,6},{6,1},{4,7},{7,4},{3,0},{0,3},{11,14},{14,11},{1... | collective-permute-start | bytes 196616 | tf_op jit(solution)/shard_map/ppermute | solution.py:72
  17.8 1.8 %collective-permute-start.5 = (f32[128,128]{1,0:T(8,128)S(1)}, f32[128,128]{1,0:T(8,128)S(1)}, u32[]{:S(2)}, u32[]{:S(2)}) collective-permute-start(f32[128,128]{1,0:T(8,128)S(1)} %add.22), channel_id=1, source_target_pairs={{2,5},{5,2},{1,6},{6,1},{4,7},{7,4},{3,0},{0,3},{11,14},{14,11},{1... | collective-permute-start | bytes 196616 | tf_op jit(solution)/shard_map/ppermute | solution.py:72
  19.7 1.6 %collective-permute-done.2 = f32[128,128]{1,0:T(8,128)S(1)} collective-permute-done((f32[128,128]{1,0:T(8,128)S(1)}, f32[128,128]{1,0:T(8,128)S(1)}, u32[]{:S(2)}, u32[]{:S(2)}) %collective-permute-start.2) | collective-permute-done | bytes 65568 | tf_op jit(solution)/shard_map/ppermute | solution.py:72
  21.2 2.9 %collective-permute-done.5 = f32[128,128]{1,0:T(8,128)S(1)} collective-permute-done((f32[128,128]{1,0:T(8,128)S(1)}, f32[128,128]{1,0:T(8,128)S(1)}, u32[]{:S(2)}, u32[]{:S(2)}) %collective-permute-start.5) | collective-permute-done | bytes 65568 | tf_op jit(solution)/shard_map/ppermute | solution.py:72
  24.7 5.6 %collective-permute-start.6 = (f32[1792,128]{1,0:T(8,128)S(1)}, f32[1792,128]{1,0:T(8,128)S(1)}, u32[]{:S(2)}, u32[]{:S(2)}) collective-permute-start(f32[1792,128]{1,0:T(8,128)S(1)} %lift_send.1.refs_3_.refs_0_), channel_id=1, source_target_pairs={{0,8},{8,0},{16,24},{24,16},{32,40},{40,32},{48,56},{56,48},{64,72... | collective-permute-start | bytes 2752520 | tf_op jit(solution)/shard_map/ppermute | solution.py:92
  30.8 1.6 %collective-permute-done.6.refs_1_ = f32[1792,128]{1,0:T(8,128)S(1)} collective-permute-done((f32[1792,128]{1,0:T(8,128)S(1)}, f32[1792,128]{1,0:T(8,128)S(1)}, u32[]{:S(2)}, u32[]{:S(2)}) %collective-permute-start.6) | collective-permute-done | bytes 917536 | tf_op jit(solution)/shard_map/ppermute | solution.py:92
  32.5 1.6 %collective-permute-start.7 = (f32[832,128]{1,0:T(8,128)S(1)}, f32[832,128]{1,0:T(8,128)S(1)}, u32[]{:S(2)}, u32[]{:S(2)}) collective-permute-start(f32[832,128]{1,0:T(8,128)S(1)} %get-tuple-element.22.refs_2_), channel_id=1, source_target_pairs={{0,24},{8,64},{16,88},{24,0},{32,56},{40,96},{48,120},{56,32},{64,... | collective-permute-start | bytes 1277960 | tf_op jit(solution)/shard_map/ppermute | solution.py:100
  34.1 2.6 %collective-permute-start.9 = (f32[128,128]{1,0:T(8,128)S(1)}, f32[128,128]{1,0:T(8,128)S(1)}, u32[]{:S(2)}, u32[]{:S(2)}) collective-permute-start(f32[128,128]{1,0:T(8,128)S(1)} %gram_pair.1.refs_0_), channel_id=1, source_target_pairs={{56,0},{240,8},{40,16},{224,24},{24,32},{208,40},{8,48},{192,56},{... | collective-permute-start | bytes 196616 | tf_op jit(solution)/shard_map/ppermute | solution.py:96
  36.7 1.9 %collective-permute-start.8 = (f32[128,128]{1,0:T(8,128)S(1)}, f32[128,128]{1,0:T(8,128)S(1)}, u32[]{:S(2)}, u32[]{:S(2)}) collective-permute-start(f32[128,128]{1,0:T(8,128)S(1)} %gram_pair.1.refs_0_), channel_id=1, source_target_pairs={{0,200},{8,192},{16,216},{24,208},{32,232},{40,224},{48,248},{56,2... | collective-permute-start | bytes 196616 | tf_op jit(solution)/shard_map/ppermute | solution.py:92
  38.6 2.6 %collective-permute-done.9.refs_2_ = f32[128,128]{1,0:T(8,128)S(1)} collective-permute-done((f32[128,128]{1,0:T(8,128)S(1)}, f32[128,128]{1,0:T(8,128)S(1)}, u32[]{:S(2)}, u32[]{:S(2)}) %collective-permute-start.9) | collective-permute-done | bytes 65568 | tf_op jit(solution)/shard_map/ppermute | solution.py:96
  42.6 2.9 %collective-permute-start.11 = (f32[416,128]{1,0:T(8,128)S(1)}, f32[416,128]{1,0:T(8,128)S(1)}, u32[]{:S(2)}, u32[]{:S(2)}) collective-permute-start(f32[416,128]{1,0:T(8,128)S(1)} %get-tuple-element.24.refs_1_), channel_id=1, source_target_pairs={{0,56},{8,192},{16,216},{24,32},{32,24},{40,224},{48,248},{56,0},{... | collective-permute-start | bytes 638984 | tf_op jit(solution)/shard_map/ppermute | solution.py:100
  45.6 4.7 %collective-permute-done.13.refs_3_.refs_1_ = f32[128,128]{1,0:T(8,128)S(1)} collective-permute-done((f32[128,128]{1,0:T(8,128)S(1)}, f32[128,128]{1,0:T(8,128)S(1)}, u32[]{:S(2)}, u32[]{:S(2)}) %collective-permute-start.13) | collective-permute-done | bytes 65568 | tf_op jit(solution)/shard_map/ppermute | solution.py:92
  50.9 1.8 %collective-permute-start.14 = (f32[416,128]{1,0:T(8,128)S(1)}, f32[416,128]{1,0:T(8,128)S(1)}, u32[]{:S(2)}, u32[]{:S(2)}) collective-permute-start(f32[416,128]{1,0:T(8,128)S(1)} %first_sum.1.refs_1_.refs_4_.refs_0_), channel_id=1, source_target_pairs={{0,200},{8,48},{16,40},{24,208},{32,232},{40,16},{48,8},{56,240},{... | collective-permute-start | bytes 638984 | tf_op jit(solution)/shard_map/ppermute | solution.py:100
  52.7 1.2 %collective-permute-done.15.refs_3_ = f32[128,128]{1,0:T(8,128)S(1)} collective-permute-done((f32[128,128]{1,0:T(8,128)S(1)}, f32[128,128]{1,0:T(8,128)S(1)}, u32[]{:S(2)}, u32[]{:S(2)}) %collective-permute-start.15) | collective-permute-done | bytes 65568 | tf_op jit(solution)/shard_map/ppermute | solution.py:92
  53.9 2.1 %eliminate0.1.refs_2_.refs_0_ = f32[128,128]{1,0:T(8,128)S(1)} custom-call(f32[128,128]{1,0:T(8,128)S(1)} %gram_four.3.refs_0_.refs_1_, f32[128,128]{1,0:T(8,128)S(1)} %gram_four.3.refs_0_.refs_1_), custom_call_target="tpu_custom_call" | custom-call | flops 4000000 | bytes 6000000 | tf_op jit(solution)/shard_map/eliminate0/pallas_call | solution.py:164
  56.1 1.4 %collective-permute-done.14.refs_1_ = f32[416,128]{1,0:T(8,128)S(1)} collective-permute-done((f32[416,128]{1,0:T(8,128)S(1)}, f32[416,128]{1,0:T(8,128)S(1)}, u32[]{:S(2)}, u32[]{:S(2)}) %collective-permute-start.14) | collective-permute-done | bytes 213024 | tf_op jit(solution)/shard_map/ppermute | solution.py:100
  57.6 2.6 %eliminate40.1.refs_2_ = f32[128,128]{1,0:T(8,128)S(1)} custom-call(f32[128,128]{1,0:T(8,128)S(1)} %eliminate0.1.refs_2_.refs_0_, f32[128,128]{1,0:T(8,128)S(1)} %gram_four.3.refs_0_.refs_1_, f32[416,128]{1,0:T(8,128)S(1)} %second_sum.1.refs_2_.refs_0_), custom_call_target="tpu_custom_call" | custom-call | flops 4000000 | bytes 13200000 | tf_op jit(solution)/shard_map/eliminate40/pallas_call | solution.py:164
  60.2 2.7 %collective-permute-done.16.refs_1_ = f32[416,128]{1,0:T(8,128)S(1)} collective-permute-done((f32[416,128]{1,0:T(8,128)S(1)}, f32[416,128]{1,0:T(8,128)S(1)}, u32[]{:S(2)}, u32[]{:S(2)}) %collective-permute-start.16) | collective-permute-done | bytes 213024 | tf_op jit(solution)/shard_map/ppermute | solution.py:100
  63.1 1.2 %collective-permute-start.17 = (bf16[416,128]{1,0:T(8,128)(2,1)S(1)}, bf16[416,128]{1,0:T(8,128)(2,1)S(1)}, u32[]{:S(2)}, u32[]{:S(2)}) collective-permute-start(bf16[416,128]{1,0:T(8,128)(2,1)S(1)} %block.1.refs_3_.refs_0_), channel_id=1, source_target_pairs={{0,56},{8,192},{16,216},{24,32},{32,24},{40,224},{48,248},{56,0},{... | collective-permute-start | bytes 319496 | tf_op jit(solution)/shard_map/ppermute | solution.py:100
  64.6 3.9 %collective-permute-done.17.refs_1_ = bf16[416,128]{1,0:T(8,128)(2,1)S(1)} collective-permute-done((bf16[416,128]{1,0:T(8,128)(2,1)S(1)}, bf16[416,128]{1,0:T(8,128)(2,1)S(1)}, u32[]{:S(2)}, u32[]{:S(2)}) %collective-permute-start.17) | collective-permute-done | bytes 106528 | tf_op jit(solution)/shard_map/ppermute | solution.py:100
  69.5 2.3 %collective-permute-start.19 = (f32[8,128]{1,0:T(8,128)S(1)}, f32[8,128]{1,0:T(8,128)S(1)}, u32[]{:S(2)}, u32[]{:S(2)}) collective-permute-start(f32[8,128]{1,0:T(8,128)S(1)} %squares.1.refs_2_), channel_id=1, source_target_pairs={{0,1},{1,0},{2,3},{3,2},{4,5},{5,4},{6,7},{7,6},{8,9},{9,8},{10,11... | collective-permute-start | bytes 12296 | tf_op jit(solution)/shard_map/ppermute | solution.py:80
  71.8 1.1 %collective-permute-done.20.refs_4_ = f32[8,128]{1,0:T(8,128)S(1)} collective-permute-done((f32[8,128]{1,0:T(8,128)S(1)}, f32[8,128]{1,0:T(8,128)S(1)}, u32[]{:S(2)}, u32[]{:S(2)}) %collective-permute-start.20) | collective-permute-done | bytes 4128 | tf_op jit(solution)/shard_map/ppermute | solution.py:80
  73.1 0.9 %collective-permute-done.18.refs_1_ = bf16[832,128]{1,0:T(8,128)(2,1)S(1)} collective-permute-done((bf16[832,128]{1,0:T(8,128)(2,1)S(1)}, bf16[832,128]{1,0:T(8,128)(2,1)S(1)}, u32[]{:S(2)}, u32[]{:S(2)}) %collective-permute-start.18) | collective-permute-done | bytes 213024 | tf_op jit(solution)/shard_map/ppermute | solution.py:100
  74.7 1.7 %collective-permute-start.23 = (f32[8,128]{1,0:T(8,128)S(1)}, f32[8,128]{1,0:T(8,128)S(1)}, u32[]{:S(2)}, u32[]{:S(2)}) collective-permute-start(f32[8,128]{1,0:T(8,128)S(1)} %get-tuple-element.26.refs_2_), channel_id=1, source_target_pairs={{13,0},{12,1},{15,2},{14,3},{9,4},{8,5},{11,6},{10,7},{5,8},{4,9},... | collective-permute-start | bytes 12296 | tf_op jit(solution)/shard_map/ppermute | solution.py:88
  76.5 2.8 %collective-permute-start.24 = (f32[8,128]{1,0:T(8,128)S(1)}, f32[8,128]{1,0:T(8,128)S(1)}, u32[]{:S(2)}, u32[]{:S(2)}) collective-permute-start(f32[8,128]{1,0:T(8,128)S(1)} %get-tuple-element.29.sq_ref), channel_id=1, source_target_pairs={{15,0},{10,1},{9,2},{12,3},{11,4},{14,5},{13,6},{8,7},{2,8},{7,9},... | collective-permute-start | bytes 12296 | tf_op jit(solution)/shard_map/ppermute | solution.py:88
  79.4 1.5 %finish_momentum.1 = (bf16[256,3328]{1,0:T(8,128)(2,1)}, f32[8,128]{1,0:T(8,128)S(1)}) custom-call(bf16[3328,128]{1,0:T(8,128)(2,1)S(1)} %get-tuple-element.27.coef_ref, bf16[256,128]{1,0:T(8,128)(2,1)S(1)} %ortho.1.refs_2_.ortho_ref, bf16[256,3328]{1,0:T(8,128)(2,1)S(1)} %get-tuple-element.20.refs_2_.b_ref), custom_call_target="tpu_custom_call" | custom-call | flops 218103808 | bytes 5000000 | tf_op jit(solution)/shard_map/finish_momentum/pallas_call | solution.py:393
  81.2 1.0 %collective-permute-done.25.other_ref = f32[16,128]{1,0:T(8,128)S(1)} collective-permute-done((f32[16,128]{1,0:T(8,128)S(1)}, f32[16,128]{1,0:T(8,128)S(1)}, u32[]{:S(2)}, u32[]{:S(2)}) %collective-permute-start.25) | collective-permute-done | bytes 8224 | tf_op jit(solution)/shard_map/ppermute | solution.py:92
  82.2 2.1 %finish_weights.1 = (bf16[256,3328]{1,0:T(8,128)(2,1)}, f32[3328,128]{1,0:T(8,128)}) custom-call(f32[8,128]{1,0:T(8,128)S(1)} %get-tuple-element.29.sq_ref, f32[16,128]{1,0:T(8,128)S(1)} %stack.1.moved_ref, f32[16,128]{1,0:T(8,128)S(1)} %collective-permute-done.25.other_ref, bf16[3328,128]{1,0:T(8,128)(2,1)S(1)} %get-tuple-element.27.coef_ref, ...), custom_call_target="tpu_custom_call" | custom-call | flops 218103808 | bytes 7000000 | tf_op jit(solution)/shard_map/finish_weights/pallas_call | solution.py:438
  (51 shorter events, 7.0 us)
Async XLA Ops:
  3.5 8.1 %collective-permute-start = (f32[128,128]{1,0:T(8,128)S(1)}, f32[128,128]{1,0:T(8,128)S(1)}, u32[]{:S(2)}, u32[]{:S(2)}) collective-permute-start(f32[128,128]{1,0:T(8,128)S(1)} %get-tuple-element.18), channel_id=1, source_target_pairs={{0,1},{1,0},{2,3},{3,2},{4,5},{5,4},{6,7},{7,6},{9,10},{10,9},{11,... | collective-permute-start | bytes 196616 | tf_op jit(solution)/shard_map/ppermute | solution.py:72
  10.0 4.3 %collective-permute-start.3 = (f32[128,128]{1,0:T(8,128)S(1)}, f32[128,128]{1,0:T(8,128)S(1)}, u32[]{:S(2)}, u32[]{:S(2)}) collective-permute-start(f32[128,128]{1,0:T(8,128)S(1)} %get-tuple-element.19), channel_id=1, source_target_pairs={{0,1},{1,0},{2,3},{3,2},{4,5},{5,4},{6,7},{7,6},{9,10},{10,9},{11,... | collective-permute-start | bytes 196616 | tf_op jit(solution)/shard_map/ppermute | solution.py:72
  11.7 3.2 %collective-permute-start.1 = (f32[128,128]{1,0:T(8,128)S(1)}, f32[128,128]{1,0:T(8,128)S(1)}, u32[]{:S(2)}, u32[]{:S(2)}) collective-permute-start(f32[128,128]{1,0:T(8,128)S(1)} %add.18), channel_id=1, source_target_pairs={{1,2},{2,1},{3,4},{4,3},{5,6},{6,5},{7,0},{0,7},{10,11},{11,10},{1... | collective-permute-start | bytes 196616 | tf_op jit(solution)/shard_map/ppermute | solution.py:72
  14.4 3.5 %collective-permute-start.4 = (f32[128,128]{1,0:T(8,128)S(1)}, f32[128,128]{1,0:T(8,128)S(1)}, u32[]{:S(2)}, u32[]{:S(2)}) collective-permute-start(f32[128,128]{1,0:T(8,128)S(1)} %add.21), channel_id=1, source_target_pairs={{1,2},{2,1},{3,4},{4,3},{5,6},{6,5},{7,0},{0,7},{10,11},{11,10},{1... | collective-permute-start | bytes 196616 | tf_op jit(solution)/shard_map/ppermute | solution.py:72
  14.9 6.3 %collective-permute-start.2 = (f32[128,128]{1,0:T(8,128)S(1)}, f32[128,128]{1,0:T(8,128)S(1)}, u32[]{:S(2)}, u32[]{:S(2)}) collective-permute-start(f32[128,128]{1,0:T(8,128)S(1)} %add.19), channel_id=1, source_target_pairs={{2,5},{5,2},{1,6},{6,1},{4,7},{7,4},{3,0},{0,3},{11,14},{14,11},{1... | collective-permute-start | bytes 196616 | tf_op jit(solution)/shard_map/ppermute | solution.py:72
  17.8 6.3 %collective-permute-start.5 = (f32[128,128]{1,0:T(8,128)S(1)}, f32[128,128]{1,0:T(8,128)S(1)}, u32[]{:S(2)}, u32[]{:S(2)}) collective-permute-start(f32[128,128]{1,0:T(8,128)S(1)} %add.22), channel_id=1, source_target_pairs={{2,5},{5,2},{1,6},{6,1},{4,7},{7,4},{3,0},{0,3},{11,14},{14,11},{1... | collective-permute-start | bytes 196616 | tf_op jit(solution)/shard_map/ppermute | solution.py:72
  24.7 7.7 %collective-permute-start.6 = (f32[1792,128]{1,0:T(8,128)S(1)}, f32[1792,128]{1,0:T(8,128)S(1)}, u32[]{:S(2)}, u32[]{:S(2)}) collective-permute-start(f32[1792,128]{1,0:T(8,128)S(1)} %lift_send.1.refs_3_.refs_0_), channel_id=1, source_target_pairs={{0,8},{8,0},{16,24},{24,16},{32,40},{40,32},{48,56},{56,48},{64,72... | collective-permute-start | bytes 2752520 | tf_op jit(solution)/shard_map/ppermute | solution.py:92
  32.5 10.1 %collective-permute-start.7 = (f32[832,128]{1,0:T(8,128)S(1)}, f32[832,128]{1,0:T(8,128)S(1)}, u32[]{:S(2)}, u32[]{:S(2)}) collective-permute-start(f32[832,128]{1,0:T(8,128)S(1)} %get-tuple-element.22.refs_2_), channel_id=1, source_target_pairs={{0,24},{8,64},{16,88},{24,0},{32,56},{40,96},{48,120},{56,32},{64,... | collective-permute-start | bytes 1277960 | tf_op jit(solution)/shard_map/ppermute | solution.py:100
  34.1 7.1 %collective-permute-start.9 = (f32[128,128]{1,0:T(8,128)S(1)}, f32[128,128]{1,0:T(8,128)S(1)}, u32[]{:S(2)}, u32[]{:S(2)}) collective-permute-start(f32[128,128]{1,0:T(8,128)S(1)} %gram_pair.1.refs_0_), channel_id=1, source_target_pairs={{56,0},{240,8},{40,16},{224,24},{24,32},{208,40},{8,48},{192,56},{... | collective-permute-start | bytes 196616 | tf_op jit(solution)/shard_map/ppermute | solution.py:96
  36.7 5.2 %collective-permute-start.8 = (f32[128,128]{1,0:T(8,128)S(1)}, f32[128,128]{1,0:T(8,128)S(1)}, u32[]{:S(2)}, u32[]{:S(2)}) collective-permute-start(f32[128,128]{1,0:T(8,128)S(1)} %gram_pair.1.refs_0_), channel_id=1, source_target_pairs={{0,200},{8,192},{16,216},{24,208},{32,232},{40,224},{48,248},{56,2... | collective-permute-start | bytes 196616 | tf_op jit(solution)/shard_map/ppermute | solution.py:92
  41.3 1.3 %collective-permute-start.10 = (f32[128,128]{1,0:T(8,128)S(1)}, f32[128,128]{1,0:T(8,128)S(1)}, u32[]{:S(2)}, u32[]{:S(2)}) collective-permute-start(f32[128,128]{1,0:T(8,128)S(1)} %collective-permute-done.9.refs_2_), channel_id=1, source_target_pairs={{0,8},{8,0},{16,24},{24,16},{32,40},{40,32},{48,56},{56,48},{64,72... | collective-permute-start | bytes 196616 | tf_op jit(solution)/shard_map/ppermute | solution.py:92
  42.6 8.2 %collective-permute-start.11 = (f32[416,128]{1,0:T(8,128)S(1)}, f32[416,128]{1,0:T(8,128)S(1)}, u32[]{:S(2)}, u32[]{:S(2)}) collective-permute-start(f32[416,128]{1,0:T(8,128)S(1)} %get-tuple-element.24.refs_1_), channel_id=1, source_target_pairs={{0,56},{8,192},{16,216},{24,32},{32,24},{40,224},{48,248},{56,0},{... | collective-permute-start | bytes 638984 | tf_op jit(solution)/shard_map/ppermute | solution.py:100
  45.5 4.8 %collective-permute-start.13 = (f32[128,128]{1,0:T(8,128)S(1)}, f32[128,128]{1,0:T(8,128)S(1)}, u32[]{:S(2)}, u32[]{:S(2)}) collective-permute-start(f32[128,128]{1,0:T(8,128)S(1)} %hold.1.refs_0_), channel_id=1, source_target_pairs={{0,80},{8,88},{16,64},{24,72},{32,112},{40,120},{48,96},{56,104},{... | collective-permute-start | bytes 196616 | tf_op jit(solution)/shard_map/ppermute | solution.py:92
  45.5 5.3 %collective-permute-start.12 = (f32[128,128]{1,0:T(8,128)S(1)}, f32[128,128]{1,0:T(8,128)S(1)}, u32[]{:S(2)}, u32[]{:S(2)}) collective-permute-start(f32[128,128]{1,0:T(8,128)S(1)} %hold.1.refs_0_), channel_id=1, source_target_pairs={{24,0},{64,8},{8,16},{80,24},{56,32},{96,40},{40,48},{112,56},{88,... | collective-permute-start | bytes 196616 | tf_op jit(solution)/shard_map/ppermute | solution.py:96
  50.9 6.6 %collective-permute-start.14 = (f32[416,128]{1,0:T(8,128)S(1)}, f32[416,128]{1,0:T(8,128)S(1)}, u32[]{:S(2)}, u32[]{:S(2)}) collective-permute-start(f32[416,128]{1,0:T(8,128)S(1)} %first_sum.1.refs_1_.refs_4_.refs_0_), channel_id=1, source_target_pairs={{0,200},{8,48},{16,40},{24,208},{32,232},{40,16},{48,8},{56,240},{... | collective-permute-start | bytes 638984 | tf_op jit(solution)/shard_map/ppermute | solution.py:100
  52.6 1.3 %collective-permute-start.15 = (f32[128,128]{1,0:T(8,128)S(1)}, f32[128,128]{1,0:T(8,128)S(1)}, u32[]{:S(2)}, u32[]{:S(2)}) collective-permute-start(f32[128,128]{1,0:T(8,128)S(1)} %hold_split.1.refs_2_), channel_id=1, source_target_pairs={{0,8},{8,0},{16,24},{24,16},{32,40},{40,32},{48,56},{56,48},{64,72... | collective-permute-start | bytes 196616 | tf_op jit(solution)/shard_map/ppermute | solution.py:92
  57.5 5.4 %collective-permute-start.16 = (f32[416,128]{1,0:T(8,128)S(1)}, f32[416,128]{1,0:T(8,128)S(1)}, u32[]{:S(2)}, u32[]{:S(2)}) collective-permute-start(f32[416,128]{1,0:T(8,128)S(1)} %second_sum.1.refs_2_.refs_0_), channel_id=1, source_target_pairs={{0,72},{8,16},{16,8},{24,80},{32,104},{40,48},{48,40},{56,112},{64... | collective-permute-start | bytes 638984 | tf_op jit(solution)/shard_map/ppermute | solution.py:100
  63.1 5.4 %collective-permute-start.17 = (bf16[416,128]{1,0:T(8,128)(2,1)S(1)}, bf16[416,128]{1,0:T(8,128)(2,1)S(1)}, u32[]{:S(2)}, u32[]{:S(2)}) collective-permute-start(bf16[416,128]{1,0:T(8,128)(2,1)S(1)} %block.1.refs_3_.refs_0_), channel_id=1, source_target_pairs={{0,56},{8,192},{16,216},{24,32},{32,24},{40,224},{48,248},{56,0},{... | collective-permute-start | bytes 319496 | tf_op jit(solution)/shard_map/ppermute | solution.py:100
  68.6 5.4 %collective-permute-start.18 = (bf16[832,128]{1,0:T(8,128)(2,1)S(1)}, bf16[832,128]{1,0:T(8,128)(2,1)S(1)}, u32[]{:S(2)}, u32[]{:S(2)}) collective-permute-start(bf16[832,128]{1,0:T(8,128)(2,1)S(1)} %join1.1.refs_0_), channel_id=1, source_target_pairs={{0,24},{8,64},{16,88},{24,0},{32,56},{40,96},{48,120},{56,32},{64,... | collective-permute-start | bytes 638984 | tf_op jit(solution)/shard_map/ppermute | solution.py:100
  68.8 4.1 %collective-permute-start.20 = (f32[8,128]{1,0:T(8,128)S(1)}, f32[8,128]{1,0:T(8,128)S(1)}, u32[]{:S(2)}, u32[]{:S(2)}) collective-permute-start(f32[8,128]{1,0:T(8,128)S(1)} %squares.1.refs_2_), channel_id=1, source_target_pairs={{0,25},{1,24},{2,27},{3,26},{4,29},{5,28},{6,31},{7,30},{8,65},{9,... | collective-permute-start | bytes 12296 | tf_op jit(solution)/shard_map/ppermute | solution.py:80
  69.5 3.6 %collective-permute-start.19 = (f32[8,128]{1,0:T(8,128)S(1)}, f32[8,128]{1,0:T(8,128)S(1)}, u32[]{:S(2)}, u32[]{:S(2)}) collective-permute-start(f32[8,128]{1,0:T(8,128)S(1)} %squares.1.refs_2_), channel_id=1, source_target_pairs={{0,1},{1,0},{2,3},{3,2},{4,5},{5,4},{6,7},{7,6},{8,9},{9,8},{10,11... | collective-permute-start | bytes 12296 | tf_op jit(solution)/shard_map/ppermute | solution.py:80
  74.1 2.3 %collective-permute-start.21 = (bf16[1664,128]{1,0:T(8,128)(2,1)S(1)}, bf16[1664,128]{1,0:T(8,128)(2,1)S(1)}, u32[]{:S(2)}, u32[]{:S(2)}) collective-permute-start(bf16[1664,128]{1,0:T(8,128)(2,1)S(1)} %get-tuple-element.25.refs_0_), channel_id=1, source_target_pairs={{0,8},{8,0},{16,24},{24,16},{32,40},{40,32},{48,56},{56,48},{64,72... | collective-permute-start | bytes 1277960 | tf_op jit(solution)/shard_map/ppermute | solution.py:92
  74.6 7.6 %copy-start = (bf16[256,3328]{1,0:T(8,128)(2,1)S(1)}, bf16[256,3328]{1,0:T(8,128)(2,1)}, u32[]{:S(2)}) copy-start(bf16[256,3328]{1,0:T(8,128)(2,1)} %weights_ref.1) | copy-start | bytes 5111812
  74.6 1.8 %collective-permute-start.22 = (f32[8,128]{1,0:T(8,128)S(1)}, f32[8,128]{1,0:T(8,128)S(1)}, u32[]{:S(2)}, u32[]{:S(2)}) collective-permute-start(f32[8,128]{1,0:T(8,128)S(1)} %get-tuple-element.26.refs_2_), channel_id=1, source_target_pairs={{0,8},{8,0},{16,24},{24,16},{32,40},{40,32},{48,56},{56,48},{64,72... | collective-permute-start | bytes 12296 | tf_op jit(solution)/shard_map/ppermute | solution.py:92
  74.7 6.2 %collective-permute-start.23 = (f32[8,128]{1,0:T(8,128)S(1)}, f32[8,128]{1,0:T(8,128)S(1)}, u32[]{:S(2)}, u32[]{:S(2)}) collective-permute-start(f32[8,128]{1,0:T(8,128)S(1)} %get-tuple-element.26.refs_2_), channel_id=1, source_target_pairs={{13,0},{12,1},{15,2},{14,3},{9,4},{8,5},{11,6},{10,7},{5,8},{4,9},... | collective-permute-start | bytes 12296 | tf_op jit(solution)/shard_map/ppermute | solution.py:88
  76.5 4.4 %collective-permute-start.24 = (f32[8,128]{1,0:T(8,128)S(1)}, f32[8,128]{1,0:T(8,128)S(1)}, u32[]{:S(2)}, u32[]{:S(2)}) collective-permute-start(f32[8,128]{1,0:T(8,128)S(1)} %get-tuple-element.29.sq_ref), channel_id=1, source_target_pairs={{15,0},{10,1},{9,2},{12,3},{11,4},{14,5},{13,6},{8,7},{2,8},{7,9},... | collective-permute-start | bytes 12296 | tf_op jit(solution)/shard_map/ppermute | solution.py:88
  80.9 1.3 %collective-permute-start.25 = (f32[16,128]{1,0:T(8,128)S(1)}, f32[16,128]{1,0:T(8,128)S(1)}, u32[]{:S(2)}, u32[]{:S(2)}) collective-permute-start(f32[16,128]{1,0:T(8,128)S(1)} %stack.1.moved_ref), channel_id=1, source_target_pairs={{0,8},{8,0},{16,24},{24,16},{32,40},{40,32},{48,56},{56,48},{64,72... | collective-permute-start | bytes 24584 | tf_op jit(solution)/shard_map/ppermute | solution.py:92

commit v9 on v7

--- a/solution.py
+++ b/solution.py
@@ -28,7 +28,7 @@
 CUT = 40
 WIDE = 256
 TILES = LOCAL_COLS // WIDE
-STRIPS = ((0, 512), (512, 768), (1280, 768), (2048, 768), (2816, 512))
+STRIPS = ((0, 512), (512, 768), (1280, 768), (2048, 768), (2816, 256), (3072, 256))
 
 X_ONE, Y_ONE, X_THREE, Y_THREE, CORE = 3, 9, 7, 25, 1
 MASKS = ((X_ONE, X_THREE, Y_THREE, Y_ONE), (Y_ONE, Y_THREE, X_THREE, X_ONE))
@@ -249,7 +249,7 @@
     return lax.rsqrt(jnp.sum(diagonal, axis=0, keepdims=True))
 
 
-def eliminate_kernel(start, stop, in_ref, gram_ref, out_ref):
+def eliminate_kernel(start, stop, in_ref, gram_ref, out_ref, terms_ref=None):
     groups = RANK // 8
     lane = lax.broadcasted_iota(jnp.int32, (8, RANK), 1)
     sub = lax.broadcasted_iota(jnp.int32, (8, RANK), 0)
@@ -305,27 +305,30 @@
             out_ref[8 * k:8 * k + 8, :] = unit * lax.rsqrt(pivot) * scale
         else:
             out_ref[8 * k:8 * k + 8, :] = t[k]
+    if stop == RANK:
+        w = out_ref[...].T
+        w_high = w.astype(jnp.bfloat16)
+        w_low = (w - w_high.astype(jnp.float32)).astype(jnp.bfloat16)
+        terms_ref[:RANK, :] = jnp.concatenate([w_high, w_low], axis=1)
+        terms_ref[RANK:, :] = jnp.concatenate([w_high, jnp.zeros_like(w_low)], axis=1)
 
 
 def eliminate(start, stop, state, gram, after=()):
+    shape = f32(RANK, RANK)
     return local(
-        functools.partial(eliminate_kernel, start, stop), f32(RANK, RANK), [state, gram], after,
+        functools.partial(eliminate_kernel, start, stop),
+        [shape, bf16(2 * RANK, 2 * RANK)] if stop == RANK else shape, [state, gram], after,
         flops=4000000, nbytes=(stop - start) * 150000, name=f"eliminate{start}",
     )
 
 
-def block_kernel(keep_ref, recv_ref, w_ref, out_ref):
-    w = w_ref[...].T
-    w_high = w.astype(jnp.bfloat16)
-    w_low = (w - w_high.astype(jnp.float32)).astype(jnp.bfloat16)
-    both = jnp.concatenate([
-        jnp.concatenate([w_high, w_low], axis=1),
-        jnp.concatenate([w_high, jnp.zeros_like(w_low)], axis=1),
-    ], axis=0)
+def block_kernel(keep_ref, recv_ref, terms_ref, out_ref):
     d = keep_ref[...] + recv_ref[...]
     high = d.astype(jnp.bfloat16)
     low = (d - high.astype(jnp.float32)).astype(jnp.bfloat16)
-    out = jnp.dot(jnp.concatenate([high, low], axis=1), both, preferred_element_type=jnp.float32)
+    out = jnp.dot(
+        jnp.concatenate([high, low], axis=1), terms_ref[...], preferred_element_type=jnp.float32
+    )
     out_ref[...] = (out[:, :RANK] + out[:, RANK:]).astype(jnp.bfloat16)
 
 
@@ -357,13 +360,12 @@
     sum_ref[...] = (sq_ref[...] + other) + (pair_ref[...] + cross_ref[...])
 
 
-def unpack_kernel(own_ref, other_ref, sq_ref, other_sq_ref, coef_ref, sum_ref):
+def unpack_kernel(own_ref, other_ref, coef_ref):
     c = team(lax.axis_index("fsdp"))
     for source, half in ((own_ref, c), (other_ref, 1 - c)):
         for i in range(0, HALF, PIECE):
             rows = source[i:i + PIECE, :].astype(jnp.float32)
             coef_ref[pl.ds(pl.multiple_of(half * HALF + i, 8), PIECE), :] = rows
-    sum_ref[...] = sq_ref[...] + other_sq_ref[...]
 
 
 def stack_kernel(opposite_ref, next_ref, out_ref):
@@ -484,10 +486,10 @@
     state = eliminate(0, CUT, gram, gram)
     d = add(d, recv, [state], "second_sum")
     recv = xor_step(d, 3)
-    inverse = eliminate(CUT, RANK, state, gram, [d])
+    inverse, terms = eliminate(CUT, RANK, state, gram, [d])
 
     coef = local(
-        block_kernel, bf16(CHUNK, RANK), [d, recv, inverse],
+        block_kernel, bf16(CHUNK, RANK), [d, recv, terms],
         flops=2 * CHUNK * 256 * 256, nbytes=700000, name="block",
     )
     ortho = local(
@@ -507,10 +509,11 @@
         nbytes=CHUNK * 4096, name="join0",
     )
     opposite = turn_z(squares, (3, 3))
-    coef, squares = local(
-        unpack_kernel, [f32(LOCAL_COLS, RANK), f32(8, RANK)],
-        [coef, xor_fsdp(coef, CORE), squares, xor_fsdp(squares, CORE)],
-        flops=3328 * 128, nbytes=20000000, name="unpack",
+    other = xor_fsdp(coef, CORE)
+    squares = add(squares, xor_fsdp(squares, CORE), [], "add_core")
+    coef = local(
+        unpack_kernel, f32(LOCAL_COLS, RANK), [coef, other], [squares],
+        flops=3328 * 128, nbytes=2600000, name="unpack",
     )
     new_momentum, done = finish_momentum(coef, ortho, blended)
     moved = local(

time: 84.3 us -> 84.4 us (level)
    pallas_call x20 -> x21, Pallas kernels: 6.97 us -> 6.95 us  [local(): pl.pallas_call(body, in_specs=[VMEM_SPEC] * (used + len(after)), out_spec...]
where the time goes in v9:
time: 84.4 us; the launch traced here: 84.3 us
  starting transfers between devices  37.7 us (45%)
  waiting for transfers between devices  32.1 us (38%)
  Pallas kernels  13.5 us (16%)
  between operations  1.02 us (1%)
    ppermute x6, starting transfers between devices, swap_z(): return lax.ppermute(x, ('fsdp', 'tp'), perm)  11.5 us
    ppermute x8, waiting for transfers between devices, xor_fsdp(): return lax.ppermute(x, 'fsdp', [(i, i ^ mask) for i in range(FSDP)])  9.73 us
    ppermute x6, waiting for transfers between devices, swap_z(): return lax.ppermute(x, ('fsdp', 'tp'), perm)  9 us
    ppermute x6, waiting for transfers between devices, xor_step(): lax.ppermute(x, 'fsdp', [(i, i ^ MASKS[team(i)][k]) for i in range(FSDP)])  8.85 us
    ppermute x8, starting transfers between devices, xor_fsdp(): return lax.ppermute(x, 'fsdp', [(i, i ^ mask) for i in range(FSDP)])  8.4 us
    ppermute x6, starting transfers between devices, xor_step(): lax.ppermute(x, 'fsdp', [(i, i ^ MASKS[team(i)][k]) for i in range(FSDP)])  7.63 us
    pallas_call x21, Pallas kernels, local(): pl.pallas_call(body, in_specs=[VMEM_SPEC] * (used + len(after)), out_spec...  6.95 us
    ppermute x2, starting transfers between devices, turn_z(): return lax.ppermute(x, ('fsdp', 'tp'), perm)  4.44 us
  transfers between devices with their start and end apart: 26, of which 19 were waited for; matrix products, arithmetic and copies ran while one was open for 0% of the time, Pallas kernels for 9%

profile of v9, /device:TPU:1, one launch (start us, length us, event | category | flops | bytes accessed | tf_op | source)
XLA Modules:
  0.0 84.3 jit_solution(7166352867752204211)
XLA Ops:
  0.6 3.1 %project.1 = (bf16[256,3328]{1,0:T(8,128)(2,1)S(1)}, f32[128,128]{1,0:T(8,128)S(1)}, f32[128,128]{1,0:T(8,128)S(1)}) custom-call(bf16[256,3328]{1,0:T(8,128)(2,1)} %m_hbm.1, bf16[256,3328]{1,0:T(8,128)(2,1)} %g_hbm.1, f32[3328,128]{1,0:T(8,128)} %s_hbm.1), custom_call_target="tpu_custom_call" | custom-call | flops 218103808 | bytes 7000000 | tf_op jit(solution)/shard_map/project/pallas_call | solution.py:140
  3.7 6.5 %collective-permute-start = (f32[128,128]{1,0:T(8,128)S(1)}, f32[128,128]{1,0:T(8,128)S(1)}, u32[]{:S(2)}, u32[]{:S(2)}) collective-permute-start(f32[128,128]{1,0:T(8,128)S(1)} %get-tuple-element.18), channel_id=1, source_target_pairs={{0,1},{1,0},{2,3},{3,2},{4,5},{5,4},{6,7},{7,6},{9,10},{10,9},{11,... | collective-permute-start | bytes 196616 | tf_op jit(solution)/shard_map/ppermute | solution.py:72
  10.3 1.6 %collective-permute-done = f32[128,128]{1,0:T(8,128)S(1)} collective-permute-done((f32[128,128]{1,0:T(8,128)S(1)}, f32[128,128]{1,0:T(8,128)S(1)}, u32[]{:S(2)}, u32[]{:S(2)}) %collective-permute-start) | collective-permute-done | bytes 65568 | tf_op jit(solution)/shard_map/ppermute | solution.py:72
  12.0 2.6 %collective-permute-done.3 = f32[128,128]{1,0:T(8,128)S(1)} collective-permute-done((f32[128,128]{1,0:T(8,128)S(1)}, f32[128,128]{1,0:T(8,128)S(1)}, u32[]{:S(2)}, u32[]{:S(2)}) %collective-permute-start.3) | collective-permute-done | bytes 65568 | tf_op jit(solution)/shard_map/ppermute | solution.py:72
  15.1 2.9 %collective-permute-start.2 = (f32[128,128]{1,0:T(8,128)S(1)}, f32[128,128]{1,0:T(8,128)S(1)}, u32[]{:S(2)}, u32[]{:S(2)}) collective-permute-start(f32[128,128]{1,0:T(8,128)S(1)} %add.19), channel_id=1, source_target_pairs={{2,5},{5,2},{1,6},{6,1},{4,7},{7,4},{3,0},{0,3},{11,14},{14,11},{1... | collective-permute-start | bytes 196616 | tf_op jit(solution)/shard_map/ppermute | solution.py:72
  18.0 1.8 %collective-permute-start.5 = (f32[128,128]{1,0:T(8,128)S(1)}, f32[128,128]{1,0:T(8,128)S(1)}, u32[]{:S(2)}, u32[]{:S(2)}) collective-permute-start(f32[128,128]{1,0:T(8,128)S(1)} %add.22), channel_id=1, source_target_pairs={{2,5},{5,2},{1,6},{6,1},{4,7},{7,4},{3,0},{0,3},{11,14},{14,11},{1... | collective-permute-start | bytes 196616 | tf_op jit(solution)/shard_map/ppermute | solution.py:72
  19.9 1.6 %collective-permute-done.2 = f32[128,128]{1,0:T(8,128)S(1)} collective-permute-done((f32[128,128]{1,0:T(8,128)S(1)}, f32[128,128]{1,0:T(8,128)S(1)}, u32[]{:S(2)}, u32[]{:S(2)}) %collective-permute-start.2) | collective-permute-done | bytes 65568 | tf_op jit(solution)/shard_map/ppermute | solution.py:72
  21.4 2.9 %collective-permute-done.5 = f32[128,128]{1,0:T(8,128)S(1)} collective-permute-done((f32[128,128]{1,0:T(8,128)S(1)}, f32[128,128]{1,0:T(8,128)S(1)}, u32[]{:S(2)}, u32[]{:S(2)}) %collective-permute-start.5) | collective-permute-done | bytes 65568 | tf_op jit(solution)/shard_map/ppermute | solution.py:72
  24.9 5.6 %collective-permute-start.6 = (f32[1792,128]{1,0:T(8,128)S(1)}, f32[1792,128]{1,0:T(8,128)S(1)}, u32[]{:S(2)}, u32[]{:S(2)}) collective-permute-start(f32[1792,128]{1,0:T(8,128)S(1)} %lift_send.1.refs_3_.refs_0_), channel_id=1, source_target_pairs={{0,8},{8,0},{16,24},{24,16},{32,40},{40,32},{48,56},{56,48},{64,72... | collective-permute-start | bytes 2752520 | tf_op jit(solution)/shard_map/ppermute | solution.py:92
  31.0 1.6 %collective-permute-done.6.refs_1_ = f32[1792,128]{1,0:T(8,128)S(1)} collective-permute-done((f32[1792,128]{1,0:T(8,128)S(1)}, f32[1792,128]{1,0:T(8,128)S(1)}, u32[]{:S(2)}, u32[]{:S(2)}) %collective-permute-start.6) | collective-permute-done | bytes 917536 | tf_op jit(solution)/shard_map/ppermute | solution.py:92
  32.7 1.6 %collective-permute-start.7 = (f32[832,128]{1,0:T(8,128)S(1)}, f32[832,128]{1,0:T(8,128)S(1)}, u32[]{:S(2)}, u32[]{:S(2)}) collective-permute-start(f32[832,128]{1,0:T(8,128)S(1)} %get-tuple-element.22.refs_2_), channel_id=1, source_target_pairs={{0,24},{8,64},{16,88},{24,0},{32,56},{40,96},{48,120},{56,32},{64,... | collective-permute-start | bytes 1277960 | tf_op jit(solution)/shard_map/ppermute | solution.py:100
  34.3 2.6 %collective-permute-start.9 = (f32[128,128]{1,0:T(8,128)S(1)}, f32[128,128]{1,0:T(8,128)S(1)}, u32[]{:S(2)}, u32[]{:S(2)}) collective-permute-start(f32[128,128]{1,0:T(8,128)S(1)} %gram_pair.1.refs_0_), channel_id=1, source_target_pairs={{56,0},{240,8},{40,16},{224,24},{24,32},{208,40},{8,48},{192,56},{... | collective-permute-start | bytes 196616 | tf_op jit(solution)/shard_map/ppermute | solution.py:96
  36.9 1.9 %collective-permute-start.8 = (f32[128,128]{1,0:T(8,128)S(1)}, f32[128,128]{1,0:T(8,128)S(1)}, u32[]{:S(2)}, u32[]{:S(2)}) collective-permute-start(f32[128,128]{1,0:T(8,128)S(1)} %gram_pair.1.refs_0_), channel_id=1, source_target_pairs={{0,200},{8,192},{16,216},{24,208},{32,232},{40,224},{48,248},{56,2... | collective-permute-start | bytes 196616 | tf_op jit(solution)/shard_map/ppermute | solution.py:92
  38.8 2.6 %collective-permute-done.9.refs_2_ = f32[128,128]{1,0:T(8,128)S(1)} collective-permute-done((f32[128,128]{1,0:T(8,128)S(1)}, f32[128,128]{1,0:T(8,128)S(1)}, u32[]{:S(2)}, u32[]{:S(2)}) %collective-permute-start.9) | collective-permute-done | bytes 65568 | tf_op jit(solution)/shard_map/ppermute | solution.py:96
  42.8 2.9 %collective-permute-start.11 = (f32[416,128]{1,0:T(8,128)S(1)}, f32[416,128]{1,0:T(8,128)S(1)}, u32[]{:S(2)}, u32[]{:S(2)}) collective-permute-start(f32[416,128]{1,0:T(8,128)S(1)} %get-tuple-element.24.refs_1_), channel_id=1, source_target_pairs={{0,56},{8,192},{16,216},{24,32},{32,24},{40,224},{48,248},{56,0},{... | collective-permute-start | bytes 638984 | tf_op jit(solution)/shard_map/ppermute | solution.py:100
  45.8 4.7 %collective-permute-done.13.refs_3_.refs_1_ = f32[128,128]{1,0:T(8,128)S(1)} collective-permute-done((f32[128,128]{1,0:T(8,128)S(1)}, f32[128,128]{1,0:T(8,128)S(1)}, u32[]{:S(2)}, u32[]{:S(2)}) %collective-permute-start.13) | collective-permute-done | bytes 65568 | tf_op jit(solution)/shard_map/ppermute | solution.py:92
  51.1 1.7 %collective-permute-start.14 = (f32[416,128]{1,0:T(8,128)S(1)}, f32[416,128]{1,0:T(8,128)S(1)}, u32[]{:S(2)}, u32[]{:S(2)}) collective-permute-start(f32[416,128]{1,0:T(8,128)S(1)} %first_sum.1.refs_1_.refs_4_.refs_0_), channel_id=1, source_target_pairs={{0,200},{8,48},{16,40},{24,208},{32,232},{40,16},{48,8},{56,240},{... | collective-permute-start | bytes 638984 | tf_op jit(solution)/shard_map/ppermute | solution.py:100
  52.8 1.2 %collective-permute-done.15.refs_3_ = f32[128,128]{1,0:T(8,128)S(1)} collective-permute-done((f32[128,128]{1,0:T(8,128)S(1)}, f32[128,128]{1,0:T(8,128)S(1)}, u32[]{:S(2)}, u32[]{:S(2)}) %collective-permute-start.15) | collective-permute-done | bytes 65568 | tf_op jit(solution)/shard_map/ppermute | solution.py:92
  54.1 2.1 %eliminate0.1.refs_2_.refs_0_ = f32[128,128]{1,0:T(8,128)S(1)} custom-call(f32[128,128]{1,0:T(8,128)S(1)} %gram_four.3.refs_0_.refs_1_, f32[128,128]{1,0:T(8,128)S(1)} %gram_four.3.refs_0_.refs_1_), custom_call_target="tpu_custom_call" | custom-call | flops 4000000 | bytes 6000000 | tf_op jit(solution)/shard_map/eliminate0/pallas_call | solution.py:164
  56.2 1.4 %collective-permute-done.14.refs_1_ = f32[416,128]{1,0:T(8,128)S(1)} collective-permute-done((f32[416,128]{1,0:T(8,128)S(1)}, f32[416,128]{1,0:T(8,128)S(1)}, u32[]{:S(2)}, u32[]{:S(2)}) %collective-permute-start.14) | collective-permute-done | bytes 213024 | tf_op jit(solution)/shard_map/ppermute | solution.py:100
  57.8 2.7 %eliminate40.1 = (f32[128,128]{1,0:T(8,128)S(1)}, bf16[256,256]{1,0:T(8,128)(2,1)S(1)}) custom-call(f32[128,128]{1,0:T(8,128)S(1)} %eliminate0.1.refs_2_.refs_0_, f32[128,128]{1,0:T(8,128)S(1)} %gram_four.3.refs_0_.refs_1_, f32[416,128]{1,0:T(8,128)S(1)} %second_sum.1.refs_2_.refs_0_), custom_call_target="tpu_custom_call" | custom-call | flops 4000000 | bytes 13200000 | tf_op jit(solution)/shard_map/eliminate40/pallas_call | solution.py:164
  60.4 2.6 %collective-permute-done.16.refs_1_ = f32[416,128]{1,0:T(8,128)S(1)} collective-permute-done((f32[416,128]{1,0:T(8,128)S(1)}, f32[416,128]{1,0:T(8,128)S(1)}, u32[]{:S(2)}, u32[]{:S(2)}) %collective-permute-start.16) | collective-permute-done | bytes 213024 | tf_op jit(solution)/shard_map/ppermute | solution.py:100
  63.3 1.2 %collective-permute-start.17 = (bf16[416,128]{1,0:T(8,128)(2,1)S(1)}, bf16[416,128]{1,0:T(8,128)(2,1)S(1)}, u32[]{:S(2)}, u32[]{:S(2)}) collective-permute-start(bf16[416,128]{1,0:T(8,128)(2,1)S(1)} %block.1.refs_3_.refs_0_), channel_id=1, source_target_pairs={{0,56},{8,192},{16,216},{24,32},{32,24},{40,224},{48,248},{56,0},{... | collective-permute-start | bytes 319496 | tf_op jit(solution)/shard_map/ppermute | solution.py:100
  64.8 3.9 %collective-permute-done.17.refs_1_ = bf16[416,128]{1,0:T(8,128)(2,1)S(1)} collective-permute-done((bf16[416,128]{1,0:T(8,128)(2,1)S(1)}, bf16[416,128]{1,0:T(8,128)(2,1)S(1)}, u32[]{:S(2)}, u32[]{:S(2)}) %collective-permute-start.17) | collective-permute-done | bytes 106528 | tf_op jit(solution)/shard_map/ppermute | solution.py:100
  69.6 2.3 %collective-permute-start.19 = (f32[8,128]{1,0:T(8,128)S(1)}, f32[8,128]{1,0:T(8,128)S(1)}, u32[]{:S(2)}, u32[]{:S(2)}) collective-permute-start(f32[8,128]{1,0:T(8,128)S(1)} %squares.1.refs_2_), channel_id=1, source_target_pairs={{0,1},{1,0},{2,3},{3,2},{4,5},{5,4},{6,7},{7,6},{8,9},{9,8},{10,11... | collective-permute-start | bytes 12296 | tf_op jit(solution)/shard_map/ppermute | solution.py:80
  71.9 1.1 %collective-permute-done.20.refs_4_ = f32[8,128]{1,0:T(8,128)S(1)} collective-permute-done((f32[8,128]{1,0:T(8,128)S(1)}, f32[8,128]{1,0:T(8,128)S(1)}, u32[]{:S(2)}, u32[]{:S(2)}) %collective-permute-start.20) | collective-permute-done | bytes 4128 | tf_op jit(solution)/shard_map/ppermute | solution.py:80
  73.2 0.9 %collective-permute-done.18.refs_1_ = bf16[832,128]{1,0:T(8,128)(2,1)S(1)} collective-permute-done((bf16[832,128]{1,0:T(8,128)(2,1)S(1)}, bf16[832,128]{1,0:T(8,128)(2,1)S(1)}, u32[]{:S(2)}, u32[]{:S(2)}) %collective-permute-start.18) | collective-permute-done | bytes 213024 | tf_op jit(solution)/shard_map/ppermute | solution.py:100
  74.9 1.7 %collective-permute-start.23 = (f32[8,128]{1,0:T(8,128)S(1)}, f32[8,128]{1,0:T(8,128)S(1)}, u32[]{:S(2)}, u32[]{:S(2)}) collective-permute-start(f32[8,128]{1,0:T(8,128)S(1)} %get-tuple-element.28.refs_0_), channel_id=1, source_target_pairs={{13,0},{12,1},{15,2},{14,3},{9,4},{8,5},{11,6},{10,7},{5,8},{4,9},... | collective-permute-start | bytes 12296 | tf_op jit(solution)/shard_map/ppermute | solution.py:88
  76.6 2.7 %collective-permute-start.24 = (f32[8,128]{1,0:T(8,128)S(1)}, f32[8,128]{1,0:T(8,128)S(1)}, u32[]{:S(2)}, u32[]{:S(2)}) collective-permute-start(f32[8,128]{1,0:T(8,128)S(1)} %add_core.1.refs_2_.sq_ref), channel_id=1, source_target_pairs={{15,0},{10,1},{9,2},{12,3},{11,4},{14,5},{13,6},{8,7},{2,8},{7,9},... | collective-permute-start | bytes 12296 | tf_op jit(solution)/shard_map/ppermute | solution.py:88
  79.5 1.5 %finish_momentum.1 = (bf16[256,3328]{1,0:T(8,128)(2,1)}, f32[8,128]{1,0:T(8,128)S(1)}) custom-call(f32[3328,128]{1,0:T(8,128)S(1)} %unpack.1.coef_ref, bf16[256,128]{1,0:T(8,128)(2,1)S(1)} %ortho.1.refs_2_.ortho_ref, bf16[256,3328]{1,0:T(8,128)(2,1)S(1)} %get-tuple-element.20.refs_2_.b_ref), custom_call_target="tpu_custom_call" | custom-call | flops 218103808 | bytes 5000000 | tf_op jit(solution)/shard_map/finish_momentum/pallas_call | solution.py:396
  81.3 0.9 %collective-permute-done.25.other_ref = f32[16,128]{1,0:T(8,128)S(1)} collective-permute-done((f32[16,128]{1,0:T(8,128)S(1)}, f32[16,128]{1,0:T(8,128)S(1)}, u32[]{:S(2)}, u32[]{:S(2)}) %collective-permute-start.25) | collective-permute-done | bytes 8224 | tf_op jit(solution)/shard_map/ppermute | solution.py:92
  82.3 1.9 %finish_weights.1 = (bf16[256,3328]{1,0:T(8,128)(2,1)}, f32[3328,128]{1,0:T(8,128)}) custom-call(f32[8,128]{1,0:T(8,128)S(1)} %add_core.1.refs_2_.sq_ref, f32[16,128]{1,0:T(8,128)S(1)} %stack.1.moved_ref, f32[16,128]{1,0:T(8,128)S(1)} %collective-permute-done.25.other_ref, f32[3328,128]{1,0:T(8,128)S(1)} %unpack.1.coef_ref, ...), custom_call_target="tpu_custom_call" | custom-call | flops 218103808 | bytes 7000000 | tf_op jit(solution)/shard_map/finish_weights/pallas_call | solution.py:441
  (52 shorter events, 7.0 us)
Async XLA Ops:
  3.7 8.1 %collective-permute-start = (f32[128,128]{1,0:T(8,128)S(1)}, f32[128,128]{1,0:T(8,128)S(1)}, u32[]{:S(2)}, u32[]{:S(2)}) collective-permute-start(f32[128,128]{1,0:T(8,128)S(1)} %get-tuple-element.18), channel_id=1, source_target_pairs={{0,1},{1,0},{2,3},{3,2},{4,5},{5,4},{6,7},{7,6},{9,10},{10,9},{11,... | collective-permute-start | bytes 196616 | tf_op jit(solution)/shard_map/ppermute | solution.py:72
  10.2 4.3 %collective-permute-start.3 = (f32[128,128]{1,0:T(8,128)S(1)}, f32[128,128]{1,0:T(8,128)S(1)}, u32[]{:S(2)}, u32[]{:S(2)}) collective-permute-start(f32[128,128]{1,0:T(8,128)S(1)} %get-tuple-element.19), channel_id=1, source_target_pairs={{0,1},{1,0},{2,3},{3,2},{4,5},{5,4},{6,7},{7,6},{9,10},{10,9},{11,... | collective-permute-start | bytes 196616 | tf_op jit(solution)/shard_map/ppermute | solution.py:72
  11.9 3.2 %collective-permute-start.1 = (f32[128,128]{1,0:T(8,128)S(1)}, f32[128,128]{1,0:T(8,128)S(1)}, u32[]{:S(2)}, u32[]{:S(2)}) collective-permute-start(f32[128,128]{1,0:T(8,128)S(1)} %add.18), channel_id=1, source_target_pairs={{1,2},{2,1},{3,4},{4,3},{5,6},{6,5},{7,0},{0,7},{10,11},{11,10},{1... | collective-permute-start | bytes 196616 | tf_op jit(solution)/shard_map/ppermute | solution.py:72
  14.6 3.5 %collective-permute-start.4 = (f32[128,128]{1,0:T(8,128)S(1)}, f32[128,128]{1,0:T(8,128)S(1)}, u32[]{:S(2)}, u32[]{:S(2)}) collective-permute-start(f32[128,128]{1,0:T(8,128)S(1)} %add.21), channel_id=1, source_target_pairs={{1,2},{2,1},{3,4},{4,3},{5,6},{6,5},{7,0},{0,7},{10,11},{11,10},{1... | collective-permute-start | bytes 196616 | tf_op jit(solution)/shard_map/ppermute | solution.py:72
  15.1 6.3 %collective-permute-start.2 = (f32[128,128]{1,0:T(8,128)S(1)}, f32[128,128]{1,0:T(8,128)S(1)}, u32[]{:S(2)}, u32[]{:S(2)}) collective-permute-start(f32[128,128]{1,0:T(8,128)S(1)} %add.19), channel_id=1, source_target_pairs={{2,5},{5,2},{1,6},{6,1},{4,7},{7,4},{3,0},{0,3},{11,14},{14,11},{1... | collective-permute-start | bytes 196616 | tf_op jit(solution)/shard_map/ppermute | solution.py:72
  18.0 6.3 %collective-permute-start.5 = (f32[128,128]{1,0:T(8,128)S(1)}, f32[128,128]{1,0:T(8,128)S(1)}, u32[]{:S(2)}, u32[]{:S(2)}) collective-permute-start(f32[128,128]{1,0:T(8,128)S(1)} %add.22), channel_id=1, source_target_pairs={{2,5},{5,2},{1,6},{6,1},{4,7},{7,4},{3,0},{0,3},{11,14},{14,11},{1... | collective-permute-start | bytes 196616 | tf_op jit(solution)/shard_map/ppermute | solution.py:72
  24.9 7.7 %collective-permute-start.6 = (f32[1792,128]{1,0:T(8,128)S(1)}, f32[1792,128]{1,0:T(8,128)S(1)}, u32[]{:S(2)}, u32[]{:S(2)}) collective-permute-start(f32[1792,128]{1,0:T(8,128)S(1)} %lift_send.1.refs_3_.refs_0_), channel_id=1, source_target_pairs={{0,8},{8,0},{16,24},{24,16},{32,40},{40,32},{48,56},{56,48},{64,72... | collective-permute-start | bytes 2752520 | tf_op jit(solution)/shard_map/ppermute | solution.py:92
  32.7 10.0 %collective-permute-start.7 = (f32[832,128]{1,0:T(8,128)S(1)}, f32[832,128]{1,0:T(8,128)S(1)}, u32[]{:S(2)}, u32[]{:S(2)}) collective-permute-start(f32[832,128]{1,0:T(8,128)S(1)} %get-tuple-element.22.refs_2_), channel_id=1, source_target_pairs={{0,24},{8,64},{16,88},{24,0},{32,56},{40,96},{48,120},{56,32},{64,... | collective-permute-start | bytes 1277960 | tf_op jit(solution)/shard_map/ppermute | solution.py:100
  34.3 7.1 %collective-permute-start.9 = (f32[128,128]{1,0:T(8,128)S(1)}, f32[128,128]{1,0:T(8,128)S(1)}, u32[]{:S(2)}, u32[]{:S(2)}) collective-permute-start(f32[128,128]{1,0:T(8,128)S(1)} %gram_pair.1.refs_0_), channel_id=1, source_target_pairs={{56,0},{240,8},{40,16},{224,24},{24,32},{208,40},{8,48},{192,56},{... | collective-permute-start | bytes 196616 | tf_op jit(solution)/shard_map/ppermute | solution.py:96
  36.9 5.2 %collective-permute-start.8 = (f32[128,128]{1,0:T(8,128)S(1)}, f32[128,128]{1,0:T(8,128)S(1)}, u32[]{:S(2)}, u32[]{:S(2)}) collective-permute-start(f32[128,128]{1,0:T(8,128)S(1)} %gram_pair.1.refs_0_), channel_id=1, source_target_pairs={{0,200},{8,192},{16,216},{24,208},{32,232},{40,224},{48,248},{56,2... | collective-permute-start | bytes 196616 | tf_op jit(solution)/shard_map/ppermute | solution.py:92
  41.5 1.3 %collective-permute-start.10 = (f32[128,128]{1,0:T(8,128)S(1)}, f32[128,128]{1,0:T(8,128)S(1)}, u32[]{:S(2)}, u32[]{:S(2)}) collective-permute-start(f32[128,128]{1,0:T(8,128)S(1)} %collective-permute-done.9.refs_2_), channel_id=1, source_target_pairs={{0,8},{8,0},{16,24},{24,16},{32,40},{40,32},{48,56},{56,48},{64,72... | collective-permute-start | bytes 196616 | tf_op jit(solution)/shard_map/ppermute | solution.py:92
  42.8 8.2 %collective-permute-start.11 = (f32[416,128]{1,0:T(8,128)S(1)}, f32[416,128]{1,0:T(8,128)S(1)}, u32[]{:S(2)}, u32[]{:S(2)}) collective-permute-start(f32[416,128]{1,0:T(8,128)S(1)} %get-tuple-element.24.refs_1_), channel_id=1, source_target_pairs={{0,56},{8,192},{16,216},{24,32},{32,24},{40,224},{48,248},{56,0},{... | collective-permute-start | bytes 638984 | tf_op jit(solution)/shard_map/ppermute | solution.py:100
  45.7 4.8 %collective-permute-start.13 = (f32[128,128]{1,0:T(8,128)S(1)}, f32[128,128]{1,0:T(8,128)S(1)}, u32[]{:S(2)}, u32[]{:S(2)}) collective-permute-start(f32[128,128]{1,0:T(8,128)S(1)} %hold.1.refs_0_), channel_id=1, source_target_pairs={{0,80},{8,88},{16,64},{24,72},{32,112},{40,120},{48,96},{56,104},{... | collective-permute-start | bytes 196616 | tf_op jit(solution)/shard_map/ppermute | solution.py:92
  45.7 5.3 %collective-permute-start.12 = (f32[128,128]{1,0:T(8,128)S(1)}, f32[128,128]{1,0:T(8,128)S(1)}, u32[]{:S(2)}, u32[]{:S(2)}) collective-permute-start(f32[128,128]{1,0:T(8,128)S(1)} %hold.1.refs_0_), channel_id=1, source_target_pairs={{24,0},{64,8},{8,16},{80,24},{56,32},{96,40},{40,48},{112,56},{88,... | collective-permute-start | bytes 196616 | tf_op jit(solution)/shard_map/ppermute | solution.py:96
  51.1 6.6 %collective-permute-start.14 = (f32[416,128]{1,0:T(8,128)S(1)}, f32[416,128]{1,0:T(8,128)S(1)}, u32[]{:S(2)}, u32[]{:S(2)}) collective-permute-start(f32[416,128]{1,0:T(8,128)S(1)} %first_sum.1.refs_1_.refs_4_.refs_0_), channel_id=1, source_target_pairs={{0,200},{8,48},{16,40},{24,208},{32,232},{40,16},{48,8},{56,240},{... | collective-permute-start | bytes 638984 | tf_op jit(solution)/shard_map/ppermute | solution.py:100
  52.8 1.3 %collective-permute-start.15 = (f32[128,128]{1,0:T(8,128)S(1)}, f32[128,128]{1,0:T(8,128)S(1)}, u32[]{:S(2)}, u32[]{:S(2)}) collective-permute-start(f32[128,128]{1,0:T(8,128)S(1)} %hold_split.1.refs_2_), channel_id=1, source_target_pairs={{0,8},{8,0},{16,24},{24,16},{32,40},{40,32},{48,56},{56,48},{64,72... | collective-permute-start | bytes 196616 | tf_op jit(solution)/shard_map/ppermute | solution.py:92
  57.7 5.4 %collective-permute-start.16 = (f32[416,128]{1,0:T(8,128)S(1)}, f32[416,128]{1,0:T(8,128)S(1)}, u32[]{:S(2)}, u32[]{:S(2)}) collective-permute-start(f32[416,128]{1,0:T(8,128)S(1)} %second_sum.1.refs_2_.refs_0_), channel_id=1, source_target_pairs={{0,72},{8,16},{16,8},{24,80},{32,104},{40,48},{48,40},{56,112},{64... | collective-permute-start | bytes 638984 | tf_op jit(solution)/shard_map/ppermute | solution.py:100
  63.3 5.4 %collective-permute-start.17 = (bf16[416,128]{1,0:T(8,128)(2,1)S(1)}, bf16[416,128]{1,0:T(8,128)(2,1)S(1)}, u32[]{:S(2)}, u32[]{:S(2)}) collective-permute-start(bf16[416,128]{1,0:T(8,128)(2,1)S(1)} %block.1.refs_3_.refs_0_), channel_id=1, source_target_pairs={{0,56},{8,192},{16,216},{24,32},{32,24},{40,224},{48,248},{56,0},{... | collective-permute-start | bytes 319496 | tf_op jit(solution)/shard_map/ppermute | solution.py:100
  68.7 5.4 %collective-permute-start.18 = (bf16[832,128]{1,0:T(8,128)(2,1)S(1)}, bf16[832,128]{1,0:T(8,128)(2,1)S(1)}, u32[]{:S(2)}, u32[]{:S(2)}) collective-permute-start(bf16[832,128]{1,0:T(8,128)(2,1)S(1)} %join1.1.refs_0_), channel_id=1, source_target_pairs={{0,24},{8,64},{16,88},{24,0},{32,56},{40,96},{48,120},{56,32},{64,... | collective-permute-start | bytes 638984 | tf_op jit(solution)/shard_map/ppermute | solution.py:100
  68.9 4.1 %collective-permute-start.20 = (f32[8,128]{1,0:T(8,128)S(1)}, f32[8,128]{1,0:T(8,128)S(1)}, u32[]{:S(2)}, u32[]{:S(2)}) collective-permute-start(f32[8,128]{1,0:T(8,128)S(1)} %squares.1.refs_2_), channel_id=1, source_target_pairs={{0,25},{1,24},{2,27},{3,26},{4,29},{5,28},{6,31},{7,30},{8,65},{9,... | collective-permute-start | bytes 12296 | tf_op jit(solution)/shard_map/ppermute | solution.py:80
  69.6 3.6 %collective-permute-start.19 = (f32[8,128]{1,0:T(8,128)S(1)}, f32[8,128]{1,0:T(8,128)S(1)}, u32[]{:S(2)}, u32[]{:S(2)}) collective-permute-start(f32[8,128]{1,0:T(8,128)S(1)} %squares.1.refs_2_), channel_id=1, source_target_pairs={{0,1},{1,0},{2,3},{3,2},{4,5},{5,4},{6,7},{7,6},{8,9},{9,8},{10,11... | collective-permute-start | bytes 12296 | tf_op jit(solution)/shard_map/ppermute | solution.py:80
  74.3 5.0 %collective-permute-start.21 = (bf16[1664,128]{1,0:T(8,128)(2,1)S(1)}, bf16[1664,128]{1,0:T(8,128)(2,1)S(1)}, u32[]{:S(2)}, u32[]{:S(2)}) collective-permute-start(bf16[1664,128]{1,0:T(8,128)(2,1)S(1)} %get-tuple-element.27.refs_0_), channel_id=1, source_target_pairs={{0,8},{8,0},{16,24},{24,16},{32,40},{40,32},{48,56},{56,48},{64,72... | collective-permute-start | bytes 1277960 | tf_op jit(solution)/shard_map/ppermute | solution.py:92
  74.7 1.8 %collective-permute-start.22 = (f32[8,128]{1,0:T(8,128)S(1)}, f32[8,128]{1,0:T(8,128)S(1)}, u32[]{:S(2)}, u32[]{:S(2)}) collective-permute-start(f32[8,128]{1,0:T(8,128)S(1)} %get-tuple-element.28.refs_0_), channel_id=1, source_target_pairs={{0,8},{8,0},{16,24},{24,16},{32,40},{40,32},{48,56},{56,48},{64,72... | collective-permute-start | bytes 12296 | tf_op jit(solution)/shard_map/ppermute | solution.py:92
  74.9 6.1 %collective-permute-start.23 = (f32[8,128]{1,0:T(8,128)S(1)}, f32[8,128]{1,0:T(8,128)S(1)}, u32[]{:S(2)}, u32[]{:S(2)}) collective-permute-start(f32[8,128]{1,0:T(8,128)S(1)} %get-tuple-element.28.refs_0_), channel_id=1, source_target_pairs={{13,0},{12,1},{15,2},{14,3},{9,4},{8,5},{11,6},{10,7},{5,8},{4,9},... | collective-permute-start | bytes 12296 | tf_op jit(solution)/shard_map/ppermute | solution.py:88
  76.6 4.4 %collective-permute-start.24 = (f32[8,128]{1,0:T(8,128)S(1)}, f32[8,128]{1,0:T(8,128)S(1)}, u32[]{:S(2)}, u32[]{:S(2)}) collective-permute-start(f32[8,128]{1,0:T(8,128)S(1)} %add_core.1.refs_2_.sq_ref), channel_id=1, source_target_pairs={{15,0},{10,1},{9,2},{12,3},{11,4},{14,5},{13,6},{8,7},{2,8},{7,9},... | collective-permute-start | bytes 12296 | tf_op jit(solution)/shard_map/ppermute | solution.py:88
  79.4 2.8 %copy-start = (bf16[256,3328]{1,0:T(8,128)(2,1)S(1)}, bf16[256,3328]{1,0:T(8,128)(2,1)}, u32[]{:S(2)}) copy-start(bf16[256,3328]{1,0:T(8,128)(2,1)} %weights_ref.1) | copy-start | bytes 5111812
  81.0 1.3 %collective-permute-start.25 = (f32[16,128]{1,0:T(8,128)S(1)}, f32[16,128]{1,0:T(8,128)S(1)}, u32[]{:S(2)}, u32[]{:S(2)}) collective-permute-start(f32[16,128]{1,0:T(8,128)S(1)} %stack.1.moved_ref), channel_id=1, source_target_pairs={{0,8},{8,0},{16,24},{24,16},{32,40},{40,32},{48,56},{56,48},{64,72... | collective-permute-start | bytes 24584 | tf_op jit(solution)/shard_map/ppermute | solution.py:92

commit v10 on v9

--- a/solution.py
+++ b/solution.py
@@ -28,7 +28,7 @@
 CUT = 40
 WIDE = 256
 TILES = LOCAL_COLS // WIDE
-STRIPS = ((0, 512), (512, 768), (1280, 768), (2048, 768), (2816, 256), (3072, 256))
+STRIPS = ((0, 512), (512, 768), (1280, 768), (2048, 768), (2816, 512))
 
 X_ONE, Y_ONE, X_THREE, Y_THREE, CORE = 3, 9, 7, 25, 1
 MASKS = ((X_ONE, X_THREE, Y_THREE, Y_ONE), (Y_ONE, Y_THREE, X_THREE, X_ONE))

time: 84.4 us -> 84.2 us (level)
  no operation moved by 1% of the time
where the time goes in v10:
time: 84.2 us; the launch traced here: 84.1 us
  starting transfers between devices  37.7 us (45%)
  waiting for transfers between devices  32.1 us (38%)
  Pallas kernels  13.2 us (16%)
  between operations  1.02 us (1%)
    ppermute x6, starting transfers between devices, swap_z(): return lax.ppermute(x, ('fsdp', 'tp'), perm)  11.5 us
    ppermute x8, waiting for transfers between devices, xor_fsdp(): return lax.ppermute(x, 'fsdp', [(i, i ^ mask) for i in range(FSDP)])  9.72 us
    ppermute x6, waiting for transfers between devices, swap_z(): return lax.ppermute(x, ('fsdp', 'tp'), perm)  9 us
    ppermute x6, waiting for transfers between devices, xor_step(): lax.ppermute(x, 'fsdp', [(i, i ^ MASKS[team(i)][k]) for i in range(FSDP)])  8.83 us
    ppermute x8, starting transfers between devices, xor_fsdp(): return lax.ppermute(x, 'fsdp', [(i, i ^ mask) for i in range(FSDP)])  8.4 us
    ppermute x6, starting transfers between devices, xor_step(): lax.ppermute(x, 'fsdp', [(i, i ^ MASKS[team(i)][k]) for i in range(FSDP)])  7.65 us
    pallas_call x21, Pallas kernels, local(): pl.pallas_call(body, in_specs=[VMEM_SPEC] * (used + len(after)), out_spec...  6.96 us
    ppermute x2, starting transfers between devices, turn_z(): return lax.ppermute(x, ('fsdp', 'tp'), perm)  4.43 us
  transfers between devices with their start and end apart: 26, of which 19 were waited for; matrix products, arithmetic and copies ran while one was open for 0% of the time, Pallas kernels for 9%

profile of v10, /device:TPU:1, one launch (start us, length us, event | category | flops | bytes accessed | tf_op | source)
XLA Modules:
  0.0 84.1 jit_solution(598816976443633363)
XLA Ops:
  0.6 2.9 %project.1 = (bf16[256,3328]{1,0:T(8,128)(2,1)S(1)}, f32[128,128]{1,0:T(8,128)S(1)}, f32[128,128]{1,0:T(8,128)S(1)}) custom-call(bf16[256,3328]{1,0:T(8,128)(2,1)} %m_hbm.1, bf16[256,3328]{1,0:T(8,128)(2,1)} %g_hbm.1, f32[3328,128]{1,0:T(8,128)} %s_hbm.1), custom_call_target="tpu_custom_call" | custom-call | flops 218103808 | bytes 7000000 | tf_op jit(solution)/shard_map/project/pallas_call | solution.py:140
  3.5 6.5 %collective-permute-start = (f32[128,128]{1,0:T(8,128)S(1)}, f32[128,128]{1,0:T(8,128)S(1)}, u32[]{:S(2)}, u32[]{:S(2)}) collective-permute-start(f32[128,128]{1,0:T(8,128)S(1)} %get-tuple-element.18), channel_id=1, source_target_pairs={{0,1},{1,0},{2,3},{3,2},{4,5},{5,4},{6,7},{7,6},{9,10},{10,9},{11,... | collective-permute-start | bytes 196616 | tf_op jit(solution)/shard_map/ppermute | solution.py:72
  10.1 1.6 %collective-permute-done = f32[128,128]{1,0:T(8,128)S(1)} collective-permute-done((f32[128,128]{1,0:T(8,128)S(1)}, f32[128,128]{1,0:T(8,128)S(1)}, u32[]{:S(2)}, u32[]{:S(2)}) %collective-permute-start) | collective-permute-done | bytes 65568 | tf_op jit(solution)/shard_map/ppermute | solution.py:72
  11.8 2.6 %collective-permute-done.3 = f32[128,128]{1,0:T(8,128)S(1)} collective-permute-done((f32[128,128]{1,0:T(8,128)S(1)}, f32[128,128]{1,0:T(8,128)S(1)}, u32[]{:S(2)}, u32[]{:S(2)}) %collective-permute-start.3) | collective-permute-done | bytes 65568 | tf_op jit(solution)/shard_map/ppermute | solution.py:72
  14.9 2.9 %collective-permute-start.2 = (f32[128,128]{1,0:T(8,128)S(1)}, f32[128,128]{1,0:T(8,128)S(1)}, u32[]{:S(2)}, u32[]{:S(2)}) collective-permute-start(f32[128,128]{1,0:T(8,128)S(1)} %add.19), channel_id=1, source_target_pairs={{2,5},{5,2},{1,6},{6,1},{4,7},{7,4},{3,0},{0,3},{11,14},{14,11},{1... | collective-permute-start | bytes 196616 | tf_op jit(solution)/shard_map/ppermute | solution.py:72
  17.8 1.8 %collective-permute-start.5 = (f32[128,128]{1,0:T(8,128)S(1)}, f32[128,128]{1,0:T(8,128)S(1)}, u32[]{:S(2)}, u32[]{:S(2)}) collective-permute-start(f32[128,128]{1,0:T(8,128)S(1)} %add.22), channel_id=1, source_target_pairs={{2,5},{5,2},{1,6},{6,1},{4,7},{7,4},{3,0},{0,3},{11,14},{14,11},{1... | collective-permute-start | bytes 196616 | tf_op jit(solution)/shard_map/ppermute | solution.py:72
  19.7 1.6 %collective-permute-done.2 = f32[128,128]{1,0:T(8,128)S(1)} collective-permute-done((f32[128,128]{1,0:T(8,128)S(1)}, f32[128,128]{1,0:T(8,128)S(1)}, u32[]{:S(2)}, u32[]{:S(2)}) %collective-permute-start.2) | collective-permute-done | bytes 65568 | tf_op jit(solution)/shard_map/ppermute | solution.py:72
  21.2 2.9 %collective-permute-done.5 = f32[128,128]{1,0:T(8,128)S(1)} collective-permute-done((f32[128,128]{1,0:T(8,128)S(1)}, f32[128,128]{1,0:T(8,128)S(1)}, u32[]{:S(2)}, u32[]{:S(2)}) %collective-permute-start.5) | collective-permute-done | bytes 65568 | tf_op jit(solution)/shard_map/ppermute | solution.py:72
  24.7 5.6 %collective-permute-start.6 = (f32[1792,128]{1,0:T(8,128)S(1)}, f32[1792,128]{1,0:T(8,128)S(1)}, u32[]{:S(2)}, u32[]{:S(2)}) collective-permute-start(f32[1792,128]{1,0:T(8,128)S(1)} %lift_send.1.refs_3_.refs_0_), channel_id=1, source_target_pairs={{0,8},{8,0},{16,24},{24,16},{32,40},{40,32},{48,56},{56,48},{64,72... | collective-permute-start | bytes 2752520 | tf_op jit(solution)/shard_map/ppermute | solution.py:92
  30.8 1.6 %collective-permute-done.6.refs_1_ = f32[1792,128]{1,0:T(8,128)S(1)} collective-permute-done((f32[1792,128]{1,0:T(8,128)S(1)}, f32[1792,128]{1,0:T(8,128)S(1)}, u32[]{:S(2)}, u32[]{:S(2)}) %collective-permute-start.6) | collective-permute-done | bytes 917536 | tf_op jit(solution)/shard_map/ppermute | solution.py:92
  32.5 1.6 %collective-permute-start.7 = (f32[832,128]{1,0:T(8,128)S(1)}, f32[832,128]{1,0:T(8,128)S(1)}, u32[]{:S(2)}, u32[]{:S(2)}) collective-permute-start(f32[832,128]{1,0:T(8,128)S(1)} %get-tuple-element.22.refs_2_), channel_id=1, source_target_pairs={{0,24},{8,64},{16,88},{24,0},{32,56},{40,96},{48,120},{56,32},{64,... | collective-permute-start | bytes 1277960 | tf_op jit(solution)/shard_map/ppermute | solution.py:100
  34.1 2.6 %collective-permute-start.9 = (f32[128,128]{1,0:T(8,128)S(1)}, f32[128,128]{1,0:T(8,128)S(1)}, u32[]{:S(2)}, u32[]{:S(2)}) collective-permute-start(f32[128,128]{1,0:T(8,128)S(1)} %gram_pair.1.refs_0_), channel_id=1, source_target_pairs={{56,0},{240,8},{40,16},{224,24},{24,32},{208,40},{8,48},{192,56},{... | collective-permute-start | bytes 196616 | tf_op jit(solution)/shard_map/ppermute | solution.py:96
  36.7 1.9 %collective-permute-start.8 = (f32[128,128]{1,0:T(8,128)S(1)}, f32[128,128]{1,0:T(8,128)S(1)}, u32[]{:S(2)}, u32[]{:S(2)}) collective-permute-start(f32[128,128]{1,0:T(8,128)S(1)} %gram_pair.1.refs_0_), channel_id=1, source_target_pairs={{0,200},{8,192},{16,216},{24,208},{32,232},{40,224},{48,248},{56,2... | collective-permute-start | bytes 196616 | tf_op jit(solution)/shard_map/ppermute | solution.py:92
  38.6 2.6 %collective-permute-done.9.refs_2_ = f32[128,128]{1,0:T(8,128)S(1)} collective-permute-done((f32[128,128]{1,0:T(8,128)S(1)}, f32[128,128]{1,0:T(8,128)S(1)}, u32[]{:S(2)}, u32[]{:S(2)}) %collective-permute-start.9) | collective-permute-done | bytes 65568 | tf_op jit(solution)/shard_map/ppermute | solution.py:96
  42.6 2.9 %collective-permute-start.11 = (f32[416,128]{1,0:T(8,128)S(1)}, f32[416,128]{1,0:T(8,128)S(1)}, u32[]{:S(2)}, u32[]{:S(2)}) collective-permute-start(f32[416,128]{1,0:T(8,128)S(1)} %get-tuple-element.24.refs_1_), channel_id=1, source_target_pairs={{0,56},{8,192},{16,216},{24,32},{32,24},{40,224},{48,248},{56,0},{... | collective-permute-start | bytes 638984 | tf_op jit(solution)/shard_map/ppermute | solution.py:100
  45.6 4.7 %collective-permute-done.13.refs_3_.refs_1_ = f32[128,128]{1,0:T(8,128)S(1)} collective-permute-done((f32[128,128]{1,0:T(8,128)S(1)}, f32[128,128]{1,0:T(8,128)S(1)}, u32[]{:S(2)}, u32[]{:S(2)}) %collective-permute-start.13) | collective-permute-done | bytes 65568 | tf_op jit(solution)/shard_map/ppermute | solution.py:92
  50.9 1.8 %collective-permute-start.14 = (f32[416,128]{1,0:T(8,128)S(1)}, f32[416,128]{1,0:T(8,128)S(1)}, u32[]{:S(2)}, u32[]{:S(2)}) collective-permute-start(f32[416,128]{1,0:T(8,128)S(1)} %first_sum.1.refs_1_.refs_4_.refs_0_), channel_id=1, source_target_pairs={{0,200},{8,48},{16,40},{24,208},{32,232},{40,16},{48,8},{56,240},{... | collective-permute-start | bytes 638984 | tf_op jit(solution)/shard_map/ppermute | solution.py:100
  52.7 1.2 %collective-permute-done.15.refs_3_ = f32[128,128]{1,0:T(8,128)S(1)} collective-permute-done((f32[128,128]{1,0:T(8,128)S(1)}, f32[128,128]{1,0:T(8,128)S(1)}, u32[]{:S(2)}, u32[]{:S(2)}) %collective-permute-start.15) | collective-permute-done | bytes 65568 | tf_op jit(solution)/shard_map/ppermute | solution.py:92
  53.9 2.1 %eliminate0.1.refs_2_.refs_0_ = f32[128,128]{1,0:T(8,128)S(1)} custom-call(f32[128,128]{1,0:T(8,128)S(1)} %gram_four.3.refs_0_.refs_1_, f32[128,128]{1,0:T(8,128)S(1)} %gram_four.3.refs_0_.refs_1_), custom_call_target="tpu_custom_call" | custom-call | flops 4000000 | bytes 6000000 | tf_op jit(solution)/shard_map/eliminate0/pallas_call | solution.py:164
  56.1 1.4 %collective-permute-done.14.refs_1_ = f32[416,128]{1,0:T(8,128)S(1)} collective-permute-done((f32[416,128]{1,0:T(8,128)S(1)}, f32[416,128]{1,0:T(8,128)S(1)}, u32[]{:S(2)}, u32[]{:S(2)}) %collective-permute-start.14) | collective-permute-done | bytes 213024 | tf_op jit(solution)/shard_map/ppermute | solution.py:100
  57.6 2.7 %eliminate40.1 = (f32[128,128]{1,0:T(8,128)S(1)}, bf16[256,256]{1,0:T(8,128)(2,1)S(1)}) custom-call(f32[128,128]{1,0:T(8,128)S(1)} %eliminate0.1.refs_2_.refs_0_, f32[128,128]{1,0:T(8,128)S(1)} %gram_four.3.refs_0_.refs_1_, f32[416,128]{1,0:T(8,128)S(1)} %second_sum.1.refs_2_.refs_0_), custom_call_target="tpu_custom_call" | custom-call | flops 4000000 | bytes 13200000 | tf_op jit(solution)/shard_map/eliminate40/pallas_call | solution.py:164
  60.2 2.6 %collective-permute-done.16.refs_1_ = f32[416,128]{1,0:T(8,128)S(1)} collective-permute-done((f32[416,128]{1,0:T(8,128)S(1)}, f32[416,128]{1,0:T(8,128)S(1)}, u32[]{:S(2)}, u32[]{:S(2)}) %collective-permute-start.16) | collective-permute-done | bytes 213024 | tf_op jit(solution)/shard_map/ppermute | solution.py:100
  63.1 1.2 %collective-permute-start.17 = (bf16[416,128]{1,0:T(8,128)(2,1)S(1)}, bf16[416,128]{1,0:T(8,128)(2,1)S(1)}, u32[]{:S(2)}, u32[]{:S(2)}) collective-permute-start(bf16[416,128]{1,0:T(8,128)(2,1)S(1)} %block.1.refs_3_.refs_0_), channel_id=1, source_target_pairs={{0,56},{8,192},{16,216},{24,32},{32,24},{40,224},{48,248},{56,0},{... | collective-permute-start | bytes 319496 | tf_op jit(solution)/shard_map/ppermute | solution.py:100
  64.5 3.9 %collective-permute-done.17.refs_1_ = bf16[416,128]{1,0:T(8,128)(2,1)S(1)} collective-permute-done((bf16[416,128]{1,0:T(8,128)(2,1)S(1)}, bf16[416,128]{1,0:T(8,128)(2,1)S(1)}, u32[]{:S(2)}, u32[]{:S(2)}) %collective-permute-start.17) | collective-permute-done | bytes 106528 | tf_op jit(solution)/shard_map/ppermute | solution.py:100
  69.4 2.3 %collective-permute-start.19 = (f32[8,128]{1,0:T(8,128)S(1)}, f32[8,128]{1,0:T(8,128)S(1)}, u32[]{:S(2)}, u32[]{:S(2)}) collective-permute-start(f32[8,128]{1,0:T(8,128)S(1)} %squares.1.refs_2_), channel_id=1, source_target_pairs={{0,1},{1,0},{2,3},{3,2},{4,5},{5,4},{6,7},{7,6},{8,9},{9,8},{10,11... | collective-permute-start | bytes 12296 | tf_op jit(solution)/shard_map/ppermute | solution.py:80
  71.7 1.1 %collective-permute-done.20.refs_4_ = f32[8,128]{1,0:T(8,128)S(1)} collective-permute-done((f32[8,128]{1,0:T(8,128)S(1)}, f32[8,128]{1,0:T(8,128)S(1)}, u32[]{:S(2)}, u32[]{:S(2)}) %collective-permute-start.20) | collective-permute-done | bytes 4128 | tf_op jit(solution)/shard_map/ppermute | solution.py:80
  73.0 0.9 %collective-permute-done.18.refs_1_ = bf16[832,128]{1,0:T(8,128)(2,1)S(1)} collective-permute-done((bf16[832,128]{1,0:T(8,128)(2,1)S(1)}, bf16[832,128]{1,0:T(8,128)(2,1)S(1)}, u32[]{:S(2)}, u32[]{:S(2)}) %collective-permute-start.18) | collective-permute-done | bytes 213024 | tf_op jit(solution)/shard_map/ppermute | solution.py:100
  74.7 1.7 %collective-permute-start.23 = (f32[8,128]{1,0:T(8,128)S(1)}, f32[8,128]{1,0:T(8,128)S(1)}, u32[]{:S(2)}, u32[]{:S(2)}) collective-permute-start(f32[8,128]{1,0:T(8,128)S(1)} %get-tuple-element.28.refs_0_), channel_id=1, source_target_pairs={{13,0},{12,1},{15,2},{14,3},{9,4},{8,5},{11,6},{10,7},{5,8},{4,9},... | collective-permute-start | bytes 12296 | tf_op jit(solution)/shard_map/ppermute | solution.py:88
  76.4 2.7 %collective-permute-start.24 = (f32[8,128]{1,0:T(8,128)S(1)}, f32[8,128]{1,0:T(8,128)S(1)}, u32[]{:S(2)}, u32[]{:S(2)}) collective-permute-start(f32[8,128]{1,0:T(8,128)S(1)} %add_core.1.refs_2_.sq_ref), channel_id=1, source_target_pairs={{15,0},{10,1},{9,2},{12,3},{11,4},{14,5},{13,6},{8,7},{2,8},{7,9},... | collective-permute-start | bytes 12296 | tf_op jit(solution)/shard_map/ppermute | solution.py:88
  79.2 1.5 %finish_momentum.1 = (bf16[256,3328]{1,0:T(8,128)(2,1)}, f32[8,128]{1,0:T(8,128)S(1)}) custom-call(f32[3328,128]{1,0:T(8,128)S(1)} %unpack.1.coef_ref, bf16[256,128]{1,0:T(8,128)(2,1)S(1)} %ortho.1.refs_2_.ortho_ref, bf16[256,3328]{1,0:T(8,128)(2,1)S(1)} %get-tuple-element.20.refs_2_.b_ref), custom_call_target="tpu_custom_call" | custom-call | flops 218103808 | bytes 5000000 | tf_op jit(solution)/shard_map/finish_momentum/pallas_call | solution.py:396
  81.1 0.9 %collective-permute-done.25.other_ref = f32[16,128]{1,0:T(8,128)S(1)} collective-permute-done((f32[16,128]{1,0:T(8,128)S(1)}, f32[16,128]{1,0:T(8,128)S(1)}, u32[]{:S(2)}, u32[]{:S(2)}) %collective-permute-start.25) | collective-permute-done | bytes 8224 | tf_op jit(solution)/shard_map/ppermute | solution.py:92
  82.1 1.9 %finish_weights.1 = (bf16[256,3328]{1,0:T(8,128)(2,1)}, f32[3328,128]{1,0:T(8,128)}) custom-call(f32[8,128]{1,0:T(8,128)S(1)} %add_core.1.refs_2_.sq_ref, f32[16,128]{1,0:T(8,128)S(1)} %stack.1.moved_ref, f32[16,128]{1,0:T(8,128)S(1)} %collective-permute-done.25.other_ref, f32[3328,128]{1,0:T(8,128)S(1)} %unpack.1.coef_ref, ...), custom_call_target="tpu_custom_call" | custom-call | flops 218103808 | bytes 7000000 | tf_op jit(solution)/shard_map/finish_weights/pallas_call | solution.py:441
  (52 shorter events, 7.0 us)
Async XLA Ops:
  3.5 8.1 %collective-permute-start = (f32[128,128]{1,0:T(8,128)S(1)}, f32[128,128]{1,0:T(8,128)S(1)}, u32[]{:S(2)}, u32[]{:S(2)}) collective-permute-start(f32[128,128]{1,0:T(8,128)S(1)} %get-tuple-element.18), channel_id=1, source_target_pairs={{0,1},{1,0},{2,3},{3,2},{4,5},{5,4},{6,7},{7,6},{9,10},{10,9},{11,... | collective-permute-start | bytes 196616 | tf_op jit(solution)/shard_map/ppermute | solution.py:72
  10.0 4.3 %collective-permute-start.3 = (f32[128,128]{1,0:T(8,128)S(1)}, f32[128,128]{1,0:T(8,128)S(1)}, u32[]{:S(2)}, u32[]{:S(2)}) collective-permute-start(f32[128,128]{1,0:T(8,128)S(1)} %get-tuple-element.19), channel_id=1, source_target_pairs={{0,1},{1,0},{2,3},{3,2},{4,5},{5,4},{6,7},{7,6},{9,10},{10,9},{11,... | collective-permute-start | bytes 196616 | tf_op jit(solution)/shard_map/ppermute | solution.py:72
  11.7 3.2 %collective-permute-start.1 = (f32[128,128]{1,0:T(8,128)S(1)}, f32[128,128]{1,0:T(8,128)S(1)}, u32[]{:S(2)}, u32[]{:S(2)}) collective-permute-start(f32[128,128]{1,0:T(8,128)S(1)} %add.18), channel_id=1, source_target_pairs={{1,2},{2,1},{3,4},{4,3},{5,6},{6,5},{7,0},{0,7},{10,11},{11,10},{1... | collective-permute-start | bytes 196616 | tf_op jit(solution)/shard_map/ppermute | solution.py:72
  14.4 3.5 %collective-permute-start.4 = (f32[128,128]{1,0:T(8,128)S(1)}, f32[128,128]{1,0:T(8,128)S(1)}, u32[]{:S(2)}, u32[]{:S(2)}) collective-permute-start(f32[128,128]{1,0:T(8,128)S(1)} %add.21), channel_id=1, source_target_pairs={{1,2},{2,1},{3,4},{4,3},{5,6},{6,5},{7,0},{0,7},{10,11},{11,10},{1... | collective-permute-start | bytes 196616 | tf_op jit(solution)/shard_map/ppermute | solution.py:72
  14.9 6.3 %collective-permute-start.2 = (f32[128,128]{1,0:T(8,128)S(1)}, f32[128,128]{1,0:T(8,128)S(1)}, u32[]{:S(2)}, u32[]{:S(2)}) collective-permute-start(f32[128,128]{1,0:T(8,128)S(1)} %add.19), channel_id=1, source_target_pairs={{2,5},{5,2},{1,6},{6,1},{4,7},{7,4},{3,0},{0,3},{11,14},{14,11},{1... | collective-permute-start | bytes 196616 | tf_op jit(solution)/shard_map/ppermute | solution.py:72
  17.8 6.3 %collective-permute-start.5 = (f32[128,128]{1,0:T(8,128)S(1)}, f32[128,128]{1,0:T(8,128)S(1)}, u32[]{:S(2)}, u32[]{:S(2)}) collective-permute-start(f32[128,128]{1,0:T(8,128)S(1)} %add.22), channel_id=1, source_target_pairs={{2,5},{5,2},{1,6},{6,1},{4,7},{7,4},{3,0},{0,3},{11,14},{14,11},{1... | collective-permute-start | bytes 196616 | tf_op jit(solution)/shard_map/ppermute | solution.py:72
  24.7 7.7 %collective-permute-start.6 = (f32[1792,128]{1,0:T(8,128)S(1)}, f32[1792,128]{1,0:T(8,128)S(1)}, u32[]{:S(2)}, u32[]{:S(2)}) collective-permute-start(f32[1792,128]{1,0:T(8,128)S(1)} %lift_send.1.refs_3_.refs_0_), channel_id=1, source_target_pairs={{0,8},{8,0},{16,24},{24,16},{32,40},{40,32},{48,56},{56,48},{64,72... | collective-permute-start | bytes 2752520 | tf_op jit(solution)/shard_map/ppermute | solution.py:92
  32.5 10.1 %collective-permute-start.7 = (f32[832,128]{1,0:T(8,128)S(1)}, f32[832,128]{1,0:T(8,128)S(1)}, u32[]{:S(2)}, u32[]{:S(2)}) collective-permute-start(f32[832,128]{1,0:T(8,128)S(1)} %get-tuple-element.22.refs_2_), channel_id=1, source_target_pairs={{0,24},{8,64},{16,88},{24,0},{32,56},{40,96},{48,120},{56,32},{64,... | collective-permute-start | bytes 1277960 | tf_op jit(solution)/shard_map/ppermute | solution.py:100
  34.1 7.1 %collective-permute-start.9 = (f32[128,128]{1,0:T(8,128)S(1)}, f32[128,128]{1,0:T(8,128)S(1)}, u32[]{:S(2)}, u32[]{:S(2)}) collective-permute-start(f32[128,128]{1,0:T(8,128)S(1)} %gram_pair.1.refs_0_), channel_id=1, source_target_pairs={{56,0},{240,8},{40,16},{224,24},{24,32},{208,40},{8,48},{192,56},{... | collective-permute-start | bytes 196616 | tf_op jit(solution)/shard_map/ppermute | solution.py:96
  36.7 5.2 %collective-permute-start.8 = (f32[128,128]{1,0:T(8,128)S(1)}, f32[128,128]{1,0:T(8,128)S(1)}, u32[]{:S(2)}, u32[]{:S(2)}) collective-permute-start(f32[128,128]{1,0:T(8,128)S(1)} %gram_pair.1.refs_0_), channel_id=1, source_target_pairs={{0,200},{8,192},{16,216},{24,208},{32,232},{40,224},{48,248},{56,2... | collective-permute-start | bytes 196616 | tf_op jit(solution)/shard_map/ppermute | solution.py:92
  41.3 1.3 %collective-permute-start.10 = (f32[128,128]{1,0:T(8,128)S(1)}, f32[128,128]{1,0:T(8,128)S(1)}, u32[]{:S(2)}, u32[]{:S(2)}) collective-permute-start(f32[128,128]{1,0:T(8,128)S(1)} %collective-permute-done.9.refs_2_), channel_id=1, source_target_pairs={{0,8},{8,0},{16,24},{24,16},{32,40},{40,32},{48,56},{56,48},{64,72... | collective-permute-start | bytes 196616 | tf_op jit(solution)/shard_map/ppermute | solution.py:92
  42.6 8.2 %collective-permute-start.11 = (f32[416,128]{1,0:T(8,128)S(1)}, f32[416,128]{1,0:T(8,128)S(1)}, u32[]{:S(2)}, u32[]{:S(2)}) collective-permute-start(f32[416,128]{1,0:T(8,128)S(1)} %get-tuple-element.24.refs_1_), channel_id=1, source_target_pairs={{0,56},{8,192},{16,216},{24,32},{32,24},{40,224},{48,248},{56,0},{... | collective-permute-start | bytes 638984 | tf_op jit(solution)/shard_map/ppermute | solution.py:100
  45.5 4.8 %collective-permute-start.13 = (f32[128,128]{1,0:T(8,128)S(1)}, f32[128,128]{1,0:T(8,128)S(1)}, u32[]{:S(2)}, u32[]{:S(2)}) collective-permute-start(f32[128,128]{1,0:T(8,128)S(1)} %hold.1.refs_0_), channel_id=1, source_target_pairs={{0,80},{8,88},{16,64},{24,72},{32,112},{40,120},{48,96},{56,104},{... | collective-permute-start | bytes 196616 | tf_op jit(solution)/shard_map/ppermute | solution.py:92
  45.5 5.3 %collective-permute-start.12 = (f32[128,128]{1,0:T(8,128)S(1)}, f32[128,128]{1,0:T(8,128)S(1)}, u32[]{:S(2)}, u32[]{:S(2)}) collective-permute-start(f32[128,128]{1,0:T(8,128)S(1)} %hold.1.refs_0_), channel_id=1, source_target_pairs={{24,0},{64,8},{8,16},{80,24},{56,32},{96,40},{40,48},{112,56},{88,... | collective-permute-start | bytes 196616 | tf_op jit(solution)/shard_map/ppermute | solution.py:96
  50.9 6.6 %collective-permute-start.14 = (f32[416,128]{1,0:T(8,128)S(1)}, f32[416,128]{1,0:T(8,128)S(1)}, u32[]{:S(2)}, u32[]{:S(2)}) collective-permute-start(f32[416,128]{1,0:T(8,128)S(1)} %first_sum.1.refs_1_.refs_4_.refs_0_), channel_id=1, source_target_pairs={{0,200},{8,48},{16,40},{24,208},{32,232},{40,16},{48,8},{56,240},{... | collective-permute-start | bytes 638984 | tf_op jit(solution)/shard_map/ppermute | solution.py:100
  52.6 1.3 %collective-permute-start.15 = (f32[128,128]{1,0:T(8,128)S(1)}, f32[128,128]{1,0:T(8,128)S(1)}, u32[]{:S(2)}, u32[]{:S(2)}) collective-permute-start(f32[128,128]{1,0:T(8,128)S(1)} %hold_split.1.refs_2_), channel_id=1, source_target_pairs={{0,8},{8,0},{16,24},{24,16},{32,40},{40,32},{48,56},{56,48},{64,72... | collective-permute-start | bytes 196616 | tf_op jit(solution)/shard_map/ppermute | solution.py:92
  57.5 5.4 %collective-permute-start.16 = (f32[416,128]{1,0:T(8,128)S(1)}, f32[416,128]{1,0:T(8,128)S(1)}, u32[]{:S(2)}, u32[]{:S(2)}) collective-permute-start(f32[416,128]{1,0:T(8,128)S(1)} %second_sum.1.refs_2_.refs_0_), channel_id=1, source_target_pairs={{0,72},{8,16},{16,8},{24,80},{32,104},{40,48},{48,40},{56,112},{64... | collective-permute-start | bytes 638984 | tf_op jit(solution)/shard_map/ppermute | solution.py:100
  63.1 5.4 %collective-permute-start.17 = (bf16[416,128]{1,0:T(8,128)(2,1)S(1)}, bf16[416,128]{1,0:T(8,128)(2,1)S(1)}, u32[]{:S(2)}, u32[]{:S(2)}) collective-permute-start(bf16[416,128]{1,0:T(8,128)(2,1)S(1)} %block.1.refs_3_.refs_0_), channel_id=1, source_target_pairs={{0,56},{8,192},{16,216},{24,32},{32,24},{40,224},{48,248},{56,0},{... | collective-permute-start | bytes 319496 | tf_op jit(solution)/shard_map/ppermute | solution.py:100
  68.5 5.4 %collective-permute-start.18 = (bf16[832,128]{1,0:T(8,128)(2,1)S(1)}, bf16[832,128]{1,0:T(8,128)(2,1)S(1)}, u32[]{:S(2)}, u32[]{:S(2)}) collective-permute-start(bf16[832,128]{1,0:T(8,128)(2,1)S(1)} %join1.1.refs_0_), channel_id=1, source_target_pairs={{0,24},{8,64},{16,88},{24,0},{32,56},{40,96},{48,120},{56,32},{64,... | collective-permute-start | bytes 638984 | tf_op jit(solution)/shard_map/ppermute | solution.py:100
  68.7 4.1 %collective-permute-start.20 = (f32[8,128]{1,0:T(8,128)S(1)}, f32[8,128]{1,0:T(8,128)S(1)}, u32[]{:S(2)}, u32[]{:S(2)}) collective-permute-start(f32[8,128]{1,0:T(8,128)S(1)} %squares.1.refs_2_), channel_id=1, source_target_pairs={{0,25},{1,24},{2,27},{3,26},{4,29},{5,28},{6,31},{7,30},{8,65},{9,... | collective-permute-start | bytes 12296 | tf_op jit(solution)/shard_map/ppermute | solution.py:80
  69.4 3.6 %collective-permute-start.19 = (f32[8,128]{1,0:T(8,128)S(1)}, f32[8,128]{1,0:T(8,128)S(1)}, u32[]{:S(2)}, u32[]{:S(2)}) collective-permute-start(f32[8,128]{1,0:T(8,128)S(1)} %squares.1.refs_2_), channel_id=1, source_target_pairs={{0,1},{1,0},{2,3},{3,2},{4,5},{5,4},{6,7},{7,6},{8,9},{9,8},{10,11... | collective-permute-start | bytes 12296 | tf_op jit(solution)/shard_map/ppermute | solution.py:80
  74.1 5.0 %collective-permute-start.21 = (bf16[1664,128]{1,0:T(8,128)(2,1)S(1)}, bf16[1664,128]{1,0:T(8,128)(2,1)S(1)}, u32[]{:S(2)}, u32[]{:S(2)}) collective-permute-start(bf16[1664,128]{1,0:T(8,128)(2,1)S(1)} %get-tuple-element.27.refs_0_), channel_id=1, source_target_pairs={{0,8},{8,0},{16,24},{24,16},{32,40},{40,32},{48,56},{56,48},{64,72... | collective-permute-start | bytes 1277960 | tf_op jit(solution)/shard_map/ppermute | solution.py:92
  74.5 1.8 %collective-permute-start.22 = (f32[8,128]{1,0:T(8,128)S(1)}, f32[8,128]{1,0:T(8,128)S(1)}, u32[]{:S(2)}, u32[]{:S(2)}) collective-permute-start(f32[8,128]{1,0:T(8,128)S(1)} %get-tuple-element.28.refs_0_), channel_id=1, source_target_pairs={{0,8},{8,0},{16,24},{24,16},{32,40},{40,32},{48,56},{56,48},{64,72... | collective-permute-start | bytes 12296 | tf_op jit(solution)/shard_map/ppermute | solution.py:92
  74.7 6.1 %collective-permute-start.23 = (f32[8,128]{1,0:T(8,128)S(1)}, f32[8,128]{1,0:T(8,128)S(1)}, u32[]{:S(2)}, u32[]{:S(2)}) collective-permute-start(f32[8,128]{1,0:T(8,128)S(1)} %get-tuple-element.28.refs_0_), channel_id=1, source_target_pairs={{13,0},{12,1},{15,2},{14,3},{9,4},{8,5},{11,6},{10,7},{5,8},{4,9},... | collective-permute-start | bytes 12296 | tf_op jit(solution)/shard_map/ppermute | solution.py:88
  76.4 4.4 %collective-permute-start.24 = (f32[8,128]{1,0:T(8,128)S(1)}, f32[8,128]{1,0:T(8,128)S(1)}, u32[]{:S(2)}, u32[]{:S(2)}) collective-permute-start(f32[8,128]{1,0:T(8,128)S(1)} %add_core.1.refs_2_.sq_ref), channel_id=1, source_target_pairs={{15,0},{10,1},{9,2},{12,3},{11,4},{14,5},{13,6},{8,7},{2,8},{7,9},... | collective-permute-start | bytes 12296 | tf_op jit(solution)/shard_map/ppermute | solution.py:88
  79.2 2.8 %copy-start = (bf16[256,3328]{1,0:T(8,128)(2,1)S(1)}, bf16[256,3328]{1,0:T(8,128)(2,1)}, u32[]{:S(2)}) copy-start(bf16[256,3328]{1,0:T(8,128)(2,1)} %weights_ref.1) | copy-start | bytes 5111812
  80.8 1.3 %collective-permute-start.25 = (f32[16,128]{1,0:T(8,128)S(1)}, f32[16,128]{1,0:T(8,128)S(1)}, u32[]{:S(2)}, u32[]{:S(2)}) collective-permute-start(f32[16,128]{1,0:T(8,128)S(1)} %stack.1.moved_ref), channel_id=1, source_target_pairs={{0,8},{8,0},{16,24},{24,16},{32,40},{40,32},{48,56},{56,48},{64,72... | collective-permute-start | bytes 24584 | tf_op jit(solution)/shard_map/ppermute | solution.py:92
